TPU v7x, 32 devices: a whole 2x2x4 slice. The times are simulated.
32 devices in a mesh: cells: 8 (over y, x, core), comp: 4 (over z).
Axes of the slice: x: 2, y: 2, z: 4, core: 2. Of those that a mesh axis runs over, the one named last changes fastest.
Arguments:
- factor_field: float32 [16, 256, 256], P(None, ('cells', 'comp')), may hold values from -90 to 90
- profile: float32 [512, 128], P('comp'), may hold values from -4 to 4
- mixing: float32 [16, 512], P(None, 'comp'), may hold values from -1.5 to 1.5
- factor_mom: float32 [16, 256, 256], P(None, ('cells', 'comp')), may hold values from -6 to 6
- profile_mom: float32 [512, 128], P('comp'), may hold values from -6 to 6
- mixing_mom: float32 [16, 512], P(None, 'comp'), may hold values from -6 to 6
- field_tau: float32 [16], replicated, may hold values from 0.5 to 5
- counts: int32 [128, 256, 256], P(None, 'cells'), may hold values from 0 to 15
- land_mask: int32 [256, 256], P('cells'), may hold values 0 or 1
- log_exposure: float32 [256, 256], P('cells'), may hold values from -4 to -2
Outputs:
- new_field: float32 [16, 256, 256], P(None, ('cells', 'comp'))
- new_profile: float32 [512, 128], P('comp')
- new_mixing: float32 [16, 512], P(None, 'comp')
- new_factor_mom: float32 [16, 256, 256], P(None, ('cells', 'comp'))
- new_profile_mom: float32 [512, 128], P('comp')
- new_mixing_mom: float32 [16, 512], P(None, 'comp')
- hamiltonian: float32 [], replicated
All inputs are finite; a program needn't handle non-finite values. No bound on the sum of `land_mask` on one device may be relied on, other than what follows from the above.
Results may differ from a plain program's by a relative error of at most 0.0003.
Values sent between devices are 32-bit elements; how exact they have to be, the bound alone decides.
No kernel may reach another device: no remote copies, remote signals or barrier semaphores. Data moves between devices by JAX's collectives and lax.ppermute only.
A program may use at most 64 MiB of HBM per device.

v0:
```python
import functools
import math

import jax
import jax.numpy as jnp
from jax import lax
from jax.experimental import pallas as pl
from jax.experimental.pallas import tpu as pltpu
from jax.sharding import PartitionSpec as P


def extended(cells, sides, width):
    for axis, dim in sides:
        count = lax.axis_size(axis)
        ends = count - 1
        head = lax.slice_in_dim(cells, 0, width, axis=dim)
        tail = lax.slice_in_dim(cells, cells.shape[dim] - width, cells.shape[dim], axis=dim)
        cells = jnp.concatenate(
            [
                lax.ppermute(tail, axis, [(i, (i + 1) % count) for i in range(ends)]),
                cells,
                lax.ppermute(head, axis, [((i + 1) % count, i) for i in range(ends)]),
            ],
            axis=dim,
        )
    return cells


def field_prior(padded, land_pad, field_tau):
    ridge = 0.1
    step_x = padded[:, 1:, :] - padded[:, :-1, :]
    edge_x = land_pad[1:, :] * land_pad[:-1, :]
    flux_x = edge_x[None, :, :] * step_x
    centre = padded[:, 1:-1, :]
    land_mid = land_pad[1:-1, :]
    step_y = centre[:, :, 1:] - centre[:, :, :-1]
    edge_y = land_mid[:, 1:] * land_mid[:, :-1]
    flux_y = edge_y[None, :, :] * step_y
    lap_x = flux_x[:, :-1, :] - flux_x[:, 1:, :]
    lap_y = jnp.pad(flux_y, ((0, 0), (0, 0), (1, 0))) - jnp.pad(flux_y, ((0, 0), (0, 0), (0, 1)))
    tau_cube = field_tau[:, None, None]
    grad = -tau_cube * (lap_x + lap_y + ridge * centre)
    energy = 0.5 * jnp.sum(tau_cube * (flux_x[:, 1:, :] * step_x[:, 1:, :]))
    energy = energy + 0.5 * jnp.sum(tau_cube * (flux_y * step_y))
    energy = energy + 0.5 * ridge * jnp.sum(tau_cube * (centre * centre))
    return (grad, energy)


def tile_scores(flat_tile, count_rows, exposure, profile, mixing):
    prof_exp = jnp.exp(profile)
    rate_total = jnp.sum(prof_exp, axis=1)
    mix_logit = jnp.dot(mixing.T, flat_tile, precision=lax.Precision.HIGHEST)
    fit_score = (
        jnp.dot(profile, count_rows, precision=lax.Precision.HIGHEST)
        - rate_total[:, None] * exposure[None, :]
    )
    return (mix_logit, mix_logit + fit_score)


def tile_grads(
    flat_tile, count_rows, land_weight, exposure, mixing, mix_logit, joint_score, log_mix, log_joint
):
    prior_share = jnp.exp(mix_logit - log_mix[None, :])
    posterior = jnp.exp(joint_score - log_joint[None, :])
    post_land = posterior * land_weight[None, :]
    gap_weight = (posterior - prior_share) * land_weight[None, :]
    grad_counts = jnp.dot(post_land, count_rows.T, precision=lax.Precision.HIGHEST)
    rate_mass = jnp.sum(post_land * exposure[None, :], axis=1)
    grad_mix = jnp.dot(flat_tile, gap_weight.T, precision=lax.Precision.HIGHEST)
    field_lik = jnp.dot(mixing, gap_weight, precision=lax.Precision.HIGHEST)
    log_dens = jnp.sum(land_weight * (log_joint - log_mix))
    return (grad_counts, rate_mass, grad_mix, field_lik, log_dens)


def log_sum(scores):
    top = jnp.max(scores, axis=0)
    return top + jnp.log(jnp.sum(jnp.exp(scores - top[None, :]), axis=0))


def plain_device(
    factor_field,
    profile,
    mixing,
    factor_mom,
    profile_mom,
    mixing_mom,
    field_tau,
    counts,
    land_mask,
    log_exposure,
):
    step_field = 0.05
    step_profile = 0.002
    step_mixing = 0.002
    tile_rows, tile_cols = land_mask.shape
    ncat = counts.shape[0]
    share_rows = factor_field.shape[1]
    comp_rank = lax.axis_index("comp")
    cells_rank = lax.axis_index("cells")
    first_cells = cells_rank == 0
    land_pad = extended(land_mask, (("cells", 0),), 1).astype(jnp.float32)
    row_start = comp_rank * share_rows
    count_rows = lax.dynamic_slice_in_dim(counts, row_start, share_rows, 1)
    count_rows = count_rows.reshape(ncat, share_rows * tile_cols).astype(jnp.float32)
    land_weight = (
        lax.dynamic_slice_in_dim(land_mask, row_start, share_rows, 0)
        .reshape(-1)
        .astype(jnp.float32)
    )
    exposure = jnp.exp(lax.dynamic_slice_in_dim(log_exposure, row_start, share_rows, 0).reshape(-1))
    land_near = lax.dynamic_slice_in_dim(land_pad, row_start, share_rows + 2, 0)

    def evaluate(share_field, profile_now, mixing_now):
        padded = extended(share_field, ((("cells", "comp"), 1),), 1)
        prior_grad, prior_energy = field_prior(padded, land_near, field_tau)
        profile_all, mixing_all = (
            lax.all_gather(profile_now, "comp", axis=0, tiled=True),
            lax.all_gather(mixing_now, "comp", axis=1, tiled=True),
        )
        flat_tile = share_field.reshape(share_field.shape[0], -1)
        mix_logit, joint_score = tile_scores(
            flat_tile, count_rows, exposure, profile_all, mixing_all
        )
        log_mix = log_sum(mix_logit)
        log_joint = log_sum(joint_score)
        grad_counts, rate_mass, grad_mix, field_lik, log_dens = tile_grads(
            flat_tile,
            count_rows,
            land_weight,
            exposure,
            mixing_all,
            mix_logit,
            joint_score,
            log_mix,
            log_joint,
        )
        grad_counts, rate_mass, mix_rows = (
            lax.psum_scatter(grad_counts, "comp", scatter_dimension=0, tiled=True),
            lax.psum_scatter(rate_mass, "comp", scatter_dimension=0, tiled=True),
            lax.psum_scatter(grad_mix.T, "comp", scatter_dimension=0, tiled=True),
        )
        grad_mix = mix_rows.T
        grad_field = prior_grad + field_lik.reshape(share_field.shape)
        log_part = log_dens - prior_energy
        grad_counts, rate_mass, grad_mix = lax.psum((grad_counts, rate_mass, grad_mix), "cells")
        grad_profile = grad_counts - jnp.exp(profile_now) * rate_mass[:, None] - 0.25 * profile_now
        grad_mixing = grad_mix - mixing_now
        param_prior = -0.125 * jnp.sum(profile_now * profile_now) - 0.5 * jnp.sum(
            mixing_now * mixing_now
        )
        log_part = log_part + jnp.where(first_cells, param_prior, 0.0)
        return (log_part, grad_field, grad_profile, grad_mixing)

    first = evaluate(factor_field, profile, mixing)
    half_field = factor_mom + 0.5 * step_field * first[1]
    half_profile = profile_mom + 0.5 * step_profile * first[2]
    half_mixing = mixing_mom + 0.5 * step_mixing * first[3]
    new_field = factor_field + step_field * half_field
    new_profile = profile + step_profile * half_profile
    new_mixing = mixing + step_mixing * half_mixing
    second = evaluate(new_field, new_profile, new_mixing)
    new_factor_mom = half_field + 0.5 * step_field * second[1]
    new_profile_mom = half_profile + 0.5 * step_profile * second[2]
    new_mixing_mom = half_mixing + 0.5 * step_mixing * second[3]
    kinetic = 0.5 * jnp.sum(new_factor_mom * new_factor_mom)
    kinetic = kinetic + jnp.where(
        first_cells,
        0.5
        * (jnp.sum(new_profile_mom * new_profile_mom) + jnp.sum(new_mixing_mom * new_mixing_mom)),
        0.0,
    )
    log_total, kinetic_total = lax.psum((second[0], kinetic), ("cells", "comp"))
    cell_count = tile_rows * tile_cols * lax.axis_size("cells")
    hamiltonian = (kinetic_total - log_total) / cell_count
    return (
        new_field,
        new_profile,
        new_mixing,
        new_factor_mom,
        new_profile_mom,
        new_mixing_mom,
        hamiltonian,
    )


STEP_FIELD = 0.05
STEP_PARAM = 0.002
RIDGE = 0.1
LOG2E = math.log2(math.e)
LN2 = math.log(2.0)
LANES = 128
F32 = jnp.float32
BF16 = jnp.bfloat16


def pieces(values, count):
    parts = []
    for _ in range(count):
        part = values.astype(BF16)
        parts.append(part)
        values = values - part.astype(F32)
    return parts


def dot(left, right, dims=((1,), (0,))):
    return lax.dot_general(left, right, (dims, ((), ())), preferred_element_type=F32)


def partner(values, axis, flip):
    count = lax.axis_size(axis)
    return lax.ppermute(values, axis, [(i, i ^ flip) for i in range(count)])


def all_sum(keep, send):
    pairs = keep.shape[0]
    ring = lax.axis_size("comp")
    chunks = keep + partner(send, "cells", 1)
    total = chunks[0]
    for part in [partner(chunks[k], "cells", 2 * k) for k in range(1, pairs)]:
        total = total + part
    parts = [partner(total, "comp", k) for k in range(1, ring)]
    for part in parts:
        total = total + part
    near = jnp.stack([total] + [partner(total, "cells", 2 * k) for k in range(1, pairs)])
    return near, partner(near, "cells", 1)


def chunk_index(cells_rank, k, other):
    core = cells_rank % 2
    return (((cells_rank // 2) ^ k) * 2) + (1 - core if other else core)


def gather_chunks(flat_ref, near_ref, far_ref, cells_rank):
    pairs, rows, _ = near_ref.shape
    for k in range(pairs):
        for source, other in ((near_ref, False), (far_ref, True)):
            start = pl.multiple_of(chunk_index(cells_rank, k, other) * rows, 8)
            flat_ref[pl.ds(start, rows), :] = source[k]


def spread_chunks(flat_ref, keep_ref, send_ref, cells_rank):
    pairs, rows, _ = keep_ref.shape
    for k in range(pairs):
        for target, other in ((keep_ref, False), (send_ref, True)):
            start = pl.multiple_of(chunk_index(cells_rank, k, other) * rows, 8)
            target[k] = flat_ref[pl.ds(start, rows), :]


def load_params(flat_ref, left_ref, mix_ref, load_ref, ncomp, nfac):
    lane = lax.broadcasted_iota(jnp.int32, (LANES, LANES), 1)
    first = 6 * nfac
    for q in range(ncomp // LANES):
        rows = pl.ds(q * LANES, LANES)
        prof = flat_ref[rows, :]
        high, mid, low = pieces(prof * LOG2E, 3)
        left_ref[rows, 0:LANES] = high
        left_ref[rows, 2 * LANES : 3 * LANES] = mid
        left_ref[rows, 3 * LANES : 4 * LANES] = low
        rate = jnp.sum(jnp.exp(prof), axis=1, keepdims=True) * LOG2E
        rate_high, rate_mid, rate_low = [part.astype(F32) for part in pieces(rate, 3)]
        load = flat_ref[pl.ds(ncomp + q * nfac, nfac), :]
        w_high, w_mid, w_low = [part.astype(F32) for part in pieces(load * LOG2E, 3)]
        stack = jnp.concatenate(
            [w_high, w_high, w_high, w_mid, w_mid, w_low, jnp.zeros((LANES - first, LANES), F32)], axis=0
        )
        turned = stack.T
        mix_ref[rows, :] = turned.astype(BF16)
        rate_part = jnp.where(
            (lane >= first) & (lane < first + 3),
            rate_high,
            jnp.where(
                (lane >= first + 3) & (lane < first + 5), rate_mid, jnp.where(lane == first + 5, rate_low, 0.0)
            ),
        )
        left_ref[rows, LANES : 2 * LANES] = (turned - rate_part).astype(BF16)
        load_high, load_mid = pieces(load, 2)
        load_ref[0:nfac, q * LANES : (q + 1) * LANES] = load_high
        load_ref[nfac : 2 * nfac, q * LANES : (q + 1) * LANES] = load_mid


def load_cells(counts_ref, field_ref, logexp_ref, right_ref, wide_ref):
    share, ncat, cols = counts_ref.shape
    nfac = field_ref.shape[1]
    exposure = jnp.exp(logexp_ref[...])
    sub = lax.broadcasted_iota(jnp.int32, (LANES - 6 * nfac, cols), 0)
    for r in range(share):
        count = counts_ref[r]
        high, mid, low = pieces(field_ref[r], 3)
        e_high, e_mid, e_low = [part.astype(F32) for part in pieces(exposure[r : r + 1, :], 3)]
        e_rows = jnp.where((sub == 0) | (sub == 3) | (sub == 5), e_high, 0.0)
        e_rows = jnp.where((sub == 1) | (sub == 4), e_mid, e_rows)
        e_rows = jnp.where(sub == 2, e_low, e_rows).astype(BF16)
        extra = jnp.concatenate([high, mid, low, high, mid, high, e_rows], axis=0)
        right_ref[r, 0:ncat, :] = count
        right_ref[r, LANES : 2 * LANES, :] = extra
        right_ref[r, 2 * LANES : 2 * LANES + ncat, :] = count
        right_ref[r, 3 * LANES : 3 * LANES + ncat, :] = count
        for side in range(2):
            wide_ref[r, 0:ncat, side * cols : (side + 1) * cols] = count
            wide_ref[r, LANES : 2 * LANES, side * cols : (side + 1) * cols] = extra


def load_prior(field_ref, low_ref, high_ref, land, tau_ref, prior_ref):
    share, nfac, cols = field_ref.shape
    row = lax.broadcasted_iota(jnp.int32, (nfac, cols), 0)
    col = lax.broadcasted_iota(jnp.int32, (nfac, cols), 1)
    tau = jnp.zeros((nfac, cols), F32)
    for j in range(nfac):
        tau = jnp.where(row == j, tau_ref[j], tau)
    inner = col < cols - 1
    energy = jnp.zeros((nfac, cols), F32)
    ups = [low_ref[0:nfac, :]] + [field_ref[r] for r in range(share)] + [high_ref[0:nfac, :]]
    lands = [low_ref[nfac : nfac + 1, :]] + [land[r : r + 1, :] for r in range(share)]
    lands = lands + [high_ref[nfac : nfac + 1, :]]
    lands = [jnp.broadcast_to(x, (nfac, cols)) for x in lands]
    for r in range(share):
        here = ups[r + 1]
        step_up = here - ups[r]
        step_down = here - ups[r + 2]
        edge_up = lands[r] * lands[r + 1]
        edge_down = lands[r + 1] * lands[r + 2]
        step_right = here - pltpu.roll(here, cols - 1, 1)
        edge_right = jnp.where(inner, lands[r + 1] * pltpu.roll(lands[r + 1], cols - 1, 1), 0.0)
        flux_right = edge_right * step_right
        flux_down = edge_down * step_down
        laplace = edge_up * step_up + flux_down + flux_right - pltpu.roll(flux_right, 1, 1)
        prior_ref[r] = -tau * (laplace + RIDGE * here)
        energy = energy + 0.5 * tau * (flux_down * step_down + flux_right * step_right + RIDGE * (here * here))
    return energy


def row_shares(
    r, ncomp, right_ref, wide_ref, left_ref, mix_ref, load_ref, land_ref, score_ref, logit_ref, post_ref, gap_ref,
    acc_ref, accw_ref,
):
    cols = right_ref.shape[2]
    nfac = load_ref.shape[0] // 2
    block = 64
    score_ref[...] = dot(left_ref[...], right_ref[r])
    logit_ref[...] = dot(mix_ref[...], right_ref[r, LANES : 2 * LANES, :])
    top_s = jnp.full((8, cols), -jnp.inf, F32)
    top_a = jnp.full((8, cols), -jnp.inf, F32)
    for i in range(0, ncomp, block):
        top_s = jnp.maximum(top_s, jnp.max(score_ref[i : i + block, :].reshape(block // 8, 8, cols), axis=0))
        top_a = jnp.maximum(top_a, jnp.max(logit_ref[i : i + block, :].reshape(block // 8, 8, cols), axis=0))
    top_s = jnp.max(top_s, axis=0, keepdims=True)
    top_a = jnp.max(top_a, axis=0, keepdims=True)
    sum_s = jnp.zeros((8, cols), F32)
    sum_a = jnp.zeros((8, cols), F32)
    for i in range(0, ncomp, block):
        part_s = jnp.exp2(score_ref[i : i + block, :] - top_s)
        part_a = jnp.exp2(logit_ref[i : i + block, :] - top_a)
        score_ref[i : i + block, :] = part_s
        logit_ref[i : i + block, :] = part_a
        sum_s = sum_s + jnp.sum(part_s.reshape(block // 8, 8, cols), axis=0)
        sum_a = sum_a + jnp.sum(part_a.reshape(block // 8, 8, cols), axis=0)
    sum_s = jnp.sum(sum_s, axis=0, keepdims=True)
    sum_a = jnp.sum(sum_a, axis=0, keepdims=True)
    land = land_ref[r][0:1, :]
    inv_s = land / sum_s
    inv_a = land / sum_a
    for i in range(0, ncomp, block):
        post = score_ref[i : i + block, :] * inv_s
        gap = post - logit_ref[i : i + block, :] * inv_a
        for target, values in ((post_ref, post), (gap_ref, gap)):
            high, low = pieces(values, 2)
            target[i : i + block, 0:cols] = high
            target[i : i + block, cols : 2 * cols] = low
    last = ((1,), (1,))
    acc_ref[...] += dot(post_ref[...], wide_ref[r], last)
    accw_ref[...] += dot(gap_ref[...], wide_ref[r, LANES : 2 * LANES, :], last)
    lik = dot(load_ref[...], gap_ref[...])
    lik = lik[0:nfac] + lik[nfac : 2 * nfac]
    lik = lik[:, 0:cols] + lik[:, cols : 2 * cols]
    log_dens = land * (LN2 * ((top_s + jnp.log2(sum_s)) - (top_a + jnp.log2(sum_a))))
    return lik, log_dens


def param_grads(flat_ref, acc_ref, accw_ref, grad_ref, ncomp, nfac):
    lane = lax.broadcasted_iota(jnp.int32, (LANES, LANES), 1)
    rate_lanes = (lane >= 6 * nfac) & (lane < 6 * nfac + 3)
    for q in range(ncomp // LANES):
        rows = pl.ds(q * LANES, LANES)
        mass = jnp.sum(jnp.where(rate_lanes, acc_ref[rows, LANES : 2 * LANES], 0.0), axis=1, keepdims=True)
        grad_ref[rows, :] = acc_ref[rows, 0:LANES] - jnp.exp(flat_ref[rows, :]) * mass
        turned = accw_ref[rows, :].T
        grad_ref[pl.ds(ncomp + q * nfac, nfac), :] = (
            turned[0:nfac] + turned[nfac : 2 * nfac] + turned[2 * nfac : 3 * nfac]
        )


def first_kernel(
    ncomp, rank_ref, tau_ref, counts_ref, field_ref, mom_ref, land_ref, logexp_ref, low_ref, high_ref, pmom_ref, wmom_ref,
    *refs,
):
    ring = ncomp // pmom_ref.shape[0]
    part_refs = refs[:ring]
    (new_ref, half_ref, top_ref, bottom_ref, grad_ref, keep_ref, send_ref) = refs[ring : ring + 7]
    (flat, left, mix, load, right, wide, prior, land_rows, score, logit, post, gap, acc, accw) = refs[ring + 7 :]
    cells_rank, comp_rank = rank_ref[0], rank_ref[1]
    share, nfac, cols = field_ref.shape
    mine = pmom_ref.shape[0]
    for k in range(ring):
        group = comp_rank ^ k
        flat[pl.ds(pl.multiple_of(group * mine, mine), mine), :] = part_refs[k][0:mine, :]
        flat[pl.ds(pl.multiple_of(ncomp + group * nfac, nfac), nfac), :] = part_refs[k][mine : mine + nfac, :]
    land = land_ref[...].astype(F32)
    for r in range(share):
        land_rows[r] = jnp.broadcast_to(land[r : r + 1, :], (8, cols))
    load_params(flat, left, mix, load, ncomp, nfac)
    load_cells(counts_ref, field_ref, logexp_ref, right, wide)
    load_prior(field_ref, low_ref, high_ref, land, tau_ref, prior)
    acc[...] = jnp.zeros_like(acc)
    accw[...] = jnp.zeros_like(accw)

    def step(r, carry):
        lik, _ = row_shares(
            r, ncomp, right, wide, left, mix, load, land_rows, score, logit, post, gap, acc, accw
        )
        prior[r] = prior[r] + lik
        return carry

    lax.fori_loop(0, share, step, 0)
    for r in range(share):
        half = mom_ref[r] + 0.5 * STEP_FIELD * prior[r]
        fresh = field_ref[r] + STEP_FIELD * half
        half_ref[r] = half
        new_ref[r] = fresh
        if r == 0:
            top_ref[...] = fresh
        if r == share - 1:
            bottom_ref[...] = fresh
    param_grads(flat, acc, accw, grad_ref, ncomp, nfac)
    nparam = grad_ref.shape[0]
    if flat.shape[0] > nparam:
        flat[nparam:, :] = jnp.zeros((flat.shape[0] - nparam, LANES), F32)
    flat[0:nparam, :] = 0.5 * STEP_PARAM * STEP_PARAM * grad_ref[...]
    own_prof, own_load = part_refs[0][0:mine, :], part_refs[0][mine : mine + nfac, :]
    owner = cells_rank == 0
    base_prof = own_prof + STEP_PARAM * (pmom_ref[...] - 0.5 * STEP_PARAM * 0.25 * own_prof)
    base_load = own_load + STEP_PARAM * (wmom_ref[...] - 0.5 * STEP_PARAM * own_load)
    flat[pl.ds(pl.multiple_of(comp_rank * mine, mine), mine), :] += jnp.where(owner, base_prof, 0.0)
    flat[pl.ds(pl.multiple_of(ncomp + comp_rank * nfac, nfac), nfac), :] += jnp.where(owner, base_load, 0.0)
    spread_chunks(flat, keep_ref, send_ref, cells_rank)


def second_kernel(
    ncomp, rank_ref, tau_ref, counts_ref, field_ref, half_ref, land_ref, logexp_ref, low_ref, high_ref, pmom_ref, wmom_ref,
    own_ref, near_ref, far_ref, grad0_ref, mom_ref, prof_ref, mixing_ref, keep_ref, send_ref,
    flat, left, mix, load, right, wide, prior, land_rows, score, logit, post, gap, acc, accw, out, grad,
):
    cells_rank, comp_rank = rank_ref[0], rank_ref[1]
    share, nfac, cols = field_ref.shape
    mine = pmom_ref.shape[0]
    nparam = grad0_ref.shape[0]
    gather_chunks(flat, near_ref, far_ref, cells_rank)
    new_prof = flat[pl.ds(pl.multiple_of(comp_rank * mine, mine), mine), :]
    new_load = flat[pl.ds(pl.multiple_of(ncomp + comp_rank * nfac, nfac), nfac), :]
    prof_ref[...] = new_prof
    mixing_ref[...] = new_load
    land = land_ref[...].astype(F32)
    for r in range(share):
        land_rows[r] = jnp.broadcast_to(land[r : r + 1, :], (8, cols))
    load_params(flat, left, mix, load, ncomp, nfac)
    load_cells(counts_ref, field_ref, logexp_ref, right, wide)
    energy = load_prior(field_ref, low_ref, high_ref, land, tau_ref, prior)
    acc[...] = jnp.zeros_like(acc)
    accw[...] = jnp.zeros_like(accw)

    def step(r, log_dens):
        lik, part = row_shares(
            r, ncomp, right, wide, left, mix, load, land_rows, score, logit, post, gap, acc, accw
        )
        prior[r] = prior[r] + lik
        return log_dens + part

    log_dens = lax.fori_loop(0, share, step, jnp.zeros((1, cols), F32))
    for r in range(share):
        fresh = half_ref[r] + 0.5 * STEP_FIELD * prior[r]
        mom_ref[r] = fresh
        energy = energy + 0.5 * (fresh * fresh)
    param_grads(flat, acc, accw, grad, ncomp, nfac)
    first_device = (cells_rank == 0) & (comp_rank == 0)
    prof_all = flat[0:ncomp, :]
    load_all = flat[ncomp:nparam, :]
    param_energy = jnp.sum(0.125 * (prof_all * prof_all)) + jnp.sum(0.5 * (load_all * load_all))
    total = jnp.sum(energy) - jnp.sum(log_dens) + jnp.where(first_device, param_energy, 0.0)
    out[0:nparam, :] = 0.5 * STEP_PARAM * (grad0_ref[...] + grad[...])
    tail = out.shape[0] - nparam
    spot = lax.broadcasted_iota(jnp.int32, (tail, LANES), 0) + lax.broadcasted_iota(jnp.int32, (tail, LANES), 1)
    out[nparam:, :] = jnp.where(spot == 0, total, 0.0)
    owner = cells_rank == 0
    old_prof, old_load = own_ref[0:mine, :], own_ref[mine : mine + nfac, :]
    base_prof = pmom_ref[...] - 0.5 * STEP_PARAM * 0.25 * (old_prof + new_prof)
    base_load = wmom_ref[...] - 0.5 * STEP_PARAM * (old_load + new_load)
    out[pl.ds(pl.multiple_of(comp_rank * mine, mine), mine), :] += jnp.where(owner, base_prof, 0.0)
    out[pl.ds(pl.multiple_of(ncomp + comp_rank * nfac, nfac), nfac), :] += jnp.where(owner, base_load, 0.0)
    spread_chunks(out, keep_ref, send_ref, cells_rank)


def last_kernel(ncomp, nparam, cells, rank_ref, near_ref, far_ref, prof_ref, mixing_ref, ham_ref, flat):
    cells_rank, comp_rank = rank_ref[0], rank_ref[1]
    mine, nfac = prof_ref.shape[0], mixing_ref.shape[0]
    gather_chunks(flat, near_ref, far_ref, cells_rank)
    prof_ref[...] = flat[pl.ds(pl.multiple_of(comp_rank * mine, mine), mine), :]
    mixing_ref[...] = flat[pl.ds(pl.multiple_of(ncomp + comp_rank * nfac, nfac), nfac), :]
    momenta = flat[0:nparam, :]
    rest = flat[nparam:, :]
    ham_ref[0, 0] = (0.5 * jnp.sum(momenta * momenta) + jnp.sum(rest)) / cells


def fast_device(
    factor_field, profile, mixing, factor_mom, profile_mom, mixing_mom, field_tau, counts, land_mask, log_exposure
):
    nfac, share, cols = factor_field.shape
    mine, ncat = profile.shape
    tile_rows = land_mask.shape[0]
    ring = lax.axis_size("comp")
    tiles = lax.axis_size("cells")
    ncomp = mine * ring
    nparam = ncomp + nfac * ncomp // LANES
    pairs = tiles // 2
    round_up = lambda rows: -(-rows // (8 * tiles)) * 8
    chunk_one = round_up(nparam)
    chunk_two = round_up(nparam + 1)
    comp_rank = lax.axis_index("comp")
    cells_rank = lax.axis_index("cells")
    ranks = jnp.stack([cells_rank, comp_rank]).astype(jnp.int32)
    pack = jnp.concatenate([profile, mixing], axis=0)
    parts = [pack] + [partner(pack, "comp", k) for k in range(1, ring)]

    count_rows = lax.dynamic_slice_in_dim(counts, comp_rank * share, share, 1).swapaxes(0, 1).astype(BF16)
    field_rows = factor_field.swapaxes(0, 1)
    mom_rows = factor_mom.swapaxes(0, 1)
    both = ("cells", "comp")
    last = tiles * ring - 1
    forward = [(i, i + 1) for i in range(last)]
    backward = [(i + 1, i) for i in range(last)]
    land_edge = lambda row: lax.dynamic_slice_in_dim(land_mask, row, 1, 0).astype(F32)
    edges = [
        jnp.concatenate([factor_field[:, r, :], jnp.broadcast_to(land_edge(comp_rank * share + r), (8, cols))], axis=0)
        for r in (share - 1, 0)
    ]
    low = lax.ppermute(edges[0], both, forward)
    high = lax.ppermute(edges[1], both, backward)

    def full(*shape):
        zeros = (0,) * len(shape)
        return pl.BlockSpec(shape, lambda i, ranks: zeros)

    smem = pl.BlockSpec(memory_space=pltpu.SMEM)
    cell_specs = [
        smem,
        full(share, ncat, cols),
        full(share, nfac, cols),
    ]
    row_spec = pl.BlockSpec((share, cols), lambda i, ranks: (ranks[1], 0))
    edge_spec = full(nfac + 8, cols)
    param_specs = [full(mine, ncat), full(nfac, mine)]
    pack_spec = full(mine + nfac, ncat)
    shape = lambda *dims: jax.ShapeDtypeStruct(dims, F32)
    work = [
        pltpu.VMEM((ncomp, 4 * LANES), BF16),
        pltpu.VMEM((ncomp, LANES), BF16),
        pltpu.VMEM((2 * nfac, ncomp), BF16),
        pltpu.VMEM((share, 4 * LANES, cols), BF16),
        pltpu.VMEM((share, 2 * LANES, 2 * cols), BF16),
        pltpu.VMEM((share, nfac, cols), F32),
        pltpu.VMEM((share, 8, cols), F32),
        pltpu.VMEM((ncomp, cols), F32),
        pltpu.VMEM((ncomp, cols), F32),
        pltpu.VMEM((ncomp, 2 * cols), BF16),
        pltpu.VMEM((ncomp, 2 * cols), BF16),
        pltpu.VMEM((ncomp, 2 * LANES), F32),
        pltpu.VMEM((ncomp, LANES), F32),
    ]
    params = pltpu.CompilerParams(vmem_limit_bytes=40 * 1024 * 1024, dimension_semantics=("arbitrary",))

    def call(body, name, ins, outs, scratch):
        return pl.pallas_call(
            body,
            name=name,
            grid_spec=pltpu.PrefetchScalarGridSpec(
                num_scalar_prefetch=1,
                grid=(1,),
                in_specs=ins,
                out_specs=[spec for spec, _ in outs],
                scratch_shapes=scratch,
            ),
            out_shape=[out for _, out in outs],
            compiler_params=params,
        )

    def block(*dims):
        return (full(*dims), shape(*dims))

    first = call(
        functools.partial(first_kernel, ncomp),
        "first_gradient",
        cell_specs + [full(share, nfac, cols), row_spec, row_spec, edge_spec, edge_spec] + param_specs + [pack_spec] * ring,
        [
            block(share, nfac, cols),
            block(share, nfac, cols),
            block(nfac, cols),
            block(nfac, cols),
            block(nparam, LANES),
            block(pairs, chunk_one, LANES),
            block(pairs, chunk_one, LANES),
        ],
        [pltpu.VMEM((tiles * chunk_one, LANES), F32)] + work,
    )
    new_field, half, top, bottom, grad, keep, send = first(
        ranks, field_tau, count_rows, field_rows, mom_rows, land_mask, log_exposure, low, high, profile_mom, mixing_mom,
        *parts,
    )
    low_next = jnp.concatenate([lax.ppermute(bottom, both, forward), low[nfac:]], axis=0)
    high_next = jnp.concatenate([lax.ppermute(top, both, backward), high[nfac:]], axis=0)
    near, far = all_sum(keep, send)
    second = call(
        functools.partial(second_kernel, ncomp),
        "second_gradient",
        cell_specs
        + [full(share, nfac, cols), row_spec, row_spec, edge_spec, edge_spec]
        + param_specs
        + [pack_spec, full(pairs, chunk_one, LANES), full(pairs, chunk_one, LANES), full(nparam, LANES)],
        [
            block(share, nfac, cols),
            block(mine, ncat),
            block(nfac, mine),
            block(pairs, chunk_two, LANES),
            block(pairs, chunk_two, LANES),
        ],
        [pltpu.VMEM((tiles * chunk_one, LANES), F32)]
        + work
        + [pltpu.VMEM((tiles * chunk_two, LANES), F32), pltpu.VMEM((nparam, LANES), F32)],
    )
    new_mom, new_profile, new_mixing, keep, send = second(
        ranks, field_tau, count_rows, new_field, half, land_mask, log_exposure, low_next, high_next, profile_mom, mixing_mom,
        pack, near, far, grad,
    )
    near, far = all_sum(keep, send)
    final = call(
        functools.partial(last_kernel, ncomp, nparam, tile_rows * cols * tiles),
        "momenta",
        [full(pairs, chunk_two, LANES), full(pairs, chunk_two, LANES)],
        [block(mine, ncat), block(nfac, mine), (smem, shape(1, 1))],
        [pltpu.VMEM((tiles * chunk_two, LANES), F32)],
    )
    new_profile_mom, new_mixing_mom, hamiltonian = final(ranks, near, far)
    return (
        new_field.swapaxes(0, 1),
        new_profile,
        new_mixing,
        new_mom.swapaxes(0, 1),
        new_profile_mom,
        new_mixing_mom,
        hamiltonian.reshape(()),
    )


def power_of_two(count):
    return count & (count - 1) == 0


def choose_device(*args):
    factor_field, profile, mixing = args[:3]
    nfac, share, cols = factor_field.shape
    mine, ncat = profile.shape
    tiles, ring = lax.axis_size("cells"), lax.axis_size("comp")
    fits = mine == LANES and ncat == LANES and nfac % 16 == 0 and 6 * nfac + 6 <= LANES
    fits = fits and share == 8 and cols % LANES == 0
    fits = fits and power_of_two(tiles) and tiles > 1 and power_of_two(ring)
    return fast_device(*args) if fits else plain_device(*args)


def solution(mesh):
    in_specs = (
        P(None, ("cells", "comp"), None),
        P("comp", None),
        P(None, "comp"),
        P(None, ("cells", "comp"), None),
        P("comp", None),
        P(None, "comp"),
        P(),
        P(None, "cells", None),
        P("cells", None),
        P("cells", None),
    )
    out_specs = (
        P(None, ("cells", "comp"), None),
        P("comp", None),
        P(None, "comp"),
        P(None, ("cells", "comp"), None),
        P("comp", None),
        P(None, "comp"),
        P(),
    )
    return jax.shard_map(
        choose_device, mesh=mesh, in_specs=in_specs, out_specs=out_specs, check_vma=False
    )
```

profile of v0, /device:TPU:0, one launch (start us, length us, event | category | flops | bytes accessed | tf_op | source)
XLA Modules:
  0.0 100.3 jit_solution(8590391545224604498)
XLA Ops:
  2.3 3.0 %collective-permute-start.2 = (f32[144,128]{1,0:T(8,128)S(1)}, f32[144,128]{1,0:T(8,128)S(1)}, u32[]{:S(2)}, u32[]{:S(2)}) collective-permute-start(f32[144,128]{1,0:T(8,128)S(1)} %constant_dynamic-update-slice_fusion.refs_0_.own_ref), channel_id=1, source_target_pairs={{0,1},{1,0},{2,3},{3,2},{4,5},{5,4},{6,7},{7,6},{8,9},{9,8},{10,11... | collective-permute-start | bytes 221192 | tf_op jit(solution)/shard_map/ppermute | solution.py:211
  5.3 2.6 %collective-permute-start.3 = (f32[144,128]{1,0:T(8,128)S(1)}, f32[144,128]{1,0:T(8,128)S(1)}, u32[]{:S(2)}, u32[]{:S(2)}) collective-permute-start(f32[144,128]{1,0:T(8,128)S(1)} %constant_dynamic-update-slice_fusion.refs_0_.own_ref), channel_id=1, source_target_pairs={{0,2},{1,3},{2,0},{3,1},{4,6},{5,7},{6,4},{7,5},{8,10},{9,11},{10,... | collective-permute-start | bytes 221192 | tf_op jit(solution)/shard_map/ppermute | solution.py:211
  9.7 2.8 %collective-permute-start = (f32[24,256]{1,0:T(8,128)S(1)}, f32[24,256]{1,0:T(8,128)S(1)}, u32[]{:S(2)}, u32[]{:S(2)}) collective-permute-start(f32[24,256]{1,0:T(8,128)S(1)} %pad_maximum_fusion.2), channel_id=1, source_target_pairs={{0,1},{1,2},{2,3},{3,4},{4,5},{5,6},{6,7},{7,8},{8,9},{9,10},{10,1... | collective-permute-start | bytes 73736 | tf_op jit(solution)/shard_map/ppermute | solution.py:544
  12.5 1.3 %collective-permute-start.1 = (f32[24,256]{1,0:T(8,128)S(1)}, f32[24,256]{1,0:T(8,128)S(1)}, u32[]{:S(2)}, u32[]{:S(2)}) collective-permute-start(f32[24,256]{1,0:T(8,128)S(1)} %pad_maximum_fusion.3), channel_id=1, source_target_pairs={{1,0},{2,1},{3,2},{4,3},{5,4},{6,5},{7,6},{8,7},{9,8},{10,9},{11,1... | collective-permute-start | bytes 73736 | tf_op jit(solution)/shard_map/ppermute | solution.py:545
  13.8 1.3 %constant_dynamic-slice_fusion = s32[128,8,256]{2,1,0:T(8,128)S(1)} fusion(s32[128,32,256]{2,1,0:T(8,128)} %param.17, s32[]{:T(128)S(6)} %select_n.7), kind=kLoop, calls=%fused_computation.31 | loop fusion | bytes 2097156 | tf_op jit(solution)/shard_map/dynamic_slice | solution.py:532
  15.6 2.7 %collective-permute-done.1.high_ref = f32[24,256]{1,0:T(8,128)S(1)} collective-permute-done((f32[24,256]{1,0:T(8,128)S(1)}, f32[24,256]{1,0:T(8,128)S(1)}, u32[]{:S(2)}, u32[]{:S(2)}) %collective-permute-start.1) | collective-permute-done | bytes 24608 | tf_op jit(solution)/shard_map/ppermute | solution.py:545
  18.3 11.2 %first_gradient.1 = (f32[8,16,256]{2,1,0:T(8,128)S(1)}, f32[8,16,256]{2,1,0:T(8,128)S(1)}, f32[16,256]{1,0:T(8,128)S(1)}, f32[16,256]{1,0:T(8,128)S(1)}, f32[576...) custom-call(s32[2]{0:T(128)S(1)} %pad_add_fusion.rank_ref, f32[16]{0:T(128)S(1)} %copy-done.4, ...), custom_call_target="tpu_custom_call" | custom-call | tf_op jit(solution)/shard_map/first_gradient/pallas_call | solution.py:612
  29.5 1.1 %collective-permute-start.7 = (f32[4,72,128]{2,1,0:T(8,128)S(1)}, f32[4,72,128]{2,1,0:T(8,128)S(1)}, u32[]{:S(2)}, u32[]{:S(2)}) collective-permute-start(f32[4,72,128]{2,1,0:T(8,128)S(1)} %get-tuple-element.27), channel_id=1, source_target_pairs={{0,4},{4,0},{8,12},{12,8},{16,20},{20,16},{24,28},{28,24},{1,5},{5... | collective-permute-start | bytes 442376 | tf_op jit(solution)/shard_map/ppermute | solution.py:211
  30.6 1.0 %collective-permute-done.7 = f32[4,72,128]{2,1,0:T(8,128)S(1)} collective-permute-done((f32[4,72,128]{2,1,0:T(8,128)S(1)}, f32[4,72,128]{2,1,0:T(8,128)S(1)}, u32[]{:S(2)}, u32[]{:S(2)}) %collective-permute-start.7) | collective-permute-done | bytes 147488 | tf_op jit(solution)/shard_map/ppermute | solution.py:211
  31.7 3.6 %collective-permute-start.10 = (f32[72,128]{1,0:T(8,128)S(1)}, f32[72,128]{1,0:T(8,128)S(1)}, u32[]{:S(2)}, u32[]{:S(2)}) collective-permute-start(f32[72,128]{1,0:T(8,128)S(1)} %get-tuple-element.48), channel_id=1, source_target_pairs={{0,24},{4,28},{8,16},{12,20},{16,8},{20,12},{24,0},{28,4},{1,25},{... | collective-permute-start | bytes 110600 | tf_op jit(solution)/shard_map/ppermute | solution.py:211
  35.2 1.5 %collective-permute-start.8 = (f32[72,128]{1,0:T(8,128)S(1)}, f32[72,128]{1,0:T(8,128)S(1)}, u32[]{:S(2)}, u32[]{:S(2)}) collective-permute-start(f32[72,128]{1,0:T(8,128)S(1)} %get-tuple-element.47), channel_id=1, source_target_pairs={{0,8},{4,12},{8,0},{12,4},{16,24},{20,28},{24,16},{28,20},{1,9},{5... | collective-permute-start | bytes 110600 | tf_op jit(solution)/shard_map/ppermute | solution.py:211
  37.2 2.0 %collective-permute-done.8 = f32[72,128]{1,0:T(8,128)S(1)} collective-permute-done((f32[72,128]{1,0:T(8,128)S(1)}, f32[72,128]{1,0:T(8,128)S(1)}, u32[]{:S(2)}, u32[]{:S(2)}) %collective-permute-start.8) | collective-permute-done | bytes 36896 | tf_op jit(solution)/shard_map/ppermute | solution.py:211
  39.2 1.5 %collective-permute-done.9 = f32[72,128]{1,0:T(8,128)S(1)} collective-permute-done((f32[72,128]{1,0:T(8,128)S(1)}, f32[72,128]{1,0:T(8,128)S(1)}, u32[]{:S(2)}, u32[]{:S(2)}) %collective-permute-start.9) | collective-permute-done | bytes 36896 | tf_op jit(solution)/shard_map/ppermute | solution.py:211
  40.7 3.9 %collective-permute-start.12 = (f32[72,128]{1,0:T(8,128)S(1)}, f32[72,128]{1,0:T(8,128)S(1)}, u32[]{:S(2)}, u32[]{:S(2)}) collective-permute-start(f32[72,128]{1,0:T(8,128)S(1)} %fusion.6), channel_id=1, source_target_pairs={{0,2},{1,3},{2,0},{3,1},{4,6},{5,7},{6,4},{7,5},{8,10},{9,11},{10,... | collective-permute-start | bytes 110600 | tf_op jit(solution)/shard_map/ppermute | solution.py:211
  45.1 1.4 %collective-permute-done.12 = f32[72,128]{1,0:T(8,128)S(1)} collective-permute-done((f32[72,128]{1,0:T(8,128)S(1)}, f32[72,128]{1,0:T(8,128)S(1)}, u32[]{:S(2)}, u32[]{:S(2)}) %collective-permute-start.12) | collective-permute-done | bytes 36896 | tf_op jit(solution)/shard_map/ppermute | solution.py:211
  46.5 3.8 %collective-permute-done.13 = f32[72,128]{1,0:T(8,128)S(1)} collective-permute-done((f32[72,128]{1,0:T(8,128)S(1)}, f32[72,128]{1,0:T(8,128)S(1)}, u32[]{:S(2)}, u32[]{:S(2)}) %collective-permute-start.13) | collective-permute-done | bytes 36896 | tf_op jit(solution)/shard_map/ppermute | solution.py:211
  51.3 2.0 %collective-permute-start.15 = (f32[72,128]{1,0:T(8,128)S(1)}, f32[72,128]{1,0:T(8,128)S(1)}, u32[]{:S(2)}, u32[]{:S(2)}) collective-permute-start(f32[72,128]{1,0:T(8,128)S(1)} %add_add_fusion.1), channel_id=1, source_target_pairs={{0,16},{4,20},{8,24},{12,28},{16,0},{20,4},{24,8},{28,12},{1,17},{... | collective-permute-start | bytes 110600 | tf_op jit(solution)/shard_map/ppermute | solution.py:211
  53.9 1.3 %collective-permute-start.6 = (f32[16,256]{1,0:T(8,128)S(1)}, f32[16,256]{1,0:T(8,128)S(1)}, u32[]{:S(2)}, u32[]{:S(2)}) collective-permute-start(f32[16,256]{1,0:T(8,128)S(1)} %get-tuple-element.25), channel_id=1, source_target_pairs={{1,0},{2,1},{3,2},{4,3},{5,4},{6,5},{7,6},{8,7},{9,8},{10,9},{11,1... | collective-permute-start | bytes 49160 | tf_op jit(solution)/shard_map/ppermute | solution.py:617
  55.2 4.5 %collective-permute-start.5 = (f32[16,256]{1,0:T(8,128)S(1)}, f32[16,256]{1,0:T(8,128)S(1)}, u32[]{:S(2)}, u32[]{:S(2)}) collective-permute-start(f32[16,256]{1,0:T(8,128)S(1)} %get-tuple-element.24), channel_id=1, source_target_pairs={{0,1},{1,2},{2,3},{3,4},{4,5},{5,6},{6,7},{7,8},{8,9},{9,10},{10,1... | collective-permute-start | bytes 49160 | tf_op jit(solution)/shard_map/ppermute | solution.py:616
  59.9 1.3 %collective-permute-done.5 = f32[16,256]{1,0:T(8,128)S(1)} collective-permute-done((f32[16,256]{1,0:T(8,128)S(1)}, f32[16,256]{1,0:T(8,128)S(1)}, u32[]{:S(2)}, u32[]{:S(2)}) %collective-permute-start.5) | collective-permute-done | bytes 16416 | tf_op jit(solution)/shard_map/ppermute | solution.py:616
  61.3 11.6 %second_gradient.1 = (f32[8,16,256]{2,1,0:T(8,128)S(1)}, f32[128,128]{1,0:T(8,128)}, f32[16,128]{1,0:T(8,128)}, f32[4,80,128]{2,1,0:T(8,128)S(1)}, f32[4,80,128]{2,1,0:T(8,128)S(1)}) custom-call(s32[2]{0:T(128)S(1)} %pad_add_fusion.rank_ref, f32[16]{0:T(128)S(1)} %copy-done.4, bf16[8,128,256]{2,1,0:T(8,128)(2,1)S(1)} %fusion.counts_ref, ...), custom_call_target="tpu_custom_call" | custom-call | tf_op jit(solution)/shard_map/second_gradient/pallas_call | solution.py:637
  72.9 2.1 %collective-permute-start.18 = (f32[4,80,128]{2,1,0:T(8,128)S(1)}, f32[4,80,128]{2,1,0:T(8,128)S(1)}, u32[]{:S(2)}, u32[]{:S(2)}) collective-permute-start(f32[4,80,128]{2,1,0:T(8,128)S(1)} %get-tuple-element.33), channel_id=1, source_target_pairs={{0,4},{4,0},{8,12},{12,8},{16,20},{20,16},{24,28},{28,24},{1,5},{5... | collective-permute-start | bytes 491528 | tf_op jit(solution)/shard_map/ppermute | solution.py:211
  75.0 1.0 %collective-permute-done.18 = f32[4,80,128]{2,1,0:T(8,128)S(1)} collective-permute-done((f32[4,80,128]{2,1,0:T(8,128)S(1)}, f32[4,80,128]{2,1,0:T(8,128)S(1)}, u32[]{:S(2)}, u32[]{:S(2)}) %collective-permute-start.18) | collective-permute-done | bytes 163872 | tf_op jit(solution)/shard_map/ppermute | solution.py:211
  76.0 1.6 %collective-permute-start.19 = (f32[80,128]{1,0:T(8,128)S(1)}, f32[80,128]{1,0:T(8,128)S(1)}, u32[]{:S(2)}, u32[]{:S(2)}) collective-permute-start(f32[80,128]{1,0:T(8,128)S(1)} %get-tuple-element.44), channel_id=1, source_target_pairs={{0,8},{4,12},{8,0},{12,4},{16,24},{20,28},{24,16},{28,20},{1,9},{5... | collective-permute-start | bytes 122888 | tf_op jit(solution)/shard_map/ppermute | solution.py:211
  77.6 2.0 %collective-permute-start.20 = (f32[80,128]{1,0:T(8,128)S(1)}, f32[80,128]{1,0:T(8,128)S(1)}, u32[]{:S(2)}, u32[]{:S(2)}) collective-permute-start(f32[80,128]{1,0:T(8,128)S(1)} %get-tuple-element.46), channel_id=1, source_target_pairs={{0,16},{4,20},{8,24},{12,28},{16,0},{20,4},{24,8},{28,12},{1,17},{... | collective-permute-start | bytes 122888 | tf_op jit(solution)/shard_map/ppermute | solution.py:211
  80.1 1.5 %collective-permute-done.20 = f32[80,128]{1,0:T(8,128)S(1)} collective-permute-done((f32[80,128]{1,0:T(8,128)S(1)}, f32[80,128]{1,0:T(8,128)S(1)}, u32[]{:S(2)}, u32[]{:S(2)}) %collective-permute-start.20) | collective-permute-done | bytes 40992 | tf_op jit(solution)/shard_map/ppermute | solution.py:211
  81.6 2.9 %collective-permute-done.21 = f32[80,128]{1,0:T(8,128)S(1)} collective-permute-done((f32[80,128]{1,0:T(8,128)S(1)}, f32[80,128]{1,0:T(8,128)S(1)}, u32[]{:S(2)}, u32[]{:S(2)}) %collective-permute-start.21) | collective-permute-done | bytes 40992 | tf_op jit(solution)/shard_map/ppermute | solution.py:211
  84.8 4.3 %collective-permute-start.24 = (f32[80,128]{1,0:T(8,128)S(1)}, f32[80,128]{1,0:T(8,128)S(1)}, u32[]{:S(2)}, u32[]{:S(2)}) collective-permute-start(f32[80,128]{1,0:T(8,128)S(1)} %fusion.3), channel_id=1, source_target_pairs={{0,3},{1,2},{2,1},{3,0},{4,7},{5,6},{6,5},{7,4},{8,11},{9,10},{10,... | collective-permute-start | bytes 122888 | tf_op jit(solution)/shard_map/ppermute | solution.py:211
  89.6 1.8 %collective-permute-done.24 = f32[80,128]{1,0:T(8,128)S(1)} collective-permute-done((f32[80,128]{1,0:T(8,128)S(1)}, f32[80,128]{1,0:T(8,128)S(1)}, u32[]{:S(2)}, u32[]{:S(2)}) %collective-permute-start.24) | collective-permute-done | bytes 40992 | tf_op jit(solution)/shard_map/ppermute | solution.py:211
  91.5 1.0 %collective-permute-start.25 = (f32[80,128]{1,0:T(8,128)S(1)}, f32[80,128]{1,0:T(8,128)S(1)}, u32[]{:S(2)}, u32[]{:S(2)}) collective-permute-start(f32[80,128]{1,0:T(8,128)S(1)} %add_add_fusion), channel_id=1, source_target_pairs={{0,8},{4,12},{8,0},{12,4},{16,24},{20,28},{24,16},{28,20},{1,9},{5... | collective-permute-start | bytes 122888 | tf_op jit(solution)/shard_map/ppermute | solution.py:211
  92.5 2.5 %collective-permute-start.27 = (f32[80,128]{1,0:T(8,128)S(1)}, f32[80,128]{1,0:T(8,128)S(1)}, u32[]{:S(2)}, u32[]{:S(2)}) collective-permute-start(f32[80,128]{1,0:T(8,128)S(1)} %add_add_fusion), channel_id=1, source_target_pairs={{0,24},{4,28},{8,16},{12,20},{16,8},{20,12},{24,0},{28,4},{1,25},{... | collective-permute-start | bytes 122888 | tf_op jit(solution)/shard_map/ppermute | solution.py:211
  99.0 1.3 %momenta.1 = (f32[128,128]{1,0:T(8,128)}, f32[16,128]{1,0:T(8,128)}, f32[1,1]{1,0:T(1,128)}) custom-call(s32[2]{0:T(128)S(1)} %pad_add_fusion.rank_ref, f32[4,80,128]{2,1,0:T(8,128)S(1)} %pad_maximum_fusion.near_ref, f32[4,80,128]{2,1,0:T(8,128)S(1)} %collective-permute-done.28.far_ref), custom_call_target="tpu_custom_call" | custom-call | tf_op jit(solution)/shard_map/momenta/pallas_call | solution.py:649
  (70 shorter events, 11.9 us)
Async XLA Ops:
  0.6 17.6 %copy-start.1 = (s32[32,256]{1,0:T(8,128)S(1)}, s32[32,256]{1,0:T(8,128)}, u32[]{:S(2)}) copy-start(s32[32,256]{1,0:T(8,128)} %land_ref.3) | copy-start | bytes 98308
  0.7 17.6 %copy-start = (f32[128,128]{1,0:T(8,128)S(1)}, f32[128,128]{1,0:T(8,128)}, u32[]{:S(2)}) copy-start(f32[128,128]{1,0:T(8,128)} %pmom_ref.3) | copy-start | bytes 196612
  0.7 17.6 %copy-start.3 = (f32[16,128]{1,0:T(8,128)S(1)}, f32[16,128]{1,0:T(8,128)}, u32[]{:S(2)}) copy-start(f32[16,128]{1,0:T(8,128)} %wmom_ref.3) | copy-start | bytes 24580
  2.3 15.9 %collective-permute-start.2 = (f32[144,128]{1,0:T(8,128)S(1)}, f32[144,128]{1,0:T(8,128)S(1)}, u32[]{:S(2)}, u32[]{:S(2)}) collective-permute-start(f32[144,128]{1,0:T(8,128)S(1)} %constant_dynamic-update-slice_fusion.refs_0_.own_ref), channel_id=1, source_target_pairs={{0,1},{1,0},{2,3},{3,2},{4,5},{5,4},{6,7},{7,6},{8,9},{9,8},{10,11... | collective-permute-start | bytes 221192 | tf_op jit(solution)/shard_map/ppermute | solution.py:211
  5.3 12.9 %collective-permute-start.3 = (f32[144,128]{1,0:T(8,128)S(1)}, f32[144,128]{1,0:T(8,128)S(1)}, u32[]{:S(2)}, u32[]{:S(2)}) collective-permute-start(f32[144,128]{1,0:T(8,128)S(1)} %constant_dynamic-update-slice_fusion.refs_0_.own_ref), channel_id=1, source_target_pairs={{0,2},{1,3},{2,0},{3,1},{4,6},{5,7},{6,4},{7,5},{8,10},{9,11},{10,... | collective-permute-start | bytes 221192 | tf_op jit(solution)/shard_map/ppermute | solution.py:211
  7.9 10.3 %collective-permute-start.4 = (f32[144,128]{1,0:T(8,128)S(1)}, f32[144,128]{1,0:T(8,128)S(1)}, u32[]{:S(2)}, u32[]{:S(2)}) collective-permute-start(f32[144,128]{1,0:T(8,128)S(1)} %constant_dynamic-update-slice_fusion.refs_0_.own_ref), channel_id=1, source_target_pairs={{0,3},{1,2},{2,1},{3,0},{4,7},{5,6},{6,5},{7,4},{8,11},{9,10},{10,... | collective-permute-start | bytes 221192 | tf_op jit(solution)/shard_map/ppermute | solution.py:211
  9.7 5.9 %collective-permute-start = (f32[24,256]{1,0:T(8,128)S(1)}, f32[24,256]{1,0:T(8,128)S(1)}, u32[]{:S(2)}, u32[]{:S(2)}) collective-permute-start(f32[24,256]{1,0:T(8,128)S(1)} %pad_maximum_fusion.2), channel_id=1, source_target_pairs={{0,1},{1,2},{2,3},{3,4},{4,5},{5,6},{6,7},{7,8},{8,9},{9,10},{10,1... | collective-permute-start | bytes 73736 | tf_op jit(solution)/shard_map/ppermute | solution.py:544
  12.5 5.7 %collective-permute-start.1 = (f32[24,256]{1,0:T(8,128)S(1)}, f32[24,256]{1,0:T(8,128)S(1)}, u32[]{:S(2)}, u32[]{:S(2)}) collective-permute-start(f32[24,256]{1,0:T(8,128)S(1)} %pad_maximum_fusion.3), channel_id=1, source_target_pairs={{1,0},{2,1},{3,2},{4,3},{5,4},{6,5},{7,6},{8,7},{9,8},{10,9},{11,1... | collective-permute-start | bytes 73736 | tf_op jit(solution)/shard_map/ppermute | solution.py:545
  29.5 2.1 %collective-permute-start.7 = (f32[4,72,128]{2,1,0:T(8,128)S(1)}, f32[4,72,128]{2,1,0:T(8,128)S(1)}, u32[]{:S(2)}, u32[]{:S(2)}) collective-permute-start(f32[4,72,128]{2,1,0:T(8,128)S(1)} %get-tuple-element.27), channel_id=1, source_target_pairs={{0,4},{4,0},{8,12},{12,8},{16,20},{20,16},{24,28},{28,24},{1,5},{5... | collective-permute-start | bytes 442376 | tf_op jit(solution)/shard_map/ppermute | solution.py:211
  31.7 5.5 %collective-permute-start.10 = (f32[72,128]{1,0:T(8,128)S(1)}, f32[72,128]{1,0:T(8,128)S(1)}, u32[]{:S(2)}, u32[]{:S(2)}) collective-permute-start(f32[72,128]{1,0:T(8,128)S(1)} %get-tuple-element.48), channel_id=1, source_target_pairs={{0,24},{4,28},{8,16},{12,20},{16,8},{20,12},{24,0},{28,4},{1,25},{... | collective-permute-start | bytes 110600 | tf_op jit(solution)/shard_map/ppermute | solution.py:211
  35.2 4.0 %collective-permute-start.8 = (f32[72,128]{1,0:T(8,128)S(1)}, f32[72,128]{1,0:T(8,128)S(1)}, u32[]{:S(2)}, u32[]{:S(2)}) collective-permute-start(f32[72,128]{1,0:T(8,128)S(1)} %get-tuple-element.47), channel_id=1, source_target_pairs={{0,8},{4,12},{8,0},{12,4},{16,24},{20,28},{24,16},{28,20},{1,9},{5... | collective-permute-start | bytes 110600 | tf_op jit(solution)/shard_map/ppermute | solution.py:211
  36.7 4.0 %collective-permute-start.9 = (f32[72,128]{1,0:T(8,128)S(1)}, f32[72,128]{1,0:T(8,128)S(1)}, u32[]{:S(2)}, u32[]{:S(2)}) collective-permute-start(f32[72,128]{1,0:T(8,128)S(1)} %get-tuple-element.49), channel_id=1, source_target_pairs={{0,16},{4,20},{8,24},{12,28},{16,0},{20,4},{24,8},{28,12},{1,17},{... | collective-permute-start | bytes 110600 | tf_op jit(solution)/shard_map/ppermute | solution.py:211
  40.7 4.5 %collective-permute-start.11 = (f32[72,128]{1,0:T(8,128)S(1)}, f32[72,128]{1,0:T(8,128)S(1)}, u32[]{:S(2)}, u32[]{:S(2)}) collective-permute-start(f32[72,128]{1,0:T(8,128)S(1)} %fusion.6), channel_id=1, source_target_pairs={{0,1},{1,0},{2,3},{3,2},{4,5},{5,4},{6,7},{7,6},{8,9},{9,8},{10,11... | collective-permute-start | bytes 110600 | tf_op jit(solution)/shard_map/ppermute | solution.py:211
  40.7 5.8 %collective-permute-start.12 = (f32[72,128]{1,0:T(8,128)S(1)}, f32[72,128]{1,0:T(8,128)S(1)}, u32[]{:S(2)}, u32[]{:S(2)}) collective-permute-start(f32[72,128]{1,0:T(8,128)S(1)} %fusion.6), channel_id=1, source_target_pairs={{0,2},{1,3},{2,0},{3,1},{4,6},{5,7},{6,4},{7,5},{8,10},{9,11},{10,... | collective-permute-start | bytes 110600 | tf_op jit(solution)/shard_map/ppermute | solution.py:211
  44.6 5.8 %collective-permute-start.13 = (f32[72,128]{1,0:T(8,128)S(1)}, f32[72,128]{1,0:T(8,128)S(1)}, u32[]{:S(2)}, u32[]{:S(2)}) collective-permute-start(f32[72,128]{1,0:T(8,128)S(1)} %fusion.6), channel_id=1, source_target_pairs={{0,3},{1,2},{2,1},{3,0},{4,7},{5,6},{6,5},{7,4},{8,11},{9,10},{10,... | collective-permute-start | bytes 110600 | tf_op jit(solution)/shard_map/ppermute | solution.py:211
  50.4 9.4 %collective-permute-start.14 = (f32[72,128]{1,0:T(8,128)S(1)}, f32[72,128]{1,0:T(8,128)S(1)}, u32[]{:S(2)}, u32[]{:S(2)}) collective-permute-start(f32[72,128]{1,0:T(8,128)S(1)} %add_add_fusion.1), channel_id=1, source_target_pairs={{0,8},{4,12},{8,0},{12,4},{16,24},{20,28},{24,16},{28,20},{1,9},{5... | collective-permute-start | bytes 110600 | tf_op jit(solution)/shard_map/ppermute | solution.py:211
  51.3 8.4 %collective-permute-start.15 = (f32[72,128]{1,0:T(8,128)S(1)}, f32[72,128]{1,0:T(8,128)S(1)}, u32[]{:S(2)}, u32[]{:S(2)}) collective-permute-start(f32[72,128]{1,0:T(8,128)S(1)} %add_add_fusion.1), channel_id=1, source_target_pairs={{0,16},{4,20},{8,24},{12,28},{16,0},{20,4},{24,8},{28,12},{1,17},{... | collective-permute-start | bytes 110600 | tf_op jit(solution)/shard_map/ppermute | solution.py:211
  53.4 6.4 %collective-permute-start.16 = (f32[72,128]{1,0:T(8,128)S(1)}, f32[72,128]{1,0:T(8,128)S(1)}, u32[]{:S(2)}, u32[]{:S(2)}) collective-permute-start(f32[72,128]{1,0:T(8,128)S(1)} %add_add_fusion.1), channel_id=1, source_target_pairs={{0,24},{4,28},{8,16},{12,20},{16,8},{20,12},{24,0},{28,4},{1,25},{... | collective-permute-start | bytes 110600 | tf_op jit(solution)/shard_map/ppermute | solution.py:211
  53.9 6.0 %collective-permute-start.6 = (f32[16,256]{1,0:T(8,128)S(1)}, f32[16,256]{1,0:T(8,128)S(1)}, u32[]{:S(2)}, u32[]{:S(2)}) collective-permute-start(f32[16,256]{1,0:T(8,128)S(1)} %get-tuple-element.25), channel_id=1, source_target_pairs={{1,0},{2,1},{3,2},{4,3},{5,4},{6,5},{7,6},{8,7},{9,8},{10,9},{11,1... | collective-permute-start | bytes 49160 | tf_op jit(solution)/shard_map/ppermute | solution.py:617
  55.2 6.0 %collective-permute-start.5 = (f32[16,256]{1,0:T(8,128)S(1)}, f32[16,256]{1,0:T(8,128)S(1)}, u32[]{:S(2)}, u32[]{:S(2)}) collective-permute-start(f32[16,256]{1,0:T(8,128)S(1)} %get-tuple-element.24), channel_id=1, source_target_pairs={{0,1},{1,2},{2,3},{3,4},{4,5},{5,6},{6,7},{7,8},{8,9},{9,10},{10,1... | collective-permute-start | bytes 49160 | tf_op jit(solution)/shard_map/ppermute | solution.py:616
  59.8 1.4 %collective-permute-start.17 = (f32[4,72,128]{2,1,0:T(8,128)S(1)}, f32[4,72,128]{2,1,0:T(8,128)S(1)}, u32[]{:S(2)}, u32[]{:S(2)}) collective-permute-start(f32[4,72,128]{2,1,0:T(8,128)S(1)} %pad_maximum_fusion.1.near_ref), channel_id=1, source_target_pairs={{0,4},{4,0},{8,12},{12,8},{16,20},{20,16},{24,28},{28,24},{1,5},{5... | collective-permute-start | bytes 442376 | tf_op jit(solution)/shard_map/ppermute | solution.py:211
  72.9 3.1 %collective-permute-start.18 = (f32[4,80,128]{2,1,0:T(8,128)S(1)}, f32[4,80,128]{2,1,0:T(8,128)S(1)}, u32[]{:S(2)}, u32[]{:S(2)}) collective-permute-start(f32[4,80,128]{2,1,0:T(8,128)S(1)} %get-tuple-element.33), channel_id=1, source_target_pairs={{0,4},{4,0},{8,12},{12,8},{16,20},{20,16},{24,28},{28,24},{1,5},{5... | collective-permute-start | bytes 491528 | tf_op jit(solution)/shard_map/ppermute | solution.py:211
  76.0 4.1 %collective-permute-start.19 = (f32[80,128]{1,0:T(8,128)S(1)}, f32[80,128]{1,0:T(8,128)S(1)}, u32[]{:S(2)}, u32[]{:S(2)}) collective-permute-start(f32[80,128]{1,0:T(8,128)S(1)} %get-tuple-element.44), channel_id=1, source_target_pairs={{0,8},{4,12},{8,0},{12,4},{16,24},{20,28},{24,16},{28,20},{1,9},{5... | collective-permute-start | bytes 122888 | tf_op jit(solution)/shard_map/ppermute | solution.py:211
  77.6 4.0 %collective-permute-start.20 = (f32[80,128]{1,0:T(8,128)S(1)}, f32[80,128]{1,0:T(8,128)S(1)}, u32[]{:S(2)}, u32[]{:S(2)}) collective-permute-start(f32[80,128]{1,0:T(8,128)S(1)} %get-tuple-element.46), channel_id=1, source_target_pairs={{0,16},{4,20},{8,24},{12,28},{16,0},{20,4},{24,8},{28,12},{1,17},{... | collective-permute-start | bytes 122888 | tf_op jit(solution)/shard_map/ppermute | solution.py:211
  79.7 4.9 %collective-permute-start.21 = (f32[80,128]{1,0:T(8,128)S(1)}, f32[80,128]{1,0:T(8,128)S(1)}, u32[]{:S(2)}, u32[]{:S(2)}) collective-permute-start(f32[80,128]{1,0:T(8,128)S(1)} %get-tuple-element.45), channel_id=1, source_target_pairs={{0,24},{4,28},{8,16},{12,20},{16,8},{20,12},{24,0},{28,4},{1,25},{... | collective-permute-start | bytes 122888 | tf_op jit(solution)/shard_map/ppermute | solution.py:211
  84.6 4.5 %collective-permute-start.22 = (f32[80,128]{1,0:T(8,128)S(1)}, f32[80,128]{1,0:T(8,128)S(1)}, u32[]{:S(2)}, u32[]{:S(2)}) collective-permute-start(f32[80,128]{1,0:T(8,128)S(1)} %fusion.3), channel_id=1, source_target_pairs={{0,1},{1,0},{2,3},{3,2},{4,5},{5,4},{6,7},{7,6},{8,9},{9,8},{10,11... | collective-permute-start | bytes 122888 | tf_op jit(solution)/shard_map/ppermute | solution.py:211
  84.6 5.0 %collective-permute-start.23 = (f32[80,128]{1,0:T(8,128)S(1)}, f32[80,128]{1,0:T(8,128)S(1)}, u32[]{:S(2)}, u32[]{:S(2)}) collective-permute-start(f32[80,128]{1,0:T(8,128)S(1)} %fusion.3), channel_id=1, source_target_pairs={{0,2},{1,3},{2,0},{3,1},{4,6},{5,7},{6,4},{7,5},{8,10},{9,11},{10,... | collective-permute-start | bytes 122888 | tf_op jit(solution)/shard_map/ppermute | solution.py:211
  84.8 6.7 %collective-permute-start.24 = (f32[80,128]{1,0:T(8,128)S(1)}, f32[80,128]{1,0:T(8,128)S(1)}, u32[]{:S(2)}, u32[]{:S(2)}) collective-permute-start(f32[80,128]{1,0:T(8,128)S(1)} %fusion.3), channel_id=1, source_target_pairs={{0,3},{1,2},{2,1},{3,0},{4,7},{5,6},{6,5},{7,4},{8,11},{9,10},{10,... | collective-permute-start | bytes 122888 | tf_op jit(solution)/shard_map/ppermute | solution.py:211
  91.5 4.1 %collective-permute-start.25 = (f32[80,128]{1,0:T(8,128)S(1)}, f32[80,128]{1,0:T(8,128)S(1)}, u32[]{:S(2)}, u32[]{:S(2)}) collective-permute-start(f32[80,128]{1,0:T(8,128)S(1)} %add_add_fusion), channel_id=1, source_target_pairs={{0,8},{4,12},{8,0},{12,4},{16,24},{20,28},{24,16},{28,20},{1,9},{5... | collective-permute-start | bytes 122888 | tf_op jit(solution)/shard_map/ppermute | solution.py:211
  92.5 4.0 %collective-permute-start.26 = (f32[80,128]{1,0:T(8,128)S(1)}, f32[80,128]{1,0:T(8,128)S(1)}, u32[]{:S(2)}, u32[]{:S(2)}) collective-permute-start(f32[80,128]{1,0:T(8,128)S(1)} %add_add_fusion), channel_id=1, source_target_pairs={{0,16},{4,20},{8,24},{12,28},{16,0},{20,4},{24,8},{28,12},{1,17},{... | collective-permute-start | bytes 122888 | tf_op jit(solution)/shard_map/ppermute | solution.py:211
  92.5 4.9 %collective-permute-start.27 = (f32[80,128]{1,0:T(8,128)S(1)}, f32[80,128]{1,0:T(8,128)S(1)}, u32[]{:S(2)}, u32[]{:S(2)}) collective-permute-start(f32[80,128]{1,0:T(8,128)S(1)} %add_add_fusion), channel_id=1, source_target_pairs={{0,24},{4,28},{8,16},{12,20},{16,8},{20,12},{24,0},{28,4},{1,25},{... | collective-permute-start | bytes 122888 | tf_op jit(solution)/shard_map/ppermute | solution.py:211
  97.4 1.6 %collective-permute-start.28 = (f32[4,80,128]{2,1,0:T(8,128)S(1)}, f32[4,80,128]{2,1,0:T(8,128)S(1)}, u32[]{:S(2)}, u32[]{:S(2)}) collective-permute-start(f32[4,80,128]{2,1,0:T(8,128)S(1)} %pad_maximum_fusion.near_ref), channel_id=1, source_target_pairs={{0,4},{4,0},{8,12},{12,8},{16,20},{20,16},{24,28},{28,24},{1,5},{5... | collective-permute-start | bytes 491528 | tf_op jit(solution)/shard_map/ppermute | solution.py:211
  (3 other events, 50.1 us)
where the time goes:
time: 101 us; the launch traced here: 100 us
  starting transfers between devices  43.9 us (43%)
  waiting for transfers between devices  24.5 us (24%)
  Pallas kernels  24.1 us (24%)
  local copies, waits for them, and re-layouts  5.43 us (5%)
  other arithmetic  1.3 us (1%)
    ppermute x25, starting transfers between devices, partner(): return lax.ppermute(values, axis, [(i, i ^ flip) for i in range(count)])  34 us
    ppermute x25, waiting for transfers between devices, partner(): return lax.ppermute(values, axis, [(i, i ^ flip) for i in range(count)])  20.6 us
    pallas_call x1, Pallas kernels, fast_device(): second(ranks, field_tau, count_rows, new_field, half, land_mask, log_expo...  11.6 us
    pallas_call x1, Pallas kernels, fast_device(): first(ranks, field_tau, count_rows, field_rows, mom_rows, land_mask, log_...  11.2 us
    ppermute x1, starting transfers between devices, fast_device(): lax.ppermute(bottom, both, forward)  4.55 us
    unnamed x17, local copies, waits for them, and re-layouts  3.4 us
    ppermute x1, starting transfers between devices, fast_device(): low = lax.ppermute(edges[0], both, forward)  2.8 us
    ppermute x1, waiting for transfers between devices, fast_device(): high = lax.ppermute(edges[1], both, backward)  2.68 us
  transfers between devices with their start and end apart: 29, of which 17 were waited for; matrix products, arithmetic and copies ran while one was open for 5% of the time, Pallas kernels for 0%

commit v1 on v0

--- a/solution.py
+++ b/solution.py
@@ -329,22 +329,22 @@
     return energy
 
 
-def row_shares(
-    r, ncomp, right_ref, wide_ref, left_ref, mix_ref, load_ref, land_ref, score_ref, logit_ref, post_ref, gap_ref,
-    acc_ref, accw_ref,
-):
-    cols = right_ref.shape[2]
-    nfac = load_ref.shape[0] // 2
-    block = 64
-    score_ref[...] = dot(left_ref[...], right_ref[r])
-    logit_ref[...] = dot(mix_ref[...], right_ref[r, LANES : 2 * LANES, :])
-    top_s = jnp.full((8, cols), -jnp.inf, F32)
-    top_a = jnp.full((8, cols), -jnp.inf, F32)
-    for i in range(0, ncomp, block):
-        top_s = jnp.maximum(top_s, jnp.max(score_ref[i : i + block, :].reshape(block // 8, 8, cols), axis=0))
-        top_a = jnp.maximum(top_a, jnp.max(logit_ref[i : i + block, :].reshape(block // 8, 8, cols), axis=0))
-    top_s = jnp.max(top_s, axis=0, keepdims=True)
-    top_a = jnp.max(top_a, axis=0, keepdims=True)
+def row_scores(r, right_ref, left_ref, mix_ref, score_ref, logit_ref):
+    tops = []
+    for target, values in (
+        (score_ref, dot(left_ref[...], right_ref[r])),
+        (logit_ref, dot(mix_ref[...], right_ref[r, LANES : 2 * LANES, :])),
+    ):
+        target[...] = values
+        ncomp, cols = values.shape
+        tops.append(jnp.max(jnp.max(values.reshape(ncomp // 8, 8, cols), axis=0), axis=0, keepdims=True))
+    return tops
+
+
+def row_shares(tops, land, score_ref, logit_ref, post_ref, gap_ref):
+    ncomp, cols = score_ref.shape
+    block = 32
+    top_s, top_a = tops
     sum_s = jnp.zeros((8, cols), F32)
     sum_a = jnp.zeros((8, cols), F32)
     for i in range(0, ncomp, block):
@@ -356,7 +356,8 @@
         sum_a = sum_a + jnp.sum(part_a.reshape(block // 8, 8, cols), axis=0)
     sum_s = jnp.sum(sum_s, axis=0, keepdims=True)
     sum_a = jnp.sum(sum_a, axis=0, keepdims=True)
-    land = land_ref[r][0:1, :]
+    log_s = top_s + jnp.log2(sum_s)
+    log_a = top_a + jnp.log2(sum_a)
     inv_s = land / sum_s
     inv_a = land / sum_a
     for i in range(0, ncomp, block):
@@ -366,14 +367,42 @@
             high, low = pieces(values, 2)
             target[i : i + block, 0:cols] = high
             target[i : i + block, cols : 2 * cols] = low
+    return land * (LN2 * (log_s - log_a))
+
+
+def row_products(r, wide_ref, load_ref, post_ref, gap_ref, acc_ref, accw_ref, prior_ref):
+    nfac = load_ref.shape[0] // 2
+    cols = prior_ref.shape[2]
     last = ((1,), (1,))
-    acc_ref[...] += dot(post_ref[...], wide_ref[r], last)
-    accw_ref[...] += dot(gap_ref[...], wide_ref[r, LANES : 2 * LANES, :], last)
+    acc = dot(post_ref[...], wide_ref[r], last)
+    accw = dot(gap_ref[...], wide_ref[r, LANES : 2 * LANES, :], last)
+    if r == 0:
+        acc_ref[...] = acc
+        accw_ref[...] = accw
+    else:
+        acc_ref[...] += acc
+        accw_ref[...] += accw
     lik = dot(load_ref[...], gap_ref[...])
     lik = lik[0:nfac] + lik[nfac : 2 * nfac]
-    lik = lik[:, 0:cols] + lik[:, cols : 2 * cols]
-    log_dens = land * (LN2 * ((top_s + jnp.log2(sum_s)) - (top_a + jnp.log2(sum_a))))
-    return lik, log_dens
+    prior_ref[r] += lik[:, 0:cols] + lik[:, cols : 2 * cols]
+
+
+def all_rows(land, right, wide, left, mix, load, scores, logits, posts, gaps, acc, accw, prior):
+    share, _, cols = prior.shape
+    log_dens = jnp.zeros((1, cols), F32)
+    tops = {}
+    for r in range(share + 2):
+        if r < share:
+            tops[r] = row_scores(r, right, left, mix, scores[r % 2], logits[r % 2])
+        if 0 <= r - 1 < share:
+            p = r - 1
+            log_dens = log_dens + row_shares(
+                tops[p], land[p : p + 1, :], scores[p % 2], logits[p % 2], posts[p % 2], gaps[p % 2]
+            )
+        if 0 <= r - 2:
+            p = r - 2
+            row_products(p, wide, load, posts[p % 2], gaps[p % 2], acc, accw, prior)
+    return log_dens
 
 
 def param_grads(flat_ref, acc_ref, accw_ref, grad_ref, ncomp, nfac):
@@ -396,7 +425,9 @@
     ring = ncomp // pmom_ref.shape[0]
     part_refs = refs[:ring]
     (new_ref, half_ref, top_ref, bottom_ref, grad_ref, keep_ref, send_ref) = refs[ring : ring + 7]
-    (flat, left, mix, load, right, wide, prior, land_rows, score, logit, post, gap, acc, accw) = refs[ring + 7 :]
+    (flat, left, mix, load, right, wide, prior, score0, score1, logit0, logit1, post0, post1, gap0, gap1, acc, accw) = (
+        refs[ring + 7 :]
+    )
     cells_rank, comp_rank = rank_ref[0], rank_ref[1]
     share, nfac, cols = field_ref.shape
     mine = pmom_ref.shape[0]
@@ -405,22 +436,14 @@
         flat[pl.ds(pl.multiple_of(group * mine, mine), mine), :] = part_refs[k][0:mine, :]
         flat[pl.ds(pl.multiple_of(ncomp + group * nfac, nfac), nfac), :] = part_refs[k][mine : mine + nfac, :]
     land = land_ref[...].astype(F32)
-    for r in range(share):
-        land_rows[r] = jnp.broadcast_to(land[r : r + 1, :], (8, cols))
     load_params(flat, left, mix, load, ncomp, nfac)
     load_cells(counts_ref, field_ref, logexp_ref, right, wide)
     load_prior(field_ref, low_ref, high_ref, land, tau_ref, prior)
-    acc[...] = jnp.zeros_like(acc)
-    accw[...] = jnp.zeros_like(accw)
-
-    def step(r, carry):
-        lik, _ = row_shares(
-            r, ncomp, right, wide, left, mix, load, land_rows, score, logit, post, gap, acc, accw
-        )
-        prior[r] = prior[r] + lik
-        return carry
-
-    lax.fori_loop(0, share, step, 0)
+
+    all_rows(
+        land, right, wide, left, mix, load, (score0, score1), (logit0, logit1), (post0, post1), (gap0, gap1), acc, accw,
+        prior,
+    )
     for r in range(share):
         half = mom_ref[r] + 0.5 * STEP_FIELD * prior[r]
         fresh = field_ref[r] + STEP_FIELD * half
@@ -447,7 +470,8 @@
 def second_kernel(
     ncomp, rank_ref, tau_ref, counts_ref, field_ref, half_ref, land_ref, logexp_ref, low_ref, high_ref, pmom_ref, wmom_ref,
     own_ref, near_ref, far_ref, grad0_ref, mom_ref, prof_ref, mixing_ref, keep_ref, send_ref,
-    flat, left, mix, load, right, wide, prior, land_rows, score, logit, post, gap, acc, accw, out, grad,
+    flat, left, mix, load, right, wide, prior, score0, score1, logit0, logit1, post0, post1, gap0, gap1, acc, accw, out,
+    grad,
 ):
     cells_rank, comp_rank = rank_ref[0], rank_ref[1]
     share, nfac, cols = field_ref.shape
@@ -459,22 +483,14 @@
     prof_ref[...] = new_prof
     mixing_ref[...] = new_load
     land = land_ref[...].astype(F32)
-    for r in range(share):
-        land_rows[r] = jnp.broadcast_to(land[r : r + 1, :], (8, cols))
     load_params(flat, left, mix, load, ncomp, nfac)
     load_cells(counts_ref, field_ref, logexp_ref, right, wide)
     energy = load_prior(field_ref, low_ref, high_ref, land, tau_ref, prior)
-    acc[...] = jnp.zeros_like(acc)
-    accw[...] = jnp.zeros_like(accw)
-
-    def step(r, log_dens):
-        lik, part = row_shares(
-            r, ncomp, right, wide, left, mix, load, land_rows, score, logit, post, gap, acc, accw
-        )
-        prior[r] = prior[r] + lik
-        return log_dens + part
-
-    log_dens = lax.fori_loop(0, share, step, jnp.zeros((1, cols), F32))
+
+    log_dens = all_rows(
+        land, right, wide, left, mix, load, (score0, score1), (logit0, logit1), (post0, post1), (gap0, gap1), acc, accw,
+        prior,
+    )
     for r in range(share):
         fresh = half_ref[r] + 0.5 * STEP_FIELD * prior[r]
         mom_ref[r] = fresh
@@ -566,11 +582,9 @@
         pltpu.VMEM((share, 4 * LANES, cols), BF16),
         pltpu.VMEM((share, 2 * LANES, 2 * cols), BF16),
         pltpu.VMEM((share, nfac, cols), F32),
-        pltpu.VMEM((share, 8, cols), F32),
-        pltpu.VMEM((ncomp, cols), F32),
-        pltpu.VMEM((ncomp, cols), F32),
-        pltpu.VMEM((ncomp, 2 * cols), BF16),
-        pltpu.VMEM((ncomp, 2 * cols), BF16),
+    ]
+    work += [pltpu.VMEM((ncomp, cols), F32)] * 4 + [pltpu.VMEM((ncomp, 2 * cols), BF16)] * 4
+    work += [
         pltpu.VMEM((ncomp, 2 * LANES), F32),
         pltpu.VMEM((ncomp, LANES), F32),
     ]

time: 101 us -> 91.6 us (0.907)
  Pallas kernels: 24.1 us -> 14.9 us
    pallas_call x1, Pallas kernels: 11.2 us -> 6.53 us  [fast_device(): first(ranks, field_tau, count_rows, field_rows, mom_rows, land_mask, log_...]
    pallas_call x1, Pallas kernels: 11.6 us -> 7.1 us  [fast_device(): second(ranks, field_tau, count_rows, new_field, half, land_mask, log_expo...]
where the time goes in v1:
time: 91.6 us; the launch traced here: 91.2 us
  starting transfers between devices  43.9 us (48%)
  waiting for transfers between devices  24.6 us (27%)
  Pallas kernels  14.9 us (16%)
  local copies, waits for them, and re-layouts  5.43 us (6%)
  other arithmetic  1.3 us (1%)
  between operations  1.1 us (1%)
    ppermute x25, starting transfers between devices, partner(): return lax.ppermute(values, axis, [(i, i ^ flip) for i in range(count)])  33.8 us
    ppermute x25, waiting for transfers between devices, partner(): return lax.ppermute(values, axis, [(i, i ^ flip) for i in range(count)])  20.8 us
    pallas_call x1, Pallas kernels, fast_device(): second(ranks, field_tau, count_rows, new_field, half, land_mask, log_expo...  7.1 us
    pallas_call x1, Pallas kernels, fast_device(): first(ranks, field_tau, count_rows, field_rows, mom_rows, land_mask, log_...  6.53 us
    ppermute x1, starting transfers between devices, fast_device(): lax.ppermute(bottom, both, forward)  4.73 us
    unnamed x17, local copies, waits for them, and re-layouts  3.4 us
    ppermute x1, starting transfers between devices, fast_device(): low = lax.ppermute(edges[0], both, forward)  2.8 us
    ppermute x1, waiting for transfers between devices, fast_device(): high = lax.ppermute(edges[1], both, backward)  2.68 us
  transfers between devices with their start and end apart: 29, of which 17 were waited for; matrix products, arithmetic and copies ran while one was open for 5% of the time, Pallas kernels for 0%

profile of v1, /device:TPU:0, one launch (start us, length us, event | category | flops | bytes accessed | tf_op | source)
XLA Modules:
  0.0 91.2 jit_solution(13307328777890887758)
XLA Ops:
  2.3 3.0 %collective-permute-start.2 = (f32[144,128]{1,0:T(8,128)S(1)}, f32[144,128]{1,0:T(8,128)S(1)}, u32[]{:S(2)}, u32[]{:S(2)}) collective-permute-start(f32[144,128]{1,0:T(8,128)S(1)} %constant_dynamic-update-slice_fusion.refs_0_.own_ref), channel_id=1, source_target_pairs={{0,1},{1,0},{2,3},{3,2},{4,5},{5,4},{6,7},{7,6},{8,9},{9,8},{10,11... | collective-permute-start | bytes 221192 | tf_op jit(solution)/shard_map/ppermute | solution.py:211
  5.3 2.6 %collective-permute-start.3 = (f32[144,128]{1,0:T(8,128)S(1)}, f32[144,128]{1,0:T(8,128)S(1)}, u32[]{:S(2)}, u32[]{:S(2)}) collective-permute-start(f32[144,128]{1,0:T(8,128)S(1)} %constant_dynamic-update-slice_fusion.refs_0_.own_ref), channel_id=1, source_target_pairs={{0,2},{1,3},{2,0},{3,1},{4,6},{5,7},{6,4},{7,5},{8,10},{9,11},{10,... | collective-permute-start | bytes 221192 | tf_op jit(solution)/shard_map/ppermute | solution.py:211
  9.7 2.8 %collective-permute-start = (f32[24,256]{1,0:T(8,128)S(1)}, f32[24,256]{1,0:T(8,128)S(1)}, u32[]{:S(2)}, u32[]{:S(2)}) collective-permute-start(f32[24,256]{1,0:T(8,128)S(1)} %pad_maximum_fusion.2), channel_id=1, source_target_pairs={{0,1},{1,2},{2,3},{3,4},{4,5},{5,6},{6,7},{7,8},{8,9},{9,10},{10,1... | collective-permute-start | bytes 73736 | tf_op jit(solution)/shard_map/ppermute | solution.py:560
  12.5 1.3 %collective-permute-start.1 = (f32[24,256]{1,0:T(8,128)S(1)}, f32[24,256]{1,0:T(8,128)S(1)}, u32[]{:S(2)}, u32[]{:S(2)}) collective-permute-start(f32[24,256]{1,0:T(8,128)S(1)} %pad_maximum_fusion.3), channel_id=1, source_target_pairs={{1,0},{2,1},{3,2},{4,3},{5,4},{6,5},{7,6},{8,7},{9,8},{10,9},{11,1... | collective-permute-start | bytes 73736 | tf_op jit(solution)/shard_map/ppermute | solution.py:561
  13.8 1.3 %constant_dynamic-slice_fusion = s32[128,8,256]{2,1,0:T(8,128)S(1)} fusion(s32[128,32,256]{2,1,0:T(8,128)} %param.17, s32[]{:T(128)S(6)} %select_n.7), kind=kLoop, calls=%fused_computation.31 | loop fusion | bytes 2097156 | tf_op jit(solution)/shard_map/dynamic_slice | solution.py:548
  15.6 2.7 %collective-permute-done.1.high_ref = f32[24,256]{1,0:T(8,128)S(1)} collective-permute-done((f32[24,256]{1,0:T(8,128)S(1)}, f32[24,256]{1,0:T(8,128)S(1)}, u32[]{:S(2)}, u32[]{:S(2)}) %collective-permute-start.1) | collective-permute-done | bytes 24608 | tf_op jit(solution)/shard_map/ppermute | solution.py:561
  18.3 6.5 %first_gradient.1 = (f32[8,16,256]{2,1,0:T(8,128)S(1)}, f32[8,16,256]{2,1,0:T(8,128)S(1)}, f32[16,256]{1,0:T(8,128)S(1)}, f32[16,256]{1,0:T(8,128)S(1)}, f32[576...) custom-call(s32[2]{0:T(128)S(1)} %pad_add_fusion.rank_ref, f32[16]{0:T(128)S(1)} %copy-done.4, ...), custom_call_target="tpu_custom_call" | custom-call | tf_op jit(solution)/shard_map/first_gradient/pallas_call | solution.py:626
  24.8 1.1 %collective-permute-start.7 = (f32[4,72,128]{2,1,0:T(8,128)S(1)}, f32[4,72,128]{2,1,0:T(8,128)S(1)}, u32[]{:S(2)}, u32[]{:S(2)}) collective-permute-start(f32[4,72,128]{2,1,0:T(8,128)S(1)} %get-tuple-element.27), channel_id=1, source_target_pairs={{0,4},{4,0},{8,12},{12,8},{16,20},{20,16},{24,28},{28,24},{1,5},{5... | collective-permute-start | bytes 442376 | tf_op jit(solution)/shard_map/ppermute | solution.py:211
  25.9 1.0 %collective-permute-done.7 = f32[4,72,128]{2,1,0:T(8,128)S(1)} collective-permute-done((f32[4,72,128]{2,1,0:T(8,128)S(1)}, f32[4,72,128]{2,1,0:T(8,128)S(1)}, u32[]{:S(2)}, u32[]{:S(2)}) %collective-permute-start.7) | collective-permute-done | bytes 147488 | tf_op jit(solution)/shard_map/ppermute | solution.py:211
  27.0 3.6 %collective-permute-start.10 = (f32[72,128]{1,0:T(8,128)S(1)}, f32[72,128]{1,0:T(8,128)S(1)}, u32[]{:S(2)}, u32[]{:S(2)}) collective-permute-start(f32[72,128]{1,0:T(8,128)S(1)} %get-tuple-element.48), channel_id=1, source_target_pairs={{0,24},{4,28},{8,16},{12,20},{16,8},{20,12},{24,0},{28,4},{1,25},{... | collective-permute-start | bytes 110600 | tf_op jit(solution)/shard_map/ppermute | solution.py:211
  30.6 1.4 %collective-permute-start.8 = (f32[72,128]{1,0:T(8,128)S(1)}, f32[72,128]{1,0:T(8,128)S(1)}, u32[]{:S(2)}, u32[]{:S(2)}) collective-permute-start(f32[72,128]{1,0:T(8,128)S(1)} %get-tuple-element.47), channel_id=1, source_target_pairs={{0,8},{4,12},{8,0},{12,4},{16,24},{20,28},{24,16},{28,20},{1,9},{5... | collective-permute-start | bytes 110600 | tf_op jit(solution)/shard_map/ppermute | solution.py:211
  32.5 2.0 %collective-permute-done.8 = f32[72,128]{1,0:T(8,128)S(1)} collective-permute-done((f32[72,128]{1,0:T(8,128)S(1)}, f32[72,128]{1,0:T(8,128)S(1)}, u32[]{:S(2)}, u32[]{:S(2)}) %collective-permute-start.8) | collective-permute-done | bytes 36896 | tf_op jit(solution)/shard_map/ppermute | solution.py:211
  34.5 1.4 %collective-permute-done.9 = f32[72,128]{1,0:T(8,128)S(1)} collective-permute-done((f32[72,128]{1,0:T(8,128)S(1)}, f32[72,128]{1,0:T(8,128)S(1)}, u32[]{:S(2)}, u32[]{:S(2)}) %collective-permute-start.9) | collective-permute-done | bytes 36896 | tf_op jit(solution)/shard_map/ppermute | solution.py:211
  36.0 3.9 %collective-permute-start.12 = (f32[72,128]{1,0:T(8,128)S(1)}, f32[72,128]{1,0:T(8,128)S(1)}, u32[]{:S(2)}, u32[]{:S(2)}) collective-permute-start(f32[72,128]{1,0:T(8,128)S(1)} %fusion.6), channel_id=1, source_target_pairs={{0,2},{1,3},{2,0},{3,1},{4,6},{5,7},{6,4},{7,5},{8,10},{9,11},{10,... | collective-permute-start | bytes 110600 | tf_op jit(solution)/shard_map/ppermute | solution.py:211
  40.4 1.4 %collective-permute-done.12 = f32[72,128]{1,0:T(8,128)S(1)} collective-permute-done((f32[72,128]{1,0:T(8,128)S(1)}, f32[72,128]{1,0:T(8,128)S(1)}, u32[]{:S(2)}, u32[]{:S(2)}) %collective-permute-start.12) | collective-permute-done | bytes 36896 | tf_op jit(solution)/shard_map/ppermute | solution.py:211
  41.9 3.8 %collective-permute-done.13 = f32[72,128]{1,0:T(8,128)S(1)} collective-permute-done((f32[72,128]{1,0:T(8,128)S(1)}, f32[72,128]{1,0:T(8,128)S(1)}, u32[]{:S(2)}, u32[]{:S(2)}) %collective-permute-start.13) | collective-permute-done | bytes 36896 | tf_op jit(solution)/shard_map/ppermute | solution.py:211
  46.6 2.0 %collective-permute-start.15 = (f32[72,128]{1,0:T(8,128)S(1)}, f32[72,128]{1,0:T(8,128)S(1)}, u32[]{:S(2)}, u32[]{:S(2)}) collective-permute-start(f32[72,128]{1,0:T(8,128)S(1)} %add_add_fusion.1), channel_id=1, source_target_pairs={{0,16},{4,20},{8,24},{12,28},{16,0},{20,4},{24,8},{28,12},{1,17},{... | collective-permute-start | bytes 110600 | tf_op jit(solution)/shard_map/ppermute | solution.py:211
  49.3 1.3 %collective-permute-start.6 = (f32[16,256]{1,0:T(8,128)S(1)}, f32[16,256]{1,0:T(8,128)S(1)}, u32[]{:S(2)}, u32[]{:S(2)}) collective-permute-start(f32[16,256]{1,0:T(8,128)S(1)} %get-tuple-element.25), channel_id=1, source_target_pairs={{1,0},{2,1},{3,2},{4,3},{5,4},{6,5},{7,6},{8,7},{9,8},{10,9},{11,1... | collective-permute-start | bytes 49160 | tf_op jit(solution)/shard_map/ppermute | solution.py:631
  50.5 4.7 %collective-permute-start.5 = (f32[16,256]{1,0:T(8,128)S(1)}, f32[16,256]{1,0:T(8,128)S(1)}, u32[]{:S(2)}, u32[]{:S(2)}) collective-permute-start(f32[16,256]{1,0:T(8,128)S(1)} %get-tuple-element.24), channel_id=1, source_target_pairs={{0,1},{1,2},{2,3},{3,4},{4,5},{5,6},{6,7},{7,8},{8,9},{9,10},{10,1... | collective-permute-start | bytes 49160 | tf_op jit(solution)/shard_map/ppermute | solution.py:630
  55.4 1.1 %collective-permute-done.5 = f32[16,256]{1,0:T(8,128)S(1)} collective-permute-done((f32[16,256]{1,0:T(8,128)S(1)}, f32[16,256]{1,0:T(8,128)S(1)}, u32[]{:S(2)}, u32[]{:S(2)}) %collective-permute-start.5) | collective-permute-done | bytes 16416 | tf_op jit(solution)/shard_map/ppermute | solution.py:630
  56.8 7.1 %second_gradient.1 = (f32[8,16,256]{2,1,0:T(8,128)S(1)}, f32[128,128]{1,0:T(8,128)}, f32[16,128]{1,0:T(8,128)}, f32[4,80,128]{2,1,0:T(8,128)S(1)}, f32[4,80,128]{2,1,0:T(8,128)S(1)}) custom-call(s32[2]{0:T(128)S(1)} %pad_add_fusion.rank_ref, f32[16]{0:T(128)S(1)} %copy-done.4, bf16[8,128,256]{2,1,0:T(8,128)(2,1)S(1)} %fusion.counts_ref, ...), custom_call_target="tpu_custom_call" | custom-call | tf_op jit(solution)/shard_map/second_gradient/pallas_call | solution.py:651
  63.9 1.9 %collective-permute-start.18 = (f32[4,80,128]{2,1,0:T(8,128)S(1)}, f32[4,80,128]{2,1,0:T(8,128)S(1)}, u32[]{:S(2)}, u32[]{:S(2)}) collective-permute-start(f32[4,80,128]{2,1,0:T(8,128)S(1)} %get-tuple-element.33), channel_id=1, source_target_pairs={{0,4},{4,0},{8,12},{12,8},{16,20},{20,16},{24,28},{28,24},{1,5},{5... | collective-permute-start | bytes 491528 | tf_op jit(solution)/shard_map/ppermute | solution.py:211
  65.7 1.0 %collective-permute-done.18 = f32[4,80,128]{2,1,0:T(8,128)S(1)} collective-permute-done((f32[4,80,128]{2,1,0:T(8,128)S(1)}, f32[4,80,128]{2,1,0:T(8,128)S(1)}, u32[]{:S(2)}, u32[]{:S(2)}) %collective-permute-start.18) | collective-permute-done | bytes 163872 | tf_op jit(solution)/shard_map/ppermute | solution.py:211
  66.8 1.6 %collective-permute-start.19 = (f32[80,128]{1,0:T(8,128)S(1)}, f32[80,128]{1,0:T(8,128)S(1)}, u32[]{:S(2)}, u32[]{:S(2)}) collective-permute-start(f32[80,128]{1,0:T(8,128)S(1)} %get-tuple-element.44), channel_id=1, source_target_pairs={{0,8},{4,12},{8,0},{12,4},{16,24},{20,28},{24,16},{28,20},{1,9},{5... | collective-permute-start | bytes 122888 | tf_op jit(solution)/shard_map/ppermute | solution.py:211
  68.4 2.0 %collective-permute-start.20 = (f32[80,128]{1,0:T(8,128)S(1)}, f32[80,128]{1,0:T(8,128)S(1)}, u32[]{:S(2)}, u32[]{:S(2)}) collective-permute-start(f32[80,128]{1,0:T(8,128)S(1)} %get-tuple-element.46), channel_id=1, source_target_pairs={{0,16},{4,20},{8,24},{12,28},{16,0},{20,4},{24,8},{28,12},{1,17},{... | collective-permute-start | bytes 122888 | tf_op jit(solution)/shard_map/ppermute | solution.py:211
  70.9 1.5 %collective-permute-done.20 = f32[80,128]{1,0:T(8,128)S(1)} collective-permute-done((f32[80,128]{1,0:T(8,128)S(1)}, f32[80,128]{1,0:T(8,128)S(1)}, u32[]{:S(2)}, u32[]{:S(2)}) %collective-permute-start.20) | collective-permute-done | bytes 40992 | tf_op jit(solution)/shard_map/ppermute | solution.py:211
  72.4 2.9 %collective-permute-done.21 = f32[80,128]{1,0:T(8,128)S(1)} collective-permute-done((f32[80,128]{1,0:T(8,128)S(1)}, f32[80,128]{1,0:T(8,128)S(1)}, u32[]{:S(2)}, u32[]{:S(2)}) %collective-permute-start.21) | collective-permute-done | bytes 40992 | tf_op jit(solution)/shard_map/ppermute | solution.py:211
  75.7 4.1 %collective-permute-start.24 = (f32[80,128]{1,0:T(8,128)S(1)}, f32[80,128]{1,0:T(8,128)S(1)}, u32[]{:S(2)}, u32[]{:S(2)}) collective-permute-start(f32[80,128]{1,0:T(8,128)S(1)} %fusion.3), channel_id=1, source_target_pairs={{0,3},{1,2},{2,1},{3,0},{4,7},{5,6},{6,5},{7,4},{8,11},{9,10},{10,... | collective-permute-start | bytes 122888 | tf_op jit(solution)/shard_map/ppermute | solution.py:211
  80.4 1.8 %collective-permute-done.24 = f32[80,128]{1,0:T(8,128)S(1)} collective-permute-done((f32[80,128]{1,0:T(8,128)S(1)}, f32[80,128]{1,0:T(8,128)S(1)}, u32[]{:S(2)}, u32[]{:S(2)}) %collective-permute-start.24) | collective-permute-done | bytes 40992 | tf_op jit(solution)/shard_map/ppermute | solution.py:211
  82.2 1.0 %collective-permute-start.25 = (f32[80,128]{1,0:T(8,128)S(1)}, f32[80,128]{1,0:T(8,128)S(1)}, u32[]{:S(2)}, u32[]{:S(2)}) collective-permute-start(f32[80,128]{1,0:T(8,128)S(1)} %add_add_fusion), channel_id=1, source_target_pairs={{0,8},{4,12},{8,0},{12,4},{16,24},{20,28},{24,16},{28,20},{1,9},{5... | collective-permute-start | bytes 122888 | tf_op jit(solution)/shard_map/ppermute | solution.py:211
  83.3 2.5 %collective-permute-start.27 = (f32[80,128]{1,0:T(8,128)S(1)}, f32[80,128]{1,0:T(8,128)S(1)}, u32[]{:S(2)}, u32[]{:S(2)}) collective-permute-start(f32[80,128]{1,0:T(8,128)S(1)} %add_add_fusion), channel_id=1, source_target_pairs={{0,24},{4,28},{8,16},{12,20},{16,8},{20,12},{24,0},{28,4},{1,25},{... | collective-permute-start | bytes 122888 | tf_op jit(solution)/shard_map/ppermute | solution.py:211
  89.7 1.3 %momenta.1 = (f32[128,128]{1,0:T(8,128)}, f32[16,128]{1,0:T(8,128)}, f32[1,1]{1,0:T(1,128)}) custom-call(s32[2]{0:T(128)S(1)} %pad_add_fusion.rank_ref, f32[4,80,128]{2,1,0:T(8,128)S(1)} %pad_maximum_fusion.near_ref, f32[4,80,128]{2,1,0:T(8,128)S(1)} %collective-permute-done.28.far_ref), custom_call_target="tpu_custom_call" | custom-call | tf_op jit(solution)/shard_map/momenta/pallas_call | solution.py:663
  (70 shorter events, 12.2 us)
Async XLA Ops:
  0.6 17.6 %copy-start.1 = (s32[32,256]{1,0:T(8,128)S(1)}, s32[32,256]{1,0:T(8,128)}, u32[]{:S(2)}) copy-start(s32[32,256]{1,0:T(8,128)} %land_ref.3) | copy-start | bytes 98308
  0.7 17.6 %copy-start = (f32[128,128]{1,0:T(8,128)S(1)}, f32[128,128]{1,0:T(8,128)}, u32[]{:S(2)}) copy-start(f32[128,128]{1,0:T(8,128)} %pmom_ref.3) | copy-start | bytes 196612
  0.7 17.6 %copy-start.3 = (f32[16,128]{1,0:T(8,128)S(1)}, f32[16,128]{1,0:T(8,128)}, u32[]{:S(2)}) copy-start(f32[16,128]{1,0:T(8,128)} %wmom_ref.3) | copy-start | bytes 24580
  2.3 15.9 %collective-permute-start.2 = (f32[144,128]{1,0:T(8,128)S(1)}, f32[144,128]{1,0:T(8,128)S(1)}, u32[]{:S(2)}, u32[]{:S(2)}) collective-permute-start(f32[144,128]{1,0:T(8,128)S(1)} %constant_dynamic-update-slice_fusion.refs_0_.own_ref), channel_id=1, source_target_pairs={{0,1},{1,0},{2,3},{3,2},{4,5},{5,4},{6,7},{7,6},{8,9},{9,8},{10,11... | collective-permute-start | bytes 221192 | tf_op jit(solution)/shard_map/ppermute | solution.py:211
  5.3 12.9 %collective-permute-start.3 = (f32[144,128]{1,0:T(8,128)S(1)}, f32[144,128]{1,0:T(8,128)S(1)}, u32[]{:S(2)}, u32[]{:S(2)}) collective-permute-start(f32[144,128]{1,0:T(8,128)S(1)} %constant_dynamic-update-slice_fusion.refs_0_.own_ref), channel_id=1, source_target_pairs={{0,2},{1,3},{2,0},{3,1},{4,6},{5,7},{6,4},{7,5},{8,10},{9,11},{10,... | collective-permute-start | bytes 221192 | tf_op jit(solution)/shard_map/ppermute | solution.py:211
  7.9 10.3 %collective-permute-start.4 = (f32[144,128]{1,0:T(8,128)S(1)}, f32[144,128]{1,0:T(8,128)S(1)}, u32[]{:S(2)}, u32[]{:S(2)}) collective-permute-start(f32[144,128]{1,0:T(8,128)S(1)} %constant_dynamic-update-slice_fusion.refs_0_.own_ref), channel_id=1, source_target_pairs={{0,3},{1,2},{2,1},{3,0},{4,7},{5,6},{6,5},{7,4},{8,11},{9,10},{10,... | collective-permute-start | bytes 221192 | tf_op jit(solution)/shard_map/ppermute | solution.py:211
  9.7 5.9 %collective-permute-start = (f32[24,256]{1,0:T(8,128)S(1)}, f32[24,256]{1,0:T(8,128)S(1)}, u32[]{:S(2)}, u32[]{:S(2)}) collective-permute-start(f32[24,256]{1,0:T(8,128)S(1)} %pad_maximum_fusion.2), channel_id=1, source_target_pairs={{0,1},{1,2},{2,3},{3,4},{4,5},{5,6},{6,7},{7,8},{8,9},{9,10},{10,1... | collective-permute-start | bytes 73736 | tf_op jit(solution)/shard_map/ppermute | solution.py:560
  12.5 5.7 %collective-permute-start.1 = (f32[24,256]{1,0:T(8,128)S(1)}, f32[24,256]{1,0:T(8,128)S(1)}, u32[]{:S(2)}, u32[]{:S(2)}) collective-permute-start(f32[24,256]{1,0:T(8,128)S(1)} %pad_maximum_fusion.3), channel_id=1, source_target_pairs={{1,0},{2,1},{3,2},{4,3},{5,4},{6,5},{7,6},{8,7},{9,8},{10,9},{11,1... | collective-permute-start | bytes 73736 | tf_op jit(solution)/shard_map/ppermute | solution.py:561
  24.8 2.1 %collective-permute-start.7 = (f32[4,72,128]{2,1,0:T(8,128)S(1)}, f32[4,72,128]{2,1,0:T(8,128)S(1)}, u32[]{:S(2)}, u32[]{:S(2)}) collective-permute-start(f32[4,72,128]{2,1,0:T(8,128)S(1)} %get-tuple-element.27), channel_id=1, source_target_pairs={{0,4},{4,0},{8,12},{12,8},{16,20},{20,16},{24,28},{28,24},{1,5},{5... | collective-permute-start | bytes 442376 | tf_op jit(solution)/shard_map/ppermute | solution.py:211
  27.0 5.5 %collective-permute-start.10 = (f32[72,128]{1,0:T(8,128)S(1)}, f32[72,128]{1,0:T(8,128)S(1)}, u32[]{:S(2)}, u32[]{:S(2)}) collective-permute-start(f32[72,128]{1,0:T(8,128)S(1)} %get-tuple-element.48), channel_id=1, source_target_pairs={{0,24},{4,28},{8,16},{12,20},{16,8},{20,12},{24,0},{28,4},{1,25},{... | collective-permute-start | bytes 110600 | tf_op jit(solution)/shard_map/ppermute | solution.py:211
  30.6 4.0 %collective-permute-start.8 = (f32[72,128]{1,0:T(8,128)S(1)}, f32[72,128]{1,0:T(8,128)S(1)}, u32[]{:S(2)}, u32[]{:S(2)}) collective-permute-start(f32[72,128]{1,0:T(8,128)S(1)} %get-tuple-element.47), channel_id=1, source_target_pairs={{0,8},{4,12},{8,0},{12,4},{16,24},{20,28},{24,16},{28,20},{1,9},{5... | collective-permute-start | bytes 110600 | tf_op jit(solution)/shard_map/ppermute | solution.py:211
  32.0 4.0 %collective-permute-start.9 = (f32[72,128]{1,0:T(8,128)S(1)}, f32[72,128]{1,0:T(8,128)S(1)}, u32[]{:S(2)}, u32[]{:S(2)}) collective-permute-start(f32[72,128]{1,0:T(8,128)S(1)} %get-tuple-element.49), channel_id=1, source_target_pairs={{0,16},{4,20},{8,24},{12,28},{16,0},{20,4},{24,8},{28,12},{1,17},{... | collective-permute-start | bytes 110600 | tf_op jit(solution)/shard_map/ppermute | solution.py:211
  36.0 4.5 %collective-permute-start.11 = (f32[72,128]{1,0:T(8,128)S(1)}, f32[72,128]{1,0:T(8,128)S(1)}, u32[]{:S(2)}, u32[]{:S(2)}) collective-permute-start(f32[72,128]{1,0:T(8,128)S(1)} %fusion.6), channel_id=1, source_target_pairs={{0,1},{1,0},{2,3},{3,2},{4,5},{5,4},{6,7},{7,6},{8,9},{9,8},{10,11... | collective-permute-start | bytes 110600 | tf_op jit(solution)/shard_map/ppermute | solution.py:211
  36.0 5.8 %collective-permute-start.12 = (f32[72,128]{1,0:T(8,128)S(1)}, f32[72,128]{1,0:T(8,128)S(1)}, u32[]{:S(2)}, u32[]{:S(2)}) collective-permute-start(f32[72,128]{1,0:T(8,128)S(1)} %fusion.6), channel_id=1, source_target_pairs={{0,2},{1,3},{2,0},{3,1},{4,6},{5,7},{6,4},{7,5},{8,10},{9,11},{10,... | collective-permute-start | bytes 110600 | tf_op jit(solution)/shard_map/ppermute | solution.py:211
  39.9 5.8 %collective-permute-start.13 = (f32[72,128]{1,0:T(8,128)S(1)}, f32[72,128]{1,0:T(8,128)S(1)}, u32[]{:S(2)}, u32[]{:S(2)}) collective-permute-start(f32[72,128]{1,0:T(8,128)S(1)} %fusion.6), channel_id=1, source_target_pairs={{0,3},{1,2},{2,1},{3,0},{4,7},{5,6},{6,5},{7,4},{8,11},{9,10},{10,... | collective-permute-start | bytes 110600 | tf_op jit(solution)/shard_map/ppermute | solution.py:211
  45.7 9.6 %collective-permute-start.14 = (f32[72,128]{1,0:T(8,128)S(1)}, f32[72,128]{1,0:T(8,128)S(1)}, u32[]{:S(2)}, u32[]{:S(2)}) collective-permute-start(f32[72,128]{1,0:T(8,128)S(1)} %add_add_fusion.1), channel_id=1, source_target_pairs={{0,8},{4,12},{8,0},{12,4},{16,24},{20,28},{24,16},{28,20},{1,9},{5... | collective-permute-start | bytes 110600 | tf_op jit(solution)/shard_map/ppermute | solution.py:211
  46.6 8.7 %collective-permute-start.15 = (f32[72,128]{1,0:T(8,128)S(1)}, f32[72,128]{1,0:T(8,128)S(1)}, u32[]{:S(2)}, u32[]{:S(2)}) collective-permute-start(f32[72,128]{1,0:T(8,128)S(1)} %add_add_fusion.1), channel_id=1, source_target_pairs={{0,16},{4,20},{8,24},{12,28},{16,0},{20,4},{24,8},{28,12},{1,17},{... | collective-permute-start | bytes 110600 | tf_op jit(solution)/shard_map/ppermute | solution.py:211
  48.7 6.6 %collective-permute-start.16 = (f32[72,128]{1,0:T(8,128)S(1)}, f32[72,128]{1,0:T(8,128)S(1)}, u32[]{:S(2)}, u32[]{:S(2)}) collective-permute-start(f32[72,128]{1,0:T(8,128)S(1)} %add_add_fusion.1), channel_id=1, source_target_pairs={{0,24},{4,28},{8,16},{12,20},{16,8},{20,12},{24,0},{28,4},{1,25},{... | collective-permute-start | bytes 110600 | tf_op jit(solution)/shard_map/ppermute | solution.py:211
  49.3 6.2 %collective-permute-start.6 = (f32[16,256]{1,0:T(8,128)S(1)}, f32[16,256]{1,0:T(8,128)S(1)}, u32[]{:S(2)}, u32[]{:S(2)}) collective-permute-start(f32[16,256]{1,0:T(8,128)S(1)} %get-tuple-element.25), channel_id=1, source_target_pairs={{1,0},{2,1},{3,2},{4,3},{5,4},{6,5},{7,6},{8,7},{9,8},{10,9},{11,1... | collective-permute-start | bytes 49160 | tf_op jit(solution)/shard_map/ppermute | solution.py:631
  50.5 6.0 %collective-permute-start.5 = (f32[16,256]{1,0:T(8,128)S(1)}, f32[16,256]{1,0:T(8,128)S(1)}, u32[]{:S(2)}, u32[]{:S(2)}) collective-permute-start(f32[16,256]{1,0:T(8,128)S(1)} %get-tuple-element.24), channel_id=1, source_target_pairs={{0,1},{1,2},{2,3},{3,4},{4,5},{5,6},{6,7},{7,8},{8,9},{9,10},{10,1... | collective-permute-start | bytes 49160 | tf_op jit(solution)/shard_map/ppermute | solution.py:630
  55.3 1.4 %collective-permute-start.17 = (f32[4,72,128]{2,1,0:T(8,128)S(1)}, f32[4,72,128]{2,1,0:T(8,128)S(1)}, u32[]{:S(2)}, u32[]{:S(2)}) collective-permute-start(f32[4,72,128]{2,1,0:T(8,128)S(1)} %pad_maximum_fusion.1.near_ref), channel_id=1, source_target_pairs={{0,4},{4,0},{8,12},{12,8},{16,20},{20,16},{24,28},{28,24},{1,5},{5... | collective-permute-start | bytes 442376 | tf_op jit(solution)/shard_map/ppermute | solution.py:211
  63.9 2.9 %collective-permute-start.18 = (f32[4,80,128]{2,1,0:T(8,128)S(1)}, f32[4,80,128]{2,1,0:T(8,128)S(1)}, u32[]{:S(2)}, u32[]{:S(2)}) collective-permute-start(f32[4,80,128]{2,1,0:T(8,128)S(1)} %get-tuple-element.33), channel_id=1, source_target_pairs={{0,4},{4,0},{8,12},{12,8},{16,20},{20,16},{24,28},{28,24},{1,5},{5... | collective-permute-start | bytes 491528 | tf_op jit(solution)/shard_map/ppermute | solution.py:211
  66.8 4.1 %collective-permute-start.19 = (f32[80,128]{1,0:T(8,128)S(1)}, f32[80,128]{1,0:T(8,128)S(1)}, u32[]{:S(2)}, u32[]{:S(2)}) collective-permute-start(f32[80,128]{1,0:T(8,128)S(1)} %get-tuple-element.44), channel_id=1, source_target_pairs={{0,8},{4,12},{8,0},{12,4},{16,24},{20,28},{24,16},{28,20},{1,9},{5... | collective-permute-start | bytes 122888 | tf_op jit(solution)/shard_map/ppermute | solution.py:211
  68.4 4.0 %collective-permute-start.20 = (f32[80,128]{1,0:T(8,128)S(1)}, f32[80,128]{1,0:T(8,128)S(1)}, u32[]{:S(2)}, u32[]{:S(2)}) collective-permute-start(f32[80,128]{1,0:T(8,128)S(1)} %get-tuple-element.46), channel_id=1, source_target_pairs={{0,16},{4,20},{8,24},{12,28},{16,0},{20,4},{24,8},{28,12},{1,17},{... | collective-permute-start | bytes 122888 | tf_op jit(solution)/shard_map/ppermute | solution.py:211
  70.4 4.9 %collective-permute-start.21 = (f32[80,128]{1,0:T(8,128)S(1)}, f32[80,128]{1,0:T(8,128)S(1)}, u32[]{:S(2)}, u32[]{:S(2)}) collective-permute-start(f32[80,128]{1,0:T(8,128)S(1)} %get-tuple-element.45), channel_id=1, source_target_pairs={{0,24},{4,28},{8,16},{12,20},{16,8},{20,12},{24,0},{28,4},{1,25},{... | collective-permute-start | bytes 122888 | tf_op jit(solution)/shard_map/ppermute | solution.py:211
  75.3 4.5 %collective-permute-start.22 = (f32[80,128]{1,0:T(8,128)S(1)}, f32[80,128]{1,0:T(8,128)S(1)}, u32[]{:S(2)}, u32[]{:S(2)}) collective-permute-start(f32[80,128]{1,0:T(8,128)S(1)} %fusion.3), channel_id=1, source_target_pairs={{0,1},{1,0},{2,3},{3,2},{4,5},{5,4},{6,7},{7,6},{8,9},{9,8},{10,11... | collective-permute-start | bytes 122888 | tf_op jit(solution)/shard_map/ppermute | solution.py:211
  75.4 5.0 %collective-permute-start.23 = (f32[80,128]{1,0:T(8,128)S(1)}, f32[80,128]{1,0:T(8,128)S(1)}, u32[]{:S(2)}, u32[]{:S(2)}) collective-permute-start(f32[80,128]{1,0:T(8,128)S(1)} %fusion.3), channel_id=1, source_target_pairs={{0,2},{1,3},{2,0},{3,1},{4,6},{5,7},{6,4},{7,5},{8,10},{9,11},{10,... | collective-permute-start | bytes 122888 | tf_op jit(solution)/shard_map/ppermute | solution.py:211
  75.7 6.5 %collective-permute-start.24 = (f32[80,128]{1,0:T(8,128)S(1)}, f32[80,128]{1,0:T(8,128)S(1)}, u32[]{:S(2)}, u32[]{:S(2)}) collective-permute-start(f32[80,128]{1,0:T(8,128)S(1)} %fusion.3), channel_id=1, source_target_pairs={{0,3},{1,2},{2,1},{3,0},{4,7},{5,6},{6,5},{7,4},{8,11},{9,10},{10,... | collective-permute-start | bytes 122888 | tf_op jit(solution)/shard_map/ppermute | solution.py:211
  82.2 4.1 %collective-permute-start.25 = (f32[80,128]{1,0:T(8,128)S(1)}, f32[80,128]{1,0:T(8,128)S(1)}, u32[]{:S(2)}, u32[]{:S(2)}) collective-permute-start(f32[80,128]{1,0:T(8,128)S(1)} %add_add_fusion), channel_id=1, source_target_pairs={{0,8},{4,12},{8,0},{12,4},{16,24},{20,28},{24,16},{28,20},{1,9},{5... | collective-permute-start | bytes 122888 | tf_op jit(solution)/shard_map/ppermute | solution.py:211
  83.3 4.0 %collective-permute-start.26 = (f32[80,128]{1,0:T(8,128)S(1)}, f32[80,128]{1,0:T(8,128)S(1)}, u32[]{:S(2)}, u32[]{:S(2)}) collective-permute-start(f32[80,128]{1,0:T(8,128)S(1)} %add_add_fusion), channel_id=1, source_target_pairs={{0,16},{4,20},{8,24},{12,28},{16,0},{20,4},{24,8},{28,12},{1,17},{... | collective-permute-start | bytes 122888 | tf_op jit(solution)/shard_map/ppermute | solution.py:211
  83.3 4.9 %collective-permute-start.27 = (f32[80,128]{1,0:T(8,128)S(1)}, f32[80,128]{1,0:T(8,128)S(1)}, u32[]{:S(2)}, u32[]{:S(2)}) collective-permute-start(f32[80,128]{1,0:T(8,128)S(1)} %add_add_fusion), channel_id=1, source_target_pairs={{0,24},{4,28},{8,16},{12,20},{16,8},{20,12},{24,0},{28,4},{1,25},{... | collective-permute-start | bytes 122888 | tf_op jit(solution)/shard_map/ppermute | solution.py:211
  88.2 1.6 %collective-permute-start.28 = (f32[4,80,128]{2,1,0:T(8,128)S(1)}, f32[4,80,128]{2,1,0:T(8,128)S(1)}, u32[]{:S(2)}, u32[]{:S(2)}) collective-permute-start(f32[4,80,128]{2,1,0:T(8,128)S(1)} %pad_maximum_fusion.near_ref), channel_id=1, source_target_pairs={{0,4},{4,0},{8,12},{12,8},{16,20},{20,16},{24,28},{28,24},{1,5},{5... | collective-permute-start | bytes 491528 | tf_op jit(solution)/shard_map/ppermute | solution.py:211
  (3 other events, 50.1 us)

commit v2 on v1

--- a/solution.py
+++ b/solution.py
@@ -211,18 +211,25 @@
     return lax.ppermute(values, axis, [(i, i ^ flip) for i in range(count)])
 
 
-def all_sum(keep, send):
-    pairs = keep.shape[0]
-    ring = lax.axis_size("comp")
+def all_sum(keep, send, near_edge=None, far_edge=None):
+    pairs, rows, _ = keep.shape
     chunks = keep + partner(send, "cells", 1)
     total = chunks[0]
     for part in [partner(chunks[k], "cells", 2 * k) for k in range(1, pairs)]:
         total = total + part
-    parts = [partner(total, "comp", k) for k in range(1, ring)]
-    for part in parts:
-        total = total + part
+    if near_edge is None:
+        parts = [partner(total, "comp", k) for k in range(1, lax.axis_size("comp"))]
+        near_got = None
+        for part in parts:
+            total = total + part
+    else:
+        first = partner(jnp.concatenate([total, near_edge], axis=0), "comp", 1)
+        second = partner(total, "comp", 2)
+        third = partner(jnp.concatenate([total, far_edge], axis=0), "comp", 3)
+        near_got = first[rows:]
+        total = jnp.concatenate([total + first[:rows] + second + third[:rows], third[rows:]], axis=0)
     near = jnp.stack([total] + [partner(total, "cells", 2 * k) for k in range(1, pairs)])
-    return near, partner(near, "cells", 1)
+    return near, partner(near, "cells", 1), near_got
 
 
 def chunk_index(cells_rank, k, other):
@@ -230,12 +237,11 @@
     return (((cells_rank // 2) ^ k) * 2) + (1 - core if other else core)
 
 
-def gather_chunks(flat_ref, near_ref, far_ref, cells_rank):
-    pairs, rows, _ = near_ref.shape
-    for k in range(pairs):
+def gather_chunks(flat_ref, near_ref, far_ref, cells_rank, rows):
+    for k in range(near_ref.shape[0]):
         for source, other in ((near_ref, False), (far_ref, True)):
             start = pl.multiple_of(chunk_index(cells_rank, k, other) * rows, 8)
-            flat_ref[pl.ds(start, rows), :] = source[k]
+            flat_ref[pl.ds(start, rows), :] = source[k, 0:rows, :]
 
 
 def spread_chunks(flat_ref, keep_ref, send_ref, cells_rank):
@@ -300,33 +306,57 @@
             wide_ref[r, LANES : 2 * LANES, side * cols : (side + 1) * cols] = extra
 
 
-def load_prior(field_ref, low_ref, high_ref, land, tau_ref, prior_ref):
-    share, nfac, cols = field_ref.shape
+def field_weights(tau_ref, nfac, cols):
     row = lax.broadcasted_iota(jnp.int32, (nfac, cols), 0)
-    col = lax.broadcasted_iota(jnp.int32, (nfac, cols), 1)
     tau = jnp.zeros((nfac, cols), F32)
     for j in range(nfac):
         tau = jnp.where(row == j, tau_ref[j], tau)
-    inner = col < cols - 1
+    return tau
+
+
+def load_prior(rows, lands, tau, prior_ref):
+    nfac, cols = tau.shape
+    inner = lax.broadcasted_iota(jnp.int32, (nfac, cols), 1) < cols - 1
     energy = jnp.zeros((nfac, cols), F32)
-    ups = [low_ref[0:nfac, :]] + [field_ref[r] for r in range(share)] + [high_ref[0:nfac, :]]
-    lands = [low_ref[nfac : nfac + 1, :]] + [land[r : r + 1, :] for r in range(share)]
-    lands = lands + [high_ref[nfac : nfac + 1, :]]
     lands = [jnp.broadcast_to(x, (nfac, cols)) for x in lands]
-    for r in range(share):
-        here = ups[r + 1]
-        step_up = here - ups[r]
-        step_down = here - ups[r + 2]
-        edge_up = lands[r] * lands[r + 1]
-        edge_down = lands[r + 1] * lands[r + 2]
+    for r in range(len(rows) - 2):
+        here = rows[r + 1]
         step_right = here - pltpu.roll(here, cols - 1, 1)
         edge_right = jnp.where(inner, lands[r + 1] * pltpu.roll(lands[r + 1], cols - 1, 1), 0.0)
         flux_right = edge_right * step_right
-        flux_down = edge_down * step_down
-        laplace = edge_up * step_up + flux_down + flux_right - pltpu.roll(flux_right, 1, 1)
+        laplace = flux_right - pltpu.roll(flux_right, 1, 1)
+        parts = flux_right * step_right + RIDGE * (here * here)
+        if rows[r] is not None:
+            laplace = laplace + lands[r] * lands[r + 1] * (here - rows[r])
+        if rows[r + 2] is not None:
+            step_down = here - rows[r + 2]
+            flux_down = lands[r + 1] * lands[r + 2] * step_down
+            laplace = laplace + flux_down
+            parts = parts + flux_down * step_down
         prior_ref[r] = -tau * (laplace + RIDGE * here)
-        energy = energy + 0.5 * tau * (flux_down * step_down + flux_right * step_right + RIDGE * (here * here))
+        energy = energy + 0.5 * tau * parts
     return energy
+
+
+def pack_edge(edge_ref, field, fresh, land):
+    nfac, cols = field.shape
+    blocks = cols // LANES
+    sub = lax.broadcasted_iota(jnp.int32, (8, LANES), 0)
+    lands = jnp.zeros((8, LANES), F32)
+    for b in range(blocks):
+        lanes = slice(b * LANES, (b + 1) * LANES)
+        edge_ref[b * nfac : (b + 1) * nfac, :] = field[:, lanes]
+        edge_ref[(blocks + b) * nfac : (blocks + b + 1) * nfac, :] = fresh[:, lanes]
+        lands = jnp.where(sub == b, land[:, lanes], lands)
+    edge_ref[2 * blocks * nfac :, :] = lands
+
+
+def unpack_edge(edge, nfac, cols):
+    blocks = cols // LANES
+    wide = lambda start, size, step: jnp.concatenate(
+        [edge[start + b * step : start + b * step + size, :] for b in range(blocks)], axis=1
+    )
+    return wide(0, nfac, nfac), wide(blocks * nfac, nfac, nfac), wide(2 * blocks * nfac, 1, 1)
 
 
 def row_scores(r, right_ref, left_ref, mix_ref, score_ref, logit_ref):
@@ -419,12 +449,11 @@
 
 
 def first_kernel(
-    ncomp, rank_ref, tau_ref, counts_ref, field_ref, mom_ref, land_ref, logexp_ref, low_ref, high_ref, pmom_ref, wmom_ref,
-    *refs,
+    ncomp, rank_ref, tau_ref, counts_ref, field_ref, mom_ref, land_ref, logexp_ref, pmom_ref, wmom_ref, *refs
 ):
     ring = ncomp // pmom_ref.shape[0]
     part_refs = refs[:ring]
-    (new_ref, half_ref, top_ref, bottom_ref, grad_ref, keep_ref, send_ref) = refs[ring : ring + 7]
+    (new_ref, half_ref, near_ref, far_ref, grad_ref, keep_ref, send_ref) = refs[ring : ring + 7]
     (flat, left, mix, load, right, wide, prior, score0, score1, logit0, logit1, post0, post1, gap0, gap1, acc, accw) = (
         refs[ring + 7 :]
     )
@@ -438,21 +467,26 @@
     land = land_ref[...].astype(F32)
     load_params(flat, left, mix, load, ncomp, nfac)
     load_cells(counts_ref, field_ref, logexp_ref, right, wide)
-    load_prior(field_ref, low_ref, high_ref, land, tau_ref, prior)
-
+    lands = [land[r : r + 1, :] for r in range(share)]
+    tau = field_weights(tau_ref, nfac, cols)
+    load_prior([None] + [field_ref[r] for r in range(share)] + [None], lands[:1] + lands + lands[-1:], tau, prior)
     all_rows(
         land, right, wide, left, mix, load, (score0, score1), (logit0, logit1), (post0, post1), (gap0, gap1), acc, accw,
         prior,
     )
     for r in range(share):
         half = mom_ref[r] + 0.5 * STEP_FIELD * prior[r]
-        fresh = field_ref[r] + STEP_FIELD * half
         half_ref[r] = half
-        new_ref[r] = fresh
-        if r == 0:
-            top_ref[...] = fresh
-        if r == share - 1:
-            bottom_ref[...] = fresh
+        new_ref[r] = field_ref[r] + STEP_FIELD * half
+    even = comp_rank % 2 == 0
+    end = share - 1
+    for target, flag in ((near_ref, even), (far_ref, jnp.logical_not(even))):
+        pack_edge(
+            target,
+            jnp.where(flag, field_ref[end], field_ref[0]),
+            jnp.where(flag, new_ref[end], new_ref[0]),
+            jnp.where(flag, lands[end], lands[0]),
+        )
     param_grads(flat, acc, accw, grad_ref, ncomp, nfac)
     nparam = grad_ref.shape[0]
     if flat.shape[0] > nparam:
@@ -468,8 +502,9 @@
 
 
 def second_kernel(
-    ncomp, rank_ref, tau_ref, counts_ref, field_ref, half_ref, land_ref, logexp_ref, low_ref, high_ref, pmom_ref, wmom_ref,
-    own_ref, near_ref, far_ref, grad0_ref, mom_ref, prof_ref, mixing_ref, keep_ref, send_ref,
+    ncomp, chunk, ring, tiles, rank_ref, tau_ref, counts_ref, field_ref, half_ref, land_ref, logexp_ref, pmom_ref, wmom_ref,
+    old_top_ref, old_bottom_ref, own_ref, near_ref, far_ref, edge_ref, grad0_ref, new_ref, mom_ref, prof_ref, mixing_ref,
+    keep_ref, send_ref,
     flat, left, mix, load, right, wide, prior, score0, score1, logit0, logit1, post0, post1, gap0, gap1, acc, accw, out,
     grad,
 ):
@@ -477,15 +512,42 @@
     share, nfac, cols = field_ref.shape
     mine = pmom_ref.shape[0]
     nparam = grad0_ref.shape[0]
-    gather_chunks(flat, near_ref, far_ref, cells_rank)
+    gather_chunks(flat, near_ref, far_ref, cells_rank, chunk)
     new_prof = flat[pl.ds(pl.multiple_of(comp_rank * mine, mine), mine), :]
     new_load = flat[pl.ds(pl.multiple_of(ncomp + comp_rank * nfac, nfac), nfac), :]
     prof_ref[...] = new_prof
     mixing_ref[...] = new_load
     land = land_ref[...].astype(F32)
+    lands = [land[r : r + 1, :] for r in range(share)]
+    tau = field_weights(tau_ref, nfac, cols)
+
+    source = jnp.where(comp_rank == 0, cells_rank - 1, jnp.where(comp_rank == ring - 1, cells_rank + 1, cells_rank))
+    source = jnp.clip(source, 0, tiles - 1)
+    slot = (source // 2) ^ (cells_rank // 2)
+    relay = jnp.where(source % 2 == cells_rank % 2, near_ref[slot, chunk:, :], far_ref[slot, chunk:, :])
+    even = comp_rank % 2 == 0
+    direct = edge_ref[...]
+    above = unpack_edge(jnp.where(even, relay, direct), nfac, cols)
+    below = unpack_edge(jnp.where(even, direct, relay), nfac, cols)
+    land_above = jnp.where((comp_rank == 0) & (cells_rank == 0), 0.0, above[2])
+    land_below = jnp.where((comp_rank == ring - 1) & (cells_rank == tiles - 1), 0.0, below[2])
+    end = share - 1
+    pull_up = -tau * (land_above * lands[0]) * (old_top_ref[0] - above[0])
+    pull_down = -tau * (land_below * lands[end]) * (old_bottom_ref[0] - below[0])
+    move = 0.5 * STEP_FIELD * STEP_FIELD
+    for r in range(share):
+        fresh = field_ref[r]
+        if r == 0:
+            fresh = fresh + move * pull_up
+        if r == end:
+            fresh = fresh + move * pull_down
+        new_ref[r] = fresh
     load_params(flat, left, mix, load, ncomp, nfac)
-    load_cells(counts_ref, field_ref, logexp_ref, right, wide)
-    energy = load_prior(field_ref, low_ref, high_ref, land, tau_ref, prior)
+    load_cells(counts_ref, new_ref, logexp_ref, right, wide)
+    rows = [above[1] - move * pull_up] + [new_ref[r] for r in range(share)] + [below[1] - move * pull_down]
+    energy = load_prior(rows, [land_above] + lands + [land_below], tau, prior)
+    prior[0] += pull_up
+    prior[end] += pull_down
 
     log_dens = all_rows(
         land, right, wide, left, mix, load, (score0, score1), (logit0, logit1), (post0, post1), (gap0, gap1), acc, accw,
@@ -514,10 +576,10 @@
     spread_chunks(out, keep_ref, send_ref, cells_rank)
 
 
-def last_kernel(ncomp, nparam, cells, rank_ref, near_ref, far_ref, prof_ref, mixing_ref, ham_ref, flat):
+def last_kernel(ncomp, nparam, chunk, cells, rank_ref, near_ref, far_ref, prof_ref, mixing_ref, ham_ref, flat):
     cells_rank, comp_rank = rank_ref[0], rank_ref[1]
     mine, nfac = prof_ref.shape[0], mixing_ref.shape[0]
-    gather_chunks(flat, near_ref, far_ref, cells_rank)
+    gather_chunks(flat, near_ref, far_ref, cells_rank, chunk)
     prof_ref[...] = flat[pl.ds(pl.multiple_of(comp_rank * mine, mine), mine), :]
     mixing_ref[...] = flat[pl.ds(pl.multiple_of(ncomp + comp_rank * nfac, nfac), nfac), :]
     momenta = flat[0:nparam, :]
@@ -536,6 +598,7 @@
     ncomp = mine * ring
     nparam = ncomp + nfac * ncomp // LANES
     pairs = tiles // 2
+    edge = 2 * nfac * cols // LANES + 8
     round_up = lambda rows: -(-rows // (8 * tiles)) * 8
     chunk_one = round_up(nparam)
     chunk_two = round_up(nparam + 1)
@@ -548,18 +611,6 @@
     count_rows = lax.dynamic_slice_in_dim(counts, comp_rank * share, share, 1).swapaxes(0, 1).astype(BF16)
     field_rows = factor_field.swapaxes(0, 1)
     mom_rows = factor_mom.swapaxes(0, 1)
-    both = ("cells", "comp")
-    last = tiles * ring - 1
-    forward = [(i, i + 1) for i in range(last)]
-    backward = [(i + 1, i) for i in range(last)]
-    land_edge = lambda row: lax.dynamic_slice_in_dim(land_mask, row, 1, 0).astype(F32)
-    edges = [
-        jnp.concatenate([factor_field[:, r, :], jnp.broadcast_to(land_edge(comp_rank * share + r), (8, cols))], axis=0)
-        for r in (share - 1, 0)
-    ]
-    low = lax.ppermute(edges[0], both, forward)
-    high = lax.ppermute(edges[1], both, backward)
-
     def full(*shape):
         zeros = (0,) * len(shape)
         return pl.BlockSpec(shape, lambda i, ranks: zeros)
@@ -571,7 +622,6 @@
         full(share, nfac, cols),
     ]
     row_spec = pl.BlockSpec((share, cols), lambda i, ranks: (ranks[1], 0))
-    edge_spec = full(nfac + 8, cols)
     param_specs = [full(mine, ncat), full(nfac, mine)]
     pack_spec = full(mine + nfac, ncat)
     shape = lambda *dims: jax.ShapeDtypeStruct(dims, F32)
@@ -611,33 +661,39 @@
     first = call(
         functools.partial(first_kernel, ncomp),
         "first_gradient",
-        cell_specs + [full(share, nfac, cols), row_spec, row_spec, edge_spec, edge_spec] + param_specs + [pack_spec] * ring,
+        cell_specs + [full(share, nfac, cols), row_spec, row_spec] + param_specs + [pack_spec] * ring,
         [
             block(share, nfac, cols),
             block(share, nfac, cols),
-            block(nfac, cols),
-            block(nfac, cols),
+            block(edge, LANES),
+            block(edge, LANES),
             block(nparam, LANES),
             block(pairs, chunk_one, LANES),
             block(pairs, chunk_one, LANES),
         ],
         [pltpu.VMEM((tiles * chunk_one, LANES), F32)] + work,
     )
-    new_field, half, top, bottom, grad, keep, send = first(
-        ranks, field_tau, count_rows, field_rows, mom_rows, land_mask, log_exposure, low, high, profile_mom, mixing_mom,
-        *parts,
-    )
-    low_next = jnp.concatenate([lax.ppermute(bottom, both, forward), low[nfac:]], axis=0)
-    high_next = jnp.concatenate([lax.ppermute(top, both, backward), high[nfac:]], axis=0)
-    near, far = all_sum(keep, send)
+    new_field, half, near_edge, far_edge, grad, keep, send = first(
+        ranks, field_tau, count_rows, field_rows, mom_rows, land_mask, log_exposure, profile_mom, mixing_mom, *parts,
+    )
+    near, far, got_edge = all_sum(keep, send, near_edge, far_edge)
     second = call(
-        functools.partial(second_kernel, ncomp),
+        functools.partial(second_kernel, ncomp, chunk_one, ring, tiles),
         "second_gradient",
         cell_specs
-        + [full(share, nfac, cols), row_spec, row_spec, edge_spec, edge_spec]
+        + [full(share, nfac, cols), row_spec, row_spec]
         + param_specs
-        + [pack_spec, full(pairs, chunk_one, LANES), full(pairs, chunk_one, LANES), full(nparam, LANES)],
+        + [
+            pl.BlockSpec((1, nfac, cols), lambda i, ranks: (0, 0, 0)),
+            pl.BlockSpec((1, nfac, cols), lambda i, ranks: (share - 1, 0, 0)),
+            pack_spec,
+            full(pairs, chunk_one + edge, LANES),
+            full(pairs, chunk_one + edge, LANES),
+            full(edge, LANES),
+            full(nparam, LANES),
+        ],
         [
+            block(share, nfac, cols),
             block(share, nfac, cols),
             block(mine, ncat),
             block(nfac, mine),
@@ -648,13 +704,13 @@
         + work
         + [pltpu.VMEM((tiles * chunk_two, LANES), F32), pltpu.VMEM((nparam, LANES), F32)],
     )
-    new_mom, new_profile, new_mixing, keep, send = second(
-        ranks, field_tau, count_rows, new_field, half, land_mask, log_exposure, low_next, high_next, profile_mom, mixing_mom,
-        pack, near, far, grad,
-    )
-    near, far = all_sum(keep, send)
+    new_field, new_mom, new_profile, new_mixing, keep, send = second(
+        ranks, field_tau, count_rows, new_field, half, land_mask, log_exposure, profile_mom, mixing_mom, field_rows,
+        field_rows, pack, near, far, got_edge, grad,
+    )
+    near, far, _ = all_sum(keep, send)
     final = call(
-        functools.partial(last_kernel, ncomp, nparam, tile_rows * cols * tiles),
+        functools.partial(last_kernel, ncomp, nparam, chunk_two, tile_rows * cols * tiles),
         "momenta",
         [full(pairs, chunk_two, LANES), full(pairs, chunk_two, LANES)],
         [block(mine, ncat), block(nfac, mine), (smem, shape(1, 1))],
@@ -682,8 +738,8 @@
     mine, ncat = profile.shape
     tiles, ring = lax.axis_size("cells"), lax.axis_size("comp")
     fits = mine == LANES and ncat == LANES and nfac % 16 == 0 and 6 * nfac + 6 <= LANES
-    fits = fits and share == 8 and cols % LANES == 0
-    fits = fits and power_of_two(tiles) and tiles > 1 and power_of_two(ring)
+    fits = fits and share % 8 == 0 and cols % LANES == 0 and cols <= 8 * LANES
+    fits = fits and power_of_two(tiles) and tiles > 1 and ring == 4
     return fast_device(*args) if fits else plain_device(*args)
 
 

time: 91.6 us -> 77.6 us (0.85)
  starting transfers between devices: 43.9 us -> 28.2 us
  waiting for transfers between devices: 24.6 us -> 27.4 us
    ppermute x4 -> x0, starting transfers between devices: 10.1 us -> none  [the longest x1 4.73 us: fast_device(): lax.ppermute(bottom, both, forward)]
    ppermute x25, waiting for transfers between devices: 20.8 us -> 27.4 us  [partner(): return lax.ppermute(values, axis, [(i, i ^ flip) for i in range(count)])]
    ppermute x25, starting transfers between devices: 33.8 us -> 28.2 us  [partner(): return lax.ppermute(values, axis, [(i, i ^ flip) for i in range(count)])]
    ppermute x4 -> x0, waiting for transfers between devices: 3.77 us -> none  [the longest x1 2.68 us: fast_device(): high = lax.ppermute(edges[1], both, backward)]
    transpose x0 -> x1, local copies, waits for them, and re-layouts: none -> 1.05 us  [fast_device(): mom_rows = factor_mom.swapaxes(0, 1)]
    unnamed x17 -> x13, local copies, waits for them, and re-layouts: 3.4 us -> 2.37 us
  transfers between devices with their start and end apart: 29 -> 25, of which waited for: 17 -> 19; matrix products, arithmetic and copies ran while one was open for 5% -> 5% of each run, Pallas kernels for 0% -> 0%
where the time goes in v2:
time: 77.6 us; the launch traced here: 77.3 us
  starting transfers between devices  28.2 us (36%)
  waiting for transfers between devices  27.4 us (35%)
  Pallas kernels  14.9 us (19%)
  local copies, waits for them, and re-layouts  5.44 us (7%)
  between operations  0.81 us (1%)
    ppermute x25, starting transfers between devices, partner(): return lax.ppermute(values, axis, [(i, i ^ flip) for i in range(count)])  28.2 us
    ppermute x25, waiting for transfers between devices, partner(): return lax.ppermute(values, axis, [(i, i ^ flip) for i in range(count)])  27.4 us
    pallas_call x1, Pallas kernels, fast_device(): second(ranks, field_tau, count_rows, new_field, half, land_mask, log_expo...  7.13 us
    pallas_call x1, Pallas kernels, fast_device(): first(ranks, field_tau, count_rows, field_rows, mom_rows, land_mask, log_...  6.53 us
    unnamed x13, local copies, waits for them, and re-layouts  2.37 us
  transfers between devices with their start and end apart: 25, of which 19 were waited for; matrix products, arithmetic and copies ran while one was open for 5% of the time, Pallas kernels for 0%

profile of v2, /device:TPU:0, one launch (start us, length us, event | category | flops | bytes accessed | tf_op | source)
XLA Modules:
  0.0 77.3 jit_solution(15409413335219357196)
XLA Ops:
  2.3 5.0 %collective-permute-start.2 = (f32[144,128]{1,0:T(8,128)S(1)}, f32[144,128]{1,0:T(8,128)S(1)}, u32[]{:S(2)}, u32[]{:S(2)}) collective-permute-start(f32[144,128]{1,0:T(8,128)S(1)} %constant_dynamic-update-slice_fusion.refs_0_.own_ref), channel_id=1, source_target_pairs={{0,3},{1,2},{2,1},{3,0},{4,7},{5,6},{6,5},{7,4},{8,11},{9,10},{10,... | collective-permute-start | bytes 221192 | tf_op jit(solution)/shard_map/ppermute | solution.py:211
  7.9 1.3 %constant_dynamic-slice_fusion = s32[128,8,256]{2,1,0:T(8,128)S(1)} fusion(s32[128,32,256]{2,1,0:T(8,128)} %param.17, s32[]{:T(128)S(6)} %select_n.3), kind=kLoop, calls=%fused_computation.30 | loop fusion | bytes 2097156 | tf_op jit(solution)/shard_map/dynamic_slice | solution.py:611
  9.5 1.1 %copy_bitcast_fusion = (f32[8,16,256]{2,1,0:T(8,128)S(1)}, f32[8,16,256]{2,1,0:T(8,128)S(1)}) fusion(f32[16,8,256]{2,1,0:T(8,128)} %param.13, f32[16,8,256]{2,1,0:T(8,128)} %param.10), kind=kLoop, calls=%fused_computation.4 | loop fusion | bytes 524288 | tf_op jit(solution)/shard_map/transpose | solution.py:613
  10.6 2.9 %collective-permute-done.1.refs_2_ = f32[144,128]{1,0:T(8,128)S(1)} collective-permute-done((f32[144,128]{1,0:T(8,128)S(1)}, f32[144,128]{1,0:T(8,128)S(1)}, u32[]{:S(2)}, u32[]{:S(2)}) %collective-permute-start.1) | collective-permute-done | bytes 73760 | tf_op jit(solution)/shard_map/ppermute | solution.py:211
  13.6 6.5 %first_gradient.1 = (f32[8,16,256]{2,1,0:T(8,128)S(1)}, f32[8,16,256]{2,1,0:T(8,128)S(1)}, f32[72,128]{1,0:T(8,128)S(1)}, f32[72,128]{1,0:T(8,128)S(1)}, f32[576...) custom-call(s32[2]{0:T(128)S(1)} %pad_add_fusion.rank_ref, f32[16]{0:T(128)S(1)} %copy-done.4, ...), custom_call_target="tpu_custom_call" | custom-call | tf_op jit(solution)/shard_map/first_gradient/pallas_call | solution.py:676
  20.2 1.4 %collective-permute-done.3 = f32[4,72,128]{2,1,0:T(8,128)S(1)} collective-permute-done((f32[4,72,128]{2,1,0:T(8,128)S(1)}, f32[4,72,128]{2,1,0:T(8,128)S(1)}, u32[]{:S(2)}, u32[]{:S(2)}) %collective-permute-start.3) | collective-permute-done | bytes 147488 | tf_op jit(solution)/shard_map/ppermute | solution.py:211
  21.6 1.6 %collective-permute-start.4 = (f32[72,128]{1,0:T(8,128)S(1)}, f32[72,128]{1,0:T(8,128)S(1)}, u32[]{:S(2)}, u32[]{:S(2)}) collective-permute-start(f32[72,128]{1,0:T(8,128)S(1)} %get-tuple-element.49), channel_id=1, source_target_pairs={{0,8},{4,12},{8,0},{12,4},{16,24},{20,28},{24,16},{28,20},{1,9},{5... | collective-permute-start | bytes 110600 | tf_op jit(solution)/shard_map/ppermute | solution.py:211
  23.1 1.5 %collective-permute-start.6 = (f32[72,128]{1,0:T(8,128)S(1)}, f32[72,128]{1,0:T(8,128)S(1)}, u32[]{:S(2)}, u32[]{:S(2)}) collective-permute-start(f32[72,128]{1,0:T(8,128)S(1)} %get-tuple-element.50), channel_id=1, source_target_pairs={{0,24},{4,28},{8,16},{12,20},{16,8},{20,12},{24,0},{28,4},{1,25},{... | collective-permute-start | bytes 110600 | tf_op jit(solution)/shard_map/ppermute | solution.py:211
  25.6 2.4 %collective-permute-done.6 = f32[72,128]{1,0:T(8,128)S(1)} collective-permute-done((f32[72,128]{1,0:T(8,128)S(1)}, f32[72,128]{1,0:T(8,128)S(1)}, u32[]{:S(2)}, u32[]{:S(2)}) %collective-permute-start.6) | collective-permute-done | bytes 36896 | tf_op jit(solution)/shard_map/ppermute | solution.py:211
  28.6 1.1 %collective-permute-start.7 = (f32[144,128]{1,0:T(8,128)S(1)}, f32[144,128]{1,0:T(8,128)S(1)}, u32[]{:S(2)}, u32[]{:S(2)}) collective-permute-start(f32[144,128]{1,0:T(8,128)S(1)} %get-tuple-element.57), channel_id=1, source_target_pairs={{0,1},{1,0},{2,3},{3,2},{4,5},{5,4},{6,7},{7,6},{8,9},{9,8},{10,11... | collective-permute-start | bytes 221192 | tf_op jit(solution)/shard_map/ppermute | solution.py:211
  29.7 1.7 %collective-permute-start.9 = (f32[144,128]{1,0:T(8,128)S(1)}, f32[144,128]{1,0:T(8,128)S(1)}, u32[]{:S(2)}, u32[]{:S(2)}) collective-permute-start(f32[144,128]{1,0:T(8,128)S(1)} %get-tuple-element.58), channel_id=1, source_target_pairs={{0,3},{1,2},{2,1},{3,0},{4,7},{5,6},{6,5},{7,4},{8,11},{9,10},{10,... | collective-permute-start | bytes 221192 | tf_op jit(solution)/shard_map/ppermute | solution.py:211
  32.2 4.1 %collective-permute-done.8 = f32[72,128]{1,0:T(8,128)S(1)} collective-permute-done((f32[72,128]{1,0:T(8,128)S(1)}, f32[72,128]{1,0:T(8,128)S(1)}, u32[]{:S(2)}, u32[]{:S(2)}) %collective-permute-start.8) | collective-permute-done | bytes 36896 | tf_op jit(solution)/shard_map/ppermute | solution.py:211
  36.3 1.1 %collective-permute-start.11 = (f32[144,128]{1,0:T(8,128)S(1)}, f32[144,128]{1,0:T(8,128)S(1)}, u32[]{:S(2)}, u32[]{:S(2)}) collective-permute-start(f32[144,128]{1,0:T(8,128)S(1)} %get-tuple-element.56), channel_id=1, source_target_pairs={{0,16},{4,20},{8,24},{12,28},{16,0},{20,4},{24,8},{28,12},{1,17},{... | collective-permute-start | bytes 221192 | tf_op jit(solution)/shard_map/ppermute | solution.py:211
  37.4 1.0 %collective-permute-start.10 = (f32[144,128]{1,0:T(8,128)S(1)}, f32[144,128]{1,0:T(8,128)S(1)}, u32[]{:S(2)}, u32[]{:S(2)}) collective-permute-start(f32[144,128]{1,0:T(8,128)S(1)} %get-tuple-element.56), channel_id=1, source_target_pairs={{0,8},{4,12},{8,0},{12,4},{16,24},{20,28},{24,16},{28,20},{1,9},{5... | collective-permute-start | bytes 221192 | tf_op jit(solution)/shard_map/ppermute | solution.py:211
  38.4 1.5 %collective-permute-start.12 = (f32[144,128]{1,0:T(8,128)S(1)}, f32[144,128]{1,0:T(8,128)S(1)}, u32[]{:S(2)}, u32[]{:S(2)}) collective-permute-start(f32[144,128]{1,0:T(8,128)S(1)} %get-tuple-element.56), channel_id=1, source_target_pairs={{0,24},{4,28},{8,16},{12,20},{16,8},{20,12},{24,0},{28,4},{1,25},{... | collective-permute-start | bytes 221192 | tf_op jit(solution)/shard_map/ppermute | solution.py:211
  40.7 1.0 %collective-permute-done.10 = f32[144,128]{1,0:T(8,128)S(1)} collective-permute-done((f32[144,128]{1,0:T(8,128)S(1)}, f32[144,128]{1,0:T(8,128)S(1)}, u32[]{:S(2)}, u32[]{:S(2)}) %collective-permute-start.10) | collective-permute-done | bytes 73760 | tf_op jit(solution)/shard_map/ppermute | solution.py:211
  41.7 1.9 %collective-permute-done.12 = f32[144,128]{1,0:T(8,128)S(1)} collective-permute-done((f32[144,128]{1,0:T(8,128)S(1)}, f32[144,128]{1,0:T(8,128)S(1)}, u32[]{:S(2)}, u32[]{:S(2)}) %collective-permute-start.12) | collective-permute-done | bytes 73760 | tf_op jit(solution)/shard_map/ppermute | solution.py:211
  43.7 1.6 %collective-permute-done.13.far_ref = f32[4,144,128]{2,1,0:T(8,128)S(1)} collective-permute-done((f32[4,144,128]{2,1,0:T(8,128)S(1)}, f32[4,144,128]{2,1,0:T(8,128)S(1)}, u32[]{:S(2)}, u32[]{:S(2)}) %collective-permute-start.13) | collective-permute-done | bytes 294944 | tf_op jit(solution)/shard_map/ppermute | solution.py:211
  45.3 7.1 %second_gradient.1 = (f32[8,16,256]{2,1,0:T(8,128)S(1)}, f32[8,16,256]{2,1,0:T(8,128)S(1)}, f32[128,128]{1,0:T(8,128)}, f32[16,128]{1,0:T(8,128)}, f32[4,80,128]{2,1,0:T(8,128)S(1)}, /*index=5*/f32[4,80,128]{2,1,0:T(8,128)S(1)}) custom-call(s32[2]{0:T(128)S(1)} %pad_add_fusion.rank_ref, f32[16]{0:T(128)S(1)} %copy-done.4, ...), custom_call_target="tpu_custom_call" | custom-call | tf_op jit(solution)/shard_map/second_gradient/pallas_call | solution.py:707
  52.6 1.3 %collective-permute-done.14 = f32[4,80,128]{2,1,0:T(8,128)S(1)} collective-permute-done((f32[4,80,128]{2,1,0:T(8,128)S(1)}, f32[4,80,128]{2,1,0:T(8,128)S(1)}, u32[]{:S(2)}, u32[]{:S(2)}) %collective-permute-start.14) | collective-permute-done | bytes 163872 | tf_op jit(solution)/shard_map/ppermute | solution.py:211
  53.9 1.1 %collective-permute-start.15 = (f32[80,128]{1,0:T(8,128)S(1)}, f32[80,128]{1,0:T(8,128)S(1)}, u32[]{:S(2)}, u32[]{:S(2)}) collective-permute-start(f32[80,128]{1,0:T(8,128)S(1)} %get-tuple-element.46), channel_id=1, source_target_pairs={{0,8},{4,12},{8,0},{12,4},{16,24},{20,28},{24,16},{28,20},{1,9},{5... | collective-permute-start | bytes 122888 | tf_op jit(solution)/shard_map/ppermute | solution.py:211
  55.0 2.0 %collective-permute-start.17 = (f32[80,128]{1,0:T(8,128)S(1)}, f32[80,128]{1,0:T(8,128)S(1)}, u32[]{:S(2)}, u32[]{:S(2)}) collective-permute-start(f32[80,128]{1,0:T(8,128)S(1)} %get-tuple-element.47), channel_id=1, source_target_pairs={{0,24},{4,28},{8,16},{12,20},{16,8},{20,12},{24,0},{28,4},{1,25},{... | collective-permute-start | bytes 122888 | tf_op jit(solution)/shard_map/ppermute | solution.py:211
  58.1 1.9 %collective-permute-done.17 = f32[80,128]{1,0:T(8,128)S(1)} collective-permute-done((f32[80,128]{1,0:T(8,128)S(1)}, f32[80,128]{1,0:T(8,128)S(1)}, u32[]{:S(2)}, u32[]{:S(2)}) %collective-permute-start.17) | collective-permute-done | bytes 40992 | tf_op jit(solution)/shard_map/ppermute | solution.py:211
  60.0 0.9 %collective-permute-done.16 = f32[80,128]{1,0:T(8,128)S(1)} collective-permute-done((f32[80,128]{1,0:T(8,128)S(1)}, f32[80,128]{1,0:T(8,128)S(1)}, u32[]{:S(2)}, u32[]{:S(2)}) %collective-permute-start.16) | collective-permute-done | bytes 40992 | tf_op jit(solution)/shard_map/ppermute | solution.py:211
  60.9 2.5 %collective-permute-start.20 = (f32[80,128]{1,0:T(8,128)S(1)}, f32[80,128]{1,0:T(8,128)S(1)}, u32[]{:S(2)}, u32[]{:S(2)}) collective-permute-start(f32[80,128]{1,0:T(8,128)S(1)} %fusion.3), channel_id=1, source_target_pairs={{0,3},{1,2},{2,1},{3,0},{4,7},{5,6},{6,5},{7,4},{8,11},{9,10},{10,... | collective-permute-start | bytes 122888 | tf_op jit(solution)/shard_map/ppermute | solution.py:211
  63.5 1.9 %collective-permute-start.18 = (f32[80,128]{1,0:T(8,128)S(1)}, f32[80,128]{1,0:T(8,128)S(1)}, u32[]{:S(2)}, u32[]{:S(2)}) collective-permute-start(f32[80,128]{1,0:T(8,128)S(1)} %fusion.3), channel_id=1, source_target_pairs={{0,1},{1,0},{2,3},{3,2},{4,5},{5,4},{6,7},{7,6},{8,9},{9,8},{10,11... | collective-permute-start | bytes 122888 | tf_op jit(solution)/shard_map/ppermute | solution.py:211
  65.4 1.4 %collective-permute-done.20 = f32[80,128]{1,0:T(8,128)S(1)} collective-permute-done((f32[80,128]{1,0:T(8,128)S(1)}, f32[80,128]{1,0:T(8,128)S(1)}, u32[]{:S(2)}, u32[]{:S(2)}) %collective-permute-start.20) | collective-permute-done | bytes 40992 | tf_op jit(solution)/shard_map/ppermute | solution.py:211
  66.8 1.6 %collective-permute-done.19 = f32[80,128]{1,0:T(8,128)S(1)} collective-permute-done((f32[80,128]{1,0:T(8,128)S(1)}, f32[80,128]{1,0:T(8,128)S(1)}, u32[]{:S(2)}, u32[]{:S(2)}) %collective-permute-start.19) | collective-permute-done | bytes 40992 | tf_op jit(solution)/shard_map/ppermute | solution.py:211
  68.4 1.4 %collective-permute-start.23 = (f32[80,128]{1,0:T(8,128)S(1)}, f32[80,128]{1,0:T(8,128)S(1)}, u32[]{:S(2)}, u32[]{:S(2)}) collective-permute-start(f32[80,128]{1,0:T(8,128)S(1)} %add_add_fusion), channel_id=1, source_target_pairs={{0,24},{4,28},{8,16},{12,20},{16,8},{20,12},{24,0},{28,4},{1,25},{... | collective-permute-start | bytes 122888 | tf_op jit(solution)/shard_map/ppermute | solution.py:211
  70.5 1.5 %collective-permute-start.21 = (f32[80,128]{1,0:T(8,128)S(1)}, f32[80,128]{1,0:T(8,128)S(1)}, u32[]{:S(2)}, u32[]{:S(2)}) collective-permute-start(f32[80,128]{1,0:T(8,128)S(1)} %add_add_fusion), channel_id=1, source_target_pairs={{0,8},{4,12},{8,0},{12,4},{16,24},{20,28},{24,16},{28,20},{1,9},{5... | collective-permute-start | bytes 122888 | tf_op jit(solution)/shard_map/ppermute | solution.py:211
  71.9 1.4 %collective-permute-done.23 = f32[80,128]{1,0:T(8,128)S(1)} collective-permute-done((f32[80,128]{1,0:T(8,128)S(1)}, f32[80,128]{1,0:T(8,128)S(1)}, u32[]{:S(2)}, u32[]{:S(2)}) %collective-permute-start.23) | collective-permute-done | bytes 40992 | tf_op jit(solution)/shard_map/ppermute | solution.py:211
  76.0 1.3 %momenta.1 = (f32[128,128]{1,0:T(8,128)}, f32[16,128]{1,0:T(8,128)}, f32[1,1]{1,0:T(1,128)}) custom-call(s32[2]{0:T(128)S(1)} %pad_add_fusion.rank_ref, f32[4,80,128]{2,1,0:T(8,128)S(1)} %pad_maximum_fusion.1.near_ref, f32[4,80,128]{2,1,0:T(8,128)S(1)} %collective-permute-done.24.far_ref), custom_call_target="tpu_custom_call" | custom-call | tf_op jit(solution)/shard_map/momenta/pallas_call | solution.py:719
  (51 shorter events, 10.7 us)
Async XLA Ops:
  0.6 12.9 %copy-start.2 = (f32[32,256]{1,0:T(8,128)S(1)}, f32[32,256]{1,0:T(8,128)}, u32[]{:S(2)}) copy-start(f32[32,256]{1,0:T(8,128)} %logexp_ref.3) | copy-start | bytes 98308
  0.6 12.9 %copy-start.1 = (s32[32,256]{1,0:T(8,128)S(1)}, s32[32,256]{1,0:T(8,128)}, u32[]{:S(2)}) copy-start(s32[32,256]{1,0:T(8,128)} %land_ref.3) | copy-start | bytes 98308
  0.7 12.9 %copy-start.4 = (f32[16]{0:T(128)S(1)}, f32[16]{0:T(128)}, u32[]{:S(2)}) copy-start(f32[16]{0:T(128)} %tau_ref.3) | copy-start | bytes 196
  0.7 12.9 %copy-start.3 = (f32[16,128]{1,0:T(8,128)S(1)}, f32[16,128]{1,0:T(8,128)}, u32[]{:S(2)}) copy-start(f32[16,128]{1,0:T(8,128)} %wmom_ref.3) | copy-start | bytes 24580
  0.7 12.9 %copy-start = (f32[128,128]{1,0:T(8,128)S(1)}, f32[128,128]{1,0:T(8,128)}, u32[]{:S(2)}) copy-start(f32[128,128]{1,0:T(8,128)} %pmom_ref.3) | copy-start | bytes 196612
  2.3 8.3 %collective-permute-start.2 = (f32[144,128]{1,0:T(8,128)S(1)}, f32[144,128]{1,0:T(8,128)S(1)}, u32[]{:S(2)}, u32[]{:S(2)}) collective-permute-start(f32[144,128]{1,0:T(8,128)S(1)} %constant_dynamic-update-slice_fusion.refs_0_.own_ref), channel_id=1, source_target_pairs={{0,3},{1,2},{2,1},{3,0},{4,7},{5,6},{6,5},{7,4},{8,11},{9,10},{10,... | collective-permute-start | bytes 221192 | tf_op jit(solution)/shard_map/ppermute | solution.py:211
  7.3 6.2 %collective-permute-start.1 = (f32[144,128]{1,0:T(8,128)S(1)}, f32[144,128]{1,0:T(8,128)S(1)}, u32[]{:S(2)}, u32[]{:S(2)}) collective-permute-start(f32[144,128]{1,0:T(8,128)S(1)} %constant_dynamic-update-slice_fusion.refs_0_.own_ref), channel_id=1, source_target_pairs={{0,2},{1,3},{2,0},{3,1},{4,6},{5,7},{6,4},{7,5},{8,10},{9,11},{10,... | collective-permute-start | bytes 221192 | tf_op jit(solution)/shard_map/ppermute | solution.py:211
  7.3 6.2 %collective-permute-start = (f32[144,128]{1,0:T(8,128)S(1)}, f32[144,128]{1,0:T(8,128)S(1)}, u32[]{:S(2)}, u32[]{:S(2)}) collective-permute-start(f32[144,128]{1,0:T(8,128)S(1)} %constant_dynamic-update-slice_fusion.refs_0_.own_ref), channel_id=1, source_target_pairs={{0,1},{1,0},{2,3},{3,2},{4,5},{5,4},{6,7},{7,6},{8,9},{9,8},{10,11... | collective-permute-start | bytes 221192 | tf_op jit(solution)/shard_map/ppermute | solution.py:211
  20.1 1.4 %collective-permute-start.3 = (f32[4,72,128]{2,1,0:T(8,128)S(1)}, f32[4,72,128]{2,1,0:T(8,128)S(1)}, u32[]{:S(2)}, u32[]{:S(2)}) collective-permute-start(f32[4,72,128]{2,1,0:T(8,128)S(1)} %get-tuple-element.26), channel_id=1, source_target_pairs={{0,4},{4,0},{8,12},{12,8},{16,20},{20,16},{24,28},{28,24},{1,5},{5... | collective-permute-start | bytes 442376 | tf_op jit(solution)/shard_map/ppermute | solution.py:211
  21.6 4.0 %collective-permute-start.4 = (f32[72,128]{1,0:T(8,128)S(1)}, f32[72,128]{1,0:T(8,128)S(1)}, u32[]{:S(2)}, u32[]{:S(2)}) collective-permute-start(f32[72,128]{1,0:T(8,128)S(1)} %get-tuple-element.49), channel_id=1, source_target_pairs={{0,8},{4,12},{8,0},{12,4},{16,24},{20,28},{24,16},{28,20},{1,9},{5... | collective-permute-start | bytes 110600 | tf_op jit(solution)/shard_map/ppermute | solution.py:211
  23.1 4.9 %collective-permute-start.6 = (f32[72,128]{1,0:T(8,128)S(1)}, f32[72,128]{1,0:T(8,128)S(1)}, u32[]{:S(2)}, u32[]{:S(2)}) collective-permute-start(f32[72,128]{1,0:T(8,128)S(1)} %get-tuple-element.50), channel_id=1, source_target_pairs={{0,24},{4,28},{8,16},{12,20},{16,8},{20,12},{24,0},{28,4},{1,25},{... | collective-permute-start | bytes 110600 | tf_op jit(solution)/shard_map/ppermute | solution.py:211
  24.6 4.0 %collective-permute-start.5 = (f32[72,128]{1,0:T(8,128)S(1)}, f32[72,128]{1,0:T(8,128)S(1)}, u32[]{:S(2)}, u32[]{:S(2)}) collective-permute-start(f32[72,128]{1,0:T(8,128)S(1)} %get-tuple-element.51), channel_id=1, source_target_pairs={{0,16},{4,20},{8,24},{12,28},{16,0},{20,4},{24,8},{28,12},{1,17},{... | collective-permute-start | bytes 110600 | tf_op jit(solution)/shard_map/ppermute | solution.py:211
  28.6 7.7 %collective-permute-start.7 = (f32[144,128]{1,0:T(8,128)S(1)}, f32[144,128]{1,0:T(8,128)S(1)}, u32[]{:S(2)}, u32[]{:S(2)}) collective-permute-start(f32[144,128]{1,0:T(8,128)S(1)} %get-tuple-element.57), channel_id=1, source_target_pairs={{0,1},{1,0},{2,3},{3,2},{4,5},{5,4},{6,7},{7,6},{8,9},{9,8},{10,11... | collective-permute-start | bytes 221192 | tf_op jit(solution)/shard_map/ppermute | solution.py:211
  29.7 6.6 %collective-permute-start.9 = (f32[144,128]{1,0:T(8,128)S(1)}, f32[144,128]{1,0:T(8,128)S(1)}, u32[]{:S(2)}, u32[]{:S(2)}) collective-permute-start(f32[144,128]{1,0:T(8,128)S(1)} %get-tuple-element.58), channel_id=1, source_target_pairs={{0,3},{1,2},{2,1},{3,0},{4,7},{5,6},{6,5},{7,4},{8,11},{9,10},{10,... | collective-permute-start | bytes 221192 | tf_op jit(solution)/shard_map/ppermute | solution.py:211
  31.4 4.9 %collective-permute-start.8 = (f32[72,128]{1,0:T(8,128)S(1)}, f32[72,128]{1,0:T(8,128)S(1)}, u32[]{:S(2)}, u32[]{:S(2)}) collective-permute-start(f32[72,128]{1,0:T(8,128)S(1)} %fusion.7), channel_id=1, source_target_pairs={{0,2},{1,3},{2,0},{3,1},{4,6},{5,7},{6,4},{7,5},{8,10},{9,11},{10,... | collective-permute-start | bytes 110600 | tf_op jit(solution)/shard_map/ppermute | solution.py:211
  36.3 4.4 %collective-permute-start.11 = (f32[144,128]{1,0:T(8,128)S(1)}, f32[144,128]{1,0:T(8,128)S(1)}, u32[]{:S(2)}, u32[]{:S(2)}) collective-permute-start(f32[144,128]{1,0:T(8,128)S(1)} %get-tuple-element.56), channel_id=1, source_target_pairs={{0,16},{4,20},{8,24},{12,28},{16,0},{20,4},{24,8},{28,12},{1,17},{... | collective-permute-start | bytes 221192 | tf_op jit(solution)/shard_map/ppermute | solution.py:211
  37.4 4.4 %collective-permute-start.10 = (f32[144,128]{1,0:T(8,128)S(1)}, f32[144,128]{1,0:T(8,128)S(1)}, u32[]{:S(2)}, u32[]{:S(2)}) collective-permute-start(f32[144,128]{1,0:T(8,128)S(1)} %get-tuple-element.56), channel_id=1, source_target_pairs={{0,8},{4,12},{8,0},{12,4},{16,24},{20,28},{24,16},{28,20},{1,9},{5... | collective-permute-start | bytes 221192 | tf_op jit(solution)/shard_map/ppermute | solution.py:211
  38.4 5.3 %collective-permute-start.12 = (f32[144,128]{1,0:T(8,128)S(1)}, f32[144,128]{1,0:T(8,128)S(1)}, u32[]{:S(2)}, u32[]{:S(2)}) collective-permute-start(f32[144,128]{1,0:T(8,128)S(1)} %get-tuple-element.56), channel_id=1, source_target_pairs={{0,24},{4,28},{8,16},{12,20},{16,8},{20,12},{24,0},{28,4},{1,25},{... | collective-permute-start | bytes 221192 | tf_op jit(solution)/shard_map/ppermute | solution.py:211
  43.7 1.6 %collective-permute-start.13 = (f32[4,144,128]{2,1,0:T(8,128)S(1)}, f32[4,144,128]{2,1,0:T(8,128)S(1)}, u32[]{:S(2)}, u32[]{:S(2)}) collective-permute-start(f32[4,144,128]{2,1,0:T(8,128)S(1)} %pad_maximum_fusion.near_ref), channel_id=1, source_target_pairs={{0,4},{4,0},{8,12},{12,8},{16,20},{20,16},{24,28},{28,24},{1,5},{5... | collective-permute-start | bytes 884744 | tf_op jit(solution)/shard_map/ppermute | solution.py:211
  52.4 1.4 %collective-permute-start.14 = (f32[4,80,128]{2,1,0:T(8,128)S(1)}, f32[4,80,128]{2,1,0:T(8,128)S(1)}, u32[]{:S(2)}, u32[]{:S(2)}) collective-permute-start(f32[4,80,128]{2,1,0:T(8,128)S(1)} %get-tuple-element.35), channel_id=1, source_target_pairs={{0,4},{4,0},{8,12},{12,8},{16,20},{20,16},{24,28},{28,24},{1,5},{5... | collective-permute-start | bytes 491528 | tf_op jit(solution)/shard_map/ppermute | solution.py:211
  53.9 4.2 %collective-permute-start.15 = (f32[80,128]{1,0:T(8,128)S(1)}, f32[80,128]{1,0:T(8,128)S(1)}, u32[]{:S(2)}, u32[]{:S(2)}) collective-permute-start(f32[80,128]{1,0:T(8,128)S(1)} %get-tuple-element.46), channel_id=1, source_target_pairs={{0,8},{4,12},{8,0},{12,4},{16,24},{20,28},{24,16},{28,20},{1,9},{5... | collective-permute-start | bytes 122888 | tf_op jit(solution)/shard_map/ppermute | solution.py:211
  55.0 5.0 %collective-permute-start.17 = (f32[80,128]{1,0:T(8,128)S(1)}, f32[80,128]{1,0:T(8,128)S(1)}, u32[]{:S(2)}, u32[]{:S(2)}) collective-permute-start(f32[80,128]{1,0:T(8,128)S(1)} %get-tuple-element.47), channel_id=1, source_target_pairs={{0,24},{4,28},{8,16},{12,20},{16,8},{20,12},{24,0},{28,4},{1,25},{... | collective-permute-start | bytes 122888 | tf_op jit(solution)/shard_map/ppermute | solution.py:211
  56.9 4.0 %collective-permute-start.16 = (f32[80,128]{1,0:T(8,128)S(1)}, f32[80,128]{1,0:T(8,128)S(1)}, u32[]{:S(2)}, u32[]{:S(2)}) collective-permute-start(f32[80,128]{1,0:T(8,128)S(1)} %get-tuple-element.48), channel_id=1, source_target_pairs={{0,16},{4,20},{8,24},{12,28},{16,0},{20,4},{24,8},{28,12},{1,17},{... | collective-permute-start | bytes 122888 | tf_op jit(solution)/shard_map/ppermute | solution.py:211
  60.9 5.9 %collective-permute-start.20 = (f32[80,128]{1,0:T(8,128)S(1)}, f32[80,128]{1,0:T(8,128)S(1)}, u32[]{:S(2)}, u32[]{:S(2)}) collective-permute-start(f32[80,128]{1,0:T(8,128)S(1)} %fusion.3), channel_id=1, source_target_pairs={{0,3},{1,2},{2,1},{3,0},{4,7},{5,6},{6,5},{7,4},{8,11},{9,10},{10,... | collective-permute-start | bytes 122888 | tf_op jit(solution)/shard_map/ppermute | solution.py:211
  63.5 4.9 %collective-permute-start.19 = (f32[80,128]{1,0:T(8,128)S(1)}, f32[80,128]{1,0:T(8,128)S(1)}, u32[]{:S(2)}, u32[]{:S(2)}) collective-permute-start(f32[80,128]{1,0:T(8,128)S(1)} %fusion.3), channel_id=1, source_target_pairs={{0,2},{1,3},{2,0},{3,1},{4,6},{5,7},{6,4},{7,5},{8,10},{9,11},{10,... | collective-permute-start | bytes 122888 | tf_op jit(solution)/shard_map/ppermute | solution.py:211
  63.5 4.8 %collective-permute-start.18 = (f32[80,128]{1,0:T(8,128)S(1)}, f32[80,128]{1,0:T(8,128)S(1)}, u32[]{:S(2)}, u32[]{:S(2)}) collective-permute-start(f32[80,128]{1,0:T(8,128)S(1)} %fusion.3), channel_id=1, source_target_pairs={{0,1},{1,0},{2,3},{3,2},{4,5},{5,4},{6,7},{7,6},{8,9},{9,8},{10,11... | collective-permute-start | bytes 122888 | tf_op jit(solution)/shard_map/ppermute | solution.py:211
  68.4 5.0 %collective-permute-start.23 = (f32[80,128]{1,0:T(8,128)S(1)}, f32[80,128]{1,0:T(8,128)S(1)}, u32[]{:S(2)}, u32[]{:S(2)}) collective-permute-start(f32[80,128]{1,0:T(8,128)S(1)} %add_add_fusion), channel_id=1, source_target_pairs={{0,24},{4,28},{8,16},{12,20},{16,8},{20,12},{24,0},{28,4},{1,25},{... | collective-permute-start | bytes 122888 | tf_op jit(solution)/shard_map/ppermute | solution.py:211
  69.8 4.0 %collective-permute-start.22 = (f32[80,128]{1,0:T(8,128)S(1)}, f32[80,128]{1,0:T(8,128)S(1)}, u32[]{:S(2)}, u32[]{:S(2)}) collective-permute-start(f32[80,128]{1,0:T(8,128)S(1)} %add_add_fusion), channel_id=1, source_target_pairs={{0,16},{4,20},{8,24},{12,28},{16,0},{20,4},{24,8},{28,12},{1,17},{... | collective-permute-start | bytes 122888 | tf_op jit(solution)/shard_map/ppermute | solution.py:211
  70.5 4.0 %collective-permute-start.21 = (f32[80,128]{1,0:T(8,128)S(1)}, f32[80,128]{1,0:T(8,128)S(1)}, u32[]{:S(2)}, u32[]{:S(2)}) collective-permute-start(f32[80,128]{1,0:T(8,128)S(1)} %add_add_fusion), channel_id=1, source_target_pairs={{0,8},{4,12},{8,0},{12,4},{16,24},{20,28},{24,16},{28,20},{1,9},{5... | collective-permute-start | bytes 122888 | tf_op jit(solution)/shard_map/ppermute | solution.py:211
  74.5 1.6 %collective-permute-start.24 = (f32[4,80,128]{2,1,0:T(8,128)S(1)}, f32[4,80,128]{2,1,0:T(8,128)S(1)}, u32[]{:S(2)}, u32[]{:S(2)}) collective-permute-start(f32[4,80,128]{2,1,0:T(8,128)S(1)} %pad_maximum_fusion.1.near_ref), channel_id=1, source_target_pairs={{0,4},{4,0},{8,12},{12,8},{16,20},{20,16},{24,28},{28,24},{1,5},{5... | collective-permute-start | bytes 491528 | tf_op jit(solution)/shard_map/ppermute | solution.py:211

commit v3 on v2

--- a/solution.py
+++ b/solution.py
@@ -189,6 +189,7 @@
 LOG2E = math.log2(math.e)
 LN2 = math.log(2.0)
 LANES = 128
+EXTRA = 16
 F32 = jnp.float32
 BF16 = jnp.bfloat16
 
@@ -211,12 +212,13 @@
     return lax.ppermute(values, axis, [(i, i ^ flip) for i in range(count)])
 
 
-def all_sum(keep, send, near_edge=None, far_edge=None):
+def all_sum(keep, send, near_edge=None, far_edge=None, beside=()):
     pairs, rows, _ = keep.shape
     chunks = keep + partner(send, "cells", 1)
     total = chunks[0]
     for part in [partner(chunks[k], "cells", 2 * k) for k in range(1, pairs)]:
         total = total + part
+    total, beside = lax.optimization_barrier((total, beside))
     if near_edge is None:
         parts = [partner(total, "comp", k) for k in range(1, lax.axis_size("comp"))]
         near_got = None
@@ -229,7 +231,17 @@
         near_got = first[rows:]
         total = jnp.concatenate([total + first[:rows] + second + third[:rows], third[rows:]], axis=0)
     near = jnp.stack([total] + [partner(total, "cells", 2 * k) for k in range(1, pairs)])
-    return near, partner(near, "cells", 1), near_got
+    return near, partner(near, "cells", 1), near_got, beside
+
+
+def gather_params(pack, cells_rank):
+    tiles, ring = lax.axis_size("cells"), lax.axis_size("comp")
+    rows = pack.shape[0]
+    spread = [(c * ring + z, c * ring + (z ^ (1 + c % 2))) for c in range(tiles) for z in range(ring)]
+    one = lax.ppermute(pack, ("cells", "comp"), spread)
+    half = lax.dynamic_slice_in_dim(pack, cells_rank % 2 * (rows // 2), rows // 2, 0)
+    got = jnp.concatenate([one, partner(half, "comp", 3)], axis=0)
+    return got, partner(got, "cells", 1)
 
 
 def chunk_index(cells_rank, k, other):
@@ -254,7 +266,7 @@
 
 def load_params(flat_ref, left_ref, mix_ref, load_ref, ncomp, nfac):
     lane = lax.broadcasted_iota(jnp.int32, (LANES, LANES), 1)
-    first = 6 * nfac
+    spare = jnp.zeros((LANES - EXTRA - 6 * nfac, LANES), F32)
     for q in range(ncomp // LANES):
         rows = pl.ds(q * LANES, LANES)
         prof = flat_ref[rows, :]
@@ -267,16 +279,12 @@
         load = flat_ref[pl.ds(ncomp + q * nfac, nfac), :]
         w_high, w_mid, w_low = [part.astype(F32) for part in pieces(load * LOG2E, 3)]
         stack = jnp.concatenate(
-            [w_high, w_high, w_high, w_mid, w_mid, w_low, jnp.zeros((LANES - first, LANES), F32)], axis=0
+            [jnp.zeros((EXTRA, LANES), F32), w_high, w_high, w_high, w_mid, w_mid, w_low, spare], axis=0
         )
         turned = stack.T
         mix_ref[rows, :] = turned.astype(BF16)
         rate_part = jnp.where(
-            (lane >= first) & (lane < first + 3),
-            rate_high,
-            jnp.where(
-                (lane >= first + 3) & (lane < first + 5), rate_mid, jnp.where(lane == first + 5, rate_low, 0.0)
-            ),
+            lane < 3, rate_high, jnp.where(lane < 5, rate_mid, jnp.where(lane == 5, rate_low, 0.0))
         )
         left_ref[rows, LANES : 2 * LANES] = (turned - rate_part).astype(BF16)
         load_high, load_mid = pieces(load, 2)
@@ -284,11 +292,12 @@
         load_ref[nfac : 2 * nfac, q * LANES : (q + 1) * LANES] = load_mid
 
 
-def load_cells(counts_ref, field_ref, logexp_ref, right_ref, wide_ref):
+def load_cells(counts_ref, field_ref, log_exposure, right_ref, wide_ref):
     share, ncat, cols = counts_ref.shape
     nfac = field_ref.shape[1]
-    exposure = jnp.exp(logexp_ref[...])
-    sub = lax.broadcasted_iota(jnp.int32, (LANES - 6 * nfac, cols), 0)
+    exposure = jnp.exp(log_exposure)
+    sub = lax.broadcasted_iota(jnp.int32, (EXTRA, cols), 0)
+    spare = jnp.zeros((LANES - EXTRA - 6 * nfac, cols), BF16)
     for r in range(share):
         count = counts_ref[r]
         high, mid, low = pieces(field_ref[r], 3)
@@ -296,7 +305,7 @@
         e_rows = jnp.where((sub == 0) | (sub == 3) | (sub == 5), e_high, 0.0)
         e_rows = jnp.where((sub == 1) | (sub == 4), e_mid, e_rows)
         e_rows = jnp.where(sub == 2, e_low, e_rows).astype(BF16)
-        extra = jnp.concatenate([high, mid, low, high, mid, high, e_rows], axis=0)
+        extra = jnp.concatenate([e_rows, high, mid, low, high, mid, high, spare], axis=0)
         right_ref[r, 0:ncat, :] = count
         right_ref[r, LANES : 2 * LANES, :] = extra
         right_ref[r, 2 * LANES : 2 * LANES + ncat, :] = count
@@ -404,8 +413,9 @@
     nfac = load_ref.shape[0] // 2
     cols = prior_ref.shape[2]
     last = ((1,), (1,))
+    start = LANES + EXTRA
     acc = dot(post_ref[...], wide_ref[r], last)
-    accw = dot(gap_ref[...], wide_ref[r, LANES : 2 * LANES, :], last)
+    accw = dot(wide_ref[r, start : start + 3 * nfac, :], gap_ref[...], last)
     if r == 0:
         acc_ref[...] = acc
         accw_ref[...] = accw
@@ -437,36 +447,42 @@
 
 def param_grads(flat_ref, acc_ref, accw_ref, grad_ref, ncomp, nfac):
     lane = lax.broadcasted_iota(jnp.int32, (LANES, LANES), 1)
-    rate_lanes = (lane >= 6 * nfac) & (lane < 6 * nfac + 3)
     for q in range(ncomp // LANES):
         rows = pl.ds(q * LANES, LANES)
-        mass = jnp.sum(jnp.where(rate_lanes, acc_ref[rows, LANES : 2 * LANES], 0.0), axis=1, keepdims=True)
+        lanes = slice(q * LANES, (q + 1) * LANES)
+        mass = jnp.sum(jnp.where(lane < 3, acc_ref[rows, LANES : 2 * LANES], 0.0), axis=1, keepdims=True)
         grad_ref[rows, :] = acc_ref[rows, 0:LANES] - jnp.exp(flat_ref[rows, :]) * mass
-        turned = accw_ref[rows, :].T
-        grad_ref[pl.ds(ncomp + q * nfac, nfac), :] = (
-            turned[0:nfac] + turned[nfac : 2 * nfac] + turned[2 * nfac : 3 * nfac]
-        )
+        load = accw_ref[:, lanes]
+        grad_ref[pl.ds(ncomp + q * nfac, nfac), :] = load[0:nfac] + load[nfac : 2 * nfac] + load[2 * nfac : 3 * nfac]
 
 
 def first_kernel(
     ncomp, rank_ref, tau_ref, counts_ref, field_ref, mom_ref, land_ref, logexp_ref, pmom_ref, wmom_ref, *refs
 ):
-    ring = ncomp // pmom_ref.shape[0]
-    part_refs = refs[:ring]
-    (new_ref, half_ref, near_ref, far_ref, grad_ref, keep_ref, send_ref) = refs[ring : ring + 7]
+    (pack_ref, got_ref, others_ref, new_ref, half_ref, near_ref, far_ref, grad_ref, keep_ref, send_ref) = refs[:10]
     (flat, left, mix, load, right, wide, prior, score0, score1, logit0, logit1, post0, post1, gap0, gap1, acc, accw) = (
-        refs[ring + 7 :]
-    )
+        refs[10:27]
+    )
+    (stage,) = refs[27:]
     cells_rank, comp_rank = rank_ref[0], rank_ref[1]
     share, nfac, cols = field_ref.shape
     mine = pmom_ref.shape[0]
-    for k in range(ring):
-        group = comp_rank ^ k
-        flat[pl.ds(pl.multiple_of(group * mine, mine), mine), :] = part_refs[k][0:mine, :]
-        flat[pl.ds(pl.multiple_of(ncomp + group * nfac, nfac), nfac), :] = part_refs[k][mine : mine + nfac, :]
-    land = land_ref[...].astype(F32)
+    core = cells_rank % 2
+    size = mine + nfac
+    for source, side in ((got_ref, core), (others_ref, 1 - core)):
+        stage[pl.ds(pl.multiple_of(side * (size // 2), 8), size // 2), :] = source[size:, :]
+    for source, group in (
+        (pack_ref, comp_rank),
+        (got_ref, comp_rank ^ (1 + core)),
+        (others_ref, comp_rank ^ (2 - core)),
+        (stage, comp_rank ^ 3),
+    ):
+        flat[pl.ds(pl.multiple_of(group * mine, mine), mine), :] = source[0:mine, :]
+        flat[pl.ds(pl.multiple_of(ncomp + group * nfac, nfac), nfac), :] = source[mine:size, :]
+    here = pl.ds(pl.multiple_of(comp_rank * share, 8), share)
+    land = land_ref[here, :].astype(F32)
     load_params(flat, left, mix, load, ncomp, nfac)
-    load_cells(counts_ref, field_ref, logexp_ref, right, wide)
+    load_cells(counts_ref, field_ref, logexp_ref[here, :], right, wide)
     lands = [land[r : r + 1, :] for r in range(share)]
     tau = field_weights(tau_ref, nfac, cols)
     load_prior([None] + [field_ref[r] for r in range(share)] + [None], lands[:1] + lands + lands[-1:], tau, prior)
@@ -492,7 +508,7 @@
     if flat.shape[0] > nparam:
         flat[nparam:, :] = jnp.zeros((flat.shape[0] - nparam, LANES), F32)
     flat[0:nparam, :] = 0.5 * STEP_PARAM * STEP_PARAM * grad_ref[...]
-    own_prof, own_load = part_refs[0][0:mine, :], part_refs[0][mine : mine + nfac, :]
+    own_prof, own_load = pack_ref[0:mine, :], pack_ref[mine:size, :]
     owner = cells_rank == 0
     base_prof = own_prof + STEP_PARAM * (pmom_ref[...] - 0.5 * STEP_PARAM * 0.25 * own_prof)
     base_load = own_load + STEP_PARAM * (wmom_ref[...] - 0.5 * STEP_PARAM * own_load)
@@ -503,7 +519,7 @@
 
 def second_kernel(
     ncomp, chunk, ring, tiles, rank_ref, tau_ref, counts_ref, field_ref, half_ref, land_ref, logexp_ref, pmom_ref, wmom_ref,
-    old_top_ref, old_bottom_ref, own_ref, near_ref, far_ref, edge_ref, grad0_ref, new_ref, mom_ref, prof_ref, mixing_ref,
+    old_ref, own_ref, near_ref, far_ref, edge_ref, grad0_ref, new_ref, mom_ref, params_ref,
     keep_ref, send_ref,
     flat, left, mix, load, right, wide, prior, score0, score1, logit0, logit1, post0, post1, gap0, gap1, acc, accw, out,
     grad,
@@ -515,9 +531,10 @@
     gather_chunks(flat, near_ref, far_ref, cells_rank, chunk)
     new_prof = flat[pl.ds(pl.multiple_of(comp_rank * mine, mine), mine), :]
     new_load = flat[pl.ds(pl.multiple_of(ncomp + comp_rank * nfac, nfac), nfac), :]
-    prof_ref[...] = new_prof
-    mixing_ref[...] = new_load
-    land = land_ref[...].astype(F32)
+    params_ref[0:mine, :] = new_prof
+    params_ref[mine:, :] = new_load
+    here = pl.ds(pl.multiple_of(comp_rank * share, 8), share)
+    land = land_ref[here, :].astype(F32)
     lands = [land[r : r + 1, :] for r in range(share)]
     tau = field_weights(tau_ref, nfac, cols)
 
@@ -532,8 +549,8 @@
     land_above = jnp.where((comp_rank == 0) & (cells_rank == 0), 0.0, above[2])
     land_below = jnp.where((comp_rank == ring - 1) & (cells_rank == tiles - 1), 0.0, below[2])
     end = share - 1
-    pull_up = -tau * (land_above * lands[0]) * (old_top_ref[0] - above[0])
-    pull_down = -tau * (land_below * lands[end]) * (old_bottom_ref[0] - below[0])
+    pull_up = -tau * (land_above * lands[0]) * (old_ref[0] - above[0])
+    pull_down = -tau * (land_below * lands[end]) * (old_ref[end] - below[0])
     move = 0.5 * STEP_FIELD * STEP_FIELD
     for r in range(share):
         fresh = field_ref[r]
@@ -543,7 +560,7 @@
             fresh = fresh + move * pull_down
         new_ref[r] = fresh
     load_params(flat, left, mix, load, ncomp, nfac)
-    load_cells(counts_ref, new_ref, logexp_ref, right, wide)
+    load_cells(counts_ref, new_ref, logexp_ref[here, :], right, wide)
     rows = [above[1] - move * pull_up] + [new_ref[r] for r in range(share)] + [below[1] - move * pull_down]
     energy = load_prior(rows, [land_above] + lands + [land_below], tau, prior)
     prior[0] += pull_up
@@ -605,25 +622,13 @@
     comp_rank = lax.axis_index("comp")
     cells_rank = lax.axis_index("cells")
     ranks = jnp.stack([cells_rank, comp_rank]).astype(jnp.int32)
-    pack = jnp.concatenate([profile, mixing], axis=0)
-    parts = [pack] + [partner(pack, "comp", k) for k in range(1, ring)]
-
+    pack = jnp.pad(profile, ((0, nfac), (0, 0))) + jnp.pad(mixing, ((mine, 0), (0, 0)))
+    got, others = gather_params(pack, cells_rank)
     count_rows = lax.dynamic_slice_in_dim(counts, comp_rank * share, share, 1).swapaxes(0, 1).astype(BF16)
     field_rows = factor_field.swapaxes(0, 1)
     mom_rows = factor_mom.swapaxes(0, 1)
-    def full(*shape):
-        zeros = (0,) * len(shape)
-        return pl.BlockSpec(shape, lambda i, ranks: zeros)
-
+    vmem = pl.BlockSpec(memory_space=pltpu.VMEM)
     smem = pl.BlockSpec(memory_space=pltpu.SMEM)
-    cell_specs = [
-        smem,
-        full(share, ncat, cols),
-        full(share, nfac, cols),
-    ]
-    row_spec = pl.BlockSpec((share, cols), lambda i, ranks: (ranks[1], 0))
-    param_specs = [full(mine, ncat), full(nfac, mine)]
-    pack_spec = full(mine + nfac, ncat)
     shape = lambda *dims: jax.ShapeDtypeStruct(dims, F32)
     work = [
         pltpu.VMEM((ncomp, 4 * LANES), BF16),
@@ -636,92 +641,72 @@
     work += [pltpu.VMEM((ncomp, cols), F32)] * 4 + [pltpu.VMEM((ncomp, 2 * cols), BF16)] * 4
     work += [
         pltpu.VMEM((ncomp, 2 * LANES), F32),
-        pltpu.VMEM((ncomp, LANES), F32),
+        pltpu.VMEM((3 * nfac, ncomp), F32),
     ]
-    params = pltpu.CompilerParams(vmem_limit_bytes=40 * 1024 * 1024, dimension_semantics=("arbitrary",))
-
-    def call(body, name, ins, outs, scratch):
+    def call(body, name, smem_count, vmem_count, outs, scratch):
         return pl.pallas_call(
             body,
             name=name,
-            grid_spec=pltpu.PrefetchScalarGridSpec(
-                num_scalar_prefetch=1,
-                grid=(1,),
-                in_specs=ins,
-                out_specs=[spec for spec, _ in outs],
-                scratch_shapes=scratch,
-            ),
-            out_shape=[out for _, out in outs],
-            compiler_params=params,
-        )
-
-    def block(*dims):
-        return (full(*dims), shape(*dims))
+            in_specs=[smem] * smem_count + [vmem] * vmem_count,
+            out_specs=[smem if out.shape == (1, 1) else vmem for out in outs],
+            scratch_shapes=scratch,
+            out_shape=outs,
+            compiler_params=pltpu.CompilerParams(vmem_limit_bytes=40 * 1024 * 1024),
+        )
 
     first = call(
         functools.partial(first_kernel, ncomp),
         "first_gradient",
-        cell_specs + [full(share, nfac, cols), row_spec, row_spec] + param_specs + [pack_spec] * ring,
+        2,
+        7 + 3,
         [
-            block(share, nfac, cols),
-            block(share, nfac, cols),
-            block(edge, LANES),
-            block(edge, LANES),
-            block(nparam, LANES),
-            block(pairs, chunk_one, LANES),
-            block(pairs, chunk_one, LANES),
+            shape(share, nfac, cols),
+            shape(share, nfac, cols),
+            shape(edge, LANES),
+            shape(edge, LANES),
+            shape(nparam, LANES),
+            shape(pairs, chunk_one, LANES),
+            shape(pairs, chunk_one, LANES),
         ],
-        [pltpu.VMEM((tiles * chunk_one, LANES), F32)] + work,
-    )
-    new_field, half, near_edge, far_edge, grad, keep, send = first(
-        ranks, field_tau, count_rows, field_rows, mom_rows, land_mask, log_exposure, profile_mom, mixing_mom, *parts,
-    )
-    near, far, got_edge = all_sum(keep, send, near_edge, far_edge)
+        [pltpu.VMEM((tiles * chunk_one, LANES), F32)] + work + [pltpu.VMEM((mine + nfac, LANES), F32)],
+    )
+    part_field, half, near_edge, far_edge, grad, keep, send = first(
+        ranks, field_tau, count_rows, field_rows, mom_rows, land_mask, log_exposure, profile_mom, mixing_mom, pack, got, others
+    )
+    near, far, got_edge, _ = all_sum(keep, send, near_edge, far_edge)
     second = call(
         functools.partial(second_kernel, ncomp, chunk_one, ring, tiles),
         "second_gradient",
-        cell_specs
-        + [full(share, nfac, cols), row_spec, row_spec]
-        + param_specs
-        + [
-            pl.BlockSpec((1, nfac, cols), lambda i, ranks: (0, 0, 0)),
-            pl.BlockSpec((1, nfac, cols), lambda i, ranks: (share - 1, 0, 0)),
-            pack_spec,
-            full(pairs, chunk_one + edge, LANES),
-            full(pairs, chunk_one + edge, LANES),
-            full(edge, LANES),
-            full(nparam, LANES),
-        ],
+        2,
+        7 + 6,
         [
-            block(share, nfac, cols),
-            block(share, nfac, cols),
-            block(mine, ncat),
-            block(nfac, mine),
-            block(pairs, chunk_two, LANES),
-            block(pairs, chunk_two, LANES),
+            shape(share, nfac, cols),
+            shape(share, nfac, cols),
+            shape(mine + nfac, ncat),
+            shape(pairs, chunk_two, LANES),
+            shape(pairs, chunk_two, LANES),
         ],
         [pltpu.VMEM((tiles * chunk_one, LANES), F32)]
         + work
         + [pltpu.VMEM((tiles * chunk_two, LANES), F32), pltpu.VMEM((nparam, LANES), F32)],
     )
-    new_field, new_mom, new_profile, new_mixing, keep, send = second(
-        ranks, field_tau, count_rows, new_field, half, land_mask, log_exposure, profile_mom, mixing_mom, field_rows,
-        field_rows, pack, near, far, got_edge, grad,
-    )
-    near, far, _ = all_sum(keep, send)
+    new_field, new_mom, new_params, keep, send = second(
+        ranks, field_tau, count_rows, part_field, half, land_mask, log_exposure, profile_mom, mixing_mom, field_rows, pack,
+        near, far, got_edge, grad,
+    )
+    done = (new_field.swapaxes(0, 1), new_params[:mine], new_params[mine:], new_mom.swapaxes(0, 1))
+    near, far, _, done = all_sum(keep, send, beside=done)
     final = call(
         functools.partial(last_kernel, ncomp, nparam, chunk_two, tile_rows * cols * tiles),
         "momenta",
-        [full(pairs, chunk_two, LANES), full(pairs, chunk_two, LANES)],
-        [block(mine, ncat), block(nfac, mine), (smem, shape(1, 1))],
+        1,
+        2,
+        [shape(mine, ncat), shape(nfac, mine), shape(1, 1)],
         [pltpu.VMEM((tiles * chunk_two, LANES), F32)],
     )
     new_profile_mom, new_mixing_mom, hamiltonian = final(ranks, near, far)
     return (
-        new_field.swapaxes(0, 1),
-        new_profile,
-        new_mixing,
-        new_mom.swapaxes(0, 1),
+        *done,
         new_profile_mom,
         new_mixing_mom,
         hamiltonian.reshape(()),
@@ -737,7 +722,7 @@
     nfac, share, cols = factor_field.shape
     mine, ncat = profile.shape
     tiles, ring = lax.axis_size("cells"), lax.axis_size("comp")
-    fits = mine == LANES and ncat == LANES and nfac % 16 == 0 and 6 * nfac + 6 <= LANES
+    fits = mine == LANES and ncat == LANES and nfac % 16 == 0 and 6 * nfac + EXTRA <= LANES
     fits = fits and share % 8 == 0 and cols % LANES == 0 and cols <= 8 * LANES
     fits = fits and power_of_two(tiles) and tiles > 1 and ring == 4
     return fast_device(*args) if fits else plain_device(*args)

time: 77.6 us -> 74.5 us (0.960)
  Pallas kernels: 14.9 us -> 12.4 us
  waiting for transfers between devices: 27.4 us -> 25.6 us
  other arithmetic: 0.54 us -> 2.22 us
    ppermute x25 -> x24, waiting for transfers between devices: 27.4 us -> 23.6 us  [partner(): return lax.ppermute(values, axis, [(i, i ^ flip) for i in range(count)])]
    ppermute x0 -> x1, waiting for transfers between devices: none -> 2.06 us  [gather_params(): one = lax.ppermute(pack, ('cells', 'comp'), spread)]
    add x0 -> x2, other arithmetic: none -> 1.69 us  [fast_device(): jnp.pad(profile, ((0, nfac), (0, 0))) + jnp.pad(mixing, ((mine, 0), (0, 0)))]
    pallas_call x1, Pallas kernels: 7.13 us -> 5.55 us  [fast_device(): second(ranks, field_tau, count_rows, part_field, half, land_mask, log_exp...]
    slice x0 -> x2, local copies, waits for them, and re-layouts: none -> 1.23 us  [the longest x1 0.63 us: fast_device(): new_params[:mine]]
    pallas_call x1, Pallas kernels: 6.53 us -> 5.59 us  [fast_device(): first(ranks, field_tau, count_rows, field_rows, mom_rows, land_mask, log_...]
    unnamed x13, local copies, waits for them, and re-layouts: 2.37 us -> 1.5 us
    ppermute x25 -> x24, starting transfers between devices: 28.2 us -> 28 us  [partner(): return lax.ppermute(values, axis, [(i, i ^ flip) for i in range(count)])]
  transfers between devices with their start and end apart: 25 -> 25, of which waited for: 19 -> 19; matrix products, arithmetic and copies ran while one was open for 5% -> 8% of each run, Pallas kernels for 0% -> 0%
where the time goes in v3:
time: 74.5 us; the launch traced here: 74.2 us
  starting transfers between devices  28 us (38%)
  waiting for transfers between devices  25.6 us (34%)
  Pallas kernels  12.4 us (17%)
  local copies, waits for them, and re-layouts  5.11 us (7%)
  other arithmetic  2.22 us (3%)
  between operations  0.86 us (1%)
    ppermute x24, starting transfers between devices, partner(): return lax.ppermute(values, axis, [(i, i ^ flip) for i in range(count)])  28 us
    ppermute x24, waiting for transfers between devices, partner(): return lax.ppermute(values, axis, [(i, i ^ flip) for i in range(count)])  23.6 us
    pallas_call x1, Pallas kernels, fast_device(): first(ranks, field_tau, count_rows, field_rows, mom_rows, land_mask, log_...  5.59 us
    pallas_call x1, Pallas kernels, fast_device(): second(ranks, field_tau, count_rows, part_field, half, land_mask, log_exp...  5.55 us
    ppermute x1, waiting for transfers between devices, gather_params(): one = lax.ppermute(pack, ('cells', 'comp'), spread)  2.06 us
    add x2, other arithmetic, fast_device(): jnp.pad(profile, ((0, nfac), (0, 0))) + jnp.pad(mixing, ((mine, 0), (0, 0)))  1.69 us
    unnamed x13, local copies, waits for them, and re-layouts  1.5 us
  transfers between devices with their start and end apart: 25, of which 19 were waited for; matrix products, arithmetic and copies ran while one was open for 8% of the time, Pallas kernels for 0%

profile of v3, /device:TPU:0, one launch (start us, length us, event | category | flops | bytes accessed | tf_op | source)
XLA Modules:
  0.0 74.2 jit_solution(1038901531329824743)
XLA Ops:
  1.5 5.1 %collective-permute-start.1 = (f32[72,128]{1,0:T(8,128)S(1)}, f32[72,128]{1,0:T(8,128)S(1)}, u32[]{:S(2)}, u32[]{:S(2)}) collective-permute-start(f32[72,128]{1,0:T(8,128)S(1)} %fusion.4), channel_id=1, source_target_pairs={{0,3},{1,2},{2,1},{3,0},{4,7},{5,6},{6,5},{7,4},{8,11},{9,10},{10,... | collective-permute-start | bytes 110600 | tf_op jit(solution)/shard_map/ppermute | solution.py:212
  7.5 1.3 %constant_dynamic-slice_fusion = s32[128,8,256]{2,1,0:T(8,128)S(1)} fusion(s32[128,32,256]{2,1,0:T(8,128)} %param.17, s32[]{:T(128)S(6)} %select_n.13), kind=kLoop, calls=%fused_computation.33 | loop fusion | bytes 2097156 | tf_op jit(solution)/shard_map/dynamic_slice | solution.py:627
  9.1 1.1 %copy_bitcast_fusion = (f32[8,16,256]{2,1,0:T(8,128)S(1)}, f32[8,16,256]{2,1,0:T(8,128)S(1)}) fusion(f32[16,8,256]{2,1,0:T(8,128)} %param.13, f32[16,8,256]{2,1,0:T(8,128)} %param.10), kind=kLoop, calls=%fused_computation.4 | loop fusion | bytes 524288 | tf_op jit(solution)/shard_map/transpose | solution.py:629
  10.2 2.1 %collective-permute-done = f32[144,128]{1,0:T(8,128)S(1)} collective-permute-done((f32[144,128]{1,0:T(8,128)S(1)}, f32[144,128]{1,0:T(8,128)S(1)}, u32[]{:S(2)}, u32[]{:S(2)}) %collective-permute-start) | collective-permute-done | bytes 73760 | tf_op jit(solution)/shard_map/ppermute | solution.py:241
  12.4 1.2 %collective-permute-done.2.refs_2_ = f32[216,128]{1,0:T(8,128)S(1)} collective-permute-done((f32[216,128]{1,0:T(8,128)S(1)}, f32[216,128]{1,0:T(8,128)S(1)}, u32[]{:S(2)}, u32[]{:S(2)}) %collective-permute-start.2) | collective-permute-done | bytes 110624 | tf_op jit(solution)/shard_map/ppermute | solution.py:212
  13.7 5.6 %first_gradient.1 = (f32[8,16,256]{2,1,0:T(8,128)S(1)}, f32[8,16,256]{2,1,0:T(8,128)S(1)}, f32[72,128]{1,0:T(8,128)S(1)}, f32[72,128]{1,0:T(8,128)S(1)}, f32[576...) custom-call(s32[2]{0:T(128)S(1)} %pad_add_fusion.1.rank_ref, f32[16]{0:T(128)S(1)} %copy-done.4, ...), custom_call_target="tpu_custom_call" | custom-call | tf_op jit(solution)/shard_map/first_gradient/pallas_call | solution.py:673
  19.5 1.2 %collective-permute-done.3 = f32[4,72,128]{2,1,0:T(8,128)S(1)} collective-permute-done((f32[4,72,128]{2,1,0:T(8,128)S(1)}, f32[4,72,128]{2,1,0:T(8,128)S(1)}, u32[]{:S(2)}, u32[]{:S(2)}) %collective-permute-start.3) | collective-permute-done | bytes 147488 | tf_op jit(solution)/shard_map/ppermute | solution.py:212
  20.7 1.6 %collective-permute-start.4 = (f32[72,128]{1,0:T(8,128)S(1)}, f32[72,128]{1,0:T(8,128)S(1)}, u32[]{:S(2)}, u32[]{:S(2)}) collective-permute-start(f32[72,128]{1,0:T(8,128)S(1)} %get-tuple-element.57), channel_id=1, source_target_pairs={{0,8},{4,12},{8,0},{12,4},{16,24},{20,28},{24,16},{28,20},{1,9},{5... | collective-permute-start | bytes 110600 | tf_op jit(solution)/shard_map/ppermute | solution.py:212
  22.3 1.5 %collective-permute-start.6 = (f32[72,128]{1,0:T(8,128)S(1)}, f32[72,128]{1,0:T(8,128)S(1)}, u32[]{:S(2)}, u32[]{:S(2)}) collective-permute-start(f32[72,128]{1,0:T(8,128)S(1)} %get-tuple-element.58), channel_id=1, source_target_pairs={{0,24},{4,28},{8,16},{12,20},{16,8},{20,12},{24,0},{28,4},{1,25},{... | collective-permute-start | bytes 110600 | tf_op jit(solution)/shard_map/ppermute | solution.py:212
  24.8 2.4 %collective-permute-done.6 = f32[72,128]{1,0:T(8,128)S(1)} collective-permute-done((f32[72,128]{1,0:T(8,128)S(1)}, f32[72,128]{1,0:T(8,128)S(1)}, u32[]{:S(2)}, u32[]{:S(2)}) %collective-permute-start.6) | collective-permute-done | bytes 36896 | tf_op jit(solution)/shard_map/ppermute | solution.py:212
  27.9 1.2 %collective-permute-start.9 = (f32[144,128]{1,0:T(8,128)S(1)}, f32[144,128]{1,0:T(8,128)S(1)}, u32[]{:S(2)}, u32[]{:S(2)}) collective-permute-start(f32[144,128]{1,0:T(8,128)S(1)} %get-tuple-element.66), channel_id=1, source_target_pairs={{0,3},{1,2},{2,1},{3,0},{4,7},{5,6},{6,5},{7,4},{8,11},{9,10},{10,... | collective-permute-start | bytes 221192 | tf_op jit(solution)/shard_map/ppermute | solution.py:212
  29.1 2.2 %collective-permute-start.8 = (f32[72,128]{1,0:T(8,128)S(1)}, f32[72,128]{1,0:T(8,128)S(1)}, u32[]{:S(2)}, u32[]{:S(2)}) collective-permute-start(f32[72,128]{1,0:T(8,128)S(1)} %fusion.8), channel_id=1, source_target_pairs={{0,2},{1,3},{2,0},{3,1},{4,6},{5,7},{6,4},{7,5},{8,10},{9,11},{10,... | collective-permute-start | bytes 110600 | tf_op jit(solution)/shard_map/ppermute | solution.py:212
  31.3 3.9 %collective-permute-done.8 = f32[72,128]{1,0:T(8,128)S(1)} collective-permute-done((f32[72,128]{1,0:T(8,128)S(1)}, f32[72,128]{1,0:T(8,128)S(1)}, u32[]{:S(2)}, u32[]{:S(2)}) %collective-permute-start.8) | collective-permute-done | bytes 36896 | tf_op jit(solution)/shard_map/ppermute | solution.py:212
  35.3 1.0 %collective-permute-start.11 = (f32[144,128]{1,0:T(8,128)S(1)}, f32[144,128]{1,0:T(8,128)S(1)}, u32[]{:S(2)}, u32[]{:S(2)}) collective-permute-start(f32[144,128]{1,0:T(8,128)S(1)} %get-tuple-element.64), channel_id=1, source_target_pairs={{0,16},{4,20},{8,24},{12,28},{16,0},{20,4},{24,8},{28,12},{1,17},{... | collective-permute-start | bytes 221192 | tf_op jit(solution)/shard_map/ppermute | solution.py:212
  36.3 1.1 %collective-permute-start.10 = (f32[144,128]{1,0:T(8,128)S(1)}, f32[144,128]{1,0:T(8,128)S(1)}, u32[]{:S(2)}, u32[]{:S(2)}) collective-permute-start(f32[144,128]{1,0:T(8,128)S(1)} %get-tuple-element.64), channel_id=1, source_target_pairs={{0,8},{4,12},{8,0},{12,4},{16,24},{20,28},{24,16},{28,20},{1,9},{5... | collective-permute-start | bytes 221192 | tf_op jit(solution)/shard_map/ppermute | solution.py:212
  37.4 1.5 %collective-permute-start.12 = (f32[144,128]{1,0:T(8,128)S(1)}, f32[144,128]{1,0:T(8,128)S(1)}, u32[]{:S(2)}, u32[]{:S(2)}) collective-permute-start(f32[144,128]{1,0:T(8,128)S(1)} %get-tuple-element.64), channel_id=1, source_target_pairs={{0,24},{4,28},{8,16},{12,20},{16,8},{20,12},{24,0},{28,4},{1,25},{... | collective-permute-start | bytes 221192 | tf_op jit(solution)/shard_map/ppermute | solution.py:212
  40.6 2.0 %collective-permute-done.12 = f32[144,128]{1,0:T(8,128)S(1)} collective-permute-done((f32[144,128]{1,0:T(8,128)S(1)}, f32[144,128]{1,0:T(8,128)S(1)}, u32[]{:S(2)}, u32[]{:S(2)}) %collective-permute-start.12) | collective-permute-done | bytes 73760 | tf_op jit(solution)/shard_map/ppermute | solution.py:212
  42.7 1.6 %collective-permute-done.13.far_ref = f32[4,144,128]{2,1,0:T(8,128)S(1)} collective-permute-done((f32[4,144,128]{2,1,0:T(8,128)S(1)}, f32[4,144,128]{2,1,0:T(8,128)S(1)}, u32[]{:S(2)}, u32[]{:S(2)}) %collective-permute-start.13) | collective-permute-done | bytes 294944 | tf_op jit(solution)/shard_map/ppermute | solution.py:212
  44.3 5.5 %second_gradient.1 = (f32[8,16,256]{2,1,0:T(8,128)S(1)}, f32[8,16,256]{2,1,0:T(8,128)S(1)}, f32[144,128]{1,0:T(8,128)S(1)}, f32[4,80,128]{2,1,0:T(8,128)S(1)}, f32[4,80,128]{2,1,0:T(8,128)S(1)}) custom-call(s32[2]{0:T(128)S(1)} %pad_add_fusion.1.rank_ref, f32[16]{0:T(128)S(1)} %copy-done.4, bf16[8,128,256]{2,1,0:T(8,128)(2,1)S(1)} %fusion.counts_ref, ...), custom_call_target="tpu_custom_call" | custom-call | tf_op jit(solution)/shard_map/second_gradient/pallas_call | solution.py:693
  50.0 1.3 %collective-permute-done.14 = f32[4,80,128]{2,1,0:T(8,128)S(1)} collective-permute-done((f32[4,80,128]{2,1,0:T(8,128)S(1)}, f32[4,80,128]{2,1,0:T(8,128)S(1)}, u32[]{:S(2)}, u32[]{:S(2)}) %collective-permute-start.14) | collective-permute-done | bytes 163872 | tf_op jit(solution)/shard_map/ppermute | solution.py:212
  51.3 1.0 %collective-permute-start.15 = (f32[80,128]{1,0:T(8,128)S(1)}, f32[80,128]{1,0:T(8,128)S(1)}, u32[]{:S(2)}, u32[]{:S(2)}) collective-permute-start(f32[80,128]{1,0:T(8,128)S(1)} %get-tuple-element.54), channel_id=1, source_target_pairs={{0,8},{4,12},{8,0},{12,4},{16,24},{20,28},{24,16},{28,20},{1,9},{5... | collective-permute-start | bytes 122888 | tf_op jit(solution)/shard_map/ppermute | solution.py:212
  52.4 2.0 %collective-permute-start.17 = (f32[80,128]{1,0:T(8,128)S(1)}, f32[80,128]{1,0:T(8,128)S(1)}, u32[]{:S(2)}, u32[]{:S(2)}) collective-permute-start(f32[80,128]{1,0:T(8,128)S(1)} %get-tuple-element.55), channel_id=1, source_target_pairs={{0,24},{4,28},{8,16},{12,20},{16,8},{20,12},{24,0},{28,4},{1,25},{... | collective-permute-start | bytes 122888 | tf_op jit(solution)/shard_map/ppermute | solution.py:212
  56.1 1.2 %collective-permute-done.17 = f32[80,128]{1,0:T(8,128)S(1)} collective-permute-done((f32[80,128]{1,0:T(8,128)S(1)}, f32[80,128]{1,0:T(8,128)S(1)}, u32[]{:S(2)}, u32[]{:S(2)}) %collective-permute-start.17) | collective-permute-done | bytes 40992 | tf_op jit(solution)/shard_map/ppermute | solution.py:212
  57.4 1.0 %collective-permute-done.16 = f32[80,128]{1,0:T(8,128)S(1)} collective-permute-done((f32[80,128]{1,0:T(8,128)S(1)}, f32[80,128]{1,0:T(8,128)S(1)}, u32[]{:S(2)}, u32[]{:S(2)}) %collective-permute-start.16) | collective-permute-done | bytes 40992 | tf_op jit(solution)/shard_map/ppermute | solution.py:212
  58.4 1.4 %collective-permute-start.20 = (f32[80,128]{1,0:T(8,128)S(1)}, f32[80,128]{1,0:T(8,128)S(1)}, u32[]{:S(2)}, u32[]{:S(2)}) collective-permute-start(f32[80,128]{1,0:T(8,128)S(1)} %fusion.3), channel_id=1, source_target_pairs={{0,3},{1,2},{2,1},{3,0},{4,7},{5,6},{6,5},{7,4},{8,11},{9,10},{10,... | collective-permute-start | bytes 122888 | tf_op jit(solution)/shard_map/ppermute | solution.py:212
  60.1 2.8 %collective-permute-start.18 = (f32[80,128]{1,0:T(8,128)S(1)}, f32[80,128]{1,0:T(8,128)S(1)}, u32[]{:S(2)}, u32[]{:S(2)}) collective-permute-start(f32[80,128]{1,0:T(8,128)S(1)} %fusion.3), channel_id=1, source_target_pairs={{0,1},{1,0},{2,3},{3,2},{4,5},{5,4},{6,7},{7,6},{8,9},{9,8},{10,11... | collective-permute-start | bytes 122888 | tf_op jit(solution)/shard_map/ppermute | solution.py:212
  62.9 1.4 %collective-permute-done.20 = f32[80,128]{1,0:T(8,128)S(1)} collective-permute-done((f32[80,128]{1,0:T(8,128)S(1)}, f32[80,128]{1,0:T(8,128)S(1)}, u32[]{:S(2)}, u32[]{:S(2)}) %collective-permute-start.20) | collective-permute-done | bytes 40992 | tf_op jit(solution)/shard_map/ppermute | solution.py:212
  64.3 1.0 %collective-permute-done.19 = f32[80,128]{1,0:T(8,128)S(1)} collective-permute-done((f32[80,128]{1,0:T(8,128)S(1)}, f32[80,128]{1,0:T(8,128)S(1)}, u32[]{:S(2)}, u32[]{:S(2)}) %collective-permute-start.19) | collective-permute-done | bytes 40992 | tf_op jit(solution)/shard_map/ppermute | solution.py:212
  65.3 1.4 %collective-permute-start.23 = (f32[80,128]{1,0:T(8,128)S(1)}, f32[80,128]{1,0:T(8,128)S(1)}, u32[]{:S(2)}, u32[]{:S(2)}) collective-permute-start(f32[80,128]{1,0:T(8,128)S(1)} %add_add_fusion), channel_id=1, source_target_pairs={{0,24},{4,28},{8,16},{12,20},{16,8},{20,12},{24,0},{28,4},{1,25},{... | collective-permute-start | bytes 122888 | tf_op jit(solution)/shard_map/ppermute | solution.py:212
  67.3 1.5 %collective-permute-start.21 = (f32[80,128]{1,0:T(8,128)S(1)}, f32[80,128]{1,0:T(8,128)S(1)}, u32[]{:S(2)}, u32[]{:S(2)}) collective-permute-start(f32[80,128]{1,0:T(8,128)S(1)} %add_add_fusion), channel_id=1, source_target_pairs={{0,8},{4,12},{8,0},{12,4},{16,24},{20,28},{24,16},{28,20},{1,9},{5... | collective-permute-start | bytes 122888 | tf_op jit(solution)/shard_map/ppermute | solution.py:212
  68.8 1.4 %collective-permute-done.23 = f32[80,128]{1,0:T(8,128)S(1)} collective-permute-done((f32[80,128]{1,0:T(8,128)S(1)}, f32[80,128]{1,0:T(8,128)S(1)}, u32[]{:S(2)}, u32[]{:S(2)}) %collective-permute-start.23) | collective-permute-done | bytes 40992 | tf_op jit(solution)/shard_map/ppermute | solution.py:212
  72.9 1.3 %momenta.1 = (f32[128,128]{1,0:T(8,128)}, f32[16,128]{1,0:T(8,128)}, f32[1,1]{1,0:T(1,128)}) custom-call(s32[2]{0:T(128)S(1)} %pad_add_fusion.1.rank_ref, f32[4,80,128]{2,1,0:T(8,128)S(1)} %pad_maximum_fusion.1.near_ref, f32[4,80,128]{2,1,0:T(8,128)S(1)} %collective-permute-done.24.far_ref), custom_call_target="tpu_custom_call" | custom-call | tf_op jit(solution)/shard_map/momenta/pallas_call | solution.py:707
  (55 shorter events, 11.6 us)
Async XLA Ops:
  0.6 13.0 %copy-start.2 = (f32[32,256]{1,0:T(8,128)S(1)}, f32[32,256]{1,0:T(8,128)}, u32[]{:S(2)}) copy-start(f32[32,256]{1,0:T(8,128)} %logexp_ref.3) | copy-start | bytes 98308
  0.6 13.0 %copy-start.1 = (s32[32,256]{1,0:T(8,128)S(1)}, s32[32,256]{1,0:T(8,128)}, u32[]{:S(2)}) copy-start(s32[32,256]{1,0:T(8,128)} %land_ref.3) | copy-start | bytes 98308
  0.7 13.0 %copy-start.4 = (f32[16]{0:T(128)S(1)}, f32[16]{0:T(128)}, u32[]{:S(2)}) copy-start(f32[16]{0:T(128)} %tau_ref.3) | copy-start | bytes 196
  0.7 13.0 %copy-start.3 = (f32[16,128]{1,0:T(8,128)S(1)}, f32[16,128]{1,0:T(8,128)}, u32[]{:S(2)}) copy-start(f32[16,128]{1,0:T(8,128)} %wmom_ref.3) | copy-start | bytes 24580
  0.7 13.0 %copy-start = (f32[128,128]{1,0:T(8,128)S(1)}, f32[128,128]{1,0:T(8,128)}, u32[]{:S(2)}) copy-start(f32[128,128]{1,0:T(8,128)} %pmom_ref.3) | copy-start | bytes 196612
  1.5 10.7 %collective-permute-start.1 = (f32[72,128]{1,0:T(8,128)S(1)}, f32[72,128]{1,0:T(8,128)S(1)}, u32[]{:S(2)}, u32[]{:S(2)}) collective-permute-start(f32[72,128]{1,0:T(8,128)S(1)} %fusion.4), channel_id=1, source_target_pairs={{0,3},{1,2},{2,1},{3,0},{4,7},{5,6},{6,5},{7,4},{8,11},{9,10},{10,... | collective-permute-start | bytes 110600 | tf_op jit(solution)/shard_map/ppermute | solution.py:212
  7.5 4.7 %collective-permute-start = (f32[144,128]{1,0:T(8,128)S(1)}, f32[144,128]{1,0:T(8,128)S(1)}, u32[]{:S(2)}, u32[]{:S(2)}) collective-permute-start(f32[144,128]{1,0:T(8,128)S(1)} %pad_add_fusion.refs_0_.own_ref), channel_id=1, source_target_pairs={{0,1},{1,0},{2,3},{3,2},{4,6},{5,7},{6,4},{7,5},{8,9},{9,8},{10,11... | collective-permute-start | bytes 221192 | tf_op jit(solution)/shard_map/ppermute | solution.py:241
  12.3 1.4 %collective-permute-start.2 = (f32[216,128]{1,0:T(8,128)S(1)}, f32[216,128]{1,0:T(8,128)S(1)}, u32[]{:S(2)}, u32[]{:S(2)}) collective-permute-start(f32[216,128]{1,0:T(8,128)S(1)} %constant_dynamic-update-slice_fusion.refs_1_), channel_id=1, source_target_pairs={{0,4},{4,0},{8,12},{12,8},{16,20},{20,16},{24,28},{28,24},{1,5},{5... | collective-permute-start | bytes 331784 | tf_op jit(solution)/shard_map/ppermute | solution.py:212
  19.3 1.4 %collective-permute-start.3 = (f32[4,72,128]{2,1,0:T(8,128)S(1)}, f32[4,72,128]{2,1,0:T(8,128)S(1)}, u32[]{:S(2)}, u32[]{:S(2)}) collective-permute-start(f32[4,72,128]{2,1,0:T(8,128)S(1)} %get-tuple-element.30), channel_id=1, source_target_pairs={{0,4},{4,0},{8,12},{12,8},{16,20},{20,16},{24,28},{28,24},{1,5},{5... | collective-permute-start | bytes 442376 | tf_op jit(solution)/shard_map/ppermute | solution.py:212
  20.7 4.0 %collective-permute-start.4 = (f32[72,128]{1,0:T(8,128)S(1)}, f32[72,128]{1,0:T(8,128)S(1)}, u32[]{:S(2)}, u32[]{:S(2)}) collective-permute-start(f32[72,128]{1,0:T(8,128)S(1)} %get-tuple-element.57), channel_id=1, source_target_pairs={{0,8},{4,12},{8,0},{12,4},{16,24},{20,28},{24,16},{28,20},{1,9},{5... | collective-permute-start | bytes 110600 | tf_op jit(solution)/shard_map/ppermute | solution.py:212
  22.3 4.9 %collective-permute-start.6 = (f32[72,128]{1,0:T(8,128)S(1)}, f32[72,128]{1,0:T(8,128)S(1)}, u32[]{:S(2)}, u32[]{:S(2)}) collective-permute-start(f32[72,128]{1,0:T(8,128)S(1)} %get-tuple-element.58), channel_id=1, source_target_pairs={{0,24},{4,28},{8,16},{12,20},{16,8},{20,12},{24,0},{28,4},{1,25},{... | collective-permute-start | bytes 110600 | tf_op jit(solution)/shard_map/ppermute | solution.py:212
  23.8 4.0 %collective-permute-start.5 = (f32[72,128]{1,0:T(8,128)S(1)}, f32[72,128]{1,0:T(8,128)S(1)}, u32[]{:S(2)}, u32[]{:S(2)}) collective-permute-start(f32[72,128]{1,0:T(8,128)S(1)} %get-tuple-element.59), channel_id=1, source_target_pairs={{0,16},{4,20},{8,24},{12,28},{16,0},{20,4},{24,8},{28,12},{1,17},{... | collective-permute-start | bytes 110600 | tf_op jit(solution)/shard_map/ppermute | solution.py:212
  27.8 7.5 %collective-permute-start.7 = (f32[144,128]{1,0:T(8,128)S(1)}, f32[144,128]{1,0:T(8,128)S(1)}, u32[]{:S(2)}, u32[]{:S(2)}) collective-permute-start(f32[144,128]{1,0:T(8,128)S(1)} %get-tuple-element.65), channel_id=1, source_target_pairs={{0,1},{1,0},{2,3},{3,2},{4,5},{5,4},{6,7},{7,6},{8,9},{9,8},{10,11... | collective-permute-start | bytes 221192 | tf_op jit(solution)/shard_map/ppermute | solution.py:212
  27.9 7.4 %collective-permute-start.9 = (f32[144,128]{1,0:T(8,128)S(1)}, f32[144,128]{1,0:T(8,128)S(1)}, u32[]{:S(2)}, u32[]{:S(2)}) collective-permute-start(f32[144,128]{1,0:T(8,128)S(1)} %get-tuple-element.66), channel_id=1, source_target_pairs={{0,3},{1,2},{2,1},{3,0},{4,7},{5,6},{6,5},{7,4},{8,11},{9,10},{10,... | collective-permute-start | bytes 221192 | tf_op jit(solution)/shard_map/ppermute | solution.py:212
  29.1 6.2 %collective-permute-start.8 = (f32[72,128]{1,0:T(8,128)S(1)}, f32[72,128]{1,0:T(8,128)S(1)}, u32[]{:S(2)}, u32[]{:S(2)}) collective-permute-start(f32[72,128]{1,0:T(8,128)S(1)} %fusion.8), channel_id=1, source_target_pairs={{0,2},{1,3},{2,0},{3,1},{4,6},{5,7},{6,4},{7,5},{8,10},{9,11},{10,... | collective-permute-start | bytes 110600 | tf_op jit(solution)/shard_map/ppermute | solution.py:212
  35.3 4.4 %collective-permute-start.11 = (f32[144,128]{1,0:T(8,128)S(1)}, f32[144,128]{1,0:T(8,128)S(1)}, u32[]{:S(2)}, u32[]{:S(2)}) collective-permute-start(f32[144,128]{1,0:T(8,128)S(1)} %get-tuple-element.64), channel_id=1, source_target_pairs={{0,16},{4,20},{8,24},{12,28},{16,0},{20,4},{24,8},{28,12},{1,17},{... | collective-permute-start | bytes 221192 | tf_op jit(solution)/shard_map/ppermute | solution.py:212
  36.3 4.4 %collective-permute-start.10 = (f32[144,128]{1,0:T(8,128)S(1)}, f32[144,128]{1,0:T(8,128)S(1)}, u32[]{:S(2)}, u32[]{:S(2)}) collective-permute-start(f32[144,128]{1,0:T(8,128)S(1)} %get-tuple-element.64), channel_id=1, source_target_pairs={{0,8},{4,12},{8,0},{12,4},{16,24},{20,28},{24,16},{28,20},{1,9},{5... | collective-permute-start | bytes 221192 | tf_op jit(solution)/shard_map/ppermute | solution.py:212
  37.4 5.3 %collective-permute-start.12 = (f32[144,128]{1,0:T(8,128)S(1)}, f32[144,128]{1,0:T(8,128)S(1)}, u32[]{:S(2)}, u32[]{:S(2)}) collective-permute-start(f32[144,128]{1,0:T(8,128)S(1)} %get-tuple-element.64), channel_id=1, source_target_pairs={{0,24},{4,28},{8,16},{12,20},{16,8},{20,12},{24,0},{28,4},{1,25},{... | collective-permute-start | bytes 221192 | tf_op jit(solution)/shard_map/ppermute | solution.py:212
  42.6 1.6 %collective-permute-start.13 = (f32[4,144,128]{2,1,0:T(8,128)S(1)}, f32[4,144,128]{2,1,0:T(8,128)S(1)}, u32[]{:S(2)}, u32[]{:S(2)}) collective-permute-start(f32[4,144,128]{2,1,0:T(8,128)S(1)} %pad_maximum_fusion.near_ref), channel_id=1, source_target_pairs={{0,4},{4,0},{8,12},{12,8},{16,20},{20,16},{24,28},{28,24},{1,5},{5... | collective-permute-start | bytes 884744 | tf_op jit(solution)/shard_map/ppermute | solution.py:212
  49.8 1.5 %collective-permute-start.14 = (f32[4,80,128]{2,1,0:T(8,128)S(1)}, f32[4,80,128]{2,1,0:T(8,128)S(1)}, u32[]{:S(2)}, u32[]{:S(2)}) collective-permute-start(f32[4,80,128]{2,1,0:T(8,128)S(1)} %get-tuple-element.35), channel_id=1, source_target_pairs={{0,4},{4,0},{8,12},{12,8},{16,20},{20,16},{24,28},{28,24},{1,5},{5... | collective-permute-start | bytes 491528 | tf_op jit(solution)/shard_map/ppermute | solution.py:212
  51.3 4.8 %collective-permute-start.15 = (f32[80,128]{1,0:T(8,128)S(1)}, f32[80,128]{1,0:T(8,128)S(1)}, u32[]{:S(2)}, u32[]{:S(2)}) collective-permute-start(f32[80,128]{1,0:T(8,128)S(1)} %get-tuple-element.54), channel_id=1, source_target_pairs={{0,8},{4,12},{8,0},{12,4},{16,24},{20,28},{24,16},{28,20},{1,9},{5... | collective-permute-start | bytes 122888 | tf_op jit(solution)/shard_map/ppermute | solution.py:212
  52.4 5.0 %collective-permute-start.17 = (f32[80,128]{1,0:T(8,128)S(1)}, f32[80,128]{1,0:T(8,128)S(1)}, u32[]{:S(2)}, u32[]{:S(2)}) collective-permute-start(f32[80,128]{1,0:T(8,128)S(1)} %get-tuple-element.55), channel_id=1, source_target_pairs={{0,24},{4,28},{8,16},{12,20},{16,8},{20,12},{24,0},{28,4},{1,25},{... | collective-permute-start | bytes 122888 | tf_op jit(solution)/shard_map/ppermute | solution.py:212
  54.4 4.0 %collective-permute-start.16 = (f32[80,128]{1,0:T(8,128)S(1)}, f32[80,128]{1,0:T(8,128)S(1)}, u32[]{:S(2)}, u32[]{:S(2)}) collective-permute-start(f32[80,128]{1,0:T(8,128)S(1)} %get-tuple-element.56), channel_id=1, source_target_pairs={{0,16},{4,20},{8,24},{12,28},{16,0},{20,4},{24,8},{28,12},{1,17},{... | collective-permute-start | bytes 122888 | tf_op jit(solution)/shard_map/ppermute | solution.py:212
  58.4 5.9 %collective-permute-start.20 = (f32[80,128]{1,0:T(8,128)S(1)}, f32[80,128]{1,0:T(8,128)S(1)}, u32[]{:S(2)}, u32[]{:S(2)}) collective-permute-start(f32[80,128]{1,0:T(8,128)S(1)} %fusion.3), channel_id=1, source_target_pairs={{0,3},{1,2},{2,1},{3,0},{4,7},{5,6},{6,5},{7,4},{8,11},{9,10},{10,... | collective-permute-start | bytes 122888 | tf_op jit(solution)/shard_map/ppermute | solution.py:212
  59.8 5.4 %collective-permute-start.19 = (f32[80,128]{1,0:T(8,128)S(1)}, f32[80,128]{1,0:T(8,128)S(1)}, u32[]{:S(2)}, u32[]{:S(2)}) collective-permute-start(f32[80,128]{1,0:T(8,128)S(1)} %fusion.3), channel_id=1, source_target_pairs={{0,2},{1,3},{2,0},{3,1},{4,6},{5,7},{6,4},{7,5},{8,10},{9,11},{10,... | collective-permute-start | bytes 122888 | tf_op jit(solution)/shard_map/ppermute | solution.py:212
  60.1 5.2 %collective-permute-start.18 = (f32[80,128]{1,0:T(8,128)S(1)}, f32[80,128]{1,0:T(8,128)S(1)}, u32[]{:S(2)}, u32[]{:S(2)}) collective-permute-start(f32[80,128]{1,0:T(8,128)S(1)} %fusion.3), channel_id=1, source_target_pairs={{0,1},{1,0},{2,3},{3,2},{4,5},{5,4},{6,7},{7,6},{8,9},{9,8},{10,11... | collective-permute-start | bytes 122888 | tf_op jit(solution)/shard_map/ppermute | solution.py:212
  65.3 5.0 %collective-permute-start.23 = (f32[80,128]{1,0:T(8,128)S(1)}, f32[80,128]{1,0:T(8,128)S(1)}, u32[]{:S(2)}, u32[]{:S(2)}) collective-permute-start(f32[80,128]{1,0:T(8,128)S(1)} %add_add_fusion), channel_id=1, source_target_pairs={{0,24},{4,28},{8,16},{12,20},{16,8},{20,12},{24,0},{28,4},{1,25},{... | collective-permute-start | bytes 122888 | tf_op jit(solution)/shard_map/ppermute | solution.py:212
  66.7 4.0 %collective-permute-start.22 = (f32[80,128]{1,0:T(8,128)S(1)}, f32[80,128]{1,0:T(8,128)S(1)}, u32[]{:S(2)}, u32[]{:S(2)}) collective-permute-start(f32[80,128]{1,0:T(8,128)S(1)} %add_add_fusion), channel_id=1, source_target_pairs={{0,16},{4,20},{8,24},{12,28},{16,0},{20,4},{24,8},{28,12},{1,17},{... | collective-permute-start | bytes 122888 | tf_op jit(solution)/shard_map/ppermute | solution.py:212
  67.3 4.0 %collective-permute-start.21 = (f32[80,128]{1,0:T(8,128)S(1)}, f32[80,128]{1,0:T(8,128)S(1)}, u32[]{:S(2)}, u32[]{:S(2)}) collective-permute-start(f32[80,128]{1,0:T(8,128)S(1)} %add_add_fusion), channel_id=1, source_target_pairs={{0,8},{4,12},{8,0},{12,4},{16,24},{20,28},{24,16},{28,20},{1,9},{5... | collective-permute-start | bytes 122888 | tf_op jit(solution)/shard_map/ppermute | solution.py:212
  71.4 1.6 %collective-permute-start.24 = (f32[4,80,128]{2,1,0:T(8,128)S(1)}, f32[4,80,128]{2,1,0:T(8,128)S(1)}, u32[]{:S(2)}, u32[]{:S(2)}) collective-permute-start(f32[4,80,128]{2,1,0:T(8,128)S(1)} %pad_maximum_fusion.1.near_ref), channel_id=1, source_target_pairs={{0,4},{4,0},{8,12},{12,8},{16,20},{20,16},{24,28},{28,24},{1,5},{5... | collective-permute-start | bytes 491528 | tf_op jit(solution)/shard_map/ppermute | solution.py:212

commit v4 on v3

--- a/solution.py
+++ b/solution.py
@@ -601,7 +601,10 @@
     mixing_ref[...] = flat[pl.ds(pl.multiple_of(ncomp + comp_rank * nfac, nfac), nfac), :]
     momenta = flat[0:nparam, :]
     rest = flat[nparam:, :]
-    ham_ref[0, 0] = (0.5 * jnp.sum(momenta * momenta) + jnp.sum(rest)) / cells
+    total = jnp.sum(0.5 * (momenta * momenta).reshape(nparam // 8, 8, LANES), axis=0)
+    total = total + jnp.sum(rest.reshape(rest.shape[0] // 8, 8, LANES), axis=0)
+    total = jnp.sum(jnp.sum(total, axis=0, keepdims=True), axis=1, keepdims=True)
+    ham_ref[...] = total / cells
 
 
 def fast_device(
@@ -622,7 +625,7 @@
     comp_rank = lax.axis_index("comp")
     cells_rank = lax.axis_index("cells")
     ranks = jnp.stack([cells_rank, comp_rank]).astype(jnp.int32)
-    pack = jnp.pad(profile, ((0, nfac), (0, 0))) + jnp.pad(mixing, ((mine, 0), (0, 0)))
+    pack = lax.optimization_barrier(jnp.pad(profile, ((0, nfac), (0, 0))) + jnp.pad(mixing, ((mine, 0), (0, 0))))
     got, others = gather_params(pack, cells_rank)
     count_rows = lax.dynamic_slice_in_dim(counts, comp_rank * share, share, 1).swapaxes(0, 1).astype(BF16)
     field_rows = factor_field.swapaxes(0, 1)
@@ -648,7 +651,7 @@
             body,
             name=name,
             in_specs=[smem] * smem_count + [vmem] * vmem_count,
-            out_specs=[smem if out.shape == (1, 1) else vmem for out in outs],
+            out_specs=[vmem] * len(outs),
             scratch_shapes=scratch,
             out_shape=outs,
             compiler_params=pltpu.CompilerParams(vmem_limit_bytes=40 * 1024 * 1024),

time: 74.5 us -> 73.7 us (0.989)
  other arithmetic: 2.22 us -> 1.42 us
    ppermute x1, starting transfers between devices: 0.01 us -> 3.02 us  [gather_params(): one = lax.ppermute(pack, ('cells', 'comp'), spread)]
    ppermute x24, starting transfers between devices: 28 us -> 25.3 us  [partner(): return lax.ppermute(values, axis, [(i, i ^ flip) for i in range(count)])]
    ppermute x1, waiting for transfers between devices: 2.06 us -> 0.01 us  [gather_params(): one = lax.ppermute(pack, ('cells', 'comp'), spread)]
    ppermute x24, waiting for transfers between devices: 23.6 us -> 25.2 us  [partner(): return lax.ppermute(values, axis, [(i, i ^ flip) for i in range(count)])]
    add x2 -> x1, other arithmetic: 1.69 us -> 0.9 us  [fast_device(): jnp.pad(profile, ((0, nfac), (0, 0))) + jnp.pad(mixing, ((mine, 0), (0, 0)))]
  transfers between devices with their start and end apart: 25 -> 25, of which waited for: 19 -> 19; matrix products, arithmetic and copies ran while one was open for 8% -> 7% of each run, Pallas kernels for 0% -> 0%
where the time goes in v4:
time: 73.7 us; the launch traced here: 73.4 us
  starting transfers between devices  28.3 us (38%)
  waiting for transfers between devices  25.2 us (34%)
  Pallas kernels  12.6 us (17%)
  local copies, waits for them, and re-layouts  5.1 us (7%)
  other arithmetic  1.42 us (2%)
  between operations  0.83 us (1%)
    ppermute x24, starting transfers between devices, partner(): return lax.ppermute(values, axis, [(i, i ^ flip) for i in range(count)])  25.3 us
    ppermute x24, waiting for transfers between devices, partner(): return lax.ppermute(values, axis, [(i, i ^ flip) for i in range(count)])  25.2 us
    pallas_call x1, Pallas kernels, fast_device(): first(ranks, field_tau, count_rows, field_rows, mom_rows, land_mask, log_...  5.67 us
    pallas_call x1, Pallas kernels, fast_device(): second(ranks, field_tau, count_rows, part_field, half, land_mask, log_exp...  5.66 us
    ppermute x1, starting transfers between devices, gather_params(): one = lax.ppermute(pack, ('cells', 'comp'), spread)  3.02 us
    unnamed x13, local copies, waits for them, and re-layouts  1.5 us
  transfers between devices with their start and end apart: 25, of which 19 were waited for; matrix products, arithmetic and copies ran while one was open for 7% of the time, Pallas kernels for 0%

profile of v4, /device:TPU:0, one launch (start us, length us, event | category | flops | bytes accessed | tf_op | source)
XLA Modules:
  0.0 73.4 jit_solution(12626532433618372828)
XLA Ops:
  1.6 3.0 %collective-permute-start = (f32[144,128]{1,0:T(8,128)S(1)}, f32[144,128]{1,0:T(8,128)S(1)}, u32[]{:S(2)}, u32[]{:S(2)}) collective-permute-start(f32[144,128]{1,0:T(8,128)S(1)} %pad_add_fusion.refs_0_.own_ref), channel_id=1, source_target_pairs={{0,1},{1,0},{2,3},{3,2},{4,6},{5,7},{6,4},{7,5},{8,9},{9,8},{10,11... | collective-permute-start | bytes 221192 | tf_op jit(solution)/shard_map/ppermute | solution.py:241
  4.6 2.5 %collective-permute-start.1 = (f32[72,128]{1,0:T(8,128)S(1)}, f32[72,128]{1,0:T(8,128)S(1)}, u32[]{:S(2)}, u32[]{:S(2)}) collective-permute-start(f32[72,128]{1,0:T(8,128)S(1)} %constant_dynamic-slice_fusion), channel_id=1, source_target_pairs={{0,3},{1,2},{2,1},{3,0},{4,7},{5,6},{6,5},{7,4},{8,11},{9,10},{10,... | collective-permute-start | bytes 110600 | tf_op jit(solution)/shard_map/ppermute | solution.py:212
  7.1 1.3 %constant_dynamic-slice_fusion.1 = s32[128,8,256]{2,1,0:T(8,128)S(1)} fusion(s32[128,32,256]{2,1,0:T(8,128)} %param.17, s32[]{:T(128)S(6)} %select_n.13), kind=kLoop, calls=%fused_computation.32 | loop fusion | bytes 2097156 | tf_op jit(solution)/shard_map/dynamic_slice | solution.py:630
  8.7 1.1 %copy_bitcast_fusion = (f32[8,16,256]{2,1,0:T(8,128)S(1)}, f32[8,16,256]{2,1,0:T(8,128)S(1)}) fusion(f32[16,8,256]{2,1,0:T(8,128)} %param.13, f32[16,8,256]{2,1,0:T(8,128)} %param.10), kind=kLoop, calls=%fused_computation.4 | loop fusion | bytes 524288 | tf_op jit(solution)/shard_map/transpose | solution.py:632
  10.5 1.2 %collective-permute-done.2.refs_2_ = f32[216,128]{1,0:T(8,128)S(1)} collective-permute-done((f32[216,128]{1,0:T(8,128)S(1)}, f32[216,128]{1,0:T(8,128)S(1)}, u32[]{:S(2)}, u32[]{:S(2)}) %collective-permute-start.2) | collective-permute-done | bytes 110624 | tf_op jit(solution)/shard_map/ppermute | solution.py:212
  11.7 5.7 %first_gradient.1 = (f32[8,16,256]{2,1,0:T(8,128)S(1)}, f32[8,16,256]{2,1,0:T(8,128)S(1)}, f32[72,128]{1,0:T(8,128)S(1)}, f32[72,128]{1,0:T(8,128)S(1)}, f32[576...) custom-call(s32[2]{0:T(128)S(1)} %pad_add_fusion.1.rank_ref, f32[16]{0:T(128)S(1)} %copy-done.4, ...), custom_call_target="tpu_custom_call" | custom-call | tf_op jit(solution)/shard_map/first_gradient/pallas_call | solution.py:676
  17.6 1.2 %collective-permute-done.3 = f32[4,72,128]{2,1,0:T(8,128)S(1)} collective-permute-done((f32[4,72,128]{2,1,0:T(8,128)S(1)}, f32[4,72,128]{2,1,0:T(8,128)S(1)}, u32[]{:S(2)}, u32[]{:S(2)}) %collective-permute-start.3) | collective-permute-done | bytes 147488 | tf_op jit(solution)/shard_map/ppermute | solution.py:212
  18.9 1.6 %collective-permute-start.4 = (f32[72,128]{1,0:T(8,128)S(1)}, f32[72,128]{1,0:T(8,128)S(1)}, u32[]{:S(2)}, u32[]{:S(2)}) collective-permute-start(f32[72,128]{1,0:T(8,128)S(1)} %get-tuple-element.57), channel_id=1, source_target_pairs={{0,8},{4,12},{8,0},{12,4},{16,24},{20,28},{24,16},{28,20},{1,9},{5... | collective-permute-start | bytes 110600 | tf_op jit(solution)/shard_map/ppermute | solution.py:212
  20.4 1.5 %collective-permute-start.6 = (f32[72,128]{1,0:T(8,128)S(1)}, f32[72,128]{1,0:T(8,128)S(1)}, u32[]{:S(2)}, u32[]{:S(2)}) collective-permute-start(f32[72,128]{1,0:T(8,128)S(1)} %get-tuple-element.58), channel_id=1, source_target_pairs={{0,24},{4,28},{8,16},{12,20},{16,8},{20,12},{24,0},{28,4},{1,25},{... | collective-permute-start | bytes 110600 | tf_op jit(solution)/shard_map/ppermute | solution.py:212
  22.9 2.4 %collective-permute-done.6 = f32[72,128]{1,0:T(8,128)S(1)} collective-permute-done((f32[72,128]{1,0:T(8,128)S(1)}, f32[72,128]{1,0:T(8,128)S(1)}, u32[]{:S(2)}, u32[]{:S(2)}) %collective-permute-start.6) | collective-permute-done | bytes 36896 | tf_op jit(solution)/shard_map/ppermute | solution.py:212
  26.1 3.0 %collective-permute-start.9 = (f32[144,128]{1,0:T(8,128)S(1)}, f32[144,128]{1,0:T(8,128)S(1)}, u32[]{:S(2)}, u32[]{:S(2)}) collective-permute-start(f32[144,128]{1,0:T(8,128)S(1)} %get-tuple-element.66), channel_id=1, source_target_pairs={{0,3},{1,2},{2,1},{3,0},{4,7},{5,6},{6,5},{7,4},{8,11},{9,10},{10,... | collective-permute-start | bytes 221192 | tf_op jit(solution)/shard_map/ppermute | solution.py:212
  29.5 4.9 %collective-permute-done.8 = f32[72,128]{1,0:T(8,128)S(1)} collective-permute-done((f32[72,128]{1,0:T(8,128)S(1)}, f32[72,128]{1,0:T(8,128)S(1)}, u32[]{:S(2)}, u32[]{:S(2)}) %collective-permute-start.8) | collective-permute-done | bytes 36896 | tf_op jit(solution)/shard_map/ppermute | solution.py:212
  34.4 1.0 %collective-permute-start.11 = (f32[144,128]{1,0:T(8,128)S(1)}, f32[144,128]{1,0:T(8,128)S(1)}, u32[]{:S(2)}, u32[]{:S(2)}) collective-permute-start(f32[144,128]{1,0:T(8,128)S(1)} %get-tuple-element.64), channel_id=1, source_target_pairs={{0,16},{4,20},{8,24},{12,28},{16,0},{20,4},{24,8},{28,12},{1,17},{... | collective-permute-start | bytes 221192 | tf_op jit(solution)/shard_map/ppermute | solution.py:212
  35.4 1.1 %collective-permute-start.10 = (f32[144,128]{1,0:T(8,128)S(1)}, f32[144,128]{1,0:T(8,128)S(1)}, u32[]{:S(2)}, u32[]{:S(2)}) collective-permute-start(f32[144,128]{1,0:T(8,128)S(1)} %get-tuple-element.64), channel_id=1, source_target_pairs={{0,8},{4,12},{8,0},{12,4},{16,24},{20,28},{24,16},{28,20},{1,9},{5... | collective-permute-start | bytes 221192 | tf_op jit(solution)/shard_map/ppermute | solution.py:212
  36.5 1.5 %collective-permute-start.12 = (f32[144,128]{1,0:T(8,128)S(1)}, f32[144,128]{1,0:T(8,128)S(1)}, u32[]{:S(2)}, u32[]{:S(2)}) collective-permute-start(f32[144,128]{1,0:T(8,128)S(1)} %get-tuple-element.64), channel_id=1, source_target_pairs={{0,24},{4,28},{8,16},{12,20},{16,8},{20,12},{24,0},{28,4},{1,25},{... | collective-permute-start | bytes 221192 | tf_op jit(solution)/shard_map/ppermute | solution.py:212
  38.9 0.9 %collective-permute-done.10 = f32[144,128]{1,0:T(8,128)S(1)} collective-permute-done((f32[144,128]{1,0:T(8,128)S(1)}, f32[144,128]{1,0:T(8,128)S(1)}, u32[]{:S(2)}, u32[]{:S(2)}) %collective-permute-start.10) | collective-permute-done | bytes 73760 | tf_op jit(solution)/shard_map/ppermute | solution.py:212
  39.8 2.0 %collective-permute-done.12 = f32[144,128]{1,0:T(8,128)S(1)} collective-permute-done((f32[144,128]{1,0:T(8,128)S(1)}, f32[144,128]{1,0:T(8,128)S(1)}, u32[]{:S(2)}, u32[]{:S(2)}) %collective-permute-start.12) | collective-permute-done | bytes 73760 | tf_op jit(solution)/shard_map/ppermute | solution.py:212
  41.9 1.6 %collective-permute-done.13.far_ref = f32[4,144,128]{2,1,0:T(8,128)S(1)} collective-permute-done((f32[4,144,128]{2,1,0:T(8,128)S(1)}, f32[4,144,128]{2,1,0:T(8,128)S(1)}, u32[]{:S(2)}, u32[]{:S(2)}) %collective-permute-start.13) | collective-permute-done | bytes 294944 | tf_op jit(solution)/shard_map/ppermute | solution.py:212
  43.4 5.7 %second_gradient.1 = (f32[8,16,256]{2,1,0:T(8,128)S(1)}, f32[8,16,256]{2,1,0:T(8,128)S(1)}, f32[144,128]{1,0:T(8,128)S(1)}, f32[4,80,128]{2,1,0:T(8,128)S(1)}, f32[4,80,128]{2,1,0:T(8,128)S(1)}) custom-call(s32[2]{0:T(128)S(1)} %pad_add_fusion.1.rank_ref, f32[16]{0:T(128)S(1)} %copy-done.4, bf16[8,128,256]{2,1,0:T(8,128)(2,1)S(1)} %fusion.counts_ref, ...), custom_call_target="tpu_custom_call" | custom-call | tf_op jit(solution)/shard_map/second_gradient/pallas_call | solution.py:696
  49.3 1.3 %collective-permute-done.14 = f32[4,80,128]{2,1,0:T(8,128)S(1)} collective-permute-done((f32[4,80,128]{2,1,0:T(8,128)S(1)}, f32[4,80,128]{2,1,0:T(8,128)S(1)}, u32[]{:S(2)}, u32[]{:S(2)}) %collective-permute-start.14) | collective-permute-done | bytes 163872 | tf_op jit(solution)/shard_map/ppermute | solution.py:212
  50.6 1.0 %collective-permute-start.15 = (f32[80,128]{1,0:T(8,128)S(1)}, f32[80,128]{1,0:T(8,128)S(1)}, u32[]{:S(2)}, u32[]{:S(2)}) collective-permute-start(f32[80,128]{1,0:T(8,128)S(1)} %get-tuple-element.54), channel_id=1, source_target_pairs={{0,8},{4,12},{8,0},{12,4},{16,24},{20,28},{24,16},{28,20},{1,9},{5... | collective-permute-start | bytes 122888 | tf_op jit(solution)/shard_map/ppermute | solution.py:212
  51.6 2.0 %collective-permute-start.17 = (f32[80,128]{1,0:T(8,128)S(1)}, f32[80,128]{1,0:T(8,128)S(1)}, u32[]{:S(2)}, u32[]{:S(2)}) collective-permute-start(f32[80,128]{1,0:T(8,128)S(1)} %get-tuple-element.55), channel_id=1, source_target_pairs={{0,24},{4,28},{8,16},{12,20},{16,8},{20,12},{24,0},{28,4},{1,25},{... | collective-permute-start | bytes 122888 | tf_op jit(solution)/shard_map/ppermute | solution.py:212
  55.4 1.2 %collective-permute-done.17 = f32[80,128]{1,0:T(8,128)S(1)} collective-permute-done((f32[80,128]{1,0:T(8,128)S(1)}, f32[80,128]{1,0:T(8,128)S(1)}, u32[]{:S(2)}, u32[]{:S(2)}) %collective-permute-start.17) | collective-permute-done | bytes 40992 | tf_op jit(solution)/shard_map/ppermute | solution.py:212
  56.6 1.0 %collective-permute-done.16 = f32[80,128]{1,0:T(8,128)S(1)} collective-permute-done((f32[80,128]{1,0:T(8,128)S(1)}, f32[80,128]{1,0:T(8,128)S(1)}, u32[]{:S(2)}, u32[]{:S(2)}) %collective-permute-start.16) | collective-permute-done | bytes 40992 | tf_op jit(solution)/shard_map/ppermute | solution.py:212
  57.7 1.7 %collective-permute-start.20 = (f32[80,128]{1,0:T(8,128)S(1)}, f32[80,128]{1,0:T(8,128)S(1)}, u32[]{:S(2)}, u32[]{:S(2)}) collective-permute-start(f32[80,128]{1,0:T(8,128)S(1)} %fusion.3), channel_id=1, source_target_pairs={{0,3},{1,2},{2,1},{3,0},{4,7},{5,6},{6,5},{7,4},{8,11},{9,10},{10,... | collective-permute-start | bytes 122888 | tf_op jit(solution)/shard_map/ppermute | solution.py:212
  59.4 2.7 %collective-permute-start.18 = (f32[80,128]{1,0:T(8,128)S(1)}, f32[80,128]{1,0:T(8,128)S(1)}, u32[]{:S(2)}, u32[]{:S(2)}) collective-permute-start(f32[80,128]{1,0:T(8,128)S(1)} %fusion.3), channel_id=1, source_target_pairs={{0,1},{1,0},{2,3},{3,2},{4,5},{5,4},{6,7},{7,6},{8,9},{9,8},{10,11... | collective-permute-start | bytes 122888 | tf_op jit(solution)/shard_map/ppermute | solution.py:212
  62.1 1.5 %collective-permute-done.20 = f32[80,128]{1,0:T(8,128)S(1)} collective-permute-done((f32[80,128]{1,0:T(8,128)S(1)}, f32[80,128]{1,0:T(8,128)S(1)}, u32[]{:S(2)}, u32[]{:S(2)}) %collective-permute-start.20) | collective-permute-done | bytes 40992 | tf_op jit(solution)/shard_map/ppermute | solution.py:212
  63.6 0.9 %collective-permute-done.19 = f32[80,128]{1,0:T(8,128)S(1)} collective-permute-done((f32[80,128]{1,0:T(8,128)S(1)}, f32[80,128]{1,0:T(8,128)S(1)}, u32[]{:S(2)}, u32[]{:S(2)}) %collective-permute-start.19) | collective-permute-done | bytes 40992 | tf_op jit(solution)/shard_map/ppermute | solution.py:212
  64.5 1.4 %collective-permute-start.23 = (f32[80,128]{1,0:T(8,128)S(1)}, f32[80,128]{1,0:T(8,128)S(1)}, u32[]{:S(2)}, u32[]{:S(2)}) collective-permute-start(f32[80,128]{1,0:T(8,128)S(1)} %add_add_fusion), channel_id=1, source_target_pairs={{0,24},{4,28},{8,16},{12,20},{16,8},{20,12},{24,0},{28,4},{1,25},{... | collective-permute-start | bytes 122888 | tf_op jit(solution)/shard_map/ppermute | solution.py:212
  66.6 1.5 %collective-permute-start.21 = (f32[80,128]{1,0:T(8,128)S(1)}, f32[80,128]{1,0:T(8,128)S(1)}, u32[]{:S(2)}, u32[]{:S(2)}) collective-permute-start(f32[80,128]{1,0:T(8,128)S(1)} %add_add_fusion), channel_id=1, source_target_pairs={{0,8},{4,12},{8,0},{12,4},{16,24},{20,28},{24,16},{28,20},{1,9},{5... | collective-permute-start | bytes 122888 | tf_op jit(solution)/shard_map/ppermute | solution.py:212
  68.1 1.4 %collective-permute-done.23 = f32[80,128]{1,0:T(8,128)S(1)} collective-permute-done((f32[80,128]{1,0:T(8,128)S(1)}, f32[80,128]{1,0:T(8,128)S(1)}, u32[]{:S(2)}, u32[]{:S(2)}) %collective-permute-start.23) | collective-permute-done | bytes 40992 | tf_op jit(solution)/shard_map/ppermute | solution.py:212
  72.2 1.3 %momenta.1 = (f32[128,128]{1,0:T(8,128)}, f32[16,128]{1,0:T(8,128)}, f32[1,1]{1,0:T(1,128)}) custom-call(s32[2]{0:T(128)S(1)} %pad_add_fusion.1.rank_ref, f32[4,80,128]{2,1,0:T(8,128)S(1)} %pad_maximum_fusion.1.near_ref, f32[4,80,128]{2,1,0:T(8,128)S(1)} %collective-permute-done.24.far_ref), custom_call_target="tpu_custom_call" | custom-call | tf_op jit(solution)/shard_map/momenta/pallas_call | solution.py:710
  (55 shorter events, 10.6 us)
Async XLA Ops:
  0.6 11.1 %copy-start.2 = (f32[32,256]{1,0:T(8,128)S(1)}, f32[32,256]{1,0:T(8,128)}, u32[]{:S(2)}) copy-start(f32[32,256]{1,0:T(8,128)} %logexp_ref.3) | copy-start | bytes 98308
  0.6 11.1 %copy-start.1 = (s32[32,256]{1,0:T(8,128)S(1)}, s32[32,256]{1,0:T(8,128)}, u32[]{:S(2)}) copy-start(s32[32,256]{1,0:T(8,128)} %land_ref.3) | copy-start | bytes 98308
  0.7 11.0 %copy-start.4 = (f32[16]{0:T(128)S(1)}, f32[16]{0:T(128)}, u32[]{:S(2)}) copy-start(f32[16]{0:T(128)} %tau_ref.3) | copy-start | bytes 196
  0.7 11.0 %copy-start.3 = (f32[16,128]{1,0:T(8,128)S(1)}, f32[16,128]{1,0:T(8,128)}, u32[]{:S(2)}) copy-start(f32[16,128]{1,0:T(8,128)} %wmom_ref.3) | copy-start | bytes 24580
  0.7 11.0 %copy-start = (f32[128,128]{1,0:T(8,128)S(1)}, f32[128,128]{1,0:T(8,128)}, u32[]{:S(2)}) copy-start(f32[128,128]{1,0:T(8,128)} %pmom_ref.3) | copy-start | bytes 196612
  1.6 8.2 %collective-permute-start = (f32[144,128]{1,0:T(8,128)S(1)}, f32[144,128]{1,0:T(8,128)S(1)}, u32[]{:S(2)}, u32[]{:S(2)}) collective-permute-start(f32[144,128]{1,0:T(8,128)S(1)} %pad_add_fusion.refs_0_.own_ref), channel_id=1, source_target_pairs={{0,1},{1,0},{2,3},{3,2},{4,6},{5,7},{6,4},{7,5},{8,9},{9,8},{10,11... | collective-permute-start | bytes 221192 | tf_op jit(solution)/shard_map/ppermute | solution.py:241
  4.6 5.8 %collective-permute-start.1 = (f32[72,128]{1,0:T(8,128)S(1)}, f32[72,128]{1,0:T(8,128)S(1)}, u32[]{:S(2)}, u32[]{:S(2)}) collective-permute-start(f32[72,128]{1,0:T(8,128)S(1)} %constant_dynamic-slice_fusion), channel_id=1, source_target_pairs={{0,3},{1,2},{2,1},{3,0},{4,7},{5,6},{6,5},{7,4},{8,11},{9,10},{10,... | collective-permute-start | bytes 110600 | tf_op jit(solution)/shard_map/ppermute | solution.py:212
  10.4 1.3 %collective-permute-start.2 = (f32[216,128]{1,0:T(8,128)S(1)}, f32[216,128]{1,0:T(8,128)S(1)}, u32[]{:S(2)}, u32[]{:S(2)}) collective-permute-start(f32[216,128]{1,0:T(8,128)S(1)} %constant_dynamic-update-slice_fusion.refs_1_), channel_id=1, source_target_pairs={{0,4},{4,0},{8,12},{12,8},{16,20},{20,16},{24,28},{28,24},{1,5},{5... | collective-permute-start | bytes 331784 | tf_op jit(solution)/shard_map/ppermute | solution.py:212
  17.4 1.4 %collective-permute-start.3 = (f32[4,72,128]{2,1,0:T(8,128)S(1)}, f32[4,72,128]{2,1,0:T(8,128)S(1)}, u32[]{:S(2)}, u32[]{:S(2)}) collective-permute-start(f32[4,72,128]{2,1,0:T(8,128)S(1)} %get-tuple-element.30), channel_id=1, source_target_pairs={{0,4},{4,0},{8,12},{12,8},{16,20},{20,16},{24,28},{28,24},{1,5},{5... | collective-permute-start | bytes 442376 | tf_op jit(solution)/shard_map/ppermute | solution.py:212
  18.9 4.0 %collective-permute-start.4 = (f32[72,128]{1,0:T(8,128)S(1)}, f32[72,128]{1,0:T(8,128)S(1)}, u32[]{:S(2)}, u32[]{:S(2)}) collective-permute-start(f32[72,128]{1,0:T(8,128)S(1)} %get-tuple-element.57), channel_id=1, source_target_pairs={{0,8},{4,12},{8,0},{12,4},{16,24},{20,28},{24,16},{28,20},{1,9},{5... | collective-permute-start | bytes 110600 | tf_op jit(solution)/shard_map/ppermute | solution.py:212
  20.4 4.9 %collective-permute-start.6 = (f32[72,128]{1,0:T(8,128)S(1)}, f32[72,128]{1,0:T(8,128)S(1)}, u32[]{:S(2)}, u32[]{:S(2)}) collective-permute-start(f32[72,128]{1,0:T(8,128)S(1)} %get-tuple-element.58), channel_id=1, source_target_pairs={{0,24},{4,28},{8,16},{12,20},{16,8},{20,12},{24,0},{28,4},{1,25},{... | collective-permute-start | bytes 110600 | tf_op jit(solution)/shard_map/ppermute | solution.py:212
  21.9 4.0 %collective-permute-start.5 = (f32[72,128]{1,0:T(8,128)S(1)}, f32[72,128]{1,0:T(8,128)S(1)}, u32[]{:S(2)}, u32[]{:S(2)}) collective-permute-start(f32[72,128]{1,0:T(8,128)S(1)} %get-tuple-element.59), channel_id=1, source_target_pairs={{0,16},{4,20},{8,24},{12,28},{16,0},{20,4},{24,8},{28,12},{1,17},{... | collective-permute-start | bytes 110600 | tf_op jit(solution)/shard_map/ppermute | solution.py:212
  25.9 8.5 %collective-permute-start.7 = (f32[144,128]{1,0:T(8,128)S(1)}, f32[144,128]{1,0:T(8,128)S(1)}, u32[]{:S(2)}, u32[]{:S(2)}) collective-permute-start(f32[144,128]{1,0:T(8,128)S(1)} %get-tuple-element.65), channel_id=1, source_target_pairs={{0,1},{1,0},{2,3},{3,2},{4,5},{5,4},{6,7},{7,6},{8,9},{9,8},{10,11... | collective-permute-start | bytes 221192 | tf_op jit(solution)/shard_map/ppermute | solution.py:212
  26.1 8.3 %collective-permute-start.9 = (f32[144,128]{1,0:T(8,128)S(1)}, f32[144,128]{1,0:T(8,128)S(1)}, u32[]{:S(2)}, u32[]{:S(2)}) collective-permute-start(f32[144,128]{1,0:T(8,128)S(1)} %get-tuple-element.66), channel_id=1, source_target_pairs={{0,3},{1,2},{2,1},{3,0},{4,7},{5,6},{6,5},{7,4},{8,11},{9,10},{10,... | collective-permute-start | bytes 221192 | tf_op jit(solution)/shard_map/ppermute | solution.py:212
  29.2 5.2 %collective-permute-start.8 = (f32[72,128]{1,0:T(8,128)S(1)}, f32[72,128]{1,0:T(8,128)S(1)}, u32[]{:S(2)}, u32[]{:S(2)}) collective-permute-start(f32[72,128]{1,0:T(8,128)S(1)} %fusion.7), channel_id=1, source_target_pairs={{0,2},{1,3},{2,0},{3,1},{4,6},{5,7},{6,4},{7,5},{8,10},{9,11},{10,... | collective-permute-start | bytes 110600 | tf_op jit(solution)/shard_map/ppermute | solution.py:212
  34.4 4.4 %collective-permute-start.11 = (f32[144,128]{1,0:T(8,128)S(1)}, f32[144,128]{1,0:T(8,128)S(1)}, u32[]{:S(2)}, u32[]{:S(2)}) collective-permute-start(f32[144,128]{1,0:T(8,128)S(1)} %get-tuple-element.64), channel_id=1, source_target_pairs={{0,16},{4,20},{8,24},{12,28},{16,0},{20,4},{24,8},{28,12},{1,17},{... | collective-permute-start | bytes 221192 | tf_op jit(solution)/shard_map/ppermute | solution.py:212
  35.4 4.4 %collective-permute-start.10 = (f32[144,128]{1,0:T(8,128)S(1)}, f32[144,128]{1,0:T(8,128)S(1)}, u32[]{:S(2)}, u32[]{:S(2)}) collective-permute-start(f32[144,128]{1,0:T(8,128)S(1)} %get-tuple-element.64), channel_id=1, source_target_pairs={{0,8},{4,12},{8,0},{12,4},{16,24},{20,28},{24,16},{28,20},{1,9},{5... | collective-permute-start | bytes 221192 | tf_op jit(solution)/shard_map/ppermute | solution.py:212
  36.5 5.3 %collective-permute-start.12 = (f32[144,128]{1,0:T(8,128)S(1)}, f32[144,128]{1,0:T(8,128)S(1)}, u32[]{:S(2)}, u32[]{:S(2)}) collective-permute-start(f32[144,128]{1,0:T(8,128)S(1)} %get-tuple-element.64), channel_id=1, source_target_pairs={{0,24},{4,28},{8,16},{12,20},{16,8},{20,12},{24,0},{28,4},{1,25},{... | collective-permute-start | bytes 221192 | tf_op jit(solution)/shard_map/ppermute | solution.py:212
  41.8 1.6 %collective-permute-start.13 = (f32[4,144,128]{2,1,0:T(8,128)S(1)}, f32[4,144,128]{2,1,0:T(8,128)S(1)}, u32[]{:S(2)}, u32[]{:S(2)}) collective-permute-start(f32[4,144,128]{2,1,0:T(8,128)S(1)} %pad_maximum_fusion.near_ref), channel_id=1, source_target_pairs={{0,4},{4,0},{8,12},{12,8},{16,20},{20,16},{24,28},{28,24},{1,5},{5... | collective-permute-start | bytes 884744 | tf_op jit(solution)/shard_map/ppermute | solution.py:212
  49.1 1.5 %collective-permute-start.14 = (f32[4,80,128]{2,1,0:T(8,128)S(1)}, f32[4,80,128]{2,1,0:T(8,128)S(1)}, u32[]{:S(2)}, u32[]{:S(2)}) collective-permute-start(f32[4,80,128]{2,1,0:T(8,128)S(1)} %get-tuple-element.35), channel_id=1, source_target_pairs={{0,4},{4,0},{8,12},{12,8},{16,20},{20,16},{24,28},{28,24},{1,5},{5... | collective-permute-start | bytes 491528 | tf_op jit(solution)/shard_map/ppermute | solution.py:212
  50.6 4.8 %collective-permute-start.15 = (f32[80,128]{1,0:T(8,128)S(1)}, f32[80,128]{1,0:T(8,128)S(1)}, u32[]{:S(2)}, u32[]{:S(2)}) collective-permute-start(f32[80,128]{1,0:T(8,128)S(1)} %get-tuple-element.54), channel_id=1, source_target_pairs={{0,8},{4,12},{8,0},{12,4},{16,24},{20,28},{24,16},{28,20},{1,9},{5... | collective-permute-start | bytes 122888 | tf_op jit(solution)/shard_map/ppermute | solution.py:212
  51.6 5.0 %collective-permute-start.17 = (f32[80,128]{1,0:T(8,128)S(1)}, f32[80,128]{1,0:T(8,128)S(1)}, u32[]{:S(2)}, u32[]{:S(2)}) collective-permute-start(f32[80,128]{1,0:T(8,128)S(1)} %get-tuple-element.55), channel_id=1, source_target_pairs={{0,24},{4,28},{8,16},{12,20},{16,8},{20,12},{24,0},{28,4},{1,25},{... | collective-permute-start | bytes 122888 | tf_op jit(solution)/shard_map/ppermute | solution.py:212
  53.6 4.0 %collective-permute-start.16 = (f32[80,128]{1,0:T(8,128)S(1)}, f32[80,128]{1,0:T(8,128)S(1)}, u32[]{:S(2)}, u32[]{:S(2)}) collective-permute-start(f32[80,128]{1,0:T(8,128)S(1)} %get-tuple-element.56), channel_id=1, source_target_pairs={{0,16},{4,20},{8,24},{12,28},{16,0},{20,4},{24,8},{28,12},{1,17},{... | collective-permute-start | bytes 122888 | tf_op jit(solution)/shard_map/ppermute | solution.py:212
  57.7 5.9 %collective-permute-start.20 = (f32[80,128]{1,0:T(8,128)S(1)}, f32[80,128]{1,0:T(8,128)S(1)}, u32[]{:S(2)}, u32[]{:S(2)}) collective-permute-start(f32[80,128]{1,0:T(8,128)S(1)} %fusion.3), channel_id=1, source_target_pairs={{0,3},{1,2},{2,1},{3,0},{4,7},{5,6},{6,5},{7,4},{8,11},{9,10},{10,... | collective-permute-start | bytes 122888 | tf_op jit(solution)/shard_map/ppermute | solution.py:212
  59.3 5.2 %collective-permute-start.19 = (f32[80,128]{1,0:T(8,128)S(1)}, f32[80,128]{1,0:T(8,128)S(1)}, u32[]{:S(2)}, u32[]{:S(2)}) collective-permute-start(f32[80,128]{1,0:T(8,128)S(1)} %fusion.3), channel_id=1, source_target_pairs={{0,2},{1,3},{2,0},{3,1},{4,6},{5,7},{6,4},{7,5},{8,10},{9,11},{10,... | collective-permute-start | bytes 122888 | tf_op jit(solution)/shard_map/ppermute | solution.py:212
  59.4 5.1 %collective-permute-start.18 = (f32[80,128]{1,0:T(8,128)S(1)}, f32[80,128]{1,0:T(8,128)S(1)}, u32[]{:S(2)}, u32[]{:S(2)}) collective-permute-start(f32[80,128]{1,0:T(8,128)S(1)} %fusion.3), channel_id=1, source_target_pairs={{0,1},{1,0},{2,3},{3,2},{4,5},{5,4},{6,7},{7,6},{8,9},{9,8},{10,11... | collective-permute-start | bytes 122888 | tf_op jit(solution)/shard_map/ppermute | solution.py:212
  64.5 5.0 %collective-permute-start.23 = (f32[80,128]{1,0:T(8,128)S(1)}, f32[80,128]{1,0:T(8,128)S(1)}, u32[]{:S(2)}, u32[]{:S(2)}) collective-permute-start(f32[80,128]{1,0:T(8,128)S(1)} %add_add_fusion), channel_id=1, source_target_pairs={{0,24},{4,28},{8,16},{12,20},{16,8},{20,12},{24,0},{28,4},{1,25},{... | collective-permute-start | bytes 122888 | tf_op jit(solution)/shard_map/ppermute | solution.py:212
  65.9 4.0 %collective-permute-start.22 = (f32[80,128]{1,0:T(8,128)S(1)}, f32[80,128]{1,0:T(8,128)S(1)}, u32[]{:S(2)}, u32[]{:S(2)}) collective-permute-start(f32[80,128]{1,0:T(8,128)S(1)} %add_add_fusion), channel_id=1, source_target_pairs={{0,16},{4,20},{8,24},{12,28},{16,0},{20,4},{24,8},{28,12},{1,17},{... | collective-permute-start | bytes 122888 | tf_op jit(solution)/shard_map/ppermute | solution.py:212
  66.6 4.0 %collective-permute-start.21 = (f32[80,128]{1,0:T(8,128)S(1)}, f32[80,128]{1,0:T(8,128)S(1)}, u32[]{:S(2)}, u32[]{:S(2)}) collective-permute-start(f32[80,128]{1,0:T(8,128)S(1)} %add_add_fusion), channel_id=1, source_target_pairs={{0,8},{4,12},{8,0},{12,4},{16,24},{20,28},{24,16},{28,20},{1,9},{5... | collective-permute-start | bytes 122888 | tf_op jit(solution)/shard_map/ppermute | solution.py:212
  70.6 1.6 %collective-permute-start.24 = (f32[4,80,128]{2,1,0:T(8,128)S(1)}, f32[4,80,128]{2,1,0:T(8,128)S(1)}, u32[]{:S(2)}, u32[]{:S(2)}) collective-permute-start(f32[4,80,128]{2,1,0:T(8,128)S(1)} %pad_maximum_fusion.1.near_ref), channel_id=1, source_target_pairs={{0,4},{4,0},{8,12},{12,8},{16,20},{20,16},{24,28},{28,24},{1,5},{5... | collective-permute-start | bytes 491528 | tf_op jit(solution)/shard_map/ppermute | solution.py:212

commit v5 on v4

--- a/solution.py
+++ b/solution.py
@@ -212,13 +212,15 @@
     return lax.ppermute(values, axis, [(i, i ^ flip) for i in range(count)])
 
 
-def all_sum(keep, send, near_edge=None, far_edge=None, beside=()):
+def all_sum(keep, send, near_edge=None, far_edge=None, late=None, beside=()):
     pairs, rows, _ = keep.shape
     chunks = keep + partner(send, "cells", 1)
     total = chunks[0]
     for part in [partner(chunks[k], "cells", 2 * k) for k in range(1, pairs)]:
         total = total + part
     total, beside = lax.optimization_barrier((total, beside))
+    if late is not None:
+        total = jnp.concatenate([total, late], axis=0)
     if near_edge is None:
         parts = [partner(total, "comp", k) for k in range(1, lax.axis_size("comp"))]
         near_got = None
@@ -380,7 +382,7 @@
     return tops
 
 
-def row_shares(tops, land, score_ref, logit_ref, post_ref, gap_ref):
+def row_shares(tops, land, score_ref, logit_ref, post_ref, gap_ref, kept_ref):
     ncomp, cols = score_ref.shape
     block = 32
     top_s, top_a = tops
@@ -402,16 +404,16 @@
     for i in range(0, ncomp, block):
         post = score_ref[i : i + block, :] * inv_s
         gap = post - logit_ref[i : i + block, :] * inv_a
-        for target, values in ((post_ref, post), (gap_ref, gap)):
+        for targets, values in (((post_ref,), post), ((gap_ref, kept_ref), gap)):
             high, low = pieces(values, 2)
-            target[i : i + block, 0:cols] = high
-            target[i : i + block, cols : 2 * cols] = low
+            for target in targets:
+                target[i : i + block, 0:cols] = high
+                target[i : i + block, cols : 2 * cols] = low
     return land * (LN2 * (log_s - log_a))
 
 
-def row_products(r, wide_ref, load_ref, post_ref, gap_ref, acc_ref, accw_ref, prior_ref):
-    nfac = load_ref.shape[0] // 2
-    cols = prior_ref.shape[2]
+def row_products(r, wide_ref, post_ref, gap_ref, acc_ref, accw_ref):
+    nfac = accw_ref.shape[0] // 3
     last = ((1,), (1,))
     start = LANES + EXTRA
     acc = dot(post_ref[...], wide_ref[r], last)
@@ -422,13 +424,18 @@
     else:
         acc_ref[...] += acc
         accw_ref[...] += accw
-    lik = dot(load_ref[...], gap_ref[...])
-    lik = lik[0:nfac] + lik[nfac : 2 * nfac]
-    prior_ref[r] += lik[:, 0:cols] + lik[:, cols : 2 * cols]
-
-
-def all_rows(land, right, wide, left, mix, load, scores, logits, posts, gaps, acc, accw, prior):
-    share, _, cols = prior.shape
+
+
+def field_grads(load_ref, gap_refs, prior_ref):
+    share, nfac, cols = prior_ref.shape
+    for r in range(share):
+        lik = dot(load_ref[...], gap_refs[r][...])
+        lik = lik[0:nfac] + lik[nfac : 2 * nfac]
+        prior_ref[r] += lik[:, 0:cols] + lik[:, cols : 2 * cols]
+
+
+def all_rows(land, right, wide, left, mix, scores, logits, posts, gaps, kept, acc, accw):
+    share, _, cols = right.shape
     log_dens = jnp.zeros((1, cols), F32)
     tops = {}
     for r in range(share + 2):
@@ -437,11 +444,11 @@
         if 0 <= r - 1 < share:
             p = r - 1
             log_dens = log_dens + row_shares(
-                tops[p], land[p : p + 1, :], scores[p % 2], logits[p % 2], posts[p % 2], gaps[p % 2]
+                tops[p], land[p : p + 1, :], scores[p % 2], logits[p % 2], posts[p % 2], gaps[p % 2], kept[p]
             )
         if 0 <= r - 2:
             p = r - 2
-            row_products(p, wide, load, posts[p % 2], gaps[p % 2], acc, accw, prior)
+            row_products(p, wide, posts[p % 2], gaps[p % 2], acc, accw)
     return log_dens
 
 
@@ -457,13 +464,11 @@
 
 
 def first_kernel(
-    ncomp, rank_ref, tau_ref, counts_ref, field_ref, mom_ref, land_ref, logexp_ref, pmom_ref, wmom_ref, *refs
+    ncomp, rank_ref, counts_ref, field_ref, land_ref, logexp_ref, pmom_ref, wmom_ref, pack_ref, got_ref, others_ref, *refs
 ):
-    (pack_ref, got_ref, others_ref, new_ref, half_ref, near_ref, far_ref, grad_ref, keep_ref, send_ref) = refs[:10]
-    (flat, left, mix, load, right, wide, prior, score0, score1, logit0, logit1, post0, post1, gap0, gap1, acc, accw) = (
-        refs[10:27]
-    )
-    (stage,) = refs[27:]
+    gaps, refs = refs[: counts_ref.shape[0]], refs[counts_ref.shape[0] :]
+    load, grad_ref, keep_ref, send_ref, flat, left, mix, right, wide, score0, score1, logit0, logit1, *refs = refs
+    post0, post1, gap0, gap1, acc, accw, stage = refs
     cells_rank, comp_rank = rank_ref[0], rank_ref[1]
     share, nfac, cols = field_ref.shape
     mine = pmom_ref.shape[0]
@@ -483,13 +488,31 @@
     land = land_ref[here, :].astype(F32)
     load_params(flat, left, mix, load, ncomp, nfac)
     load_cells(counts_ref, field_ref, logexp_ref[here, :], right, wide)
+    all_rows(land, right, wide, left, mix, (score0, score1), (logit0, logit1), (post0, post1), (gap0, gap1), gaps, acc, accw)
+    param_grads(flat, acc, accw, grad_ref, ncomp, nfac)
+    nparam = grad_ref.shape[0]
+    if flat.shape[0] > nparam:
+        flat[nparam:, :] = jnp.zeros((flat.shape[0] - nparam, LANES), F32)
+    flat[0:nparam, :] = 0.5 * STEP_PARAM * STEP_PARAM * grad_ref[...]
+    own_prof, own_load = pack_ref[0:mine, :], pack_ref[mine:size, :]
+    owner = cells_rank == 0
+    base_prof = own_prof + STEP_PARAM * (pmom_ref[...] - 0.5 * STEP_PARAM * 0.25 * own_prof)
+    base_load = own_load + STEP_PARAM * (wmom_ref[...] - 0.5 * STEP_PARAM * own_load)
+    flat[pl.ds(pl.multiple_of(comp_rank * mine, mine), mine), :] += jnp.where(owner, base_prof, 0.0)
+    flat[pl.ds(pl.multiple_of(ncomp + comp_rank * nfac, nfac), nfac), :] += jnp.where(owner, base_load, 0.0)
+    spread_chunks(flat, keep_ref, send_ref, cells_rank)
+
+
+def first_field(rank_ref, tau_ref, field_ref, mom_ref, land_ref, load_ref, *refs):
+    gap_refs, refs = refs[: field_ref.shape[0]], refs[field_ref.shape[0] :]
+    new_ref, half_ref, near_ref, far_ref, prior = refs
+    comp_rank = rank_ref[1]
+    share, nfac, cols = field_ref.shape
+    land = land_ref[pl.ds(pl.multiple_of(comp_rank * share, 8), share), :].astype(F32)
     lands = [land[r : r + 1, :] for r in range(share)]
     tau = field_weights(tau_ref, nfac, cols)
     load_prior([None] + [field_ref[r] for r in range(share)] + [None], lands[:1] + lands + lands[-1:], tau, prior)
-    all_rows(
-        land, right, wide, left, mix, load, (score0, score1), (logit0, logit1), (post0, post1), (gap0, gap1), acc, accw,
-        prior,
-    )
+    field_grads(load_ref, gap_refs, prior)
     for r in range(share):
         half = mom_ref[r] + 0.5 * STEP_FIELD * prior[r]
         half_ref[r] = half
@@ -503,27 +526,33 @@
             jnp.where(flag, new_ref[end], new_ref[0]),
             jnp.where(flag, lands[end], lands[0]),
         )
-    param_grads(flat, acc, accw, grad_ref, ncomp, nfac)
-    nparam = grad_ref.shape[0]
-    if flat.shape[0] > nparam:
-        flat[nparam:, :] = jnp.zeros((flat.shape[0] - nparam, LANES), F32)
-    flat[0:nparam, :] = 0.5 * STEP_PARAM * STEP_PARAM * grad_ref[...]
-    own_prof, own_load = pack_ref[0:mine, :], pack_ref[mine:size, :]
-    owner = cells_rank == 0
-    base_prof = own_prof + STEP_PARAM * (pmom_ref[...] - 0.5 * STEP_PARAM * 0.25 * own_prof)
-    base_load = own_load + STEP_PARAM * (wmom_ref[...] - 0.5 * STEP_PARAM * own_load)
-    flat[pl.ds(pl.multiple_of(comp_rank * mine, mine), mine), :] += jnp.where(owner, base_prof, 0.0)
-    flat[pl.ds(pl.multiple_of(ncomp + comp_rank * nfac, nfac), nfac), :] += jnp.where(owner, base_load, 0.0)
-    spread_chunks(flat, keep_ref, send_ref, cells_rank)
+
+
+def edge_terms(chunk, ring, tiles, rank_ref, tau, lands, old_ref, near_ref, far_ref, edge_ref):
+    cells_rank, comp_rank = rank_ref[0], rank_ref[1]
+    nfac, cols = tau.shape
+    source = jnp.where(comp_rank == 0, cells_rank - 1, jnp.where(comp_rank == ring - 1, cells_rank + 1, cells_rank))
+    source = jnp.clip(source, 0, tiles - 1)
+    slot = (source // 2) ^ (cells_rank // 2)
+    relay = jnp.where(source % 2 == cells_rank % 2, near_ref[slot, chunk:, :], far_ref[slot, chunk:, :])
+    even = comp_rank % 2 == 0
+    direct = edge_ref[...]
+    above = unpack_edge(jnp.where(even, relay, direct), nfac, cols)
+    below = unpack_edge(jnp.where(even, direct, relay), nfac, cols)
+    land_above = jnp.where((comp_rank == 0) & (cells_rank == 0), 0.0, above[2])
+    land_below = jnp.where((comp_rank == ring - 1) & (cells_rank == tiles - 1), 0.0, below[2])
+    pull_up = -tau * (land_above * lands[0]) * (old_ref[0] - above[0])
+    pull_down = -tau * (land_below * lands[-1]) * (old_ref[old_ref.shape[0] - 1] - below[0])
+    return (above[1], below[1]), (land_above, land_below), (pull_up, pull_down)
 
 
 def second_kernel(
-    ncomp, chunk, ring, tiles, rank_ref, tau_ref, counts_ref, field_ref, half_ref, land_ref, logexp_ref, pmom_ref, wmom_ref,
-    old_ref, own_ref, near_ref, far_ref, edge_ref, grad0_ref, new_ref, mom_ref, params_ref,
-    keep_ref, send_ref,
-    flat, left, mix, load, right, wide, prior, score0, score1, logit0, logit1, post0, post1, gap0, gap1, acc, accw, out,
-    grad,
+    ncomp, chunk, ring, tiles, rank_ref, tau_ref, counts_ref, field_ref, land_ref, logexp_ref, pmom_ref, wmom_ref, old_ref,
+    own_ref, near_ref, far_ref, edge_ref, grad0_ref, *refs
 ):
+    gaps, refs = refs[: counts_ref.shape[0]], refs[counts_ref.shape[0] :]
+    load, new_ref, params_ref, stats_ref, keep_ref, send_ref, flat, left, mix, right, wide, *refs = refs
+    score0, score1, logit0, logit1, post0, post1, gap0, gap1, acc, accw, out, grad = refs
     cells_rank, comp_rank = rank_ref[0], rank_ref[1]
     share, nfac, cols = field_ref.shape
     mine = pmom_ref.shape[0]
@@ -537,53 +566,35 @@
     land = land_ref[here, :].astype(F32)
     lands = [land[r : r + 1, :] for r in range(share)]
     tau = field_weights(tau_ref, nfac, cols)
-
-    source = jnp.where(comp_rank == 0, cells_rank - 1, jnp.where(comp_rank == ring - 1, cells_rank + 1, cells_rank))
-    source = jnp.clip(source, 0, tiles - 1)
-    slot = (source // 2) ^ (cells_rank // 2)
-    relay = jnp.where(source % 2 == cells_rank % 2, near_ref[slot, chunk:, :], far_ref[slot, chunk:, :])
-    even = comp_rank % 2 == 0
-    direct = edge_ref[...]
-    above = unpack_edge(jnp.where(even, relay, direct), nfac, cols)
-    below = unpack_edge(jnp.where(even, direct, relay), nfac, cols)
-    land_above = jnp.where((comp_rank == 0) & (cells_rank == 0), 0.0, above[2])
-    land_below = jnp.where((comp_rank == ring - 1) & (cells_rank == tiles - 1), 0.0, below[2])
-    end = share - 1
-    pull_up = -tau * (land_above * lands[0]) * (old_ref[0] - above[0])
-    pull_down = -tau * (land_below * lands[end]) * (old_ref[end] - below[0])
+    _, _, pulls = edge_terms(chunk, ring, tiles, rank_ref, tau, lands, old_ref, near_ref, far_ref, edge_ref)
     move = 0.5 * STEP_FIELD * STEP_FIELD
     for r in range(share):
         fresh = field_ref[r]
         if r == 0:
-            fresh = fresh + move * pull_up
-        if r == end:
-            fresh = fresh + move * pull_down
+            fresh = fresh + move * pulls[0]
+        if r == share - 1:
+            fresh = fresh + move * pulls[1]
         new_ref[r] = fresh
     load_params(flat, left, mix, load, ncomp, nfac)
     load_cells(counts_ref, new_ref, logexp_ref[here, :], right, wide)
-    rows = [above[1] - move * pull_up] + [new_ref[r] for r in range(share)] + [below[1] - move * pull_down]
-    energy = load_prior(rows, [land_above] + lands + [land_below], tau, prior)
-    prior[0] += pull_up
-    prior[end] += pull_down
-
-    log_dens = all_rows(
-        land, right, wide, left, mix, load, (score0, score1), (logit0, logit1), (post0, post1), (gap0, gap1), acc, accw,
-        prior,
-    )
-    for r in range(share):
-        fresh = half_ref[r] + 0.5 * STEP_FIELD * prior[r]
-        mom_ref[r] = fresh
-        energy = energy + 0.5 * (fresh * fresh)
+    log_dens = all_rows(land, right, wide, left, mix, (score0, score1), (logit0, logit1), (post0, post1), (gap0, gap1), gaps, acc, accw)
     param_grads(flat, acc, accw, grad, ncomp, nfac)
     first_device = (cells_rank == 0) & (comp_rank == 0)
     prof_all = flat[0:ncomp, :]
     load_all = flat[ncomp:nparam, :]
-    param_energy = jnp.sum(0.125 * (prof_all * prof_all)) + jnp.sum(0.5 * (load_all * load_all))
-    total = jnp.sum(energy) - jnp.sum(log_dens) + jnp.where(first_device, param_energy, 0.0)
+    param_energy = jnp.sum(0.125 * (prof_all * prof_all).reshape(ncomp // 8, 8, LANES), axis=0)
+    param_energy = param_energy + jnp.sum(
+        0.5 * (load_all * load_all).reshape((nparam - ncomp) // 8, 8, LANES), axis=0
+    )
+    stats_ref[0:8, :] = jnp.where(first_device, param_energy, 0.0)
+    sub = lax.broadcasted_iota(jnp.int32, (8, LANES), 0)
+    dens = jnp.zeros((8, LANES), F32)
+    for b in range(cols // LANES):
+        dens = jnp.where(sub == b, -log_dens[:, b * LANES : (b + 1) * LANES], dens)
+    stats_ref[8:16, :] = dens
+    if out.shape[0] > nparam:
+        out[nparam:, :] = jnp.zeros((out.shape[0] - nparam, LANES), F32)
     out[0:nparam, :] = 0.5 * STEP_PARAM * (grad0_ref[...] + grad[...])
-    tail = out.shape[0] - nparam
-    spot = lax.broadcasted_iota(jnp.int32, (tail, LANES), 0) + lax.broadcasted_iota(jnp.int32, (tail, LANES), 1)
-    out[nparam:, :] = jnp.where(spot == 0, total, 0.0)
     owner = cells_rank == 0
     old_prof, old_load = own_ref[0:mine, :], own_ref[mine : mine + nfac, :]
     base_prof = pmom_ref[...] - 0.5 * STEP_PARAM * 0.25 * (old_prof + new_prof)
@@ -593,6 +604,36 @@
     spread_chunks(out, keep_ref, send_ref, cells_rank)
 
 
+def second_field(
+    chunk, ring, tiles, rank_ref, tau_ref, new_ref, half_ref, old_ref, land_ref, load_ref, stats_ref, near_ref, far_ref,
+    edge_ref, *refs
+):
+    gap_refs, (mom_ref, energy_ref, prior) = refs[: new_ref.shape[0]], refs[new_ref.shape[0] :]
+    comp_rank = rank_ref[1]
+    share, nfac, cols = new_ref.shape
+    land = land_ref[pl.ds(pl.multiple_of(comp_rank * share, 8), share), :].astype(F32)
+    lands = [land[r : r + 1, :] for r in range(share)]
+    tau = field_weights(tau_ref, nfac, cols)
+    (above, below), (land_above, land_below), (pull_up, pull_down) = edge_terms(
+        chunk, ring, tiles, rank_ref, tau, lands, old_ref, near_ref, far_ref, edge_ref
+    )
+    move = 0.5 * STEP_FIELD * STEP_FIELD
+    rows = [above - move * pull_up] + [new_ref[r] for r in range(share)] + [below - move * pull_down]
+    energy = load_prior(rows, [land_above] + lands + [land_below], tau, prior)
+    prior[0] += pull_up
+    prior[share - 1] += pull_down
+    field_grads(load_ref, gap_refs, prior)
+    for r in range(share):
+        fresh = half_ref[r] + 0.5 * STEP_FIELD * prior[r]
+        mom_ref[r] = fresh
+        energy = energy + 0.5 * (fresh * fresh)
+    tiles_sum = stats_ref[0:8, :] + stats_ref[8:16, :]
+    for i in range(0, nfac, 8):
+        for b in range(0, cols, LANES):
+            tiles_sum = tiles_sum + energy[i : i + 8, b : b + LANES]
+    energy_ref[...] = tiles_sum
+
+
 def last_kernel(ncomp, nparam, chunk, cells, rank_ref, near_ref, far_ref, prof_ref, mixing_ref, ham_ref, flat):
     cells_rank, comp_rank = rank_ref[0], rank_ref[1]
     mine, nfac = prof_ref.shape[0], mixing_ref.shape[0]
@@ -600,9 +641,9 @@
     prof_ref[...] = flat[pl.ds(pl.multiple_of(comp_rank * mine, mine), mine), :]
     mixing_ref[...] = flat[pl.ds(pl.multiple_of(ncomp + comp_rank * nfac, nfac), nfac), :]
     momenta = flat[0:nparam, :]
-    rest = flat[nparam:, :]
     total = jnp.sum(0.5 * (momenta * momenta).reshape(nparam // 8, 8, LANES), axis=0)
-    total = total + jnp.sum(rest.reshape(rest.shape[0] // 8, 8, LANES), axis=0)
+    for source in (near_ref, far_ref):
+        total = total + jnp.sum(source[:, chunk:, :], axis=0)
     total = jnp.sum(jnp.sum(total, axis=0, keepdims=True), axis=1, keepdims=True)
     ham_ref[...] = total / cells
 
@@ -620,8 +661,7 @@
     pairs = tiles // 2
     edge = 2 * nfac * cols // LANES + 8
     round_up = lambda rows: -(-rows // (8 * tiles)) * 8
-    chunk_one = round_up(nparam)
-    chunk_two = round_up(nparam + 1)
+    chunk = round_up(nparam)
     comp_rank = lax.axis_index("comp")
     cells_rank = lax.axis_index("cells")
     ranks = jnp.stack([cells_rank, comp_rank]).astype(jnp.int32)
@@ -634,19 +674,25 @@
     smem = pl.BlockSpec(memory_space=pltpu.SMEM)
     shape = lambda *dims: jax.ShapeDtypeStruct(dims, F32)
     work = [
+        pltpu.VMEM((tiles * chunk, LANES), F32),
         pltpu.VMEM((ncomp, 4 * LANES), BF16),
         pltpu.VMEM((ncomp, LANES), BF16),
-        pltpu.VMEM((2 * nfac, ncomp), BF16),
         pltpu.VMEM((share, 4 * LANES, cols), BF16),
         pltpu.VMEM((share, 2 * LANES, 2 * cols), BF16),
-        pltpu.VMEM((share, nfac, cols), F32),
     ]
     work += [pltpu.VMEM((ncomp, cols), F32)] * 4 + [pltpu.VMEM((ncomp, 2 * cols), BF16)] * 4
     work += [
         pltpu.VMEM((ncomp, 2 * LANES), F32),
         pltpu.VMEM((3 * nfac, ncomp), F32),
     ]
-    def call(body, name, smem_count, vmem_count, outs, scratch):
+    field_shape = shape(share, nfac, cols)
+    chunk_shape = shape(pairs, chunk, LANES)
+    gap_shapes = [jax.ShapeDtypeStruct((ncomp, 2 * cols), BF16)] * share
+    load_shape = jax.ShapeDtypeStruct((2 * nfac, ncomp), BF16)
+    field_flops = 2 * 2 * nfac * ncomp * 2 * cols * share
+    field_cost = pl.CostEstimate(flops=field_flops, bytes_accessed=4 * share * ncomp * cols, transcendentals=0)
+
+    def call(body, name, smem_count, vmem_count, outs, scratch, cost=None):
         return pl.pallas_call(
             body,
             name=name,
@@ -654,58 +700,59 @@
             out_specs=[vmem] * len(outs),
             scratch_shapes=scratch,
             out_shape=outs,
+            cost_estimate=cost,
             compiler_params=pltpu.CompilerParams(vmem_limit_bytes=40 * 1024 * 1024),
         )
 
+    prior = [pltpu.VMEM((share, nfac, cols), F32)]
     first = call(
         functools.partial(first_kernel, ncomp),
         "first_gradient",
-        2,
-        7 + 3,
-        [
-            shape(share, nfac, cols),
-            shape(share, nfac, cols),
-            shape(edge, LANES),
-            shape(edge, LANES),
-            shape(nparam, LANES),
-            shape(pairs, chunk_one, LANES),
-            shape(pairs, chunk_one, LANES),
-        ],
-        [pltpu.VMEM((tiles * chunk_one, LANES), F32)] + work + [pltpu.VMEM((mine + nfac, LANES), F32)],
-    )
-    part_field, half, near_edge, far_edge, grad, keep, send = first(
-        ranks, field_tau, count_rows, field_rows, mom_rows, land_mask, log_exposure, profile_mom, mixing_mom, pack, got, others
-    )
+        1,
+        9,
+        gap_shapes + [load_shape, shape(nparam, LANES), chunk_shape, chunk_shape],
+        work + [pltpu.VMEM((mine + nfac, LANES), F32)],
+    )
+    *gaps, load, grad, keep, send = first(
+        ranks, count_rows, field_rows, land_mask, log_exposure, profile_mom, mixing_mom, pack, got, others
+    )
+    edge_shape = shape(edge, LANES)
+    part_field, half, near_edge, far_edge = call(
+        first_field, "first_field", 2, 4 + share, [field_shape, field_shape, edge_shape, edge_shape], prior, field_cost
+    )(ranks, field_tau, field_rows, mom_rows, land_mask, load, *gaps)
     near, far, got_edge, _ = all_sum(keep, send, near_edge, far_edge)
     second = call(
-        functools.partial(second_kernel, ncomp, chunk_one, ring, tiles),
+        functools.partial(second_kernel, ncomp, chunk, ring, tiles),
         "second_gradient",
         2,
-        7 + 6,
-        [
-            shape(share, nfac, cols),
-            shape(share, nfac, cols),
+        12,
+        gap_shapes
+        + [
+            load_shape,
+            field_shape,
             shape(mine + nfac, ncat),
-            shape(pairs, chunk_two, LANES),
-            shape(pairs, chunk_two, LANES),
+            shape(16, LANES),
+            chunk_shape,
+            chunk_shape,
         ],
-        [pltpu.VMEM((tiles * chunk_one, LANES), F32)]
-        + work
-        + [pltpu.VMEM((tiles * chunk_two, LANES), F32), pltpu.VMEM((nparam, LANES), F32)],
-    )
-    new_field, new_mom, new_params, keep, send = second(
-        ranks, field_tau, count_rows, part_field, half, land_mask, log_exposure, profile_mom, mixing_mom, field_rows, pack,
-        near, far, got_edge, grad,
-    )
+        work + [pltpu.VMEM((tiles * chunk, LANES), F32), pltpu.VMEM((nparam, LANES), F32)],
+    )
+    *gaps, load, new_field, new_params, stats, keep, send = second(
+        ranks, field_tau, count_rows, part_field, land_mask, log_exposure, profile_mom, mixing_mom, field_rows, pack, near,
+        far, got_edge, grad,
+    )
+    new_mom, energy = call(
+        functools.partial(second_field, chunk, ring, tiles), "second_field", 2, 9 + share, [field_shape, shape(8, LANES)], prior, field_cost
+    )(ranks, field_tau, new_field, half, field_rows, land_mask, load, stats, near, far, got_edge, *gaps)
     done = (new_field.swapaxes(0, 1), new_params[:mine], new_params[mine:], new_mom.swapaxes(0, 1))
-    near, far, _, done = all_sum(keep, send, beside=done)
+    near, far, _, done = all_sum(keep, send, late=energy, beside=done)
     final = call(
-        functools.partial(last_kernel, ncomp, nparam, chunk_two, tile_rows * cols * tiles),
+        functools.partial(last_kernel, ncomp, nparam, chunk, tile_rows * cols * tiles),
         "momenta",
         1,
         2,
         [shape(mine, ncat), shape(nfac, mine), shape(1, 1)],
-        [pltpu.VMEM((tiles * chunk_two, LANES), F32)],
+        [pltpu.VMEM((tiles * chunk, LANES), F32)],
     )
     new_profile_mom, new_mixing_mom, hamiltonian = final(ranks, near, far)
     return (

time: 73.7 us -> 73.1 us (level)
  waiting for transfers between devices: 25.2 us -> 22.4 us
  Pallas kernels: 12.6 us -> 14.8 us
    ppermute x24, waiting for transfers between devices: 25.2 us -> 22.4 us  [partner(): return lax.ppermute(values, axis, [(i, i ^ flip) for i in range(count)])]
    pallas_call x2 -> x4, Pallas kernels: 11.3 us -> 13.5 us  [the longest x1 5.4 us: fast_device(): first(ranks, count_rows, field_rows, land_mask, log_exposure, profile_mom...]
    transpose x1 -> x0, local copies, waits for them, and re-layouts: 1.05 us -> none  [fast_device(): mom_rows = factor_mom.swapaxes(0, 1)]
    unnamed x13 -> x18, local copies, waits for them, and re-layouts: 1.5 us -> 2.5 us
  transfers between devices with their start and end apart: 25 -> 25, of which waited for: 19 -> 17; matrix products, arithmetic and copies ran while one was open for 7% -> 7% of each run, Pallas kernels for 0% -> 4%
where the time goes in v5:
time: 73.1 us; the launch traced here: 72.8 us
  starting transfers between devices  28.3 us (39%)
  waiting for transfers between devices  22.4 us (31%)
  Pallas kernels  14.8 us (20%)
  local copies, waits for them, and re-layouts  5.06 us (7%)
  other arithmetic  1.45 us (2%)
  between operations  0.89 us (1%)
    ppermute x24, starting transfers between devices, partner(): return lax.ppermute(values, axis, [(i, i ^ flip) for i in range(count)])  25.3 us
    ppermute x24, waiting for transfers between devices, partner(): return lax.ppermute(values, axis, [(i, i ^ flip) for i in range(count)])  22.4 us
    pallas_call x1, Pallas kernels, fast_device(): first(ranks, count_rows, field_rows, land_mask, log_exposure, profile_mom...  5.4 us
    pallas_call x1, Pallas kernels, fast_device(): second(ranks, field_tau, count_rows, part_field, land_mask, log_exposure,...  5.34 us
    ppermute x1, starting transfers between devices, gather_params(): one = lax.ppermute(pack, ('cells', 'comp'), spread)  3.02 us
    unnamed x18, local copies, waits for them, and re-layouts  2.5 us
  transfers between devices with their start and end apart: 25, of which 17 were waited for; matrix products, arithmetic and copies ran while one was open for 7% of the time, Pallas kernels for 4%

profile of v5, /device:TPU:0, one launch (start us, length us, event | category | flops | bytes accessed | tf_op | source)
XLA Modules:
  0.0 72.8 jit_solution(5343567942081316532)
XLA Ops:
  1.6 3.0 %collective-permute-start = (f32[144,128]{1,0:T(8,128)S(1)}, f32[144,128]{1,0:T(8,128)S(1)}, u32[]{:S(2)}, u32[]{:S(2)}) collective-permute-start(f32[144,128]{1,0:T(8,128)S(1)} %pad_add_fusion.pack_ref.own_ref), channel_id=1, source_target_pairs={{0,1},{1,0},{2,3},{3,2},{4,6},{5,7},{6,4},{7,5},{8,9},{9,8},{10,11... | collective-permute-start | bytes 221192 | tf_op jit(solution)/shard_map/ppermute | solution.py:243
  4.6 2.5 %collective-permute-start.1 = (f32[72,128]{1,0:T(8,128)S(1)}, f32[72,128]{1,0:T(8,128)S(1)}, u32[]{:S(2)}, u32[]{:S(2)}) collective-permute-start(f32[72,128]{1,0:T(8,128)S(1)} %constant_dynamic-slice_fusion), channel_id=1, source_target_pairs={{0,3},{1,2},{2,1},{3,0},{4,7},{5,6},{6,5},{7,4},{8,11},{9,10},{10,... | collective-permute-start | bytes 110600 | tf_op jit(solution)/shard_map/ppermute | solution.py:212
  7.1 1.3 %constant_dynamic-slice_fusion.1 = s32[128,8,256]{2,1,0:T(8,128)S(1)} fusion(s32[128,32,256]{2,1,0:T(8,128)} %param.17, s32[]{:T(128)S(6)} %select_n.13), kind=kLoop, calls=%fused_computation.34 | loop fusion | bytes 2097156 | tf_op jit(solution)/shard_map/dynamic_slice | solution.py:670
  8.7 1.0 %copy.29 = f32[16,8,256]{2,0,1:T(8,128)S(1)} copy(f32[16,8,256]{2,1,0:T(8,128)} %param.10) | data formatting | bytes 262144 | tf_op args[0]
  10.5 1.2 %collective-permute-done.2.others_ref = f32[216,128]{1,0:T(8,128)S(1)} collective-permute-done((f32[216,128]{1,0:T(8,128)S(1)}, f32[216,128]{1,0:T(8,128)S(1)}, u32[]{:S(2)}, u32[]{:S(2)}) %collective-permute-start.2) | collective-permute-done | bytes 110624 | tf_op jit(solution)/shard_map/ppermute | solution.py:212
  11.7 5.4 %first_gradient.1 = (bf16[512,512]{1,0:T(8,128)(2,1)S(1)}, bf16[512,512]{1,0:T(8,128)(2,1)S(1)}, bf16[512,512]{1,0:T(8,128)(2,1)S(1)}, bf16[512,512]{1,0:T(8,128...) custom-call(s32[2]{0:T(128)S(1)} %pad_add_fusion.1.rank_ref, ...), custom_call_target="tpu_custom_call" | custom-call | tf_op jit(solution)/shard_map/first_gradient/pallas_call | solution.py:716
  17.4 1.2 %collective-permute-done.3 = f32[4,72,128]{2,1,0:T(8,128)S(1)} collective-permute-done((f32[4,72,128]{2,1,0:T(8,128)S(1)}, f32[4,72,128]{2,1,0:T(8,128)S(1)}, u32[]{:S(2)}, u32[]{:S(2)}) %collective-permute-start.3) | collective-permute-done | bytes 147488 | tf_op jit(solution)/shard_map/ppermute | solution.py:212
  18.6 1.6 %collective-permute-start.4 = (f32[72,128]{1,0:T(8,128)S(1)}, f32[72,128]{1,0:T(8,128)S(1)}, u32[]{:S(2)}, u32[]{:S(2)}) collective-permute-start(f32[72,128]{1,0:T(8,128)S(1)} %get-tuple-element.97), channel_id=1, source_target_pairs={{0,8},{4,12},{8,0},{12,4},{16,24},{20,28},{24,16},{28,20},{1,9},{5... | collective-permute-start | bytes 110600 | tf_op jit(solution)/shard_map/ppermute | solution.py:212
  20.2 1.5 %collective-permute-start.6 = (f32[72,128]{1,0:T(8,128)S(1)}, f32[72,128]{1,0:T(8,128)S(1)}, u32[]{:S(2)}, u32[]{:S(2)}) collective-permute-start(f32[72,128]{1,0:T(8,128)S(1)} %get-tuple-element.98), channel_id=1, source_target_pairs={{0,24},{4,28},{8,16},{12,20},{16,8},{20,12},{24,0},{28,4},{1,25},{... | collective-permute-start | bytes 110600 | tf_op jit(solution)/shard_map/ppermute | solution.py:212
  22.3 1.4 %first_field.1 = (f32[8,16,256]{2,1,0:T(8,128)S(1)}, f32[8,16,256]{2,1,0:T(8,128)S(1)}, f32[72,128]{1,0:T(8,128)S(1)}, f32[72,128]{1,0:T(8,128)S(1)}) custom-call(s32[2]{0:T(128)S(1)} %pad_add_fusion.1.rank_ref, f32[16]{0:T(128)S(1)} %copy-done.4, f32[8,16,256]{2,1,0:T(8,128)S(1)} %bitcast.51, f32[8,16,256]{2,1,0:T(8,128)S(1)} %bitcast.55, ...), custom_call_target="tpu_custom_call" | custom-call | flops 134217728 | bytes 4194304 | tf_op jit(solution)/shard_map/first_field/pallas_call | solution.py:720
  23.6 1.4 %collective-permute-done.6 = f32[72,128]{1,0:T(8,128)S(1)} collective-permute-done((f32[72,128]{1,0:T(8,128)S(1)}, f32[72,128]{1,0:T(8,128)S(1)}, u32[]{:S(2)}, u32[]{:S(2)}) %collective-permute-start.6) | collective-permute-done | bytes 36896 | tf_op jit(solution)/shard_map/ppermute | solution.py:212
  25.8 3.1 %collective-permute-start.9 = (f32[144,128]{1,0:T(8,128)S(1)}, f32[144,128]{1,0:T(8,128)S(1)}, u32[]{:S(2)}, u32[]{:S(2)}) collective-permute-start(f32[144,128]{1,0:T(8,128)S(1)} %get-tuple-element.106), channel_id=1, source_target_pairs={{0,3},{1,2},{2,1},{3,0},{4,7},{5,6},{6,5},{7,4},{8,11},{9,10},{10,... | collective-permute-start | bytes 221192 | tf_op jit(solution)/shard_map/ppermute | solution.py:212
  29.2 4.9 %collective-permute-done.8 = f32[72,128]{1,0:T(8,128)S(1)} collective-permute-done((f32[72,128]{1,0:T(8,128)S(1)}, f32[72,128]{1,0:T(8,128)S(1)}, u32[]{:S(2)}, u32[]{:S(2)}) %collective-permute-start.8) | collective-permute-done | bytes 36896 | tf_op jit(solution)/shard_map/ppermute | solution.py:212
  34.2 1.0 %collective-permute-start.11 = (f32[144,128]{1,0:T(8,128)S(1)}, f32[144,128]{1,0:T(8,128)S(1)}, u32[]{:S(2)}, u32[]{:S(2)}) collective-permute-start(f32[144,128]{1,0:T(8,128)S(1)} %get-tuple-element.104), channel_id=1, source_target_pairs={{0,16},{4,20},{8,24},{12,28},{16,0},{20,4},{24,8},{28,12},{1,17},{... | collective-permute-start | bytes 221192 | tf_op jit(solution)/shard_map/ppermute | solution.py:212
  35.2 1.1 %collective-permute-start.10 = (f32[144,128]{1,0:T(8,128)S(1)}, f32[144,128]{1,0:T(8,128)S(1)}, u32[]{:S(2)}, u32[]{:S(2)}) collective-permute-start(f32[144,128]{1,0:T(8,128)S(1)} %get-tuple-element.104), channel_id=1, source_target_pairs={{0,8},{4,12},{8,0},{12,4},{16,24},{20,28},{24,16},{28,20},{1,9},{5... | collective-permute-start | bytes 221192 | tf_op jit(solution)/shard_map/ppermute | solution.py:212
  36.3 1.5 %collective-permute-start.12 = (f32[144,128]{1,0:T(8,128)S(1)}, f32[144,128]{1,0:T(8,128)S(1)}, u32[]{:S(2)}, u32[]{:S(2)}) collective-permute-start(f32[144,128]{1,0:T(8,128)S(1)} %get-tuple-element.104), channel_id=1, source_target_pairs={{0,24},{4,28},{8,16},{12,20},{16,8},{20,12},{24,0},{28,4},{1,25},{... | collective-permute-start | bytes 221192 | tf_op jit(solution)/shard_map/ppermute | solution.py:212
  38.6 0.9 %collective-permute-done.10 = f32[144,128]{1,0:T(8,128)S(1)} collective-permute-done((f32[144,128]{1,0:T(8,128)S(1)}, f32[144,128]{1,0:T(8,128)S(1)}, u32[]{:S(2)}, u32[]{:S(2)}) %collective-permute-start.10) | collective-permute-done | bytes 73760 | tf_op jit(solution)/shard_map/ppermute | solution.py:212
  39.5 2.0 %collective-permute-done.12 = f32[144,128]{1,0:T(8,128)S(1)} collective-permute-done((f32[144,128]{1,0:T(8,128)S(1)}, f32[144,128]{1,0:T(8,128)S(1)}, u32[]{:S(2)}, u32[]{:S(2)}) %collective-permute-start.12) | collective-permute-done | bytes 73760 | tf_op jit(solution)/shard_map/ppermute | solution.py:212
  41.6 1.6 %collective-permute-done.13.far_ref = f32[4,144,128]{2,1,0:T(8,128)S(1)} collective-permute-done((f32[4,144,128]{2,1,0:T(8,128)S(1)}, f32[4,144,128]{2,1,0:T(8,128)S(1)}, u32[]{:S(2)}, u32[]{:S(2)}) %collective-permute-start.13) | collective-permute-done | bytes 294944 | tf_op jit(solution)/shard_map/ppermute | solution.py:212
  43.2 5.3 %second_gradient.1 = (bf16[512,512]{1,0:T(8,128)(2,1)S(1)}, bf16[512,512]{1,0:T(8,128)(2,1)S(1)}, bf16[512,512]{1,0:T(8,128)(2,1)S(1)}, bf16[512,512]{1,0:T(8,12...) custom-call(s32[2]{0:T(128)S(1)} %pad_add_fusion.1.rank_ref, ...), custom_call_target="tpu_custom_call" | custom-call | tf_op jit(solution)/shard_map/second_gradient/pallas_call | solution.py:740
  48.7 1.2 %collective-permute-done.14 = f32[4,72,128]{2,1,0:T(8,128)S(1)} collective-permute-done((f32[4,72,128]{2,1,0:T(8,128)S(1)}, f32[4,72,128]{2,1,0:T(8,128)S(1)}, u32[]{:S(2)}, u32[]{:S(2)}) %collective-permute-start.14) | collective-permute-done | bytes 147488 | tf_op jit(solution)/shard_map/ppermute | solution.py:212
  50.0 1.0 %collective-permute-start.15 = (f32[72,128]{1,0:T(8,128)S(1)}, f32[72,128]{1,0:T(8,128)S(1)}, u32[]{:S(2)}, u32[]{:S(2)}) collective-permute-start(f32[72,128]{1,0:T(8,128)S(1)} %get-tuple-element.94), channel_id=1, source_target_pairs={{0,8},{4,12},{8,0},{12,4},{16,24},{20,28},{24,16},{28,20},{1,9},{5... | collective-permute-start | bytes 110600 | tf_op jit(solution)/shard_map/ppermute | solution.py:212
  51.0 2.0 %collective-permute-start.17 = (f32[72,128]{1,0:T(8,128)S(1)}, f32[72,128]{1,0:T(8,128)S(1)}, u32[]{:S(2)}, u32[]{:S(2)}) collective-permute-start(f32[72,128]{1,0:T(8,128)S(1)} %get-tuple-element.95), channel_id=1, source_target_pairs={{0,24},{4,28},{8,16},{12,20},{16,8},{20,12},{24,0},{28,4},{1,25},{... | collective-permute-start | bytes 110600 | tf_op jit(solution)/shard_map/ppermute | solution.py:212
  54.8 1.4 %second_field.1 = (f32[8,16,256]{2,1,0:T(8,128)S(1)}, f32[8,128]{1,0:T(8,128)S(1)}) custom-call(s32[2]{0:T(128)S(1)} %pad_add_fusion.1.rank_ref, f32[16]{0:T(128)S(1)} %copy-done.4, f32[8,16,256]{2,1,0:T(8,128)S(1)} %get-tuple-element.64.new_ref, f32[8,16,256]{2,1,0:T(8,128)S(1)} %get-tuple-element.66.half_ref, f32[8,16,256]{2,1,0:T(8,128)S(1)} %bitcast.53, ...), custom_call_target="tpu_custom_call" | custom-call | flops 134217728 | bytes 4194304 | tf_op jit(solution)/shard_map/second_field/pallas_call | solution.py:744
  57.1 1.6 %collective-permute-start.20 = (f32[80,128]{1,0:T(8,128)S(1)}, f32[80,128]{1,0:T(8,128)S(1)}, u32[]{:S(2)}, u32[]{:S(2)}) collective-permute-start(f32[80,128]{1,0:T(8,128)S(1)} %constant_dynamic-update-slice_fusion.2), channel_id=1, source_target_pairs={{0,3},{1,2},{2,1},{3,0},{4,7},{5,6},{6,5},{7,4},{8,11},{9,10},{10,... | collective-permute-start | bytes 122888 | tf_op jit(solution)/shard_map/ppermute | solution.py:212
  58.8 2.7 %collective-permute-start.18 = (f32[80,128]{1,0:T(8,128)S(1)}, f32[80,128]{1,0:T(8,128)S(1)}, u32[]{:S(2)}, u32[]{:S(2)}) collective-permute-start(f32[80,128]{1,0:T(8,128)S(1)} %constant_dynamic-update-slice_fusion.2), channel_id=1, source_target_pairs={{0,1},{1,0},{2,3},{3,2},{4,5},{5,4},{6,7},{7,6},{8,9},{9,8},{10,11... | collective-permute-start | bytes 122888 | tf_op jit(solution)/shard_map/ppermute | solution.py:212
  61.5 1.5 %collective-permute-done.20 = f32[80,128]{1,0:T(8,128)S(1)} collective-permute-done((f32[80,128]{1,0:T(8,128)S(1)}, f32[80,128]{1,0:T(8,128)S(1)}, u32[]{:S(2)}, u32[]{:S(2)}) %collective-permute-start.20) | collective-permute-done | bytes 40992 | tf_op jit(solution)/shard_map/ppermute | solution.py:212
  63.0 0.9 %collective-permute-done.19 = f32[80,128]{1,0:T(8,128)S(1)} collective-permute-done((f32[80,128]{1,0:T(8,128)S(1)}, f32[80,128]{1,0:T(8,128)S(1)}, u32[]{:S(2)}, u32[]{:S(2)}) %collective-permute-start.19) | collective-permute-done | bytes 40992 | tf_op jit(solution)/shard_map/ppermute | solution.py:212
  63.9 1.4 %collective-permute-start.23 = (f32[80,128]{1,0:T(8,128)S(1)}, f32[80,128]{1,0:T(8,128)S(1)}, u32[]{:S(2)}, u32[]{:S(2)}) collective-permute-start(f32[80,128]{1,0:T(8,128)S(1)} %add_add_fusion), channel_id=1, source_target_pairs={{0,24},{4,28},{8,16},{12,20},{16,8},{20,12},{24,0},{28,4},{1,25},{... | collective-permute-start | bytes 122888 | tf_op jit(solution)/shard_map/ppermute | solution.py:212
  66.0 1.5 %collective-permute-start.21 = (f32[80,128]{1,0:T(8,128)S(1)}, f32[80,128]{1,0:T(8,128)S(1)}, u32[]{:S(2)}, u32[]{:S(2)}) collective-permute-start(f32[80,128]{1,0:T(8,128)S(1)} %add_add_fusion), channel_id=1, source_target_pairs={{0,8},{4,12},{8,0},{12,4},{16,24},{20,28},{24,16},{28,20},{1,9},{5... | collective-permute-start | bytes 122888 | tf_op jit(solution)/shard_map/ppermute | solution.py:212
  67.5 1.4 %collective-permute-done.23 = f32[80,128]{1,0:T(8,128)S(1)} collective-permute-done((f32[80,128]{1,0:T(8,128)S(1)}, f32[80,128]{1,0:T(8,128)S(1)}, u32[]{:S(2)}, u32[]{:S(2)}) %collective-permute-start.23) | collective-permute-done | bytes 40992 | tf_op jit(solution)/shard_map/ppermute | solution.py:212
  71.6 1.3 %momenta.1 = (f32[128,128]{1,0:T(8,128)}, f32[16,128]{1,0:T(8,128)}, f32[1,1]{1,0:T(1,128)}) custom-call(s32[2]{0:T(128)S(1)} %pad_add_fusion.1.rank_ref, f32[4,80,128]{2,1,0:T(8,128)S(1)} %pad_maximum_fusion.1.near_ref, f32[4,80,128]{2,1,0:T(8,128)S(1)} %collective-permute-done.24.far_ref), custom_call_target="tpu_custom_call" | custom-call | tf_op jit(solution)/shard_map/momenta/pallas_call | solution.py:757
  (62 shorter events, 11.2 us)
Async XLA Ops:
  0.6 11.1 %copy-start = (s32[32,256]{1,0:T(8,128)S(1)}, s32[32,256]{1,0:T(8,128)}, u32[]{:S(2)}) copy-start(s32[32,256]{1,0:T(8,128)} %land_ref.7) | copy-start | bytes 98308
  0.6 11.1 %copy-start.2 = (f32[32,256]{1,0:T(8,128)S(1)}, f32[32,256]{1,0:T(8,128)}, u32[]{:S(2)}) copy-start(f32[32,256]{1,0:T(8,128)} %logexp_ref.3) | copy-start | bytes 98308
  0.7 11.1 %copy-start.3 = (f32[16,128]{1,0:T(8,128)S(1)}, f32[16,128]{1,0:T(8,128)}, u32[]{:S(2)}) copy-start(f32[16,128]{1,0:T(8,128)} %wmom_ref.3) | copy-start | bytes 24580
  0.7 11.1 %copy-start.1 = (f32[128,128]{1,0:T(8,128)S(1)}, f32[128,128]{1,0:T(8,128)}, u32[]{:S(2)}) copy-start(f32[128,128]{1,0:T(8,128)} %pmom_ref.3) | copy-start | bytes 196612
  0.7 21.5 %copy-start.5 = (f32[16,8,256]{2,1,0:T(8,128)S(1)}, f32[16,8,256]{2,1,0:T(8,128)}, u32[]{:S(2)}) copy-start(f32[16,8,256]{2,1,0:T(8,128)} %param.13) | copy-start | bytes 393220
  0.7 21.6 %copy-start.4 = (f32[16]{0:T(128)S(1)}, f32[16]{0:T(128)}, u32[]{:S(2)}) copy-start(f32[16]{0:T(128)} %tau_ref.5) | copy-start | bytes 196
  1.6 8.1 %collective-permute-start = (f32[144,128]{1,0:T(8,128)S(1)}, f32[144,128]{1,0:T(8,128)S(1)}, u32[]{:S(2)}, u32[]{:S(2)}) collective-permute-start(f32[144,128]{1,0:T(8,128)S(1)} %pad_add_fusion.pack_ref.own_ref), channel_id=1, source_target_pairs={{0,1},{1,0},{2,3},{3,2},{4,6},{5,7},{6,4},{7,5},{8,9},{9,8},{10,11... | collective-permute-start | bytes 221192 | tf_op jit(solution)/shard_map/ppermute | solution.py:243
  4.6 5.8 %collective-permute-start.1 = (f32[72,128]{1,0:T(8,128)S(1)}, f32[72,128]{1,0:T(8,128)S(1)}, u32[]{:S(2)}, u32[]{:S(2)}) collective-permute-start(f32[72,128]{1,0:T(8,128)S(1)} %constant_dynamic-slice_fusion), channel_id=1, source_target_pairs={{0,3},{1,2},{2,1},{3,0},{4,7},{5,6},{6,5},{7,4},{8,11},{9,10},{10,... | collective-permute-start | bytes 110600 | tf_op jit(solution)/shard_map/ppermute | solution.py:212
  10.4 1.3 %collective-permute-start.2 = (f32[216,128]{1,0:T(8,128)S(1)}, f32[216,128]{1,0:T(8,128)S(1)}, u32[]{:S(2)}, u32[]{:S(2)}) collective-permute-start(f32[216,128]{1,0:T(8,128)S(1)} %constant_dynamic-update-slice_fusion.got_ref), channel_id=1, source_target_pairs={{0,4},{4,0},{8,12},{12,8},{16,20},{20,16},{24,28},{28,24},{1,5},{5... | collective-permute-start | bytes 331784 | tf_op jit(solution)/shard_map/ppermute | solution.py:212
  17.2 1.4 %collective-permute-start.3 = (f32[4,72,128]{2,1,0:T(8,128)S(1)}, f32[4,72,128]{2,1,0:T(8,128)S(1)}, u32[]{:S(2)}, u32[]{:S(2)}) collective-permute-start(f32[4,72,128]{2,1,0:T(8,128)S(1)} %get-tuple-element.58), channel_id=1, source_target_pairs={{0,4},{4,0},{8,12},{12,8},{16,20},{20,16},{24,28},{28,24},{1,5},{5... | collective-permute-start | bytes 442376 | tf_op jit(solution)/shard_map/ppermute | solution.py:212
  18.6 5.0 %collective-permute-start.4 = (f32[72,128]{1,0:T(8,128)S(1)}, f32[72,128]{1,0:T(8,128)S(1)}, u32[]{:S(2)}, u32[]{:S(2)}) collective-permute-start(f32[72,128]{1,0:T(8,128)S(1)} %get-tuple-element.97), channel_id=1, source_target_pairs={{0,8},{4,12},{8,0},{12,4},{16,24},{20,28},{24,16},{28,20},{1,9},{5... | collective-permute-start | bytes 110600 | tf_op jit(solution)/shard_map/ppermute | solution.py:212
  20.2 4.9 %collective-permute-start.6 = (f32[72,128]{1,0:T(8,128)S(1)}, f32[72,128]{1,0:T(8,128)S(1)}, u32[]{:S(2)}, u32[]{:S(2)}) collective-permute-start(f32[72,128]{1,0:T(8,128)S(1)} %get-tuple-element.98), channel_id=1, source_target_pairs={{0,24},{4,28},{8,16},{12,20},{16,8},{20,12},{24,0},{28,4},{1,25},{... | collective-permute-start | bytes 110600 | tf_op jit(solution)/shard_map/ppermute | solution.py:212
  21.7 4.0 %collective-permute-start.5 = (f32[72,128]{1,0:T(8,128)S(1)}, f32[72,128]{1,0:T(8,128)S(1)}, u32[]{:S(2)}, u32[]{:S(2)}) collective-permute-start(f32[72,128]{1,0:T(8,128)S(1)} %get-tuple-element.99), channel_id=1, source_target_pairs={{0,16},{4,20},{8,24},{12,28},{16,0},{20,4},{24,8},{28,12},{1,17},{... | collective-permute-start | bytes 110600 | tf_op jit(solution)/shard_map/ppermute | solution.py:212
  25.7 8.5 %collective-permute-start.7 = (f32[144,128]{1,0:T(8,128)S(1)}, f32[144,128]{1,0:T(8,128)S(1)}, u32[]{:S(2)}, u32[]{:S(2)}) collective-permute-start(f32[144,128]{1,0:T(8,128)S(1)} %get-tuple-element.105), channel_id=1, source_target_pairs={{0,1},{1,0},{2,3},{3,2},{4,5},{5,4},{6,7},{7,6},{8,9},{9,8},{10,11... | collective-permute-start | bytes 221192 | tf_op jit(solution)/shard_map/ppermute | solution.py:212
  25.8 8.3 %collective-permute-start.9 = (f32[144,128]{1,0:T(8,128)S(1)}, f32[144,128]{1,0:T(8,128)S(1)}, u32[]{:S(2)}, u32[]{:S(2)}) collective-permute-start(f32[144,128]{1,0:T(8,128)S(1)} %get-tuple-element.106), channel_id=1, source_target_pairs={{0,3},{1,2},{2,1},{3,0},{4,7},{5,6},{6,5},{7,4},{8,11},{9,10},{10,... | collective-permute-start | bytes 221192 | tf_op jit(solution)/shard_map/ppermute | solution.py:212
  28.9 5.2 %collective-permute-start.8 = (f32[72,128]{1,0:T(8,128)S(1)}, f32[72,128]{1,0:T(8,128)S(1)}, u32[]{:S(2)}, u32[]{:S(2)}) collective-permute-start(f32[72,128]{1,0:T(8,128)S(1)} %fusion.7), channel_id=1, source_target_pairs={{0,2},{1,3},{2,0},{3,1},{4,6},{5,7},{6,4},{7,5},{8,10},{9,11},{10,... | collective-permute-start | bytes 110600 | tf_op jit(solution)/shard_map/ppermute | solution.py:212
  34.2 4.4 %collective-permute-start.11 = (f32[144,128]{1,0:T(8,128)S(1)}, f32[144,128]{1,0:T(8,128)S(1)}, u32[]{:S(2)}, u32[]{:S(2)}) collective-permute-start(f32[144,128]{1,0:T(8,128)S(1)} %get-tuple-element.104), channel_id=1, source_target_pairs={{0,16},{4,20},{8,24},{12,28},{16,0},{20,4},{24,8},{28,12},{1,17},{... | collective-permute-start | bytes 221192 | tf_op jit(solution)/shard_map/ppermute | solution.py:212
  35.2 4.4 %collective-permute-start.10 = (f32[144,128]{1,0:T(8,128)S(1)}, f32[144,128]{1,0:T(8,128)S(1)}, u32[]{:S(2)}, u32[]{:S(2)}) collective-permute-start(f32[144,128]{1,0:T(8,128)S(1)} %get-tuple-element.104), channel_id=1, source_target_pairs={{0,8},{4,12},{8,0},{12,4},{16,24},{20,28},{24,16},{28,20},{1,9},{5... | collective-permute-start | bytes 221192 | tf_op jit(solution)/shard_map/ppermute | solution.py:212
  36.3 5.3 %collective-permute-start.12 = (f32[144,128]{1,0:T(8,128)S(1)}, f32[144,128]{1,0:T(8,128)S(1)}, u32[]{:S(2)}, u32[]{:S(2)}) collective-permute-start(f32[144,128]{1,0:T(8,128)S(1)} %get-tuple-element.104), channel_id=1, source_target_pairs={{0,24},{4,28},{8,16},{12,20},{16,8},{20,12},{24,0},{28,4},{1,25},{... | collective-permute-start | bytes 221192 | tf_op jit(solution)/shard_map/ppermute | solution.py:212
  41.5 1.6 %collective-permute-start.13 = (f32[4,144,128]{2,1,0:T(8,128)S(1)}, f32[4,144,128]{2,1,0:T(8,128)S(1)}, u32[]{:S(2)}, u32[]{:S(2)}) collective-permute-start(f32[4,144,128]{2,1,0:T(8,128)S(1)} %pad_maximum_fusion.near_ref), channel_id=1, source_target_pairs={{0,4},{4,0},{8,12},{12,8},{16,20},{20,16},{24,28},{28,24},{1,5},{5... | collective-permute-start | bytes 884744 | tf_op jit(solution)/shard_map/ppermute | solution.py:212
  48.5 1.4 %collective-permute-start.14 = (f32[4,72,128]{2,1,0:T(8,128)S(1)}, f32[4,72,128]{2,1,0:T(8,128)S(1)}, u32[]{:S(2)}, u32[]{:S(2)}) collective-permute-start(f32[4,72,128]{2,1,0:T(8,128)S(1)} %get-tuple-element.63), channel_id=1, source_target_pairs={{0,4},{4,0},{8,12},{12,8},{16,20},{20,16},{24,28},{28,24},{1,5},{5... | collective-permute-start | bytes 442376 | tf_op jit(solution)/shard_map/ppermute | solution.py:212
  50.0 6.2 %collective-permute-start.15 = (f32[72,128]{1,0:T(8,128)S(1)}, f32[72,128]{1,0:T(8,128)S(1)}, u32[]{:S(2)}, u32[]{:S(2)}) collective-permute-start(f32[72,128]{1,0:T(8,128)S(1)} %get-tuple-element.94), channel_id=1, source_target_pairs={{0,8},{4,12},{8,0},{12,4},{16,24},{20,28},{24,16},{28,20},{1,9},{5... | collective-permute-start | bytes 110600 | tf_op jit(solution)/shard_map/ppermute | solution.py:212
  51.0 5.2 %collective-permute-start.17 = (f32[72,128]{1,0:T(8,128)S(1)}, f32[72,128]{1,0:T(8,128)S(1)}, u32[]{:S(2)}, u32[]{:S(2)}) collective-permute-start(f32[72,128]{1,0:T(8,128)S(1)} %get-tuple-element.95), channel_id=1, source_target_pairs={{0,24},{4,28},{8,16},{12,20},{16,8},{20,12},{24,0},{28,4},{1,25},{... | collective-permute-start | bytes 110600 | tf_op jit(solution)/shard_map/ppermute | solution.py:212
  53.1 4.0 %collective-permute-start.16 = (f32[72,128]{1,0:T(8,128)S(1)}, f32[72,128]{1,0:T(8,128)S(1)}, u32[]{:S(2)}, u32[]{:S(2)}) collective-permute-start(f32[72,128]{1,0:T(8,128)S(1)} %get-tuple-element.96), channel_id=1, source_target_pairs={{0,16},{4,20},{8,24},{12,28},{16,0},{20,4},{24,8},{28,12},{1,17},{... | collective-permute-start | bytes 110600 | tf_op jit(solution)/shard_map/ppermute | solution.py:212
  57.1 5.9 %collective-permute-start.20 = (f32[80,128]{1,0:T(8,128)S(1)}, f32[80,128]{1,0:T(8,128)S(1)}, u32[]{:S(2)}, u32[]{:S(2)}) collective-permute-start(f32[80,128]{1,0:T(8,128)S(1)} %constant_dynamic-update-slice_fusion.2), channel_id=1, source_target_pairs={{0,3},{1,2},{2,1},{3,0},{4,7},{5,6},{6,5},{7,4},{8,11},{9,10},{10,... | collective-permute-start | bytes 122888 | tf_op jit(solution)/shard_map/ppermute | solution.py:212
  58.7 5.2 %collective-permute-start.19 = (f32[80,128]{1,0:T(8,128)S(1)}, f32[80,128]{1,0:T(8,128)S(1)}, u32[]{:S(2)}, u32[]{:S(2)}) collective-permute-start(f32[80,128]{1,0:T(8,128)S(1)} %constant_dynamic-update-slice_fusion.2), channel_id=1, source_target_pairs={{0,2},{1,3},{2,0},{3,1},{4,6},{5,7},{6,4},{7,5},{8,10},{9,11},{10,... | collective-permute-start | bytes 122888 | tf_op jit(solution)/shard_map/ppermute | solution.py:212
  58.8 5.1 %collective-permute-start.18 = (f32[80,128]{1,0:T(8,128)S(1)}, f32[80,128]{1,0:T(8,128)S(1)}, u32[]{:S(2)}, u32[]{:S(2)}) collective-permute-start(f32[80,128]{1,0:T(8,128)S(1)} %constant_dynamic-update-slice_fusion.2), channel_id=1, source_target_pairs={{0,1},{1,0},{2,3},{3,2},{4,5},{5,4},{6,7},{7,6},{8,9},{9,8},{10,11... | collective-permute-start | bytes 122888 | tf_op jit(solution)/shard_map/ppermute | solution.py:212
  63.9 5.0 %collective-permute-start.23 = (f32[80,128]{1,0:T(8,128)S(1)}, f32[80,128]{1,0:T(8,128)S(1)}, u32[]{:S(2)}, u32[]{:S(2)}) collective-permute-start(f32[80,128]{1,0:T(8,128)S(1)} %add_add_fusion), channel_id=1, source_target_pairs={{0,24},{4,28},{8,16},{12,20},{16,8},{20,12},{24,0},{28,4},{1,25},{... | collective-permute-start | bytes 122888 | tf_op jit(solution)/shard_map/ppermute | solution.py:212
  65.3 4.0 %collective-permute-start.22 = (f32[80,128]{1,0:T(8,128)S(1)}, f32[80,128]{1,0:T(8,128)S(1)}, u32[]{:S(2)}, u32[]{:S(2)}) collective-permute-start(f32[80,128]{1,0:T(8,128)S(1)} %add_add_fusion), channel_id=1, source_target_pairs={{0,16},{4,20},{8,24},{12,28},{16,0},{20,4},{24,8},{28,12},{1,17},{... | collective-permute-start | bytes 122888 | tf_op jit(solution)/shard_map/ppermute | solution.py:212
  66.0 4.0 %collective-permute-start.21 = (f32[80,128]{1,0:T(8,128)S(1)}, f32[80,128]{1,0:T(8,128)S(1)}, u32[]{:S(2)}, u32[]{:S(2)}) collective-permute-start(f32[80,128]{1,0:T(8,128)S(1)} %add_add_fusion), channel_id=1, source_target_pairs={{0,8},{4,12},{8,0},{12,4},{16,24},{20,28},{24,16},{28,20},{1,9},{5... | collective-permute-start | bytes 122888 | tf_op jit(solution)/shard_map/ppermute | solution.py:212
  70.0 1.6 %collective-permute-start.24 = (f32[4,80,128]{2,1,0:T(8,128)S(1)}, f32[4,80,128]{2,1,0:T(8,128)S(1)}, u32[]{:S(2)}, u32[]{:S(2)}) collective-permute-start(f32[4,80,128]{2,1,0:T(8,128)S(1)} %pad_maximum_fusion.1.near_ref), channel_id=1, source_target_pairs={{0,4},{4,0},{8,12},{12,8},{16,20},{20,16},{24,28},{28,24},{1,5},{5... | collective-permute-start | bytes 491528 | tf_op jit(solution)/shard_map/ppermute | solution.py:212

commit v6 on v5

--- a/solution.py
+++ b/solution.py
@@ -212,28 +212,36 @@
     return lax.ppermute(values, axis, [(i, i ^ flip) for i in range(count)])
 
 
-def all_sum(keep, send, near_edge=None, far_edge=None, late=None, beside=()):
+def all_sum(keep, send, near_edge, far_edge):
     pairs, rows, _ = keep.shape
     chunks = keep + partner(send, "cells", 1)
     total = chunks[0]
     for part in [partner(chunks[k], "cells", 2 * k) for k in range(1, pairs)]:
         total = total + part
+    first = partner(jnp.concatenate([total, near_edge], axis=0), "comp", 1)
+    second = partner(total, "comp", 2)
+    third = partner(jnp.concatenate([total, far_edge], axis=0), "comp", 3)
+    total = jnp.concatenate([total + first[:rows] + second + third[:rows], third[rows:]], axis=0)
+    near = jnp.stack([total] + [partner(total, "cells", 2 * k) for k in range(1, pairs)])
+    return near, partner(near, "cells", 1), first[rows:]
+
+
+def group_sum(keep, send, energy, beside):
+    ring, rows, _ = keep.shape
+    pairs = lax.axis_size("cells") // 2
+    halves = keep + partner(send, "cells", 1)
+    total = halves[0]
+    for part in [partner(halves[k], "comp", k) for k in range(1, ring)]:
+        total = total + part
     total, beside = lax.optimization_barrier((total, beside))
-    if late is not None:
-        total = jnp.concatenate([total, late], axis=0)
-    if near_edge is None:
-        parts = [partner(total, "comp", k) for k in range(1, lax.axis_size("comp"))]
-        near_got = None
-        for part in parts:
-            total = total + part
-    else:
-        first = partner(jnp.concatenate([total, near_edge], axis=0), "comp", 1)
-        second = partner(total, "comp", 2)
-        third = partner(jnp.concatenate([total, far_edge], axis=0), "comp", 3)
-        near_got = first[rows:]
-        total = jnp.concatenate([total + first[:rows] + second + third[:rows], third[rows:]], axis=0)
-    near = jnp.stack([total] + [partner(total, "cells", 2 * k) for k in range(1, pairs)])
-    return near, partner(near, "cells", 1), near_got, beside
+    total = jnp.concatenate([total, energy], axis=0)
+    for part in [partner(total, "cells", 2 * k) for k in range(1, pairs)]:
+        total = total + part
+    other = partner(total, "cells", 1)
+    upper = lax.axis_index("cells") % 2 == 1
+    low = jnp.where(upper, other, total)[:rows]
+    high = jnp.where(upper, total, other)[:rows]
+    return jnp.concatenate([low, high], axis=0), total[rows:] + other[rows:], beside
 
 
 def gather_params(pack, cells_rank):
@@ -592,16 +600,23 @@
     for b in range(cols // LANES):
         dens = jnp.where(sub == b, -log_dens[:, b * LANES : (b + 1) * LANES], dens)
     stats_ref[8:16, :] = dens
-    if out.shape[0] > nparam:
-        out[nparam:, :] = jnp.zeros((out.shape[0] - nparam, LANES), F32)
-    out[0:nparam, :] = 0.5 * STEP_PARAM * (grad0_ref[...] + grad[...])
+    out[...] = 0.5 * STEP_PARAM * (grad0_ref[...] + grad[...])
     owner = cells_rank == 0
     old_prof, old_load = own_ref[0:mine, :], own_ref[mine : mine + nfac, :]
     base_prof = pmom_ref[...] - 0.5 * STEP_PARAM * 0.25 * (old_prof + new_prof)
     base_load = wmom_ref[...] - 0.5 * STEP_PARAM * (old_load + new_load)
     out[pl.ds(pl.multiple_of(comp_rank * mine, mine), mine), :] += jnp.where(owner, base_prof, 0.0)
     out[pl.ds(pl.multiple_of(ncomp + comp_rank * nfac, nfac), nfac), :] += jnp.where(owner, base_load, 0.0)
-    spread_chunks(out, keep_ref, send_ref, cells_rank)
+    ring, rows, _ = keep_ref.shape
+    upper = cells_rank % 2 == 1
+    for k in range(ring):
+        group = comp_rank ^ k
+        start = pl.multiple_of(group * mine, mine)
+        low = out[pl.ds(start, rows), :]
+        tail = out[pl.ds(pl.multiple_of(ncomp + group * nfac, nfac), nfac), :]
+        high = jnp.concatenate([out[pl.ds(start + rows, mine - rows), :], tail], axis=0)
+        keep_ref[k] = jnp.where(upper, high, low)
+        send_ref[k] = jnp.where(upper, low, high)
 
 
 def second_field(
@@ -634,18 +649,12 @@
     energy_ref[...] = tiles_sum
 
 
-def last_kernel(ncomp, nparam, chunk, cells, rank_ref, near_ref, far_ref, prof_ref, mixing_ref, ham_ref, flat):
-    cells_rank, comp_rank = rank_ref[0], rank_ref[1]
-    mine, nfac = prof_ref.shape[0], mixing_ref.shape[0]
-    gather_chunks(flat, near_ref, far_ref, cells_rank, chunk)
-    prof_ref[...] = flat[pl.ds(pl.multiple_of(comp_rank * mine, mine), mine), :]
-    mixing_ref[...] = flat[pl.ds(pl.multiple_of(ncomp + comp_rank * nfac, nfac), nfac), :]
-    momenta = flat[0:nparam, :]
-    total = jnp.sum(0.5 * (momenta * momenta).reshape(nparam // 8, 8, LANES), axis=0)
-    for source in (near_ref, far_ref):
-        total = total + jnp.sum(source[:, chunk:, :], axis=0)
+def last_kernel(cells, *refs):
+    total = refs[0][...]
+    for part in refs[1:-1]:
+        total = total + part[...]
     total = jnp.sum(jnp.sum(total, axis=0, keepdims=True), axis=1, keepdims=True)
-    ham_ref[...] = total / cells
+    refs[-1][...] = total / cells
 
 
 def fast_device(
@@ -687,6 +696,7 @@
     ]
     field_shape = shape(share, nfac, cols)
     chunk_shape = shape(pairs, chunk, LANES)
+    half_shape = shape(ring, (mine + nfac) // 2, LANES)
     gap_shapes = [jax.ShapeDtypeStruct((ncomp, 2 * cols), BF16)] * share
     load_shape = jax.ShapeDtypeStruct((2 * nfac, ncomp), BF16)
     field_flops = 2 * 2 * nfac * ncomp * 2 * cols * share
@@ -720,7 +730,7 @@
     part_field, half, near_edge, far_edge = call(
         first_field, "first_field", 2, 4 + share, [field_shape, field_shape, edge_shape, edge_shape], prior, field_cost
     )(ranks, field_tau, field_rows, mom_rows, land_mask, load, *gaps)
-    near, far, got_edge, _ = all_sum(keep, send, near_edge, far_edge)
+    near, far, got_edge = all_sum(keep, send, near_edge, far_edge)
     second = call(
         functools.partial(second_kernel, ncomp, chunk, ring, tiles),
         "second_gradient",
@@ -732,10 +742,10 @@
             field_shape,
             shape(mine + nfac, ncat),
             shape(16, LANES),
-            chunk_shape,
-            chunk_shape,
+            half_shape,
+            half_shape,
         ],
-        work + [pltpu.VMEM((tiles * chunk, LANES), F32), pltpu.VMEM((nparam, LANES), F32)],
+        work + [pltpu.VMEM((nparam, LANES), F32)] * 2,
     )
     *gaps, load, new_field, new_params, stats, keep, send = second(
         ranks, field_tau, count_rows, part_field, land_mask, log_exposure, profile_mom, mixing_mom, field_rows, pack, near,
@@ -745,20 +755,16 @@
         functools.partial(second_field, chunk, ring, tiles), "second_field", 2, 9 + share, [field_shape, shape(8, LANES)], prior, field_cost
     )(ranks, field_tau, new_field, half, field_rows, land_mask, load, stats, near, far, got_edge, *gaps)
     done = (new_field.swapaxes(0, 1), new_params[:mine], new_params[mine:], new_mom.swapaxes(0, 1))
-    near, far, _, done = all_sum(keep, send, late=energy, beside=done)
-    final = call(
-        functools.partial(last_kernel, ncomp, nparam, chunk, tile_rows * cols * tiles),
-        "momenta",
-        1,
-        2,
-        [shape(mine, ncat), shape(nfac, mine), shape(1, 1)],
-        [pltpu.VMEM((tiles * chunk, LANES), F32)],
-    )
-    new_profile_mom, new_mixing_mom, hamiltonian = final(ranks, near, far)
+    momenta, energy, done = group_sum(keep, send, energy, done)
+    kinetic = jnp.sum(0.5 * (momenta * momenta).reshape(-1, 8, LANES), axis=0)
+    total = energy + kinetic
+    parts = [total] + [partner(total, "comp", k) for k in range(1, ring)]
+    cells = tile_rows * cols * tiles
+    (hamiltonian,) = call(functools.partial(last_kernel, cells), "total_energy", 0, ring, [shape(1, 1)], [])(*parts)
     return (
         *done,
-        new_profile_mom,
-        new_mixing_mom,
+        momenta[:mine],
+        momenta[mine:],
         hamiltonian.reshape(()),
     )
 
@@ -773,7 +779,7 @@
     mine, ncat = profile.shape
     tiles, ring = lax.axis_size("cells"), lax.axis_size("comp")
     fits = mine == LANES and ncat == LANES and nfac % 16 == 0 and 6 * nfac + EXTRA <= LANES
-    fits = fits and share % 8 == 0 and cols % LANES == 0 and cols <= 8 * LANES
+    fits = fits and (mine + nfac) % 16 == 0 and mine >= nfac and share % 8 == 0 and cols % LANES == 0 and cols <= 8 * LANES
     fits = fits and power_of_two(tiles) and tiles > 1 and ring == 4
     return fast_device(*args) if fits else plain_device(*args)
 

time: 73.1 us -> 72.5 us (level)
  waiting for transfers between devices: 22.4 us -> 21.3 us
  Pallas kernels: 14.8 us -> 14 us
    ppermute x24, waiting for transfers between devices: 22.4 us -> 21.3 us  [partner(): return lax.ppermute(values, axis, [(i, i ^ flip) for i in range(count)])]
  transfers between devices with their start and end apart: 25 -> 25, of which waited for: 17 -> 16; matrix products, arithmetic and copies ran while one was open for 7% -> 9% of each run, Pallas kernels for 4% -> 4%
where the time goes in v6:
time: 72.5 us; the launch traced here: 72.3 us
  starting transfers between devices  28.3 us (39%)
  waiting for transfers between devices  21.3 us (29%)
  Pallas kernels  14 us (19%)
  local copies, waits for them, and re-layouts  5.66 us (8%)
  other arithmetic  2.11 us (3%)
  between operations  0.91 us (1%)
    ppermute x24, starting transfers between devices, partner(): return lax.ppermute(values, axis, [(i, i ^ flip) for i in range(count)])  25.3 us
    ppermute x24, waiting for transfers between devices, partner(): return lax.ppermute(values, axis, [(i, i ^ flip) for i in range(count)])  21.3 us
    pallas_call x1, Pallas kernels, fast_device(): first(ranks, count_rows, field_rows, land_mask, log_exposure, profile_mom...  5.39 us
    pallas_call x1, Pallas kernels, fast_device(): second(ranks, field_tau, count_rows, part_field, land_mask, log_exposure,...  5.34 us
    ppermute x1, starting transfers between devices, gather_params(): one = lax.ppermute(pack, ('cells', 'comp'), spread)  3.02 us
    unnamed x18, local copies, waits for them, and re-layouts  2.5 us
  transfers between devices with their start and end apart: 25, of which 16 were waited for; matrix products, arithmetic and copies ran while one was open for 9% of the time, Pallas kernels for 4%

profile of v6, /device:TPU:0, one launch (start us, length us, event | category | flops | bytes accessed | tf_op | source)
XLA Modules:
  0.0 72.3 jit_solution(11477984271740163312)
XLA Ops:
  0.7 0.9 %pad_add_fusion.pack_ref.own_ref = f32[144,128]{1,0:T(8,128)S(1)} fusion(f32[16,128]{1,0:T(8,128)} %param.12, f32[128,128]{1,0:T(8,128)} %param.11), kind=kLoop, calls=%fused_computation.15 | loop fusion | flops 18432 | bytes 147456 | tf_op jit(solution)/shard_map/add | solution.py:677
  1.6 3.0 %collective-permute-start = (f32[144,128]{1,0:T(8,128)S(1)}, f32[144,128]{1,0:T(8,128)S(1)}, u32[]{:S(2)}, u32[]{:S(2)}) collective-permute-start(f32[144,128]{1,0:T(8,128)S(1)} %pad_add_fusion.pack_ref.own_ref), channel_id=1, source_target_pairs={{0,1},{1,0},{2,3},{3,2},{4,6},{5,7},{6,4},{7,5},{8,9},{9,8},{10,11... | collective-permute-start | bytes 221192 | tf_op jit(solution)/shard_map/ppermute | solution.py:251
  4.6 2.5 %collective-permute-start.1 = (f32[72,128]{1,0:T(8,128)S(1)}, f32[72,128]{1,0:T(8,128)S(1)}, u32[]{:S(2)}, u32[]{:S(2)}) collective-permute-start(f32[72,128]{1,0:T(8,128)S(1)} %constant_dynamic-slice_fusion), channel_id=1, source_target_pairs={{0,3},{1,2},{2,1},{3,0},{4,7},{5,6},{6,5},{7,4},{8,11},{9,10},{10,... | collective-permute-start | bytes 110600 | tf_op jit(solution)/shard_map/ppermute | solution.py:212
  7.1 1.3 %constant_dynamic-slice_fusion.1 = s32[128,8,256]{2,1,0:T(8,128)S(1)} fusion(s32[128,32,256]{2,1,0:T(8,128)} %param.17, s32[]{:T(128)S(6)} %select_n.27), kind=kLoop, calls=%fused_computation.45 | loop fusion | bytes 2097156 | tf_op jit(solution)/shard_map/dynamic_slice | solution.py:679
  8.7 1.0 %copy.29 = f32[16,8,256]{2,0,1:T(8,128)S(1)} copy(f32[16,8,256]{2,1,0:T(8,128)} %param.10) | data formatting | bytes 262144 | tf_op args[0]
  10.5 1.2 %collective-permute-done.2.others_ref = f32[216,128]{1,0:T(8,128)S(1)} collective-permute-done((f32[216,128]{1,0:T(8,128)S(1)}, f32[216,128]{1,0:T(8,128)S(1)}, u32[]{:S(2)}, u32[]{:S(2)}) %collective-permute-start.2) | collective-permute-done | bytes 110624 | tf_op jit(solution)/shard_map/ppermute | solution.py:212
  11.7 5.4 %first_gradient.1 = (bf16[512,512]{1,0:T(8,128)(2,1)S(1)}, bf16[512,512]{1,0:T(8,128)(2,1)S(1)}, bf16[512,512]{1,0:T(8,128)(2,1)S(1)}, bf16[512,512]{1,0:T(8,128...) custom-call(s32[2]{0:T(128)S(1)} %pad_add_fusion.1.rank_ref, ...), custom_call_target="tpu_custom_call" | custom-call | tf_op jit(solution)/shard_map/first_gradient/pallas_call | solution.py:726
  17.4 1.2 %collective-permute-done.3 = f32[4,72,128]{2,1,0:T(8,128)S(1)} collective-permute-done((f32[4,72,128]{2,1,0:T(8,128)S(1)}, f32[4,72,128]{2,1,0:T(8,128)S(1)}, u32[]{:S(2)}, u32[]{:S(2)}) %collective-permute-start.3) | collective-permute-done | bytes 147488 | tf_op jit(solution)/shard_map/ppermute | solution.py:212
  18.6 1.6 %collective-permute-start.4 = (f32[72,128]{1,0:T(8,128)S(1)}, f32[72,128]{1,0:T(8,128)S(1)}, u32[]{:S(2)}, u32[]{:S(2)}) collective-permute-start(f32[72,128]{1,0:T(8,128)S(1)} %get-tuple-element.91), channel_id=1, source_target_pairs={{0,8},{4,12},{8,0},{12,4},{16,24},{20,28},{24,16},{28,20},{1,9},{5... | collective-permute-start | bytes 110600 | tf_op jit(solution)/shard_map/ppermute | solution.py:212
  20.2 1.5 %collective-permute-start.6 = (f32[72,128]{1,0:T(8,128)S(1)}, f32[72,128]{1,0:T(8,128)S(1)}, u32[]{:S(2)}, u32[]{:S(2)}) collective-permute-start(f32[72,128]{1,0:T(8,128)S(1)} %get-tuple-element.92), channel_id=1, source_target_pairs={{0,24},{4,28},{8,16},{12,20},{16,8},{20,12},{24,0},{28,4},{1,25},{... | collective-permute-start | bytes 110600 | tf_op jit(solution)/shard_map/ppermute | solution.py:212
  22.2 1.4 %first_field.1 = (f32[8,16,256]{2,1,0:T(8,128)S(1)}, f32[8,16,256]{2,1,0:T(8,128)S(1)}, f32[72,128]{1,0:T(8,128)S(1)}, f32[72,128]{1,0:T(8,128)S(1)}) custom-call(s32[2]{0:T(128)S(1)} %pad_add_fusion.1.rank_ref, f32[16]{0:T(128)S(1)} %copy-done.4, f32[8,16,256]{2,1,0:T(8,128)S(1)} %bitcast.51, f32[8,16,256]{2,1,0:T(8,128)S(1)} %bitcast.55, ...), custom_call_target="tpu_custom_call" | custom-call | flops 134217728 | bytes 4194304 | tf_op jit(solution)/shard_map/first_field/pallas_call | solution.py:730
  23.6 1.4 %collective-permute-done.6 = f32[72,128]{1,0:T(8,128)S(1)} collective-permute-done((f32[72,128]{1,0:T(8,128)S(1)}, f32[72,128]{1,0:T(8,128)S(1)}, u32[]{:S(2)}, u32[]{:S(2)}) %collective-permute-start.6) | collective-permute-done | bytes 36896 | tf_op jit(solution)/shard_map/ppermute | solution.py:212
  25.8 3.1 %collective-permute-start.9 = (f32[144,128]{1,0:T(8,128)S(1)}, f32[144,128]{1,0:T(8,128)S(1)}, u32[]{:S(2)}, u32[]{:S(2)}) collective-permute-start(f32[144,128]{1,0:T(8,128)S(1)} %get-tuple-element.100), channel_id=1, source_target_pairs={{0,3},{1,2},{2,1},{3,0},{4,7},{5,6},{6,5},{7,4},{8,11},{9,10},{10,... | collective-permute-start | bytes 221192 | tf_op jit(solution)/shard_map/ppermute | solution.py:212
  29.2 4.9 %collective-permute-done.8 = f32[72,128]{1,0:T(8,128)S(1)} collective-permute-done((f32[72,128]{1,0:T(8,128)S(1)}, f32[72,128]{1,0:T(8,128)S(1)}, u32[]{:S(2)}, u32[]{:S(2)}) %collective-permute-start.8) | collective-permute-done | bytes 36896 | tf_op jit(solution)/shard_map/ppermute | solution.py:212
  34.2 1.0 %collective-permute-start.11 = (f32[144,128]{1,0:T(8,128)S(1)}, f32[144,128]{1,0:T(8,128)S(1)}, u32[]{:S(2)}, u32[]{:S(2)}) collective-permute-start(f32[144,128]{1,0:T(8,128)S(1)} %get-tuple-element.98), channel_id=1, source_target_pairs={{0,16},{4,20},{8,24},{12,28},{16,0},{20,4},{24,8},{28,12},{1,17},{... | collective-permute-start | bytes 221192 | tf_op jit(solution)/shard_map/ppermute | solution.py:212
  35.2 1.1 %collective-permute-start.10 = (f32[144,128]{1,0:T(8,128)S(1)}, f32[144,128]{1,0:T(8,128)S(1)}, u32[]{:S(2)}, u32[]{:S(2)}) collective-permute-start(f32[144,128]{1,0:T(8,128)S(1)} %get-tuple-element.98), channel_id=1, source_target_pairs={{0,8},{4,12},{8,0},{12,4},{16,24},{20,28},{24,16},{28,20},{1,9},{5... | collective-permute-start | bytes 221192 | tf_op jit(solution)/shard_map/ppermute | solution.py:212
  36.2 1.5 %collective-permute-start.12 = (f32[144,128]{1,0:T(8,128)S(1)}, f32[144,128]{1,0:T(8,128)S(1)}, u32[]{:S(2)}, u32[]{:S(2)}) collective-permute-start(f32[144,128]{1,0:T(8,128)S(1)} %get-tuple-element.98), channel_id=1, source_target_pairs={{0,24},{4,28},{8,16},{12,20},{16,8},{20,12},{24,0},{28,4},{1,25},{... | collective-permute-start | bytes 221192 | tf_op jit(solution)/shard_map/ppermute | solution.py:212
  38.6 0.9 %collective-permute-done.10 = f32[144,128]{1,0:T(8,128)S(1)} collective-permute-done((f32[144,128]{1,0:T(8,128)S(1)}, f32[144,128]{1,0:T(8,128)S(1)}, u32[]{:S(2)}, u32[]{:S(2)}) %collective-permute-start.10) | collective-permute-done | bytes 73760 | tf_op jit(solution)/shard_map/ppermute | solution.py:212
  39.5 2.0 %collective-permute-done.12 = f32[144,128]{1,0:T(8,128)S(1)} collective-permute-done((f32[144,128]{1,0:T(8,128)S(1)}, f32[144,128]{1,0:T(8,128)S(1)}, u32[]{:S(2)}, u32[]{:S(2)}) %collective-permute-start.12) | collective-permute-done | bytes 73760 | tf_op jit(solution)/shard_map/ppermute | solution.py:212
  41.6 1.6 %collective-permute-done.13.far_ref = f32[4,144,128]{2,1,0:T(8,128)S(1)} collective-permute-done((f32[4,144,128]{2,1,0:T(8,128)S(1)}, f32[4,144,128]{2,1,0:T(8,128)S(1)}, u32[]{:S(2)}, u32[]{:S(2)}) %collective-permute-start.13) | collective-permute-done | bytes 294944 | tf_op jit(solution)/shard_map/ppermute | solution.py:212
  43.2 5.3 %second_gradient.1 = (bf16[512,512]{1,0:T(8,128)(2,1)S(1)}, bf16[512,512]{1,0:T(8,128)(2,1)S(1)}, bf16[512,512]{1,0:T(8,128)(2,1)S(1)}, bf16[512,512]{1,0:T(8,12...) custom-call(s32[2]{0:T(128)S(1)} %pad_add_fusion.1.rank_ref, ...), custom_call_target="tpu_custom_call" | custom-call | tf_op jit(solution)/shard_map/second_gradient/pallas_call | solution.py:750
  48.7 1.2 %collective-permute-done.14 = f32[4,72,128]{2,1,0:T(8,128)S(1)} collective-permute-done((f32[4,72,128]{2,1,0:T(8,128)S(1)}, f32[4,72,128]{2,1,0:T(8,128)S(1)}, u32[]{:S(2)}, u32[]{:S(2)}) %collective-permute-start.14) | collective-permute-done | bytes 147488 | tf_op jit(solution)/shard_map/ppermute | solution.py:212
  50.3 1.8 %collective-permute-start.17 = (f32[72,128]{1,0:T(8,128)S(1)}, f32[72,128]{1,0:T(8,128)S(1)}, u32[]{:S(2)}, u32[]{:S(2)}) collective-permute-start(f32[72,128]{1,0:T(8,128)S(1)} %get-tuple-element.89), channel_id=1, source_target_pairs={{0,3},{1,2},{2,1},{3,0},{4,7},{5,6},{6,5},{7,4},{8,11},{9,10},{10,... | collective-permute-start | bytes 110600 | tf_op jit(solution)/shard_map/ppermute | solution.py:212
  52.1 1.5 %collective-permute-start.16 = (f32[72,128]{1,0:T(8,128)S(1)}, f32[72,128]{1,0:T(8,128)S(1)}, u32[]{:S(2)}, u32[]{:S(2)}) collective-permute-start(f32[72,128]{1,0:T(8,128)S(1)} %get-tuple-element.90), channel_id=1, source_target_pairs={{0,2},{1,3},{2,0},{3,1},{4,6},{5,7},{6,4},{7,5},{8,10},{9,11},{10,... | collective-permute-start | bytes 110600 | tf_op jit(solution)/shard_map/ppermute | solution.py:212
  54.8 1.4 %second_field.1 = (f32[8,16,256]{2,1,0:T(8,128)S(1)}, f32[8,128]{1,0:T(8,128)S(1)}) custom-call(s32[2]{0:T(128)S(1)} %pad_add_fusion.1.rank_ref, f32[16]{0:T(128)S(1)} %copy-done.4, f32[8,16,256]{2,1,0:T(8,128)S(1)} %get-tuple-element.61.new_ref, f32[8,16,256]{2,1,0:T(8,128)S(1)} %get-tuple-element.63.half_ref, f32[8,16,256]{2,1,0:T(8,128)S(1)} %bitcast.53, ...), custom_call_target="tpu_custom_call" | custom-call | flops 134217728 | bytes 4194304 | tf_op jit(solution)/shard_map/second_field/pallas_call | solution.py:754
  56.2 1.3 %collective-permute-done.16 = f32[72,128]{1,0:T(8,128)S(1)} collective-permute-done((f32[72,128]{1,0:T(8,128)S(1)}, f32[72,128]{1,0:T(8,128)S(1)}, u32[]{:S(2)}, u32[]{:S(2)}) %collective-permute-start.16) | collective-permute-done | bytes 36896 | tf_op jit(solution)/shard_map/ppermute | solution.py:212
  57.5 1.6 %collective-permute-start.20 = (f32[80,128]{1,0:T(8,128)S(1)}, f32[80,128]{1,0:T(8,128)S(1)}, u32[]{:S(2)}, u32[]{:S(2)}) collective-permute-start(f32[80,128]{1,0:T(8,128)S(1)} %constant_dynamic-update-slice_fusion.2), channel_id=1, source_target_pairs={{0,24},{4,28},{8,16},{12,20},{16,8},{20,12},{24,0},{28,4},{1,25},{... | collective-permute-start | bytes 122888 | tf_op jit(solution)/shard_map/ppermute | solution.py:212
  59.0 0.9 %collective-permute-start.19 = (f32[80,128]{1,0:T(8,128)S(1)}, f32[80,128]{1,0:T(8,128)S(1)}, u32[]{:S(2)}, u32[]{:S(2)}) collective-permute-start(f32[80,128]{1,0:T(8,128)S(1)} %constant_dynamic-update-slice_fusion.2), channel_id=1, source_target_pairs={{0,16},{4,20},{8,24},{12,28},{16,0},{20,4},{24,8},{28,12},{1,17},{... | collective-permute-start | bytes 122888 | tf_op jit(solution)/shard_map/ppermute | solution.py:212
  60.0 1.1 %collective-permute-start.18 = (f32[80,128]{1,0:T(8,128)S(1)}, f32[80,128]{1,0:T(8,128)S(1)}, u32[]{:S(2)}, u32[]{:S(2)}) collective-permute-start(f32[80,128]{1,0:T(8,128)S(1)} %constant_dynamic-update-slice_fusion.2), channel_id=1, source_target_pairs={{0,8},{4,12},{8,0},{12,4},{16,24},{20,28},{24,16},{28,20},{1,9},{5... | collective-permute-start | bytes 122888 | tf_op jit(solution)/shard_map/ppermute | solution.py:212
  61.0 1.9 %collective-permute-done.20 = f32[80,128]{1,0:T(8,128)S(1)} collective-permute-done((f32[80,128]{1,0:T(8,128)S(1)}, f32[80,128]{1,0:T(8,128)S(1)}, u32[]{:S(2)}, u32[]{:S(2)}) %collective-permute-start.20) | collective-permute-done | bytes 40992 | tf_op jit(solution)/shard_map/ppermute | solution.py:212
  65.6 1.6 %collective-permute-start.24 = (f32[8,128]{1,0:T(8,128)S(1)}, f32[8,128]{1,0:T(8,128)S(1)}, u32[]{:S(2)}, u32[]{:S(2)}) collective-permute-start(f32[8,128]{1,0:T(8,128)S(1)} %fusion.13.refs_0_), channel_id=1, source_target_pairs={{0,3},{1,2},{2,1},{3,0},{4,7},{5,6},{6,5},{7,4},{8,11},{9,10},{10,... | collective-permute-start | bytes 12296 | tf_op jit(solution)/shard_map/ppermute | solution.py:212
  67.4 2.7 %collective-permute-start.22 = (f32[8,128]{1,0:T(8,128)S(1)}, f32[8,128]{1,0:T(8,128)S(1)}, u32[]{:S(2)}, u32[]{:S(2)}) collective-permute-start(f32[8,128]{1,0:T(8,128)S(1)} %fusion.13.refs_0_), channel_id=1, source_target_pairs={{0,1},{1,0},{2,3},{3,2},{4,5},{5,4},{6,7},{7,6},{8,9},{9,8},{10,11... | collective-permute-start | bytes 12296 | tf_op jit(solution)/shard_map/ppermute | solution.py:212
  (68 shorter events, 10.8 us)
Async XLA Ops:
  0.6 11.1 %copy-start = (s32[32,256]{1,0:T(8,128)S(1)}, s32[32,256]{1,0:T(8,128)}, u32[]{:S(2)}) copy-start(s32[32,256]{1,0:T(8,128)} %land_ref.7) | copy-start | bytes 98308
  0.6 11.1 %copy-start.2 = (f32[32,256]{1,0:T(8,128)S(1)}, f32[32,256]{1,0:T(8,128)}, u32[]{:S(2)}) copy-start(f32[32,256]{1,0:T(8,128)} %logexp_ref.3) | copy-start | bytes 98308
  0.7 11.1 %copy-start.3 = (f32[16,128]{1,0:T(8,128)S(1)}, f32[16,128]{1,0:T(8,128)}, u32[]{:S(2)}) copy-start(f32[16,128]{1,0:T(8,128)} %wmom_ref.3) | copy-start | bytes 24580
  0.7 11.1 %copy-start.1 = (f32[128,128]{1,0:T(8,128)S(1)}, f32[128,128]{1,0:T(8,128)}, u32[]{:S(2)}) copy-start(f32[128,128]{1,0:T(8,128)} %pmom_ref.3) | copy-start | bytes 196612
  0.7 21.5 %copy-start.5 = (f32[16,8,256]{2,1,0:T(8,128)S(1)}, f32[16,8,256]{2,1,0:T(8,128)}, u32[]{:S(2)}) copy-start(f32[16,8,256]{2,1,0:T(8,128)} %param.13) | copy-start | bytes 393220
  0.7 21.5 %copy-start.4 = (f32[16]{0:T(128)S(1)}, f32[16]{0:T(128)}, u32[]{:S(2)}) copy-start(f32[16]{0:T(128)} %tau_ref.5) | copy-start | bytes 196
  1.6 8.1 %collective-permute-start = (f32[144,128]{1,0:T(8,128)S(1)}, f32[144,128]{1,0:T(8,128)S(1)}, u32[]{:S(2)}, u32[]{:S(2)}) collective-permute-start(f32[144,128]{1,0:T(8,128)S(1)} %pad_add_fusion.pack_ref.own_ref), channel_id=1, source_target_pairs={{0,1},{1,0},{2,3},{3,2},{4,6},{5,7},{6,4},{7,5},{8,9},{9,8},{10,11... | collective-permute-start | bytes 221192 | tf_op jit(solution)/shard_map/ppermute | solution.py:251
  4.6 5.8 %collective-permute-start.1 = (f32[72,128]{1,0:T(8,128)S(1)}, f32[72,128]{1,0:T(8,128)S(1)}, u32[]{:S(2)}, u32[]{:S(2)}) collective-permute-start(f32[72,128]{1,0:T(8,128)S(1)} %constant_dynamic-slice_fusion), channel_id=1, source_target_pairs={{0,3},{1,2},{2,1},{3,0},{4,7},{5,6},{6,5},{7,4},{8,11},{9,10},{10,... | collective-permute-start | bytes 110600 | tf_op jit(solution)/shard_map/ppermute | solution.py:212
  10.4 1.3 %collective-permute-start.2 = (f32[216,128]{1,0:T(8,128)S(1)}, f32[216,128]{1,0:T(8,128)S(1)}, u32[]{:S(2)}, u32[]{:S(2)}) collective-permute-start(f32[216,128]{1,0:T(8,128)S(1)} %constant_dynamic-update-slice_fusion.got_ref), channel_id=1, source_target_pairs={{0,4},{4,0},{8,12},{12,8},{16,20},{20,16},{24,28},{28,24},{1,5},{5... | collective-permute-start | bytes 331784 | tf_op jit(solution)/shard_map/ppermute | solution.py:212
  17.2 1.4 %collective-permute-start.3 = (f32[4,72,128]{2,1,0:T(8,128)S(1)}, f32[4,72,128]{2,1,0:T(8,128)S(1)}, u32[]{:S(2)}, u32[]{:S(2)}) collective-permute-start(f32[4,72,128]{2,1,0:T(8,128)S(1)} %get-tuple-element.55), channel_id=1, source_target_pairs={{0,4},{4,0},{8,12},{12,8},{16,20},{20,16},{24,28},{28,24},{1,5},{5... | collective-permute-start | bytes 442376 | tf_op jit(solution)/shard_map/ppermute | solution.py:212
  18.6 5.0 %collective-permute-start.4 = (f32[72,128]{1,0:T(8,128)S(1)}, f32[72,128]{1,0:T(8,128)S(1)}, u32[]{:S(2)}, u32[]{:S(2)}) collective-permute-start(f32[72,128]{1,0:T(8,128)S(1)} %get-tuple-element.91), channel_id=1, source_target_pairs={{0,8},{4,12},{8,0},{12,4},{16,24},{20,28},{24,16},{28,20},{1,9},{5... | collective-permute-start | bytes 110600 | tf_op jit(solution)/shard_map/ppermute | solution.py:212
  20.2 4.9 %collective-permute-start.6 = (f32[72,128]{1,0:T(8,128)S(1)}, f32[72,128]{1,0:T(8,128)S(1)}, u32[]{:S(2)}, u32[]{:S(2)}) collective-permute-start(f32[72,128]{1,0:T(8,128)S(1)} %get-tuple-element.92), channel_id=1, source_target_pairs={{0,24},{4,28},{8,16},{12,20},{16,8},{20,12},{24,0},{28,4},{1,25},{... | collective-permute-start | bytes 110600 | tf_op jit(solution)/shard_map/ppermute | solution.py:212
  21.7 4.0 %collective-permute-start.5 = (f32[72,128]{1,0:T(8,128)S(1)}, f32[72,128]{1,0:T(8,128)S(1)}, u32[]{:S(2)}, u32[]{:S(2)}) collective-permute-start(f32[72,128]{1,0:T(8,128)S(1)} %get-tuple-element.93), channel_id=1, source_target_pairs={{0,16},{4,20},{8,24},{12,28},{16,0},{20,4},{24,8},{28,12},{1,17},{... | collective-permute-start | bytes 110600 | tf_op jit(solution)/shard_map/ppermute | solution.py:212
  25.7 8.5 %collective-permute-start.7 = (f32[144,128]{1,0:T(8,128)S(1)}, f32[144,128]{1,0:T(8,128)S(1)}, u32[]{:S(2)}, u32[]{:S(2)}) collective-permute-start(f32[144,128]{1,0:T(8,128)S(1)} %get-tuple-element.99), channel_id=1, source_target_pairs={{0,1},{1,0},{2,3},{3,2},{4,5},{5,4},{6,7},{7,6},{8,9},{9,8},{10,11... | collective-permute-start | bytes 221192 | tf_op jit(solution)/shard_map/ppermute | solution.py:212
  25.8 8.4 %collective-permute-start.9 = (f32[144,128]{1,0:T(8,128)S(1)}, f32[144,128]{1,0:T(8,128)S(1)}, u32[]{:S(2)}, u32[]{:S(2)}) collective-permute-start(f32[144,128]{1,0:T(8,128)S(1)} %get-tuple-element.100), channel_id=1, source_target_pairs={{0,3},{1,2},{2,1},{3,0},{4,7},{5,6},{6,5},{7,4},{8,11},{9,10},{10,... | collective-permute-start | bytes 221192 | tf_op jit(solution)/shard_map/ppermute | solution.py:212
  28.9 5.2 %collective-permute-start.8 = (f32[72,128]{1,0:T(8,128)S(1)}, f32[72,128]{1,0:T(8,128)S(1)}, u32[]{:S(2)}, u32[]{:S(2)}) collective-permute-start(f32[72,128]{1,0:T(8,128)S(1)} %fusion.12), channel_id=1, source_target_pairs={{0,2},{1,3},{2,0},{3,1},{4,6},{5,7},{6,4},{7,5},{8,10},{9,11},{10,... | collective-permute-start | bytes 110600 | tf_op jit(solution)/shard_map/ppermute | solution.py:212
  34.2 4.4 %collective-permute-start.11 = (f32[144,128]{1,0:T(8,128)S(1)}, f32[144,128]{1,0:T(8,128)S(1)}, u32[]{:S(2)}, u32[]{:S(2)}) collective-permute-start(f32[144,128]{1,0:T(8,128)S(1)} %get-tuple-element.98), channel_id=1, source_target_pairs={{0,16},{4,20},{8,24},{12,28},{16,0},{20,4},{24,8},{28,12},{1,17},{... | collective-permute-start | bytes 221192 | tf_op jit(solution)/shard_map/ppermute | solution.py:212
  35.2 4.4 %collective-permute-start.10 = (f32[144,128]{1,0:T(8,128)S(1)}, f32[144,128]{1,0:T(8,128)S(1)}, u32[]{:S(2)}, u32[]{:S(2)}) collective-permute-start(f32[144,128]{1,0:T(8,128)S(1)} %get-tuple-element.98), channel_id=1, source_target_pairs={{0,8},{4,12},{8,0},{12,4},{16,24},{20,28},{24,16},{28,20},{1,9},{5... | collective-permute-start | bytes 221192 | tf_op jit(solution)/shard_map/ppermute | solution.py:212
  36.2 5.3 %collective-permute-start.12 = (f32[144,128]{1,0:T(8,128)S(1)}, f32[144,128]{1,0:T(8,128)S(1)}, u32[]{:S(2)}, u32[]{:S(2)}) collective-permute-start(f32[144,128]{1,0:T(8,128)S(1)} %get-tuple-element.98), channel_id=1, source_target_pairs={{0,24},{4,28},{8,16},{12,20},{16,8},{20,12},{24,0},{28,4},{1,25},{... | collective-permute-start | bytes 221192 | tf_op jit(solution)/shard_map/ppermute | solution.py:212
  41.5 1.6 %collective-permute-start.13 = (f32[4,144,128]{2,1,0:T(8,128)S(1)}, f32[4,144,128]{2,1,0:T(8,128)S(1)}, u32[]{:S(2)}, u32[]{:S(2)}) collective-permute-start(f32[4,144,128]{2,1,0:T(8,128)S(1)} %pad_maximum_fusion.near_ref), channel_id=1, source_target_pairs={{0,4},{4,0},{8,12},{12,8},{16,20},{20,16},{24,28},{28,24},{1,5},{5... | collective-permute-start | bytes 884744 | tf_op jit(solution)/shard_map/ppermute | solution.py:212
  48.5 1.4 %collective-permute-start.14 = (f32[4,72,128]{2,1,0:T(8,128)S(1)}, f32[4,72,128]{2,1,0:T(8,128)S(1)}, u32[]{:S(2)}, u32[]{:S(2)}) collective-permute-start(f32[4,72,128]{2,1,0:T(8,128)S(1)} %get-tuple-element.60), channel_id=1, source_target_pairs={{0,4},{4,0},{8,12},{12,8},{16,20},{20,16},{24,28},{28,24},{1,5},{5... | collective-permute-start | bytes 442376 | tf_op jit(solution)/shard_map/ppermute | solution.py:212
  50.0 6.2 %collective-permute-start.15 = (f32[72,128]{1,0:T(8,128)S(1)}, f32[72,128]{1,0:T(8,128)S(1)}, u32[]{:S(2)}, u32[]{:S(2)}) collective-permute-start(f32[72,128]{1,0:T(8,128)S(1)} %get-tuple-element.88), channel_id=1, source_target_pairs={{0,1},{1,0},{2,3},{3,2},{4,5},{5,4},{6,7},{7,6},{8,9},{9,8},{10,11... | collective-permute-start | bytes 110600 | tf_op jit(solution)/shard_map/ppermute | solution.py:212
  50.3 5.9 %collective-permute-start.17 = (f32[72,128]{1,0:T(8,128)S(1)}, f32[72,128]{1,0:T(8,128)S(1)}, u32[]{:S(2)}, u32[]{:S(2)}) collective-permute-start(f32[72,128]{1,0:T(8,128)S(1)} %get-tuple-element.89), channel_id=1, source_target_pairs={{0,3},{1,2},{2,1},{3,0},{4,7},{5,6},{6,5},{7,4},{8,11},{9,10},{10,... | collective-permute-start | bytes 110600 | tf_op jit(solution)/shard_map/ppermute | solution.py:212
  52.1 5.4 %collective-permute-start.16 = (f32[72,128]{1,0:T(8,128)S(1)}, f32[72,128]{1,0:T(8,128)S(1)}, u32[]{:S(2)}, u32[]{:S(2)}) collective-permute-start(f32[72,128]{1,0:T(8,128)S(1)} %get-tuple-element.90), channel_id=1, source_target_pairs={{0,2},{1,3},{2,0},{3,1},{4,6},{5,7},{6,4},{7,5},{8,10},{9,11},{10,... | collective-permute-start | bytes 110600 | tf_op jit(solution)/shard_map/ppermute | solution.py:212
  57.5 5.4 %collective-permute-start.20 = (f32[80,128]{1,0:T(8,128)S(1)}, f32[80,128]{1,0:T(8,128)S(1)}, u32[]{:S(2)}, u32[]{:S(2)}) collective-permute-start(f32[80,128]{1,0:T(8,128)S(1)} %constant_dynamic-update-slice_fusion.2), channel_id=1, source_target_pairs={{0,24},{4,28},{8,16},{12,20},{16,8},{20,12},{24,0},{28,4},{1,25},{... | collective-permute-start | bytes 122888 | tf_op jit(solution)/shard_map/ppermute | solution.py:212
  59.0 4.1 %collective-permute-start.19 = (f32[80,128]{1,0:T(8,128)S(1)}, f32[80,128]{1,0:T(8,128)S(1)}, u32[]{:S(2)}, u32[]{:S(2)}) collective-permute-start(f32[80,128]{1,0:T(8,128)S(1)} %constant_dynamic-update-slice_fusion.2), channel_id=1, source_target_pairs={{0,16},{4,20},{8,24},{12,28},{16,0},{20,4},{24,8},{28,12},{1,17},{... | collective-permute-start | bytes 122888 | tf_op jit(solution)/shard_map/ppermute | solution.py:212
  60.0 4.0 %collective-permute-start.18 = (f32[80,128]{1,0:T(8,128)S(1)}, f32[80,128]{1,0:T(8,128)S(1)}, u32[]{:S(2)}, u32[]{:S(2)}) collective-permute-start(f32[80,128]{1,0:T(8,128)S(1)} %constant_dynamic-update-slice_fusion.2), channel_id=1, source_target_pairs={{0,8},{4,12},{8,0},{12,4},{16,24},{20,28},{24,16},{28,20},{1,9},{5... | collective-permute-start | bytes 122888 | tf_op jit(solution)/shard_map/ppermute | solution.py:212
  64.0 1.6 %collective-permute-start.21 = (f32[80,128]{1,0:T(8,128)S(1)}, f32[80,128]{1,0:T(8,128)S(1)}, u32[]{:S(2)}, u32[]{:S(2)}) collective-permute-start(f32[80,128]{1,0:T(8,128)S(1)} %add_add_fusion), channel_id=1, source_target_pairs={{0,4},{4,0},{8,12},{12,8},{16,20},{20,16},{24,28},{28,24},{1,5},{5... | collective-permute-start | bytes 122888 | tf_op jit(solution)/shard_map/ppermute | solution.py:212
  65.6 5.7 %collective-permute-start.24 = (f32[8,128]{1,0:T(8,128)S(1)}, f32[8,128]{1,0:T(8,128)S(1)}, u32[]{:S(2)}, u32[]{:S(2)}) collective-permute-start(f32[8,128]{1,0:T(8,128)S(1)} %fusion.13.refs_0_), channel_id=1, source_target_pairs={{0,3},{1,2},{2,1},{3,0},{4,7},{5,6},{6,5},{7,4},{8,11},{9,10},{10,... | collective-permute-start | bytes 12296 | tf_op jit(solution)/shard_map/ppermute | solution.py:212
  67.2 4.5 %collective-permute-start.23 = (f32[8,128]{1,0:T(8,128)S(1)}, f32[8,128]{1,0:T(8,128)S(1)}, u32[]{:S(2)}, u32[]{:S(2)}) collective-permute-start(f32[8,128]{1,0:T(8,128)S(1)} %fusion.13.refs_0_), channel_id=1, source_target_pairs={{0,2},{1,3},{2,0},{3,1},{4,6},{5,7},{6,4},{7,5},{8,10},{9,11},{10,... | collective-permute-start | bytes 12296 | tf_op jit(solution)/shard_map/ppermute | solution.py:212
  67.4 4.3 %collective-permute-start.22 = (f32[8,128]{1,0:T(8,128)S(1)}, f32[8,128]{1,0:T(8,128)S(1)}, u32[]{:S(2)}, u32[]{:S(2)}) collective-permute-start(f32[8,128]{1,0:T(8,128)S(1)} %fusion.13.refs_0_), channel_id=1, source_target_pairs={{0,1},{1,0},{2,3},{3,2},{4,5},{5,4},{6,7},{7,6},{8,9},{9,8},{10,11... | collective-permute-start | bytes 12296 | tf_op jit(solution)/shard_map/ppermute | solution.py:212

commit v7 on v6

--- a/solution.py
+++ b/solution.py
@@ -214,6 +214,8 @@
 
 def all_sum(keep, send, near_edge, far_edge):
     pairs, rows, _ = keep.shape
+    comp_rank, cells_rank = lax.axis_index("comp"), lax.axis_index("cells")
+    chip, core = cells_rank // 2, cells_rank % 2
     chunks = keep + partner(send, "cells", 1)
     total = chunks[0]
     for part in [partner(chunks[k], "cells", 2 * k) for k in range(1, pairs)]:
@@ -221,9 +223,20 @@
     first = partner(jnp.concatenate([total, near_edge], axis=0), "comp", 1)
     second = partner(total, "comp", 2)
     third = partner(jnp.concatenate([total, far_edge], axis=0), "comp", 3)
-    total = jnp.concatenate([total + first[:rows] + second + third[:rows], third[rows:]], axis=0)
-    near = jnp.stack([total] + [partner(total, "cells", 2 * k) for k in range(1, pairs)])
-    return near, partner(near, "cells", 1), first[rows:]
+    total = total + first[:rows] + second + third[:rows]
+    crossed = third[rows:]
+    message = jnp.concatenate([total, crossed], axis=0)
+    parts = [partner(message if k & (k + 1) == 0 else total, "cells", 2 * k) for k in range(1, pairs)]
+    near = jnp.concatenate([total] + [part[:rows] for part in parts], axis=0)
+    neighbour = chip ^ jnp.where(core == 0, chip + 1, chip - 1)
+    passed = crossed
+    for k in range(1, pairs):
+        if k & (k + 1) == 0:
+            passed = jnp.where(neighbour == k, parts[k - 1][rows:], passed)
+    passed = jnp.where((comp_rank == 0) == (core == 0), crossed, passed)
+    far = partner(jnp.concatenate([near, passed], axis=0), "cells", 1)
+    at_end = (comp_rank == 0) | (comp_rank == lax.axis_size("comp") - 1)
+    return near, far, first[rows:], jnp.where(at_end, far[pairs * rows :], crossed)
 
 
 def group_sum(keep, send, energy, beside):
@@ -260,10 +273,10 @@
 
 
 def gather_chunks(flat_ref, near_ref, far_ref, cells_rank, rows):
-    for k in range(near_ref.shape[0]):
+    for k in range(near_ref.shape[0] // rows):
         for source, other in ((near_ref, False), (far_ref, True)):
             start = pl.multiple_of(chunk_index(cells_rank, k, other) * rows, 8)
-            flat_ref[pl.ds(start, rows), :] = source[k, 0:rows, :]
+            flat_ref[pl.ds(start, rows), :] = source[k * rows : (k + 1) * rows, :]
 
 
 def spread_chunks(flat_ref, keep_ref, send_ref, cells_rank):
@@ -460,15 +473,16 @@
     return log_dens
 
 
-def param_grads(flat_ref, acc_ref, accw_ref, grad_ref, ncomp, nfac):
+def param_grads(flat_ref, acc_ref, accw_ref, grad_ref, ncomp, nfac, flip=0):
     lane = lax.broadcasted_iota(jnp.int32, (LANES, LANES), 1)
     for q in range(ncomp // LANES):
         rows = pl.ds(q * LANES, LANES)
         lanes = slice(q * LANES, (q + 1) * LANES)
         mass = jnp.sum(jnp.where(lane < 3, acc_ref[rows, LANES : 2 * LANES], 0.0), axis=1, keepdims=True)
-        grad_ref[rows, :] = acc_ref[rows, 0:LANES] - jnp.exp(flat_ref[rows, :]) * mass
+        group = flip ^ q
+        grad_ref[pl.ds(pl.multiple_of(group * LANES, LANES), LANES), :] = acc_ref[rows, 0:LANES] - jnp.exp(flat_ref[rows, :]) * mass
         load = accw_ref[:, lanes]
-        grad_ref[pl.ds(ncomp + q * nfac, nfac), :] = load[0:nfac] + load[nfac : 2 * nfac] + load[2 * nfac : 3 * nfac]
+        grad_ref[pl.ds(pl.multiple_of(ncomp + group * nfac, nfac), nfac), :] = load[0:nfac] + load[nfac : 2 * nfac] + load[2 * nfac : 3 * nfac]
 
 
 def first_kernel(
@@ -476,28 +490,25 @@
 ):
     gaps, refs = refs[: counts_ref.shape[0]], refs[counts_ref.shape[0] :]
     load, grad_ref, keep_ref, send_ref, flat, left, mix, right, wide, score0, score1, logit0, logit1, *refs = refs
-    post0, post1, gap0, gap1, acc, accw, stage = refs
+    post0, post1, gap0, gap1, acc, accw = refs
     cells_rank, comp_rank = rank_ref[0], rank_ref[1]
     share, nfac, cols = field_ref.shape
     mine = pmom_ref.shape[0]
-    core = cells_rank % 2
     size = mine + nfac
-    for source, side in ((got_ref, core), (others_ref, 1 - core)):
-        stage[pl.ds(pl.multiple_of(side * (size // 2), 8), size // 2), :] = source[size:, :]
-    for source, group in (
-        (pack_ref, comp_rank),
-        (got_ref, comp_rank ^ (1 + core)),
-        (others_ref, comp_rank ^ (2 - core)),
-        (stage, comp_rank ^ 3),
-    ):
-        flat[pl.ds(pl.multiple_of(group * mine, mine), mine), :] = source[0:mine, :]
-        flat[pl.ds(pl.multiple_of(ncomp + group * nfac, nfac), nfac), :] = source[mine:size, :]
+    middle = size // 2
+    swap = cells_rank % 2 == 1
+    lower, upper = got_ref[...], others_ref[...]
+    one, two = jnp.where(swap, upper, lower), jnp.where(swap, lower, upper)
+    three = jnp.concatenate([one[size : size + middle], two[size : size + middle]], axis=0)
+    for k, source in enumerate((pack_ref[...], one, two, three)):
+        flat[k * mine : (k + 1) * mine, :] = source[0:mine]
+        flat[ncomp + k * nfac : ncomp + (k + 1) * nfac, :] = source[mine:size]
     here = pl.ds(pl.multiple_of(comp_rank * share, 8), share)
     land = land_ref[here, :].astype(F32)
     load_params(flat, left, mix, load, ncomp, nfac)
     load_cells(counts_ref, field_ref, logexp_ref[here, :], right, wide)
     all_rows(land, right, wide, left, mix, (score0, score1), (logit0, logit1), (post0, post1), (gap0, gap1), gaps, acc, accw)
-    param_grads(flat, acc, accw, grad_ref, ncomp, nfac)
+    param_grads(flat, acc, accw, grad_ref, ncomp, nfac, comp_rank)
     nparam = grad_ref.shape[0]
     if flat.shape[0] > nparam:
         flat[nparam:, :] = jnp.zeros((flat.shape[0] - nparam, LANES), F32)
@@ -536,15 +547,11 @@
         )
 
 
-def edge_terms(chunk, ring, tiles, rank_ref, tau, lands, old_ref, near_ref, far_ref, edge_ref):
+def edge_terms(ring, tiles, rank_ref, tau, lands, old_ref, edge_ref, other_ref):
     cells_rank, comp_rank = rank_ref[0], rank_ref[1]
     nfac, cols = tau.shape
-    source = jnp.where(comp_rank == 0, cells_rank - 1, jnp.where(comp_rank == ring - 1, cells_rank + 1, cells_rank))
-    source = jnp.clip(source, 0, tiles - 1)
-    slot = (source // 2) ^ (cells_rank // 2)
-    relay = jnp.where(source % 2 == cells_rank % 2, near_ref[slot, chunk:, :], far_ref[slot, chunk:, :])
     even = comp_rank % 2 == 0
-    direct = edge_ref[...]
+    direct, relay = edge_ref[...], other_ref[...]
     above = unpack_edge(jnp.where(even, relay, direct), nfac, cols)
     below = unpack_edge(jnp.where(even, direct, relay), nfac, cols)
     land_above = jnp.where((comp_rank == 0) & (cells_rank == 0), 0.0, above[2])
@@ -556,7 +563,7 @@
 
 def second_kernel(
     ncomp, chunk, ring, tiles, rank_ref, tau_ref, counts_ref, field_ref, land_ref, logexp_ref, pmom_ref, wmom_ref, old_ref,
-    own_ref, near_ref, far_ref, edge_ref, grad0_ref, *refs
+    own_ref, near_ref, far_ref, edge_ref, other_ref, grad0_ref, *refs
 ):
     gaps, refs = refs[: counts_ref.shape[0]], refs[counts_ref.shape[0] :]
     load, new_ref, params_ref, stats_ref, keep_ref, send_ref, flat, left, mix, right, wide, *refs = refs
@@ -574,7 +581,7 @@
     land = land_ref[here, :].astype(F32)
     lands = [land[r : r + 1, :] for r in range(share)]
     tau = field_weights(tau_ref, nfac, cols)
-    _, _, pulls = edge_terms(chunk, ring, tiles, rank_ref, tau, lands, old_ref, near_ref, far_ref, edge_ref)
+    _, _, pulls = edge_terms(ring, tiles, rank_ref, tau, lands, old_ref, edge_ref, other_ref)
     move = 0.5 * STEP_FIELD * STEP_FIELD
     for r in range(share):
         fresh = field_ref[r]
@@ -620,8 +627,7 @@
 
 
 def second_field(
-    chunk, ring, tiles, rank_ref, tau_ref, new_ref, half_ref, old_ref, land_ref, load_ref, stats_ref, near_ref, far_ref,
-    edge_ref, *refs
+    ring, tiles, rank_ref, tau_ref, new_ref, half_ref, old_ref, land_ref, load_ref, stats_ref, edge_ref, other_ref, *refs
 ):
     gap_refs, (mom_ref, energy_ref, prior) = refs[: new_ref.shape[0]], refs[new_ref.shape[0] :]
     comp_rank = rank_ref[1]
@@ -630,7 +636,7 @@
     lands = [land[r : r + 1, :] for r in range(share)]
     tau = field_weights(tau_ref, nfac, cols)
     (above, below), (land_above, land_below), (pull_up, pull_down) = edge_terms(
-        chunk, ring, tiles, rank_ref, tau, lands, old_ref, near_ref, far_ref, edge_ref
+        ring, tiles, rank_ref, tau, lands, old_ref, edge_ref, other_ref
     )
     move = 0.5 * STEP_FIELD * STEP_FIELD
     rows = [above - move * pull_up] + [new_ref[r] for r in range(share)] + [below - move * pull_down]
@@ -721,7 +727,7 @@
         1,
         9,
         gap_shapes + [load_shape, shape(nparam, LANES), chunk_shape, chunk_shape],
-        work + [pltpu.VMEM((mine + nfac, LANES), F32)],
+        work,
     )
     *gaps, load, grad, keep, send = first(
         ranks, count_rows, field_rows, land_mask, log_exposure, profile_mom, mixing_mom, pack, got, others
@@ -730,12 +736,12 @@
     part_field, half, near_edge, far_edge = call(
         first_field, "first_field", 2, 4 + share, [field_shape, field_shape, edge_shape, edge_shape], prior, field_cost
     )(ranks, field_tau, field_rows, mom_rows, land_mask, load, *gaps)
-    near, far, got_edge = all_sum(keep, send, near_edge, far_edge)
+    near, far, *edges = all_sum(keep, send, near_edge, far_edge)
     second = call(
         functools.partial(second_kernel, ncomp, chunk, ring, tiles),
         "second_gradient",
         2,
-        12,
+        13,
         gap_shapes
         + [
             load_shape,
@@ -749,11 +755,11 @@
     )
     *gaps, load, new_field, new_params, stats, keep, send = second(
         ranks, field_tau, count_rows, part_field, land_mask, log_exposure, profile_mom, mixing_mom, field_rows, pack, near,
-        far, got_edge, grad,
+        far, *edges, grad,
     )
     new_mom, energy = call(
-        functools.partial(second_field, chunk, ring, tiles), "second_field", 2, 9 + share, [field_shape, shape(8, LANES)], prior, field_cost
-    )(ranks, field_tau, new_field, half, field_rows, land_mask, load, stats, near, far, got_edge, *gaps)
+        functools.partial(second_field, ring, tiles), "second_field", 2, 8 + share, [field_shape, shape(8, LANES)], prior, field_cost
+    )(ranks, field_tau, new_field, half, field_rows, land_mask, load, stats, *edges, *gaps)
     done = (new_field.swapaxes(0, 1), new_params[:mine], new_params[mine:], new_mom.swapaxes(0, 1))
     momenta, energy, done = group_sum(keep, send, energy, done)
     kinetic = jnp.sum(0.5 * (momenta * momenta).reshape(-1, 8, LANES), axis=0)

time: 72.5 us -> 72.3 us (level)
    unnamed x18 -> x21, local copies, waits for them, and re-layouts: 2.5 us -> 2.51 us
where the time goes in v7:
time: 72.3 us; the launch traced here: 72.2 us
  starting transfers between devices  28.3 us (39%)
  waiting for transfers between devices  21.1 us (29%)
  Pallas kernels  14.1 us (20%)
  local copies, waits for them, and re-layouts  5.67 us (8%)
  other arithmetic  2.11 us (3%)
  between operations  0.94 us (1%)
    ppermute x24, starting transfers between devices, partner(): return lax.ppermute(values, axis, [(i, i ^ flip) for i in range(count)])  25.3 us
    ppermute x24, waiting for transfers between devices, partner(): return lax.ppermute(values, axis, [(i, i ^ flip) for i in range(count)])  21.1 us
    pallas_call x1, Pallas kernels, fast_device(): first(ranks, count_rows, field_rows, land_mask, log_exposure, profile_mom...  5.42 us
    pallas_call x1, Pallas kernels, fast_device(): second(ranks, field_tau, count_rows, part_field, land_mask, log_exposure,...  5.32 us
    ppermute x1, starting transfers between devices, gather_params(): one = lax.ppermute(pack, ('cells', 'comp'), spread)  3.02 us
    unnamed x21, local copies, waits for them, and re-layouts  2.51 us
  transfers between devices with their start and end apart: 25, of which 16 were waited for; matrix products, arithmetic and copies ran while one was open for 9% of the time, Pallas kernels for 4%

profile of v7, /device:TPU:0, one launch (start us, length us, event | category | flops | bytes accessed | tf_op | source)
XLA Modules:
  0.0 72.2 jit_solution(4718306435624777262)
XLA Ops:
  0.7 0.9 %pad_add_fusion.pack_ref.own_ref = f32[144,128]{1,0:T(8,128)S(1)} fusion(f32[16,128]{1,0:T(8,128)} %param.12, f32[128,128]{1,0:T(8,128)} %param.11), kind=kLoop, calls=%fused_computation.15 | loop fusion | flops 18432 | bytes 147456 | tf_op jit(solution)/shard_map/add | solution.py:683
  1.6 3.0 %collective-permute-start = (f32[144,128]{1,0:T(8,128)S(1)}, f32[144,128]{1,0:T(8,128)S(1)}, u32[]{:S(2)}, u32[]{:S(2)}) collective-permute-start(f32[144,128]{1,0:T(8,128)S(1)} %pad_add_fusion.pack_ref.own_ref), channel_id=1, source_target_pairs={{0,1},{1,0},{2,3},{3,2},{4,6},{5,7},{6,4},{7,5},{8,9},{9,8},{10,11... | collective-permute-start | bytes 221192 | tf_op jit(solution)/shard_map/ppermute | solution.py:264
  4.6 2.5 %collective-permute-start.1 = (f32[72,128]{1,0:T(8,128)S(1)}, f32[72,128]{1,0:T(8,128)S(1)}, u32[]{:S(2)}, u32[]{:S(2)}) collective-permute-start(f32[72,128]{1,0:T(8,128)S(1)} %constant_dynamic-slice_fusion), channel_id=1, source_target_pairs={{0,3},{1,2},{2,1},{3,0},{4,7},{5,6},{6,5},{7,4},{8,11},{9,10},{10,... | collective-permute-start | bytes 110600 | tf_op jit(solution)/shard_map/ppermute | solution.py:212
  7.1 1.3 %constant_dynamic-slice_fusion.1 = s32[128,8,256]{2,1,0:T(8,128)S(1)} fusion(s32[128,32,256]{2,1,0:T(8,128)} %param.17, s32[]{:T(128)S(6)} %select_n.62), kind=kLoop, calls=%fused_computation.54 | loop fusion | bytes 2097156 | tf_op jit(solution)/shard_map/dynamic_slice | solution.py:685
  8.7 1.0 %copy.29 = f32[16,8,256]{2,0,1:T(8,128)S(1)} copy(f32[16,8,256]{2,1,0:T(8,128)} %param.10) | data formatting | bytes 262144 | tf_op args[0]
  10.5 1.2 %collective-permute-done.2.others_ref = f32[216,128]{1,0:T(8,128)S(1)} collective-permute-done((f32[216,128]{1,0:T(8,128)S(1)}, f32[216,128]{1,0:T(8,128)S(1)}, u32[]{:S(2)}, u32[]{:S(2)}) %collective-permute-start.2) | collective-permute-done | bytes 110624 | tf_op jit(solution)/shard_map/ppermute | solution.py:212
  11.7 5.4 %first_gradient.1 = (bf16[512,512]{1,0:T(8,128)(2,1)S(1)}, bf16[512,512]{1,0:T(8,128)(2,1)S(1)}, bf16[512,512]{1,0:T(8,128)(2,1)S(1)}, bf16[512,512]{1,0:T(8,128...) custom-call(s32[2]{0:T(128)S(1)} %pad_add_fusion.1.rank_ref, ...), custom_call_target="tpu_custom_call" | custom-call | tf_op jit(solution)/shard_map/first_gradient/pallas_call | solution.py:732
  17.4 1.2 %collective-permute-done.3 = f32[4,72,128]{2,1,0:T(8,128)S(1)} collective-permute-done((f32[4,72,128]{2,1,0:T(8,128)S(1)}, f32[4,72,128]{2,1,0:T(8,128)S(1)}, u32[]{:S(2)}, u32[]{:S(2)}) %collective-permute-start.3) | collective-permute-done | bytes 147488 | tf_op jit(solution)/shard_map/ppermute | solution.py:212
  18.6 1.6 %collective-permute-start.4 = (f32[72,128]{1,0:T(8,128)S(1)}, f32[72,128]{1,0:T(8,128)S(1)}, u32[]{:S(2)}, u32[]{:S(2)}) collective-permute-start(f32[72,128]{1,0:T(8,128)S(1)} %get-tuple-element.93), channel_id=1, source_target_pairs={{0,8},{4,12},{8,0},{12,4},{16,24},{20,28},{24,16},{28,20},{1,9},{5... | collective-permute-start | bytes 110600 | tf_op jit(solution)/shard_map/ppermute | solution.py:212
  20.2 1.5 %collective-permute-start.6 = (f32[72,128]{1,0:T(8,128)S(1)}, f32[72,128]{1,0:T(8,128)S(1)}, u32[]{:S(2)}, u32[]{:S(2)}) collective-permute-start(f32[72,128]{1,0:T(8,128)S(1)} %get-tuple-element.94), channel_id=1, source_target_pairs={{0,24},{4,28},{8,16},{12,20},{16,8},{20,12},{24,0},{28,4},{1,25},{... | collective-permute-start | bytes 110600 | tf_op jit(solution)/shard_map/ppermute | solution.py:212
  22.3 1.4 %first_field.1 = (f32[8,16,256]{2,1,0:T(8,128)S(1)}, f32[8,16,256]{2,1,0:T(8,128)S(1)}, f32[72,128]{1,0:T(8,128)S(1)}, f32[72,128]{1,0:T(8,128)S(1)}) custom-call(s32[2]{0:T(128)S(1)} %pad_add_fusion.1.rank_ref, f32[16]{0:T(128)S(1)} %copy-done.4, f32[8,16,256]{2,1,0:T(8,128)S(1)} %bitcast.46, f32[8,16,256]{2,1,0:T(8,128)S(1)} %bitcast.49, ...), custom_call_target="tpu_custom_call" | custom-call | flops 134217728 | bytes 4194304 | tf_op jit(solution)/shard_map/first_field/pallas_call | solution.py:736
  23.6 1.4 %collective-permute-done.6 = f32[72,128]{1,0:T(8,128)S(1)} collective-permute-done((f32[72,128]{1,0:T(8,128)S(1)}, f32[72,128]{1,0:T(8,128)S(1)}, u32[]{:S(2)}, u32[]{:S(2)}) %collective-permute-start.6) | collective-permute-done | bytes 36896 | tf_op jit(solution)/shard_map/ppermute | solution.py:212
  25.8 3.1 %collective-permute-start.9 = (f32[144,128]{1,0:T(8,128)S(1)}, f32[144,128]{1,0:T(8,128)S(1)}, u32[]{:S(2)}, u32[]{:S(2)}) collective-permute-start(f32[144,128]{1,0:T(8,128)S(1)} %get-tuple-element.102), channel_id=1, source_target_pairs={{0,3},{1,2},{2,1},{3,0},{4,7},{5,6},{6,5},{7,4},{8,11},{9,10},{10,... | collective-permute-start | bytes 221192 | tf_op jit(solution)/shard_map/ppermute | solution.py:212
  29.3 4.9 %collective-permute-done.8 = f32[72,128]{1,0:T(8,128)S(1)} collective-permute-done((f32[72,128]{1,0:T(8,128)S(1)}, f32[72,128]{1,0:T(8,128)S(1)}, u32[]{:S(2)}, u32[]{:S(2)}) %collective-permute-start.8) | collective-permute-done | bytes 36896 | tf_op jit(solution)/shard_map/ppermute | solution.py:212
  34.2 1.6 %collective-permute-start.10 = (f32[144,128]{1,0:T(8,128)S(1)}, f32[144,128]{1,0:T(8,128)S(1)}, u32[]{:S(2)}, u32[]{:S(2)}) collective-permute-start(f32[144,128]{1,0:T(8,128)S(1)} %pad_maximum_fusion.4), channel_id=1, source_target_pairs={{0,8},{4,12},{8,0},{12,4},{16,24},{20,28},{24,16},{28,20},{1,9},{5... | collective-permute-start | bytes 221192 | tf_op jit(solution)/shard_map/ppermute | solution.py:212
  36.3 1.5 %collective-permute-start.12 = (f32[144,128]{1,0:T(8,128)S(1)}, f32[144,128]{1,0:T(8,128)S(1)}, u32[]{:S(2)}, u32[]{:S(2)}) collective-permute-start(f32[144,128]{1,0:T(8,128)S(1)} %pad_maximum_fusion.4), channel_id=1, source_target_pairs={{0,24},{4,28},{8,16},{12,20},{16,8},{20,12},{24,0},{28,4},{1,25},{... | collective-permute-start | bytes 221192 | tf_op jit(solution)/shard_map/ppermute | solution.py:212
  37.8 0.9 %collective-permute-done.10 = f32[144,128]{1,0:T(8,128)S(1)} collective-permute-done((f32[144,128]{1,0:T(8,128)S(1)}, f32[144,128]{1,0:T(8,128)S(1)}, u32[]{:S(2)}, u32[]{:S(2)}) %collective-permute-start.10) | collective-permute-done | bytes 73760 | tf_op jit(solution)/shard_map/ppermute | solution.py:212
  38.6 1.1 %collective-permute-done.11 = f32[72,128]{1,0:T(8,128)S(1)} collective-permute-done((f32[72,128]{1,0:T(8,128)S(1)}, f32[72,128]{1,0:T(8,128)S(1)}, u32[]{:S(2)}, u32[]{:S(2)}) %collective-permute-start.11) | collective-permute-done | bytes 36896 | tf_op jit(solution)/shard_map/ppermute | solution.py:212
  39.7 1.8 %collective-permute-done.12 = f32[144,128]{1,0:T(8,128)S(1)} collective-permute-done((f32[144,128]{1,0:T(8,128)S(1)}, f32[144,128]{1,0:T(8,128)S(1)}, u32[]{:S(2)}, u32[]{:S(2)}) %collective-permute-start.12) | collective-permute-done | bytes 73760 | tf_op jit(solution)/shard_map/ppermute | solution.py:212
  41.6 1.4 %collective-permute-done.13.far_ref = f32[360,128]{1,0:T(8,128)S(1)} collective-permute-done((f32[360,128]{1,0:T(8,128)S(1)}, f32[360,128]{1,0:T(8,128)S(1)}, u32[]{:S(2)}, u32[]{:S(2)}) %collective-permute-start.13) | collective-permute-done | bytes 184352 | tf_op jit(solution)/shard_map/ppermute | solution.py:212
  43.0 5.3 %second_gradient.1 = (bf16[512,512]{1,0:T(8,128)(2,1)S(1)}, bf16[512,512]{1,0:T(8,128)(2,1)S(1)}, bf16[512,512]{1,0:T(8,128)(2,1)S(1)}, bf16[512,512]{1,0:T(8,12...) custom-call(s32[2]{0:T(128)S(1)} %pad_add_fusion.1.rank_ref, ...), custom_call_target="tpu_custom_call" | custom-call | tf_op jit(solution)/shard_map/second_gradient/pallas_call | solution.py:756
  48.6 1.2 %collective-permute-done.14 = f32[4,72,128]{2,1,0:T(8,128)S(1)} collective-permute-done((f32[4,72,128]{2,1,0:T(8,128)S(1)}, f32[4,72,128]{2,1,0:T(8,128)S(1)}, u32[]{:S(2)}, u32[]{:S(2)}) %collective-permute-start.14) | collective-permute-done | bytes 147488 | tf_op jit(solution)/shard_map/ppermute | solution.py:212
  50.1 1.8 %collective-permute-start.17 = (f32[72,128]{1,0:T(8,128)S(1)}, f32[72,128]{1,0:T(8,128)S(1)}, u32[]{:S(2)}, u32[]{:S(2)}) collective-permute-start(f32[72,128]{1,0:T(8,128)S(1)} %get-tuple-element.91), channel_id=1, source_target_pairs={{0,3},{1,2},{2,1},{3,0},{4,7},{5,6},{6,5},{7,4},{8,11},{9,10},{10,... | collective-permute-start | bytes 110600 | tf_op jit(solution)/shard_map/ppermute | solution.py:212
  51.9 1.5 %collective-permute-start.16 = (f32[72,128]{1,0:T(8,128)S(1)}, f32[72,128]{1,0:T(8,128)S(1)}, u32[]{:S(2)}, u32[]{:S(2)}) collective-permute-start(f32[72,128]{1,0:T(8,128)S(1)} %get-tuple-element.92), channel_id=1, source_target_pairs={{0,2},{1,3},{2,0},{3,1},{4,6},{5,7},{6,4},{7,5},{8,10},{9,11},{10,... | collective-permute-start | bytes 110600 | tf_op jit(solution)/shard_map/ppermute | solution.py:212
  54.6 1.4 %second_field.1 = (f32[8,16,256]{2,1,0:T(8,128)S(1)}, f32[8,128]{1,0:T(8,128)S(1)}) custom-call(s32[2]{0:T(128)S(1)} %pad_add_fusion.1.rank_ref, f32[16]{0:T(128)S(1)} %copy-done.4, f32[8,16,256]{2,1,0:T(8,128)S(1)} %get-tuple-element.61.new_ref, f32[8,16,256]{2,1,0:T(8,128)S(1)} %get-tuple-element.63.half_ref, f32[8,16,256]{2,1,0:T(8,128)S(1)} %bitcast.48, ...), custom_call_target="tpu_custom_call" | custom-call | flops 134217728 | bytes 4194304 | tf_op jit(solution)/shard_map/second_field/pallas_call | solution.py:760
  56.0 1.3 %collective-permute-done.16 = f32[72,128]{1,0:T(8,128)S(1)} collective-permute-done((f32[72,128]{1,0:T(8,128)S(1)}, f32[72,128]{1,0:T(8,128)S(1)}, u32[]{:S(2)}, u32[]{:S(2)}) %collective-permute-start.16) | collective-permute-done | bytes 36896 | tf_op jit(solution)/shard_map/ppermute | solution.py:212
  57.3 1.6 %collective-permute-start.20 = (f32[80,128]{1,0:T(8,128)S(1)}, f32[80,128]{1,0:T(8,128)S(1)}, u32[]{:S(2)}, u32[]{:S(2)}) collective-permute-start(f32[80,128]{1,0:T(8,128)S(1)} %constant_dynamic-update-slice_fusion.6), channel_id=1, source_target_pairs={{0,24},{4,28},{8,16},{12,20},{16,8},{20,12},{24,0},{28,4},{1,25},{... | collective-permute-start | bytes 122888 | tf_op jit(solution)/shard_map/ppermute | solution.py:212
  58.9 0.9 %collective-permute-start.19 = (f32[80,128]{1,0:T(8,128)S(1)}, f32[80,128]{1,0:T(8,128)S(1)}, u32[]{:S(2)}, u32[]{:S(2)}) collective-permute-start(f32[80,128]{1,0:T(8,128)S(1)} %constant_dynamic-update-slice_fusion.6), channel_id=1, source_target_pairs={{0,16},{4,20},{8,24},{12,28},{16,0},{20,4},{24,8},{28,12},{1,17},{... | collective-permute-start | bytes 122888 | tf_op jit(solution)/shard_map/ppermute | solution.py:212
  59.8 1.1 %collective-permute-start.18 = (f32[80,128]{1,0:T(8,128)S(1)}, f32[80,128]{1,0:T(8,128)S(1)}, u32[]{:S(2)}, u32[]{:S(2)}) collective-permute-start(f32[80,128]{1,0:T(8,128)S(1)} %constant_dynamic-update-slice_fusion.6), channel_id=1, source_target_pairs={{0,8},{4,12},{8,0},{12,4},{16,24},{20,28},{24,16},{28,20},{1,9},{5... | collective-permute-start | bytes 122888 | tf_op jit(solution)/shard_map/ppermute | solution.py:212
  60.9 1.9 %collective-permute-done.20 = f32[80,128]{1,0:T(8,128)S(1)} collective-permute-done((f32[80,128]{1,0:T(8,128)S(1)}, f32[80,128]{1,0:T(8,128)S(1)}, u32[]{:S(2)}, u32[]{:S(2)}) %collective-permute-start.20) | collective-permute-done | bytes 40992 | tf_op jit(solution)/shard_map/ppermute | solution.py:212
  65.5 1.6 %collective-permute-start.24 = (f32[8,128]{1,0:T(8,128)S(1)}, f32[8,128]{1,0:T(8,128)S(1)}, u32[]{:S(2)}, u32[]{:S(2)}) collective-permute-start(f32[8,128]{1,0:T(8,128)S(1)} %fusion.16.refs_0_), channel_id=1, source_target_pairs={{0,3},{1,2},{2,1},{3,0},{4,7},{5,6},{6,5},{7,4},{8,11},{9,10},{10,... | collective-permute-start | bytes 12296 | tf_op jit(solution)/shard_map/ppermute | solution.py:212
  67.3 2.7 %collective-permute-start.22 = (f32[8,128]{1,0:T(8,128)S(1)}, f32[8,128]{1,0:T(8,128)S(1)}, u32[]{:S(2)}, u32[]{:S(2)}) collective-permute-start(f32[8,128]{1,0:T(8,128)S(1)} %fusion.16.refs_0_), channel_id=1, source_target_pairs={{0,1},{1,0},{2,3},{3,2},{4,5},{5,4},{6,7},{7,6},{8,9},{9,8},{10,11... | collective-permute-start | bytes 12296 | tf_op jit(solution)/shard_map/ppermute | solution.py:212
  (73 shorter events, 10.5 us)
Async XLA Ops:
  0.6 11.1 %copy-start = (s32[32,256]{1,0:T(8,128)S(1)}, s32[32,256]{1,0:T(8,128)}, u32[]{:S(2)}) copy-start(s32[32,256]{1,0:T(8,128)} %land_ref.7) | copy-start | bytes 98308
  0.6 11.1 %copy-start.2 = (f32[32,256]{1,0:T(8,128)S(1)}, f32[32,256]{1,0:T(8,128)}, u32[]{:S(2)}) copy-start(f32[32,256]{1,0:T(8,128)} %logexp_ref.3) | copy-start | bytes 98308
  0.7 11.1 %copy-start.3 = (f32[16,128]{1,0:T(8,128)S(1)}, f32[16,128]{1,0:T(8,128)}, u32[]{:S(2)}) copy-start(f32[16,128]{1,0:T(8,128)} %wmom_ref.3) | copy-start | bytes 24580
  0.7 11.1 %copy-start.1 = (f32[128,128]{1,0:T(8,128)S(1)}, f32[128,128]{1,0:T(8,128)}, u32[]{:S(2)}) copy-start(f32[128,128]{1,0:T(8,128)} %pmom_ref.3) | copy-start | bytes 196612
  0.7 21.5 %copy-start.5 = (f32[16,8,256]{2,1,0:T(8,128)S(1)}, f32[16,8,256]{2,1,0:T(8,128)}, u32[]{:S(2)}) copy-start(f32[16,8,256]{2,1,0:T(8,128)} %param.13) | copy-start | bytes 393220
  0.7 21.6 %copy-start.4 = (f32[16]{0:T(128)S(1)}, f32[16]{0:T(128)}, u32[]{:S(2)}) copy-start(f32[16]{0:T(128)} %tau_ref.5) | copy-start | bytes 196
  1.6 8.1 %collective-permute-start = (f32[144,128]{1,0:T(8,128)S(1)}, f32[144,128]{1,0:T(8,128)S(1)}, u32[]{:S(2)}, u32[]{:S(2)}) collective-permute-start(f32[144,128]{1,0:T(8,128)S(1)} %pad_add_fusion.pack_ref.own_ref), channel_id=1, source_target_pairs={{0,1},{1,0},{2,3},{3,2},{4,6},{5,7},{6,4},{7,5},{8,9},{9,8},{10,11... | collective-permute-start | bytes 221192 | tf_op jit(solution)/shard_map/ppermute | solution.py:264
  4.6 5.8 %collective-permute-start.1 = (f32[72,128]{1,0:T(8,128)S(1)}, f32[72,128]{1,0:T(8,128)S(1)}, u32[]{:S(2)}, u32[]{:S(2)}) collective-permute-start(f32[72,128]{1,0:T(8,128)S(1)} %constant_dynamic-slice_fusion), channel_id=1, source_target_pairs={{0,3},{1,2},{2,1},{3,0},{4,7},{5,6},{6,5},{7,4},{8,11},{9,10},{10,... | collective-permute-start | bytes 110600 | tf_op jit(solution)/shard_map/ppermute | solution.py:212
  10.4 1.3 %collective-permute-start.2 = (f32[216,128]{1,0:T(8,128)S(1)}, f32[216,128]{1,0:T(8,128)S(1)}, u32[]{:S(2)}, u32[]{:S(2)}) collective-permute-start(f32[216,128]{1,0:T(8,128)S(1)} %constant_dynamic-update-slice_fusion.got_ref), channel_id=1, source_target_pairs={{0,4},{4,0},{8,12},{12,8},{16,20},{20,16},{24,28},{28,24},{1,5},{5... | collective-permute-start | bytes 331784 | tf_op jit(solution)/shard_map/ppermute | solution.py:212
  17.2 1.4 %collective-permute-start.3 = (f32[4,72,128]{2,1,0:T(8,128)S(1)}, f32[4,72,128]{2,1,0:T(8,128)S(1)}, u32[]{:S(2)}, u32[]{:S(2)}) collective-permute-start(f32[4,72,128]{2,1,0:T(8,128)S(1)} %get-tuple-element.55), channel_id=1, source_target_pairs={{0,4},{4,0},{8,12},{12,8},{16,20},{20,16},{24,28},{28,24},{1,5},{5... | collective-permute-start | bytes 442376 | tf_op jit(solution)/shard_map/ppermute | solution.py:212
  18.6 5.0 %collective-permute-start.4 = (f32[72,128]{1,0:T(8,128)S(1)}, f32[72,128]{1,0:T(8,128)S(1)}, u32[]{:S(2)}, u32[]{:S(2)}) collective-permute-start(f32[72,128]{1,0:T(8,128)S(1)} %get-tuple-element.93), channel_id=1, source_target_pairs={{0,8},{4,12},{8,0},{12,4},{16,24},{20,28},{24,16},{28,20},{1,9},{5... | collective-permute-start | bytes 110600 | tf_op jit(solution)/shard_map/ppermute | solution.py:212
  20.2 4.9 %collective-permute-start.6 = (f32[72,128]{1,0:T(8,128)S(1)}, f32[72,128]{1,0:T(8,128)S(1)}, u32[]{:S(2)}, u32[]{:S(2)}) collective-permute-start(f32[72,128]{1,0:T(8,128)S(1)} %get-tuple-element.94), channel_id=1, source_target_pairs={{0,24},{4,28},{8,16},{12,20},{16,8},{20,12},{24,0},{28,4},{1,25},{... | collective-permute-start | bytes 110600 | tf_op jit(solution)/shard_map/ppermute | solution.py:212
  21.7 4.0 %collective-permute-start.5 = (f32[72,128]{1,0:T(8,128)S(1)}, f32[72,128]{1,0:T(8,128)S(1)}, u32[]{:S(2)}, u32[]{:S(2)}) collective-permute-start(f32[72,128]{1,0:T(8,128)S(1)} %get-tuple-element.95), channel_id=1, source_target_pairs={{0,16},{4,20},{8,24},{12,28},{16,0},{20,4},{24,8},{28,12},{1,17},{... | collective-permute-start | bytes 110600 | tf_op jit(solution)/shard_map/ppermute | solution.py:212
  25.7 8.5 %collective-permute-start.7 = (f32[144,128]{1,0:T(8,128)S(1)}, f32[144,128]{1,0:T(8,128)S(1)}, u32[]{:S(2)}, u32[]{:S(2)}) collective-permute-start(f32[144,128]{1,0:T(8,128)S(1)} %get-tuple-element.101), channel_id=1, source_target_pairs={{0,1},{1,0},{2,3},{3,2},{4,5},{5,4},{6,7},{7,6},{8,9},{9,8},{10,11... | collective-permute-start | bytes 221192 | tf_op jit(solution)/shard_map/ppermute | solution.py:212
  25.8 8.3 %collective-permute-start.9 = (f32[144,128]{1,0:T(8,128)S(1)}, f32[144,128]{1,0:T(8,128)S(1)}, u32[]{:S(2)}, u32[]{:S(2)}) collective-permute-start(f32[144,128]{1,0:T(8,128)S(1)} %get-tuple-element.102), channel_id=1, source_target_pairs={{0,3},{1,2},{2,1},{3,0},{4,7},{5,6},{6,5},{7,4},{8,11},{9,10},{10,... | collective-permute-start | bytes 221192 | tf_op jit(solution)/shard_map/ppermute | solution.py:212
  29.0 5.2 %collective-permute-start.8 = (f32[72,128]{1,0:T(8,128)S(1)}, f32[72,128]{1,0:T(8,128)S(1)}, u32[]{:S(2)}, u32[]{:S(2)}) collective-permute-start(f32[72,128]{1,0:T(8,128)S(1)} %fusion.15), channel_id=1, source_target_pairs={{0,2},{1,3},{2,0},{3,1},{4,6},{5,7},{6,4},{7,5},{8,10},{9,11},{10,... | collective-permute-start | bytes 110600 | tf_op jit(solution)/shard_map/ppermute | solution.py:212
  34.2 4.4 %collective-permute-start.10 = (f32[144,128]{1,0:T(8,128)S(1)}, f32[144,128]{1,0:T(8,128)S(1)}, u32[]{:S(2)}, u32[]{:S(2)}) collective-permute-start(f32[144,128]{1,0:T(8,128)S(1)} %pad_maximum_fusion.4), channel_id=1, source_target_pairs={{0,8},{4,12},{8,0},{12,4},{16,24},{20,28},{24,16},{28,20},{1,9},{5... | collective-permute-start | bytes 221192 | tf_op jit(solution)/shard_map/ppermute | solution.py:212
  35.8 4.0 %collective-permute-start.11 = (f32[72,128]{1,0:T(8,128)S(1)}, f32[72,128]{1,0:T(8,128)S(1)}, u32[]{:S(2)}, u32[]{:S(2)}) collective-permute-start(f32[72,128]{1,0:T(8,128)S(1)} %get-tuple-element.89), channel_id=1, source_target_pairs={{0,16},{4,20},{8,24},{12,28},{16,0},{20,4},{24,8},{28,12},{1,17},{... | collective-permute-start | bytes 110600 | tf_op jit(solution)/shard_map/ppermute | solution.py:212
  36.3 5.3 %collective-permute-start.12 = (f32[144,128]{1,0:T(8,128)S(1)}, f32[144,128]{1,0:T(8,128)S(1)}, u32[]{:S(2)}, u32[]{:S(2)}) collective-permute-start(f32[144,128]{1,0:T(8,128)S(1)} %pad_maximum_fusion.4), channel_id=1, source_target_pairs={{0,24},{4,28},{8,16},{12,20},{16,8},{20,12},{24,0},{28,4},{1,25},{... | collective-permute-start | bytes 221192 | tf_op jit(solution)/shard_map/ppermute | solution.py:212
  41.5 1.5 %collective-permute-start.13 = (f32[360,128]{1,0:T(8,128)S(1)}, f32[360,128]{1,0:T(8,128)S(1)}, u32[]{:S(2)}, u32[]{:S(2)}) collective-permute-start(f32[360,128]{1,0:T(8,128)S(1)} %get-tuple-element.98), channel_id=1, source_target_pairs={{0,4},{4,0},{8,12},{12,8},{16,20},{20,16},{24,28},{28,24},{1,5},{5... | collective-permute-start | bytes 552968 | tf_op jit(solution)/shard_map/ppermute | solution.py:212
  48.4 1.4 %collective-permute-start.14 = (f32[4,72,128]{2,1,0:T(8,128)S(1)}, f32[4,72,128]{2,1,0:T(8,128)S(1)}, u32[]{:S(2)}, u32[]{:S(2)}) collective-permute-start(f32[4,72,128]{2,1,0:T(8,128)S(1)} %get-tuple-element.60), channel_id=1, source_target_pairs={{0,4},{4,0},{8,12},{12,8},{16,20},{20,16},{24,28},{28,24},{1,5},{5... | collective-permute-start | bytes 442376 | tf_op jit(solution)/shard_map/ppermute | solution.py:212
  49.8 6.2 %collective-permute-start.15 = (f32[72,128]{1,0:T(8,128)S(1)}, f32[72,128]{1,0:T(8,128)S(1)}, u32[]{:S(2)}, u32[]{:S(2)}) collective-permute-start(f32[72,128]{1,0:T(8,128)S(1)} %get-tuple-element.90), channel_id=1, source_target_pairs={{0,1},{1,0},{2,3},{3,2},{4,5},{5,4},{6,7},{7,6},{8,9},{9,8},{10,11... | collective-permute-start | bytes 110600 | tf_op jit(solution)/shard_map/ppermute | solution.py:212
  50.1 5.9 %collective-permute-start.17 = (f32[72,128]{1,0:T(8,128)S(1)}, f32[72,128]{1,0:T(8,128)S(1)}, u32[]{:S(2)}, u32[]{:S(2)}) collective-permute-start(f32[72,128]{1,0:T(8,128)S(1)} %get-tuple-element.91), channel_id=1, source_target_pairs={{0,3},{1,2},{2,1},{3,0},{4,7},{5,6},{6,5},{7,4},{8,11},{9,10},{10,... | collective-permute-start | bytes 110600 | tf_op jit(solution)/shard_map/ppermute | solution.py:212
  51.9 5.4 %collective-permute-start.16 = (f32[72,128]{1,0:T(8,128)S(1)}, f32[72,128]{1,0:T(8,128)S(1)}, u32[]{:S(2)}, u32[]{:S(2)}) collective-permute-start(f32[72,128]{1,0:T(8,128)S(1)} %get-tuple-element.92), channel_id=1, source_target_pairs={{0,2},{1,3},{2,0},{3,1},{4,6},{5,7},{6,4},{7,5},{8,10},{9,11},{10,... | collective-permute-start | bytes 110600 | tf_op jit(solution)/shard_map/ppermute | solution.py:212
  57.3 5.4 %collective-permute-start.20 = (f32[80,128]{1,0:T(8,128)S(1)}, f32[80,128]{1,0:T(8,128)S(1)}, u32[]{:S(2)}, u32[]{:S(2)}) collective-permute-start(f32[80,128]{1,0:T(8,128)S(1)} %constant_dynamic-update-slice_fusion.6), channel_id=1, source_target_pairs={{0,24},{4,28},{8,16},{12,20},{16,8},{20,12},{24,0},{28,4},{1,25},{... | collective-permute-start | bytes 122888 | tf_op jit(solution)/shard_map/ppermute | solution.py:212
  58.9 4.1 %collective-permute-start.19 = (f32[80,128]{1,0:T(8,128)S(1)}, f32[80,128]{1,0:T(8,128)S(1)}, u32[]{:S(2)}, u32[]{:S(2)}) collective-permute-start(f32[80,128]{1,0:T(8,128)S(1)} %constant_dynamic-update-slice_fusion.6), channel_id=1, source_target_pairs={{0,16},{4,20},{8,24},{12,28},{16,0},{20,4},{24,8},{28,12},{1,17},{... | collective-permute-start | bytes 122888 | tf_op jit(solution)/shard_map/ppermute | solution.py:212
  59.8 4.0 %collective-permute-start.18 = (f32[80,128]{1,0:T(8,128)S(1)}, f32[80,128]{1,0:T(8,128)S(1)}, u32[]{:S(2)}, u32[]{:S(2)}) collective-permute-start(f32[80,128]{1,0:T(8,128)S(1)} %constant_dynamic-update-slice_fusion.6), channel_id=1, source_target_pairs={{0,8},{4,12},{8,0},{12,4},{16,24},{20,28},{24,16},{28,20},{1,9},{5... | collective-permute-start | bytes 122888 | tf_op jit(solution)/shard_map/ppermute | solution.py:212
  63.8 1.6 %collective-permute-start.21 = (f32[80,128]{1,0:T(8,128)S(1)}, f32[80,128]{1,0:T(8,128)S(1)}, u32[]{:S(2)}, u32[]{:S(2)}) collective-permute-start(f32[80,128]{1,0:T(8,128)S(1)} %add_add_fusion), channel_id=1, source_target_pairs={{0,4},{4,0},{8,12},{12,8},{16,20},{20,16},{24,28},{28,24},{1,5},{5... | collective-permute-start | bytes 122888 | tf_op jit(solution)/shard_map/ppermute | solution.py:212
  65.5 5.7 %collective-permute-start.24 = (f32[8,128]{1,0:T(8,128)S(1)}, f32[8,128]{1,0:T(8,128)S(1)}, u32[]{:S(2)}, u32[]{:S(2)}) collective-permute-start(f32[8,128]{1,0:T(8,128)S(1)} %fusion.16.refs_0_), channel_id=1, source_target_pairs={{0,3},{1,2},{2,1},{3,0},{4,7},{5,6},{6,5},{7,4},{8,11},{9,10},{10,... | collective-permute-start | bytes 12296 | tf_op jit(solution)/shard_map/ppermute | solution.py:212
  67.0 4.5 %collective-permute-start.23 = (f32[8,128]{1,0:T(8,128)S(1)}, f32[8,128]{1,0:T(8,128)S(1)}, u32[]{:S(2)}, u32[]{:S(2)}) collective-permute-start(f32[8,128]{1,0:T(8,128)S(1)} %fusion.16.refs_0_), channel_id=1, source_target_pairs={{0,2},{1,3},{2,0},{3,1},{4,6},{5,7},{6,4},{7,5},{8,10},{9,11},{10,... | collective-permute-start | bytes 12296 | tf_op jit(solution)/shard_map/ppermute | solution.py:212
  67.3 4.3 %collective-permute-start.22 = (f32[8,128]{1,0:T(8,128)S(1)}, f32[8,128]{1,0:T(8,128)S(1)}, u32[]{:S(2)}, u32[]{:S(2)}) collective-permute-start(f32[8,128]{1,0:T(8,128)S(1)} %fusion.16.refs_0_), channel_id=1, source_target_pairs={{0,1},{1,0},{2,3},{3,2},{4,5},{5,4},{6,7},{7,6},{8,9},{9,8},{10,11... | collective-permute-start | bytes 12296 | tf_op jit(solution)/shard_map/ppermute | solution.py:212

commit v8 on v7

--- a/solution.py
+++ b/solution.py
@@ -646,7 +646,7 @@
     field_grads(load_ref, gap_refs, prior)
     for r in range(share):
         fresh = half_ref[r] + 0.5 * STEP_FIELD * prior[r]
-        mom_ref[r] = fresh
+        mom_ref[:, r, :] = fresh
         energy = energy + 0.5 * (fresh * fresh)
     tiles_sum = stats_ref[0:8, :] + stats_ref[8:16, :]
     for i in range(0, nfac, 8):
@@ -758,9 +758,9 @@
         far, *edges, grad,
     )
     new_mom, energy = call(
-        functools.partial(second_field, ring, tiles), "second_field", 2, 8 + share, [field_shape, shape(8, LANES)], prior, field_cost
+        functools.partial(second_field, ring, tiles), "second_field", 2, 8 + share, [shape(nfac, share, cols), shape(8, LANES)], prior, field_cost
     )(ranks, field_tau, new_field, half, field_rows, land_mask, load, stats, *edges, *gaps)
-    done = (new_field.swapaxes(0, 1), new_params[:mine], new_params[mine:], new_mom.swapaxes(0, 1))
+    done = (new_field.swapaxes(0, 1), new_params[:mine], new_params[mine:], new_mom)
     momenta, energy, done = group_sum(keep, send, energy, done)
     kinetic = jnp.sum(0.5 * (momenta * momenta).reshape(-1, 8, LANES), axis=0)
     total = energy + kinetic

time: 72.3 us -> 72.1 us (level)
  local copies, waits for them, and re-layouts: 5.67 us -> 4.94 us
    unnamed x21 -> x20, local copies, waits for them, and re-layouts: 2.51 us -> 1.78 us
  transfers between devices with their start and end apart: 25 -> 25, of which waited for: 16 -> 17; matrix products, arithmetic and copies ran while one was open for 9% -> 8% of each run, Pallas kernels for 4% -> 5%
where the time goes in v8:
time: 72.1 us; the launch traced here: 71.9 us
  starting transfers between devices  28.3 us (39%)
  waiting for transfers between devices  20.9 us (29%)
  Pallas kernels  14.7 us (20%)
  local copies, waits for them, and re-layouts  4.94 us (7%)
  other arithmetic  2.12 us (3%)
  between operations  0.91 us (1%)
    ppermute x24, starting transfers between devices, partner(): return lax.ppermute(values, axis, [(i, i ^ flip) for i in range(count)])  25.2 us
    ppermute x24, waiting for transfers between devices, partner(): return lax.ppermute(values, axis, [(i, i ^ flip) for i in range(count)])  20.9 us
    pallas_call x1, Pallas kernels, fast_device(): first(ranks, count_rows, field_rows, land_mask, log_exposure, profile_mom...  5.44 us
    pallas_call x1, Pallas kernels, fast_device(): second(ranks, field_tau, count_rows, part_field, land_mask, log_exposure,...  5.32 us
    ppermute x1, starting transfers between devices, gather_params(): one = lax.ppermute(pack, ('cells', 'comp'), spread)  3.02 us
    pallas_call x1, Pallas kernels, fast_device(): call(functools.partial(second_field, ring, tiles), 'second_field', 2, 8 +...  2.03 us
    unnamed x20, local copies, waits for them, and re-layouts  1.78 us
  transfers between devices with their start and end apart: 25, of which 17 were waited for; matrix products, arithmetic and copies ran while one was open for 8% of the time, Pallas kernels for 5%

profile of v8, /device:TPU:0, one launch (start us, length us, event | category | flops | bytes accessed | tf_op | source)
XLA Modules:
  0.0 71.9 jit_solution(16637593242588008077)
XLA Ops:
  0.7 0.9 %pad_add_fusion.pack_ref.own_ref = f32[144,128]{1,0:T(8,128)S(1)} fusion(f32[16,128]{1,0:T(8,128)} %param.12, f32[128,128]{1,0:T(8,128)} %param.11), kind=kLoop, calls=%fused_computation.15 | loop fusion | flops 18432 | bytes 147456 | tf_op jit(solution)/shard_map/add | solution.py:683
  1.6 3.0 %collective-permute-start = (f32[144,128]{1,0:T(8,128)S(1)}, f32[144,128]{1,0:T(8,128)S(1)}, u32[]{:S(2)}, u32[]{:S(2)}) collective-permute-start(f32[144,128]{1,0:T(8,128)S(1)} %pad_add_fusion.pack_ref.own_ref), channel_id=1, source_target_pairs={{0,1},{1,0},{2,3},{3,2},{4,6},{5,7},{6,4},{7,5},{8,9},{9,8},{10,11... | collective-permute-start | bytes 221192 | tf_op jit(solution)/shard_map/ppermute | solution.py:264
  4.6 2.5 %collective-permute-start.1 = (f32[72,128]{1,0:T(8,128)S(1)}, f32[72,128]{1,0:T(8,128)S(1)}, u32[]{:S(2)}, u32[]{:S(2)}) collective-permute-start(f32[72,128]{1,0:T(8,128)S(1)} %constant_dynamic-slice_fusion), channel_id=1, source_target_pairs={{0,3},{1,2},{2,1},{3,0},{4,7},{5,6},{6,5},{7,4},{8,11},{9,10},{10,... | collective-permute-start | bytes 110600 | tf_op jit(solution)/shard_map/ppermute | solution.py:212
  7.1 1.3 %constant_dynamic-slice_fusion.1 = s32[128,8,256]{2,1,0:T(8,128)S(1)} fusion(s32[128,32,256]{2,1,0:T(8,128)} %param.17, s32[]{:T(128)S(6)} %select_n.62), kind=kLoop, calls=%fused_computation.54 | loop fusion | bytes 2097156 | tf_op jit(solution)/shard_map/dynamic_slice | solution.py:685
  8.7 1.0 %copy.28 = f32[16,8,256]{2,0,1:T(8,128)S(1)} copy(f32[16,8,256]{2,1,0:T(8,128)} %param.10) | data formatting | bytes 262144 | tf_op args[0]
  10.5 1.2 %collective-permute-done.2.others_ref = f32[216,128]{1,0:T(8,128)S(1)} collective-permute-done((f32[216,128]{1,0:T(8,128)S(1)}, f32[216,128]{1,0:T(8,128)S(1)}, u32[]{:S(2)}, u32[]{:S(2)}) %collective-permute-start.2) | collective-permute-done | bytes 110624 | tf_op jit(solution)/shard_map/ppermute | solution.py:212
  11.7 5.4 %first_gradient.1 = (bf16[512,512]{1,0:T(8,128)(2,1)S(1)}, bf16[512,512]{1,0:T(8,128)(2,1)S(1)}, bf16[512,512]{1,0:T(8,128)(2,1)S(1)}, bf16[512,512]{1,0:T(8,128...) custom-call(s32[2]{0:T(128)S(1)} %pad_add_fusion.1.rank_ref, ...), custom_call_target="tpu_custom_call" | custom-call | tf_op jit(solution)/shard_map/first_gradient/pallas_call | solution.py:732
  17.4 1.2 %collective-permute-done.3 = f32[4,72,128]{2,1,0:T(8,128)S(1)} collective-permute-done((f32[4,72,128]{2,1,0:T(8,128)S(1)}, f32[4,72,128]{2,1,0:T(8,128)S(1)}, u32[]{:S(2)}, u32[]{:S(2)}) %collective-permute-start.3) | collective-permute-done | bytes 147488 | tf_op jit(solution)/shard_map/ppermute | solution.py:212
  18.7 1.6 %collective-permute-start.4 = (f32[72,128]{1,0:T(8,128)S(1)}, f32[72,128]{1,0:T(8,128)S(1)}, u32[]{:S(2)}, u32[]{:S(2)}) collective-permute-start(f32[72,128]{1,0:T(8,128)S(1)} %get-tuple-element.93), channel_id=1, source_target_pairs={{0,8},{4,12},{8,0},{12,4},{16,24},{20,28},{24,16},{28,20},{1,9},{5... | collective-permute-start | bytes 110600 | tf_op jit(solution)/shard_map/ppermute | solution.py:212
  20.2 1.5 %collective-permute-start.6 = (f32[72,128]{1,0:T(8,128)S(1)}, f32[72,128]{1,0:T(8,128)S(1)}, u32[]{:S(2)}, u32[]{:S(2)}) collective-permute-start(f32[72,128]{1,0:T(8,128)S(1)} %get-tuple-element.94), channel_id=1, source_target_pairs={{0,24},{4,28},{8,16},{12,20},{16,8},{20,12},{24,0},{28,4},{1,25},{... | collective-permute-start | bytes 110600 | tf_op jit(solution)/shard_map/ppermute | solution.py:212
  22.3 1.4 %first_field.1 = (f32[8,16,256]{2,1,0:T(8,128)S(1)}, f32[8,16,256]{2,1,0:T(8,128)S(1)}, f32[72,128]{1,0:T(8,128)S(1)}, f32[72,128]{1,0:T(8,128)S(1)}) custom-call(s32[2]{0:T(128)S(1)} %pad_add_fusion.1.rank_ref, f32[16]{0:T(128)S(1)} %copy-done.4, f32[8,16,256]{2,1,0:T(8,128)S(1)} %bitcast.45, f32[8,16,256]{2,1,0:T(8,128)S(1)} %bitcast.48, ...), custom_call_target="tpu_custom_call" | custom-call | flops 134217728 | bytes 4194304 | tf_op jit(solution)/shard_map/first_field/pallas_call | solution.py:736
  23.7 1.4 %collective-permute-done.6 = f32[72,128]{1,0:T(8,128)S(1)} collective-permute-done((f32[72,128]{1,0:T(8,128)S(1)}, f32[72,128]{1,0:T(8,128)S(1)}, u32[]{:S(2)}, u32[]{:S(2)}) %collective-permute-start.6) | collective-permute-done | bytes 36896 | tf_op jit(solution)/shard_map/ppermute | solution.py:212
  25.8 3.1 %collective-permute-start.9 = (f32[144,128]{1,0:T(8,128)S(1)}, f32[144,128]{1,0:T(8,128)S(1)}, u32[]{:S(2)}, u32[]{:S(2)}) collective-permute-start(f32[144,128]{1,0:T(8,128)S(1)} %get-tuple-element.102), channel_id=1, source_target_pairs={{0,3},{1,2},{2,1},{3,0},{4,7},{5,6},{6,5},{7,4},{8,11},{9,10},{10,... | collective-permute-start | bytes 221192 | tf_op jit(solution)/shard_map/ppermute | solution.py:212
  29.3 4.9 %collective-permute-done.8 = f32[72,128]{1,0:T(8,128)S(1)} collective-permute-done((f32[72,128]{1,0:T(8,128)S(1)}, f32[72,128]{1,0:T(8,128)S(1)}, u32[]{:S(2)}, u32[]{:S(2)}) %collective-permute-start.8) | collective-permute-done | bytes 36896 | tf_op jit(solution)/shard_map/ppermute | solution.py:212
  34.2 1.6 %collective-permute-start.10 = (f32[144,128]{1,0:T(8,128)S(1)}, f32[144,128]{1,0:T(8,128)S(1)}, u32[]{:S(2)}, u32[]{:S(2)}) collective-permute-start(f32[144,128]{1,0:T(8,128)S(1)} %pad_maximum_fusion.4), channel_id=1, source_target_pairs={{0,8},{4,12},{8,0},{12,4},{16,24},{20,28},{24,16},{28,20},{1,9},{5... | collective-permute-start | bytes 221192 | tf_op jit(solution)/shard_map/ppermute | solution.py:212
  36.3 1.5 %collective-permute-start.12 = (f32[144,128]{1,0:T(8,128)S(1)}, f32[144,128]{1,0:T(8,128)S(1)}, u32[]{:S(2)}, u32[]{:S(2)}) collective-permute-start(f32[144,128]{1,0:T(8,128)S(1)} %pad_maximum_fusion.4), channel_id=1, source_target_pairs={{0,24},{4,28},{8,16},{12,20},{16,8},{20,12},{24,0},{28,4},{1,25},{... | collective-permute-start | bytes 221192 | tf_op jit(solution)/shard_map/ppermute | solution.py:212
  37.8 0.9 %collective-permute-done.10 = f32[144,128]{1,0:T(8,128)S(1)} collective-permute-done((f32[144,128]{1,0:T(8,128)S(1)}, f32[144,128]{1,0:T(8,128)S(1)}, u32[]{:S(2)}, u32[]{:S(2)}) %collective-permute-start.10) | collective-permute-done | bytes 73760 | tf_op jit(solution)/shard_map/ppermute | solution.py:212
  38.6 1.1 %collective-permute-done.11 = f32[72,128]{1,0:T(8,128)S(1)} collective-permute-done((f32[72,128]{1,0:T(8,128)S(1)}, f32[72,128]{1,0:T(8,128)S(1)}, u32[]{:S(2)}, u32[]{:S(2)}) %collective-permute-start.11) | collective-permute-done | bytes 36896 | tf_op jit(solution)/shard_map/ppermute | solution.py:212
  39.7 1.8 %collective-permute-done.12 = f32[144,128]{1,0:T(8,128)S(1)} collective-permute-done((f32[144,128]{1,0:T(8,128)S(1)}, f32[144,128]{1,0:T(8,128)S(1)}, u32[]{:S(2)}, u32[]{:S(2)}) %collective-permute-start.12) | collective-permute-done | bytes 73760 | tf_op jit(solution)/shard_map/ppermute | solution.py:212
  41.7 1.4 %collective-permute-done.13.far_ref = f32[360,128]{1,0:T(8,128)S(1)} collective-permute-done((f32[360,128]{1,0:T(8,128)S(1)}, f32[360,128]{1,0:T(8,128)S(1)}, u32[]{:S(2)}, u32[]{:S(2)}) %collective-permute-start.13) | collective-permute-done | bytes 184352 | tf_op jit(solution)/shard_map/ppermute | solution.py:212
  43.1 5.3 %second_gradient.1 = (bf16[512,512]{1,0:T(8,128)(2,1)S(1)}, bf16[512,512]{1,0:T(8,128)(2,1)S(1)}, bf16[512,512]{1,0:T(8,128)(2,1)S(1)}, bf16[512,512]{1,0:T(8,12...) custom-call(s32[2]{0:T(128)S(1)} %pad_add_fusion.1.rank_ref, ...), custom_call_target="tpu_custom_call" | custom-call | tf_op jit(solution)/shard_map/second_gradient/pallas_call | solution.py:756
  48.6 1.2 %collective-permute-done.14 = f32[4,72,128]{2,1,0:T(8,128)S(1)} collective-permute-done((f32[4,72,128]{2,1,0:T(8,128)S(1)}, f32[4,72,128]{2,1,0:T(8,128)S(1)}, u32[]{:S(2)}, u32[]{:S(2)}) %collective-permute-start.14) | collective-permute-done | bytes 147488 | tf_op jit(solution)/shard_map/ppermute | solution.py:212
  50.1 1.8 %collective-permute-start.17 = (f32[72,128]{1,0:T(8,128)S(1)}, f32[72,128]{1,0:T(8,128)S(1)}, u32[]{:S(2)}, u32[]{:S(2)}) collective-permute-start(f32[72,128]{1,0:T(8,128)S(1)} %get-tuple-element.91), channel_id=1, source_target_pairs={{0,3},{1,2},{2,1},{3,0},{4,7},{5,6},{6,5},{7,4},{8,11},{9,10},{10,... | collective-permute-start | bytes 110600 | tf_op jit(solution)/shard_map/ppermute | solution.py:212
  51.9 1.5 %collective-permute-start.16 = (f32[72,128]{1,0:T(8,128)S(1)}, f32[72,128]{1,0:T(8,128)S(1)}, u32[]{:S(2)}, u32[]{:S(2)}) collective-permute-start(f32[72,128]{1,0:T(8,128)S(1)} %get-tuple-element.92), channel_id=1, source_target_pairs={{0,2},{1,3},{2,0},{3,1},{4,6},{5,7},{6,4},{7,5},{8,10},{9,11},{10,... | collective-permute-start | bytes 110600 | tf_op jit(solution)/shard_map/ppermute | solution.py:212
  54.6 2.0 %second_field.1 = (f32[16,8,256]{2,1,0:T(8,128)}, f32[8,128]{1,0:T(8,128)S(1)}) custom-call(s32[2]{0:T(128)S(1)} %pad_add_fusion.1.rank_ref, f32[16]{0:T(128)S(1)} %copy-done.4, f32[8,16,256]{2,1,0:T(8,128)S(1)} %get-tuple-element.61.new_ref, f32[8,16,256]{2,1,0:T(8,128)S(1)} %get-tuple-element.63.half_ref, f32[8,16,256]{2,1,0:T(8,128)S(1)} %bitcast.47, ...), custom_call_target="tpu_custom_call" | custom-call | flops 134217728 | bytes 4194304 | tf_op jit(solution)/shard_map/second_field/pallas_call | solution.py:760
  57.4 1.6 %collective-permute-start.20 = (f32[80,128]{1,0:T(8,128)S(1)}, f32[80,128]{1,0:T(8,128)S(1)}, u32[]{:S(2)}, u32[]{:S(2)}) collective-permute-start(f32[80,128]{1,0:T(8,128)S(1)} %constant_dynamic-update-slice_fusion.6), channel_id=1, source_target_pairs={{0,24},{4,28},{8,16},{12,20},{16,8},{20,12},{24,0},{28,4},{1,25},{... | collective-permute-start | bytes 122888 | tf_op jit(solution)/shard_map/ppermute | solution.py:212
  58.9 0.9 %collective-permute-start.19 = (f32[80,128]{1,0:T(8,128)S(1)}, f32[80,128]{1,0:T(8,128)S(1)}, u32[]{:S(2)}, u32[]{:S(2)}) collective-permute-start(f32[80,128]{1,0:T(8,128)S(1)} %constant_dynamic-update-slice_fusion.6), channel_id=1, source_target_pairs={{0,16},{4,20},{8,24},{12,28},{16,0},{20,4},{24,8},{28,12},{1,17},{... | collective-permute-start | bytes 122888 | tf_op jit(solution)/shard_map/ppermute | solution.py:212
  59.8 1.1 %collective-permute-start.18 = (f32[80,128]{1,0:T(8,128)S(1)}, f32[80,128]{1,0:T(8,128)S(1)}, u32[]{:S(2)}, u32[]{:S(2)}) collective-permute-start(f32[80,128]{1,0:T(8,128)S(1)} %constant_dynamic-update-slice_fusion.6), channel_id=1, source_target_pairs={{0,8},{4,12},{8,0},{12,4},{16,24},{20,28},{24,16},{28,20},{1,9},{5... | collective-permute-start | bytes 122888 | tf_op jit(solution)/shard_map/ppermute | solution.py:212
  60.9 1.9 %collective-permute-done.20 = f32[80,128]{1,0:T(8,128)S(1)} collective-permute-done((f32[80,128]{1,0:T(8,128)S(1)}, f32[80,128]{1,0:T(8,128)S(1)}, u32[]{:S(2)}, u32[]{:S(2)}) %collective-permute-start.20) | collective-permute-done | bytes 40992 | tf_op jit(solution)/shard_map/ppermute | solution.py:212
  63.1 0.8 %collective-permute-done.18 = f32[80,128]{1,0:T(8,128)S(1)} collective-permute-done((f32[80,128]{1,0:T(8,128)S(1)}, f32[80,128]{1,0:T(8,128)S(1)}, u32[]{:S(2)}, u32[]{:S(2)}) %collective-permute-start.18) | collective-permute-done | bytes 40992 | tf_op jit(solution)/shard_map/ppermute | solution.py:212
  65.2 1.6 %collective-permute-start.24 = (f32[8,128]{1,0:T(8,128)S(1)}, f32[8,128]{1,0:T(8,128)S(1)}, u32[]{:S(2)}, u32[]{:S(2)}) collective-permute-start(f32[8,128]{1,0:T(8,128)S(1)} %fusion.16.refs_0_), channel_id=1, source_target_pairs={{0,3},{1,2},{2,1},{3,0},{4,7},{5,6},{6,5},{7,4},{8,11},{9,10},{10,... | collective-permute-start | bytes 12296 | tf_op jit(solution)/shard_map/ppermute | solution.py:212
  67.2 2.4 %collective-permute-start.22 = (f32[8,128]{1,0:T(8,128)S(1)}, f32[8,128]{1,0:T(8,128)S(1)}, u32[]{:S(2)}, u32[]{:S(2)}) collective-permute-start(f32[8,128]{1,0:T(8,128)S(1)} %fusion.16.refs_0_), channel_id=1, source_target_pairs={{0,1},{1,0},{2,3},{3,2},{4,5},{5,4},{6,7},{7,6},{8,9},{9,8},{10,11... | collective-permute-start | bytes 12296 | tf_op jit(solution)/shard_map/ppermute | solution.py:212
  (72 shorter events, 10.3 us)
Async XLA Ops:
  0.6 11.1 %copy-start = (s32[32,256]{1,0:T(8,128)S(1)}, s32[32,256]{1,0:T(8,128)}, u32[]{:S(2)}) copy-start(s32[32,256]{1,0:T(8,128)} %land_ref.7) | copy-start | bytes 98308
  0.6 11.1 %copy-start.2 = (f32[32,256]{1,0:T(8,128)S(1)}, f32[32,256]{1,0:T(8,128)}, u32[]{:S(2)}) copy-start(f32[32,256]{1,0:T(8,128)} %logexp_ref.3) | copy-start | bytes 98308
  0.7 11.1 %copy-start.3 = (f32[16,128]{1,0:T(8,128)S(1)}, f32[16,128]{1,0:T(8,128)}, u32[]{:S(2)}) copy-start(f32[16,128]{1,0:T(8,128)} %wmom_ref.3) | copy-start | bytes 24580
  0.7 11.1 %copy-start.1 = (f32[128,128]{1,0:T(8,128)S(1)}, f32[128,128]{1,0:T(8,128)}, u32[]{:S(2)}) copy-start(f32[128,128]{1,0:T(8,128)} %pmom_ref.3) | copy-start | bytes 196612
  0.7 21.6 %copy-start.5 = (f32[16,8,256]{2,1,0:T(8,128)S(1)}, f32[16,8,256]{2,1,0:T(8,128)}, u32[]{:S(2)}) copy-start(f32[16,8,256]{2,1,0:T(8,128)} %param.13) | copy-start | bytes 393220
  0.7 21.6 %copy-start.4 = (f32[16]{0:T(128)S(1)}, f32[16]{0:T(128)}, u32[]{:S(2)}) copy-start(f32[16]{0:T(128)} %tau_ref.5) | copy-start | bytes 196
  1.6 8.1 %collective-permute-start = (f32[144,128]{1,0:T(8,128)S(1)}, f32[144,128]{1,0:T(8,128)S(1)}, u32[]{:S(2)}, u32[]{:S(2)}) collective-permute-start(f32[144,128]{1,0:T(8,128)S(1)} %pad_add_fusion.pack_ref.own_ref), channel_id=1, source_target_pairs={{0,1},{1,0},{2,3},{3,2},{4,6},{5,7},{6,4},{7,5},{8,9},{9,8},{10,11... | collective-permute-start | bytes 221192 | tf_op jit(solution)/shard_map/ppermute | solution.py:264
  4.6 5.8 %collective-permute-start.1 = (f32[72,128]{1,0:T(8,128)S(1)}, f32[72,128]{1,0:T(8,128)S(1)}, u32[]{:S(2)}, u32[]{:S(2)}) collective-permute-start(f32[72,128]{1,0:T(8,128)S(1)} %constant_dynamic-slice_fusion), channel_id=1, source_target_pairs={{0,3},{1,2},{2,1},{3,0},{4,7},{5,6},{6,5},{7,4},{8,11},{9,10},{10,... | collective-permute-start | bytes 110600 | tf_op jit(solution)/shard_map/ppermute | solution.py:212
  10.4 1.3 %collective-permute-start.2 = (f32[216,128]{1,0:T(8,128)S(1)}, f32[216,128]{1,0:T(8,128)S(1)}, u32[]{:S(2)}, u32[]{:S(2)}) collective-permute-start(f32[216,128]{1,0:T(8,128)S(1)} %constant_dynamic-update-slice_fusion.got_ref), channel_id=1, source_target_pairs={{0,4},{4,0},{8,12},{12,8},{16,20},{20,16},{24,28},{28,24},{1,5},{5... | collective-permute-start | bytes 331784 | tf_op jit(solution)/shard_map/ppermute | solution.py:212
  17.2 1.4 %collective-permute-start.3 = (f32[4,72,128]{2,1,0:T(8,128)S(1)}, f32[4,72,128]{2,1,0:T(8,128)S(1)}, u32[]{:S(2)}, u32[]{:S(2)}) collective-permute-start(f32[4,72,128]{2,1,0:T(8,128)S(1)} %get-tuple-element.55), channel_id=1, source_target_pairs={{0,4},{4,0},{8,12},{12,8},{16,20},{20,16},{24,28},{28,24},{1,5},{5... | collective-permute-start | bytes 442376 | tf_op jit(solution)/shard_map/ppermute | solution.py:212
  18.7 5.0 %collective-permute-start.4 = (f32[72,128]{1,0:T(8,128)S(1)}, f32[72,128]{1,0:T(8,128)S(1)}, u32[]{:S(2)}, u32[]{:S(2)}) collective-permute-start(f32[72,128]{1,0:T(8,128)S(1)} %get-tuple-element.93), channel_id=1, source_target_pairs={{0,8},{4,12},{8,0},{12,4},{16,24},{20,28},{24,16},{28,20},{1,9},{5... | collective-permute-start | bytes 110600 | tf_op jit(solution)/shard_map/ppermute | solution.py:212
  20.2 4.9 %collective-permute-start.6 = (f32[72,128]{1,0:T(8,128)S(1)}, f32[72,128]{1,0:T(8,128)S(1)}, u32[]{:S(2)}, u32[]{:S(2)}) collective-permute-start(f32[72,128]{1,0:T(8,128)S(1)} %get-tuple-element.94), channel_id=1, source_target_pairs={{0,24},{4,28},{8,16},{12,20},{16,8},{20,12},{24,0},{28,4},{1,25},{... | collective-permute-start | bytes 110600 | tf_op jit(solution)/shard_map/ppermute | solution.py:212
  21.7 4.0 %collective-permute-start.5 = (f32[72,128]{1,0:T(8,128)S(1)}, f32[72,128]{1,0:T(8,128)S(1)}, u32[]{:S(2)}, u32[]{:S(2)}) collective-permute-start(f32[72,128]{1,0:T(8,128)S(1)} %get-tuple-element.95), channel_id=1, source_target_pairs={{0,16},{4,20},{8,24},{12,28},{16,0},{20,4},{24,8},{28,12},{1,17},{... | collective-permute-start | bytes 110600 | tf_op jit(solution)/shard_map/ppermute | solution.py:212
  25.7 8.5 %collective-permute-start.7 = (f32[144,128]{1,0:T(8,128)S(1)}, f32[144,128]{1,0:T(8,128)S(1)}, u32[]{:S(2)}, u32[]{:S(2)}) collective-permute-start(f32[144,128]{1,0:T(8,128)S(1)} %get-tuple-element.101), channel_id=1, source_target_pairs={{0,1},{1,0},{2,3},{3,2},{4,5},{5,4},{6,7},{7,6},{8,9},{9,8},{10,11... | collective-permute-start | bytes 221192 | tf_op jit(solution)/shard_map/ppermute | solution.py:212
  25.8 8.3 %collective-permute-start.9 = (f32[144,128]{1,0:T(8,128)S(1)}, f32[144,128]{1,0:T(8,128)S(1)}, u32[]{:S(2)}, u32[]{:S(2)}) collective-permute-start(f32[144,128]{1,0:T(8,128)S(1)} %get-tuple-element.102), channel_id=1, source_target_pairs={{0,3},{1,2},{2,1},{3,0},{4,7},{5,6},{6,5},{7,4},{8,11},{9,10},{10,... | collective-permute-start | bytes 221192 | tf_op jit(solution)/shard_map/ppermute | solution.py:212
  29.0 5.2 %collective-permute-start.8 = (f32[72,128]{1,0:T(8,128)S(1)}, f32[72,128]{1,0:T(8,128)S(1)}, u32[]{:S(2)}, u32[]{:S(2)}) collective-permute-start(f32[72,128]{1,0:T(8,128)S(1)} %fusion.15), channel_id=1, source_target_pairs={{0,2},{1,3},{2,0},{3,1},{4,6},{5,7},{6,4},{7,5},{8,10},{9,11},{10,... | collective-permute-start | bytes 110600 | tf_op jit(solution)/shard_map/ppermute | solution.py:212
  34.2 4.4 %collective-permute-start.10 = (f32[144,128]{1,0:T(8,128)S(1)}, f32[144,128]{1,0:T(8,128)S(1)}, u32[]{:S(2)}, u32[]{:S(2)}) collective-permute-start(f32[144,128]{1,0:T(8,128)S(1)} %pad_maximum_fusion.4), channel_id=1, source_target_pairs={{0,8},{4,12},{8,0},{12,4},{16,24},{20,28},{24,16},{28,20},{1,9},{5... | collective-permute-start | bytes 221192 | tf_op jit(solution)/shard_map/ppermute | solution.py:212
  35.8 4.0 %collective-permute-start.11 = (f32[72,128]{1,0:T(8,128)S(1)}, f32[72,128]{1,0:T(8,128)S(1)}, u32[]{:S(2)}, u32[]{:S(2)}) collective-permute-start(f32[72,128]{1,0:T(8,128)S(1)} %get-tuple-element.89), channel_id=1, source_target_pairs={{0,16},{4,20},{8,24},{12,28},{16,0},{20,4},{24,8},{28,12},{1,17},{... | collective-permute-start | bytes 110600 | tf_op jit(solution)/shard_map/ppermute | solution.py:212
  36.3 5.3 %collective-permute-start.12 = (f32[144,128]{1,0:T(8,128)S(1)}, f32[144,128]{1,0:T(8,128)S(1)}, u32[]{:S(2)}, u32[]{:S(2)}) collective-permute-start(f32[144,128]{1,0:T(8,128)S(1)} %pad_maximum_fusion.4), channel_id=1, source_target_pairs={{0,24},{4,28},{8,16},{12,20},{16,8},{20,12},{24,0},{28,4},{1,25},{... | collective-permute-start | bytes 221192 | tf_op jit(solution)/shard_map/ppermute | solution.py:212
  41.6 1.5 %collective-permute-start.13 = (f32[360,128]{1,0:T(8,128)S(1)}, f32[360,128]{1,0:T(8,128)S(1)}, u32[]{:S(2)}, u32[]{:S(2)}) collective-permute-start(f32[360,128]{1,0:T(8,128)S(1)} %get-tuple-element.98), channel_id=1, source_target_pairs={{0,4},{4,0},{8,12},{12,8},{16,20},{20,16},{24,28},{28,24},{1,5},{5... | collective-permute-start | bytes 552968 | tf_op jit(solution)/shard_map/ppermute | solution.py:212
  48.4 1.4 %collective-permute-start.14 = (f32[4,72,128]{2,1,0:T(8,128)S(1)}, f32[4,72,128]{2,1,0:T(8,128)S(1)}, u32[]{:S(2)}, u32[]{:S(2)}) collective-permute-start(f32[4,72,128]{2,1,0:T(8,128)S(1)} %get-tuple-element.60), channel_id=1, source_target_pairs={{0,4},{4,0},{8,12},{12,8},{16,20},{20,16},{24,28},{28,24},{1,5},{5... | collective-permute-start | bytes 442376 | tf_op jit(solution)/shard_map/ppermute | solution.py:212
  49.9 6.8 %collective-permute-start.15 = (f32[72,128]{1,0:T(8,128)S(1)}, f32[72,128]{1,0:T(8,128)S(1)}, u32[]{:S(2)}, u32[]{:S(2)}) collective-permute-start(f32[72,128]{1,0:T(8,128)S(1)} %get-tuple-element.90), channel_id=1, source_target_pairs={{0,1},{1,0},{2,3},{3,2},{4,5},{5,4},{6,7},{7,6},{8,9},{9,8},{10,11... | collective-permute-start | bytes 110600 | tf_op jit(solution)/shard_map/ppermute | solution.py:212
  50.1 6.6 %collective-permute-start.17 = (f32[72,128]{1,0:T(8,128)S(1)}, f32[72,128]{1,0:T(8,128)S(1)}, u32[]{:S(2)}, u32[]{:S(2)}) collective-permute-start(f32[72,128]{1,0:T(8,128)S(1)} %get-tuple-element.91), channel_id=1, source_target_pairs={{0,3},{1,2},{2,1},{3,0},{4,7},{5,6},{6,5},{7,4},{8,11},{9,10},{10,... | collective-permute-start | bytes 110600 | tf_op jit(solution)/shard_map/ppermute | solution.py:212
  51.9 5.4 %collective-permute-start.16 = (f32[72,128]{1,0:T(8,128)S(1)}, f32[72,128]{1,0:T(8,128)S(1)}, u32[]{:S(2)}, u32[]{:S(2)}) collective-permute-start(f32[72,128]{1,0:T(8,128)S(1)} %get-tuple-element.92), channel_id=1, source_target_pairs={{0,2},{1,3},{2,0},{3,1},{4,6},{5,7},{6,4},{7,5},{8,10},{9,11},{10,... | collective-permute-start | bytes 110600 | tf_op jit(solution)/shard_map/ppermute | solution.py:212
  57.4 5.4 %collective-permute-start.20 = (f32[80,128]{1,0:T(8,128)S(1)}, f32[80,128]{1,0:T(8,128)S(1)}, u32[]{:S(2)}, u32[]{:S(2)}) collective-permute-start(f32[80,128]{1,0:T(8,128)S(1)} %constant_dynamic-update-slice_fusion.6), channel_id=1, source_target_pairs={{0,24},{4,28},{8,16},{12,20},{16,8},{20,12},{24,0},{28,4},{1,25},{... | collective-permute-start | bytes 122888 | tf_op jit(solution)/shard_map/ppermute | solution.py:212
  58.9 4.1 %collective-permute-start.19 = (f32[80,128]{1,0:T(8,128)S(1)}, f32[80,128]{1,0:T(8,128)S(1)}, u32[]{:S(2)}, u32[]{:S(2)}) collective-permute-start(f32[80,128]{1,0:T(8,128)S(1)} %constant_dynamic-update-slice_fusion.6), channel_id=1, source_target_pairs={{0,16},{4,20},{8,24},{12,28},{16,0},{20,4},{24,8},{28,12},{1,17},{... | collective-permute-start | bytes 122888 | tf_op jit(solution)/shard_map/ppermute | solution.py:212
  59.8 4.0 %collective-permute-start.18 = (f32[80,128]{1,0:T(8,128)S(1)}, f32[80,128]{1,0:T(8,128)S(1)}, u32[]{:S(2)}, u32[]{:S(2)}) collective-permute-start(f32[80,128]{1,0:T(8,128)S(1)} %constant_dynamic-update-slice_fusion.6), channel_id=1, source_target_pairs={{0,8},{4,12},{8,0},{12,4},{16,24},{20,28},{24,16},{28,20},{1,9},{5... | collective-permute-start | bytes 122888 | tf_op jit(solution)/shard_map/ppermute | solution.py:212
  63.9 1.3 %collective-permute-start.21 = (f32[80,128]{1,0:T(8,128)S(1)}, f32[80,128]{1,0:T(8,128)S(1)}, u32[]{:S(2)}, u32[]{:S(2)}) collective-permute-start(f32[80,128]{1,0:T(8,128)S(1)} %add_add_fusion), channel_id=1, source_target_pairs={{0,4},{4,0},{8,12},{12,8},{16,20},{20,16},{24,28},{28,24},{1,5},{5... | collective-permute-start | bytes 122888 | tf_op jit(solution)/shard_map/ppermute | solution.py:212
  65.2 5.7 %collective-permute-start.24 = (f32[8,128]{1,0:T(8,128)S(1)}, f32[8,128]{1,0:T(8,128)S(1)}, u32[]{:S(2)}, u32[]{:S(2)}) collective-permute-start(f32[8,128]{1,0:T(8,128)S(1)} %fusion.16.refs_0_), channel_id=1, source_target_pairs={{0,3},{1,2},{2,1},{3,0},{4,7},{5,6},{6,5},{7,4},{8,11},{9,10},{10,... | collective-permute-start | bytes 12296 | tf_op jit(solution)/shard_map/ppermute | solution.py:212
  66.8 4.5 %collective-permute-start.23 = (f32[8,128]{1,0:T(8,128)S(1)}, f32[8,128]{1,0:T(8,128)S(1)}, u32[]{:S(2)}, u32[]{:S(2)}) collective-permute-start(f32[8,128]{1,0:T(8,128)S(1)} %fusion.16.refs_0_), channel_id=1, source_target_pairs={{0,2},{1,3},{2,0},{3,1},{4,6},{5,7},{6,4},{7,5},{8,10},{9,11},{10,... | collective-permute-start | bytes 12296 | tf_op jit(solution)/shard_map/ppermute | solution.py:212
  67.2 4.1 %collective-permute-start.22 = (f32[8,128]{1,0:T(8,128)S(1)}, f32[8,128]{1,0:T(8,128)S(1)}, u32[]{:S(2)}, u32[]{:S(2)}) collective-permute-start(f32[8,128]{1,0:T(8,128)S(1)} %fusion.16.refs_0_), channel_id=1, source_target_pairs={{0,1},{1,0},{2,3},{3,2},{4,5},{5,4},{6,7},{7,6},{8,9},{9,8},{10,11... | collective-permute-start | bytes 12296 | tf_op jit(solution)/shard_map/ppermute | solution.py:212
